TPU v7x, 32 devices: a whole 2x2x4 slice. The times are simulated.
32 devices in a mesh: wide: 8 (over z, y), narrow: 4 (over x, core).
Axes of the slice: x: 2, y: 2, z: 4, core: 2. Of those that a mesh axis runs over, the one named last changes fastest.
Arguments:
- hidden: bfloat16 [4, 2048, 768], P('narrow', 'wide'), may hold values from -6 to 6
- doc_start: int32 [4, 2048], P('narrow', 'wide'), may hold values from 0 to 1, as said below
- expert_choice: int32 [2, 4, 2048], P(None, 'narrow', 'wide'), may hold values from 0 to 15, as said below
- slot_index: int32 [2, 4, 2048], P(None, 'narrow', 'wide'), may hold values from -1 to 19, as said below
- norm_mix: float32 [2, 768], replicated, may hold values from 0.1 to 1.9
- in_weight: bfloat16 [2, 768, 3072], replicated, may hold values from -0.21875 to 0.21875
- conv_weight: float32 [2, 4, 1536], replicated, may hold values from -3 to 3
- conv_bias: float32 [2, 1536], replicated, may hold values from -3 to 3
- state_weight: bfloat16 [2, 1536, 80], replicated, may hold values from -0.15625 to 0.15625
- step_weight: bfloat16 [2, 48, 1536], replicated, may hold values from -0.875 to 0.875
- step_bias: float32 [2, 1536], replicated, may hold values from -4 to -2
- decay_log: float32 [2, 16, 1536], replicated, may hold values from -11.6 to 0.5
- skip_weight: float32 [2, 1536], replicated, may hold values from 0.5 to 1.5
- out_weight: bfloat16 [2, 1536, 768], replicated, may hold values from -0.15625 to 0.15625
- norm_expert: float32 [2, 768], replicated, may hold values from 0.1 to 1.9
- router: bfloat16 [2, 768, 16], replicated, may hold values from -0.15625 to 0.15625
- expert_up: bfloat16 [2, 16, 768, 3072], P(None, 'narrow', None, 'wide'), may hold values from -0.21875 to 0.21875
- expert_down: bfloat16 [2, 16, 3072, 768], P(None, 'narrow', 'wide'), may hold values from -4 to 4
- cotangent: bfloat16 [4, 2048, 768], P('narrow', 'wide'), may hold values from -6 to 6
Outputs:
- output: bfloat16 [4, 2048, 768], P('narrow', 'wide')
- hidden_input_gradient: float32 [4, 2048, 768], P('narrow', 'wide')
- grad_norm_mix: float32 [2, 768], P(None, ('wide', 'narrow'))
- grad_in_weight: float32 [2, 768, 3072], P(None, None, ('wide', 'narrow'))
- grad_conv_weight: float32 [2, 4, 1536], P(None, None, ('wide', 'narrow'))
- grad_conv_bias: float32 [2, 1536], P(None, ('wide', 'narrow'))
- grad_state_weight: float32 [2, 1536, 80], P(None, ('wide', 'narrow'))
- grad_step_weight: float32 [2, 48, 1536], P(None, None, ('wide', 'narrow'))
- grad_step_bias: float32 [2, 1536], P(None, ('wide', 'narrow'))
- grad_decay_log: float32 [2, 16, 1536], P(None, None, ('wide', 'narrow'))
- grad_skip_weight: float32 [2, 1536], P(None, ('wide', 'narrow'))
- grad_out_weight: float32 [2, 1536, 768], P(None, ('wide', 'narrow'))
- grad_norm_expert: float32 [2, 768], P(None, ('wide', 'narrow'))
- grad_router: float32 [2, 768, 16], P(None, ('wide', 'narrow'))
- grad_expert_up: float32 [2, 16, 768, 3072], P(None, 'narrow', None, 'wide')
- grad_expert_down: float32 [2, 16, 3072, 768], P(None, 'narrow', 'wide')
Inputs may be any that keep to these rules, and one draw needn't show every extreme that they name: `doc_start`: position 0 of every sequence starts a document; in one sequence, drawn from the seed, no other position does. `expert_choice`: in every layer and every aligned block of 256 tokens of a sequence, some expert is named by more than 20 tokens. `slot_index`: A token's slot is the number of earlier tokens of its aligned block of 256 with the same expert in the same layer, or -1 where that number is 20 or more.
All inputs are finite; a program needn't handle non-finite values.
Results may differ from a plain program's by a relative error of at most 0.02.
The roundings to bfloat16 on the way count: a program that leaves them out, or rounds other values in their place, can miss the bound.
Values may be sent and summed in bfloat16 or wider, within the bound.
A program may use at most 256 MiB of HBM per device.

v0:
```python
import jax
import jax.numpy as jnp
from jax import lax
from jax.sharding import PartitionSpec as P

BLOCK = 16


EPS = 1e-05
TOP_PRECISION = lax.Precision.HIGHEST


def passed_along(x, axis, by):
    size = lax.axis_size(axis)
    pairs = [(i, i + by) for i in range(size) if 0 <= i + by < size]
    return lax.ppermute(x, axis, pairs)


def entering(value, axis, join, neutral):
    count, mine = (lax.axis_size(axis), lax.axis_index(axis))
    pieces = jax.tree.map(lambda part: lax.all_gather(part, axis), value)
    subtotal = jax.tree.map(
        lambda part, zero: jnp.full_like(part, 0) + jnp.asarray(zero, part.dtype), value, neutral
    )

    def entering_step(position, subtotal):
        longer = join(subtotal, jax.tree.map(lambda part: part[position], pieces))
        return jax.tree.map(lambda new, old: jnp.where(position < mine, new, old), longer, subtotal)

    return lax.fori_loop(0, count - 1, entering_step, subtotal)


def carried_in(x, axis, combine, identity):
    size, here = (lax.axis_size(axis), lax.axis_index(axis))
    everything = jax.tree.map(
        lambda part, kind: lax.all_gather(part.astype(kind), axis), x, (jnp.bfloat16, jnp.bfloat16)
    )
    start = jax.tree.map(
        lambda part, zero: jnp.broadcast_to(jnp.asarray(zero, part.dtype), part.shape), x, identity
    )

    def carried_step(k, before):
        at = size - 1 - k
        reached = at > here
        new = combine(
            before, jax.tree.map(lambda part, own: part[at].astype(own.dtype), everything, x)
        )
        return jax.tree.map(lambda a, b: jnp.where(reached, a, b), new, before)

    return lax.fori_loop(0, size, carried_step, start)


def rms_scale(values, gain):
    return values * lax.rsqrt(jnp.mean(values * values, axis=-1, keepdims=True) + EPS) * gain


def forward_dot(left_operand, right_operand):
    return jnp.dot(left_operand, right_operand, preferred_element_type=jnp.float32)


def rows_dot(left_operand, right_operand):
    return lax.dot_general(
        left_operand, right_operand, (((0,), (0,)), ((), ())), preferred_element_type=jnp.float32
    )


def back_dot(left_operand, right_operand):
    return lax.dot_general(
        left_operand, right_operand, (((1,), (1,)), ((), ())), preferred_element_type=jnp.float32
    )


def exact_gelu(values):
    return jax.nn.gelu(values, approximate=False)


def link_states(earlier, later):
    return (earlier[0] * later[0], later[0] * earlier[1] + later[1])


def to_blocks(values, block):
    return values.reshape((values.shape[0] // block, block) + values.shape[1:])


def rim_keep(starts, width):
    tail = 1.0 - starts[starts.shape[0] - (width - 1) :]
    later = jnp.cumprod(tail[::-1])[::-1]
    return jnp.concatenate([later[1:], jnp.ones((1,), jnp.float32)])


def conv_apply(inner_value, rim, starts, kernel, shift_bias):
    width = kernel.shape[0]
    length = inner_value.shape[0]
    extended = jnp.concatenate([rim, inner_value], axis=0)
    padded_start = jnp.concatenate([jnp.zeros((width - 1,), jnp.float32), starts])
    total = shift_bias + kernel[0] * inner_value
    alive = jnp.ones((length,), jnp.float32)
    for offset in range(1, width):
        alive = alive * (1.0 - padded_start[width - offset : width - offset + length])
        total = (
            total
            + kernel[offset]
            * extended[width - 1 - offset : width - 1 - offset + length]
            * alive[:, None]
        )
    return total


def send_rim(inner_value, keep_mask):
    edge = inner_value[inner_value.shape[0] - keep_mask.shape[0] :] * keep_mask[:, None]
    return passed_along(edge, "wide", 1)


def return_rim(grad_rim):
    return passed_along(grad_rim, "wide", -1)


def block_run(start_state, step_size, input_map, output_map, activated, starts, decay_rate):
    size = step_size.shape[0]
    level = jnp.cumsum(step_size, axis=0)[:, None, :] * decay_rate
    segment = jnp.cumsum(starts)
    position = jnp.arange(size)
    linked = (
        (position[:, None] >= position[None, :]) & (segment[:, None] == segment[None, :])
    ).astype(jnp.float32)
    inflow = (step_size * activated)[:, None, :] * input_map[:, :, None] * jnp.exp(-level)
    summed = jnp.dot(linked, inflow.reshape(size, -1), precision=TOP_PRECISION).reshape(
        inflow.shape
    )
    untouched = (segment == 0.0).astype(jnp.float32)
    states = jnp.exp(level) * (summed + untouched[:, None, None] * start_state)
    return (jnp.sum(output_map[:, :, None] * states, axis=1), states[-1])


def scan_forward(step_size, input_map, output_map, activated, starts, decay_rate, block):
    pieces = tuple(
        (
            to_blocks(values, block)
            for values in (step_size, input_map, output_map, activated, starts)
        )
    )
    zero_state = jnp.zeros(decay_rate.shape, jnp.float32)

    def advance(carry, piece):
        outputs, last = block_run(
            carry, piece[0], piece[1], piece[2], piece[3], piece[4], decay_rate
        )
        return (last, (outputs, carry))

    final_state, (outputs, begins) = lax.scan(advance, zero_state, pieces)
    combined_decay = jnp.exp(jnp.sum(step_size, axis=0) * decay_rate) * jnp.prod(1.0 - starts)
    incoming = entering(
        (combined_decay, final_state), "wide", link_states, (jnp.ones_like(decay_rate), zero_state)
    )[1]
    running = jnp.cumsum(step_size, axis=0)
    alive = jnp.cumprod(1.0 - starts)

    def carried(piece):
        running_part, alive_part, output_part = piece
        weight = (
            jnp.exp(running_part[:, None, :] * decay_rate) * alive_part[:, None, None] * incoming
        )
        return jnp.sum(output_part[:, :, None] * weight, axis=1)

    extra = lax.map(
        carried, (to_blocks(running, block), to_blocks(alive, block), to_blocks(output_map, block))
    )
    before_running = (running - step_size)[::block]
    before_alive = jnp.concatenate([jnp.ones((1,), jnp.float32), alive[:-1]])[::block]
    begins = (
        begins
        + jnp.exp(before_running[:, None, :] * decay_rate) * before_alive[:, None, None] * incoming
    )
    return ((outputs + extra).reshape(step_size.shape), begins)


def scan_backward(
    grad_y, step_size, input_map, output_map, activated, starts, decay_rate, begins, block
):
    running = jnp.cumsum(step_size, axis=0)
    alive = jnp.cumprod(1.0 - starts)

    def weighted(piece):
        running_part, alive_part, output_part, grad_part = piece
        weight = jnp.exp(running_part[:, None, :] * decay_rate) * alive_part[:, None, None]
        return jnp.sum(weight * output_part[:, :, None] * grad_part[:, None, :], axis=0)

    pushed = jnp.sum(
        lax.map(
            weighted,
            (
                to_blocks(running, block),
                to_blocks(alive, block),
                to_blocks(output_map, block),
                to_blocks(grad_y, block),
            ),
        ),
        axis=0,
    )
    combined_decay = jnp.exp(jnp.sum(step_size, axis=0) * decay_rate) * jnp.prod(1.0 - starts)
    zero_state = jnp.zeros(decay_rate.shape, jnp.float32)
    tail = carried_in(
        (combined_decay, pushed), "wide", link_states, (jnp.ones_like(decay_rate), zero_state)
    )[1]
    pieces = (begins,) + tuple(
        (
            to_blocks(values, block)
            for values in (step_size, input_map, output_map, activated, starts, grad_y)
        )
    )

    def retreat(carry, piece):
        begin, size_part, input_part, output_part, value_part, start_part, grad_part = piece

        def run(state, size_arg, input_arg, output_arg, value_arg, rate_arg):
            return block_run(
                state, size_arg, input_arg, output_arg, value_arg, start_part, rate_arg
            )

        unused, pullback = jax.vjp(
            run, begin, size_part, input_part, output_part, value_part, decay_rate
        )
        grads = pullback((grad_part, carry))
        return (grads[0], grads[1:])

    unused_state, (grad_size, grad_input, grad_output, grad_value, grad_rate) = lax.scan(
        retreat, tail, pieces, reverse=True
    )
    return (
        grad_size.reshape(step_size.shape),
        grad_input.reshape(input_map.shape),
        grad_output.reshape(output_map.shape),
        grad_value.reshape(activated.shape),
        jnp.sum(grad_rate, axis=0),
    )


def fill_rows(values, place, count):
    return jnp.zeros((count + 1, values.shape[1]), values.dtype).at[place].set(values)[:count]


def take_rows(table, place):
    return jnp.concatenate([table, jnp.zeros((1, table.shape[1]), table.dtype)], axis=0)[place]


def to_experts(values):
    return lax.all_to_all(values, "narrow", split_axis=0, concat_axis=0, tiled=True)


def to_owners(values):
    return lax.all_to_all(values, "narrow", split_axis=0, concat_axis=0, tiled=True)


def spread(values):
    return lax.all_gather(values, "wide", axis=0, tiled=True)


def partials(values):
    return lax.psum_scatter(values, "wide", scatter_dimension=0, tiled=True)


def on_device(
    hidden,
    doc_start,
    expert_choice,
    slot_index,
    norm_mix,
    in_weight,
    conv_weight,
    conv_bias,
    state_weight,
    step_weight,
    step_bias,
    decay_log,
    skip_weight,
    out_weight,
    norm_expert,
    router,
    expert_up,
    expert_down,
    cotangent,
):
    layers = in_weight.shape[0]
    tokens = hidden.shape[1]
    width = hidden.shape[2]
    inner = skip_weight.shape[1]
    rank = step_weight.shape[1]
    states = decay_log.shape[1]
    experts = router.shape[2]
    groups = lax.axis_size("narrow")
    per_group = experts // groups
    capacity = max(2, 5 * tokens // (4 * experts))
    slot_count = experts * capacity
    starts = doc_start[0].astype(jnp.float32)
    keep_mask = rim_keep(starts, conv_weight.shape[1])
    current = hidden[0].astype(jnp.float32)
    saved = []
    for layer in range(layers):
        start_value = current
        normed = rms_scale(current, norm_mix[layer]).astype(jnp.bfloat16)
        projected = forward_dot(normed, in_weight[layer])
        inner_value = projected[:, :inner]
        inner_gate = projected[:, inner:]
        rim = send_rim(inner_value, keep_mask)
        convolved = conv_apply(inner_value, rim, starts, conv_weight[layer], conv_bias[layer])
        activated_low = jax.nn.silu(convolved).astype(jnp.bfloat16)
        activated = activated_low.astype(jnp.float32)
        selection = forward_dot(activated_low, state_weight[layer])
        rank_low = selection[:, :rank].astype(jnp.bfloat16)
        step_linear = forward_dot(rank_low, step_weight[layer]) + step_bias[layer]
        step_size = jax.nn.softplus(step_linear)
        input_map = selection[:, rank : rank + states]
        output_map = selection[:, rank + states :]
        decay_rate = -jnp.exp(decay_log[layer])
        scanned, begins = scan_forward(
            step_size, input_map, output_map, activated, starts, decay_rate, BLOCK
        )
        mixer_out = scanned + skip_weight[layer] * activated
        gate_amount = jax.nn.silu(inner_gate)
        gated_low = (mixer_out * gate_amount).astype(jnp.bfloat16)
        current = current + forward_dot(gated_low, out_weight[layer])
        middle = current
        routed = rms_scale(current, norm_expert[layer]).astype(jnp.bfloat16)
        logits = forward_dot(routed, router[layer])
        shares = jax.nn.softmax(logits, axis=-1)
        chosen = expert_choice[layer, 0]
        slot_row = slot_index[layer, 0]
        onehot = (chosen[:, None] == jnp.arange(experts, dtype=jnp.int32)[None, :]).astype(
            jnp.float32
        )
        gate = jnp.sum(shares * onehot, axis=1)
        keep = (slot_row >= 0).astype(jnp.float32)
        place = jnp.where(slot_row >= 0, chosen * capacity + slot_row, slot_count)
        outbound = fill_rows(routed, place, slot_count).reshape(groups, per_group * capacity, width)
        arrived = to_experts(outbound).reshape(groups, per_group, capacity, width)
        kept_rows = spread(arrived)
        pre_act = jnp.einsum(
            "sgcd,gdf->sgcf", kept_rows, expert_up[layer], preferred_element_type=jnp.float32
        )
        hidden_low = exact_gelu(pre_act).astype(jnp.bfloat16)
        expert_rows = partials(
            jnp.einsum(
                "sgcf,gfd->sgcd", hidden_low, expert_down[layer], preferred_element_type=jnp.float32
            )
        )
        returned = to_owners(
            expert_rows.astype(jnp.bfloat16).reshape(groups, per_group * capacity, width)
        )
        back_rows = take_rows(returned.reshape(slot_count, width), place).astype(jnp.float32)
        current = current + (keep * gate)[:, None] * back_rows
        saved.append(
            {
                "start": start_value,
                "normed": normed,
                "inner_value": inner_value,
                "inner_gate": inner_gate,
                "rim": rim,
                "convolved": convolved,
                "activated_low": activated_low,
                "activated": activated,
                "rank_low": rank_low,
                "step_linear": step_linear,
                "step_size": step_size,
                "input_map": input_map,
                "output_map": output_map,
                "decay_rate": decay_rate,
                "begins": begins,
                "mixer_out": mixer_out,
                "gate_value": gate_amount,
                "gated_low": gated_low,
                "middle": middle,
                "routed": routed,
                "shares": shares,
                "onehot": onehot,
                "gate": gate,
                "keep": keep,
                "place": place,
                "kept_rows": kept_rows,
                "pre_act": pre_act,
                "hidden_low": hidden_low,
                "back_rows": back_rows,
            }
        )
    output = current.astype(jnp.bfloat16)[None]
    grad = cotangent[0].astype(jnp.float32)
    collected = [None] * layers
    up_grads = [None] * layers
    down_grads = [None] * layers
    for layer in range(layers - 1, -1, -1):
        entry = saved[layer]
        place = entry["place"]
        grad_rows_low = ((entry["keep"] * entry["gate"])[:, None] * grad).astype(jnp.bfloat16)
        grad_gate = entry["keep"] * jnp.sum(grad * entry["back_rows"], axis=1)
        outbound = fill_rows(grad_rows_low, place, slot_count).reshape(
            groups, per_group * capacity, width
        )
        grad_arrived = to_experts(outbound).reshape(groups, per_group, capacity, width)
        unused_gelu, gelu_back = jax.vjp(exact_gelu, entry["pre_act"])
        grad_spread = spread(grad_arrived)
        grad_down = jnp.einsum(
            "sgcf,sgcd->gfd", entry["hidden_low"], grad_spread, preferred_element_type=jnp.float32
        )
        grad_hidden_rows = jnp.einsum(
            "sgcd,gfd->sgcf", grad_spread, expert_down[layer], preferred_element_type=jnp.float32
        )
        grad_pre = gelu_back(grad_hidden_rows)[0].astype(jnp.bfloat16)
        grad_up = jnp.einsum(
            "sgcd,sgcf->gdf", entry["kept_rows"], grad_pre, preferred_element_type=jnp.float32
        )
        grad_rows_in = partials(
            jnp.einsum(
                "sgcf,gdf->sgcd", grad_pre, expert_up[layer], preferred_element_type=jnp.float32
            )
        )
        up_grads[layer] = grad_up
        down_grads[layer] = grad_down
        inbound = to_owners(
            grad_rows_in.astype(jnp.bfloat16).reshape(groups, per_group * capacity, width)
        )
        grad_sent = take_rows(inbound.reshape(slot_count, width), place).astype(jnp.float32)
        grad_logits_low = (
            (grad_gate * entry["gate"])[:, None] * (entry["onehot"] - entry["shares"])
        ).astype(jnp.bfloat16)
        grad_router = rows_dot(entry["routed"], grad_logits_low)
        grad_routed = grad_sent + back_dot(grad_logits_low, router[layer])
        unused_norm, norm_back = jax.vjp(rms_scale, entry["middle"], norm_expert[layer])
        grad_middle, grad_norm_expert = norm_back(grad_routed)
        grad = grad + grad_middle
        grad_low = grad.astype(jnp.bfloat16)
        grad_out_weight = rows_dot(entry["gated_low"], grad_low)
        grad_gated = back_dot(grad_low, out_weight[layer])
        grad_y = grad_gated * entry["gate_value"]
        unused_silu, silu_back = jax.vjp(jax.nn.silu, entry["inner_gate"])
        grad_igate = silu_back(grad_gated * entry["mixer_out"])[0]
        grad_skip_weight = jnp.sum(grad_y * entry["activated"], axis=0)
        grad_size, grad_input_map, grad_output_map, scan_value_gradient, grad_rate = scan_backward(
            grad_y,
            entry["step_size"],
            entry["input_map"],
            entry["output_map"],
            entry["activated"],
            starts,
            entry["decay_rate"],
            entry["begins"],
            BLOCK,
        )
        grad_activated = grad_y * skip_weight[layer] + scan_value_gradient
        grad_decay_log = grad_rate * entry["decay_rate"]
        unused_soft, soft_back = jax.vjp(jax.nn.softplus, entry["step_linear"])
        grad_linear = soft_back(grad_size)[0]
        grad_step_bias = jnp.sum(grad_linear, axis=0)
        grad_linear_low = grad_linear.astype(jnp.bfloat16)
        grad_step_weight = rows_dot(entry["rank_low"], grad_linear_low)
        grad_selection = jnp.concatenate(
            [back_dot(grad_linear_low, step_weight[layer]), grad_input_map, grad_output_map], axis=1
        ).astype(jnp.bfloat16)
        grad_state_weight = rows_dot(entry["activated_low"], grad_selection)
        grad_activated = grad_activated + back_dot(grad_selection, state_weight[layer])
        unused_conv, conv_silu_back = jax.vjp(jax.nn.silu, entry["convolved"])
        grad_convolved = conv_silu_back(grad_activated)[0]

        def convolve(values, edge, kernel, shift_bias):
            return conv_apply(values, edge, starts, kernel, shift_bias)

        unused_mix, conv_back = jax.vjp(
            convolve, entry["inner_value"], entry["rim"], conv_weight[layer], conv_bias[layer]
        )
        grad_value, grad_rim, grad_conv_weight, grad_conv_bias = conv_back(grad_convolved)
        handed = return_rim(grad_rim)
        grad_value = grad_value.at[tokens - keep_mask.shape[0] :].add(handed * keep_mask[:, None])
        grad_projected = jnp.concatenate([grad_value, grad_igate], axis=1).astype(jnp.bfloat16)
        grad_in_weight = rows_dot(entry["normed"], grad_projected)
        grad_normed = back_dot(grad_projected, in_weight[layer])
        unused_first, first_back = jax.vjp(rms_scale, entry["start"], norm_mix[layer])
        grad_start, grad_norm_mix = first_back(grad_normed)
        grad = grad + grad_start
        collected[layer] = (
            grad_norm_mix,
            grad_in_weight,
            grad_conv_weight,
            grad_conv_bias,
            grad_state_weight,
            grad_step_weight,
            grad_step_bias,
            grad_decay_log,
            grad_skip_weight,
            grad_out_weight,
            grad_norm_expert,
            grad_router,
        )
    stacked = [jnp.stack([collected[index][item] for index in range(layers)]) for item in range(12)]
    stacked = (
        lax.psum_scatter(stacked[0], ("wide", "narrow"), scatter_dimension=1, tiled=True),
        lax.psum_scatter(stacked[1], ("wide", "narrow"), scatter_dimension=2, tiled=True),
        lax.psum_scatter(stacked[2], ("wide", "narrow"), scatter_dimension=2, tiled=True),
        lax.psum_scatter(stacked[3], ("wide", "narrow"), scatter_dimension=1, tiled=True),
        lax.psum_scatter(stacked[4], ("wide", "narrow"), scatter_dimension=1, tiled=True),
        lax.psum_scatter(stacked[5], ("wide", "narrow"), scatter_dimension=2, tiled=True),
        lax.psum_scatter(stacked[6], ("wide", "narrow"), scatter_dimension=1, tiled=True),
        lax.psum_scatter(stacked[7], ("wide", "narrow"), scatter_dimension=2, tiled=True),
        lax.psum_scatter(stacked[8], ("wide", "narrow"), scatter_dimension=1, tiled=True),
        lax.psum_scatter(stacked[9], ("wide", "narrow"), scatter_dimension=1, tiled=True),
        lax.psum_scatter(stacked[10], ("wide", "narrow"), scatter_dimension=1, tiled=True),
        lax.psum_scatter(stacked[11], ("wide", "narrow"), scatter_dimension=1, tiled=True),
    )
    return (
        output,
        grad[None],
        stacked[0],
        stacked[1],
        stacked[2],
        stacked[3],
        stacked[4],
        stacked[5],
        stacked[6],
        stacked[7],
        stacked[8],
        stacked[9],
        stacked[10],
        stacked[11],
        jnp.stack(up_grads),
        jnp.stack(down_grads),
    )


def solution(mesh):
    placed = (
        P("narrow", "wide", None),
        P("narrow", "wide"),
        P(None, "narrow", "wide"),
        P(None, "narrow", "wide"),
        P(),
        P(),
        P(),
        P(),
        P(),
        P(),
        P(),
        P(),
        P(),
        P(),
        P(),
        P(),
        P(None, "narrow", None, "wide"),
        P(None, "narrow", "wide", None),
        P("narrow", "wide", None),
    )
    return jax.shard_map(
        on_device,
        mesh=mesh,
        in_specs=placed,
        out_specs=(
            P("narrow", "wide", None),
            P("narrow", "wide", None),
            P(None, ("wide", "narrow")),
            P(None, None, ("wide", "narrow")),
            P(None, None, ("wide", "narrow")),
            P(None, ("wide", "narrow")),
            P(None, ("wide", "narrow"), None),
            P(None, None, ("wide", "narrow")),
            P(None, ("wide", "narrow")),
            P(None, None, ("wide", "narrow")),
            P(None, ("wide", "narrow")),
            P(None, ("wide", "narrow"), None),
            P(None, ("wide", "narrow")),
            P(None, ("wide", "narrow"), None),
            P(None, "narrow", None, "wide"),
            P(None, "narrow", "wide", None),
        ),
        check_vma=False,
    )
```

profile of v0, /device:TPU:0, one launch (start us, length us, event | category | flops | bytes accessed | tf_op | source)
XLA Modules:
  0.0 4024.5 jit_solution(6891556829414421044)
XLA Ops:
  49.1 147.2 %while.190 = (s32[]{:T(128)}, f32[16,1536]{1,0:T(8,128)S(1)}, f32[16,16,1536]{2,1,0:T(8,128)}, f32[16,16,1536]{2,1,0:T(8,128)}, f32[16,16,1536]{2,1,0:T(8,128)},...) while((s32[]{:T(128)}, f32[16,1536]{1,0:T(8,128)S(1)}, ...), condition=%wide.wide.region_6.7_spmd, body=%wide.wide.region_2.6_spmd.sunk | while | flops 79799312 | bytes 19867072 | solution.py:150
  196.3 32.4 all-gather
  228.7 43.8 %all_gather.48 = f32[8,16,1536]{2,1,0:T(8,128)S(1)} all-gather(f32[1,16,1536]{2,1,0:T(8,128)} %get-tuple-element.2178), channel_id=1, replica_groups=mesh['wide'=8,'narrow'=4] {'wide'}, dimensions={0}, use_global_device_ids=true | all-gather | bytes 884736 | tf_op jit(solution)/shard_map/all_gather | solution.py:21
  273.1 47.1 %while.182 = (s32[]{:T(128)}, f32[16,16,1536]{2,1,0:T(8,128)S(1)}, f32[16,16,16]{2,1,0:T(8,128)}, f32[16,16,1536]{2,1,0:T(8,128)}, f32[16,1536]{1,0:T(8,128)S(1)...) while((s32[]{:T(128)}, f32[16,16,1536]{2,1,0:T(8,128)S(1)}, f32[16,16,16]{2,1,0:T(8,128)}, ...), condition=%wide.region_17.18_spmd, body=%wide.region_15.17_spmd.sunk | while | flops 1941506 | bytes 789797 | solution.py:165
  328.7 11.0 all_to_all.40
  343.5 65.5 %all-gather.9.cloned.1.call-done = bf16[32,4,20,768]{3,1,2,0:T(4,128)(2,1)} async-done(((bf16[4,4,20,768]{3,1,2,0:T(4,128)(2,1)}), bf16[32,4,20,768]{3,1,2,0:T(4,128)(2,1)}) %all-gather.9.cloned.1.call-update) | async-done | bytes 3932176 | tf_op jit(solution)/shard_map/all_gather | solution.py:255
  409.0 15.8 fusion.115
  426.1 7.1 convolution_bitcast_fusion.7
  433.2 304.4 %all-reduce.39 = bf16[32,4,20,768]{3,0,2,1:T(8,128)(2,1)} all-reduce(f32[32,4,20,768]{3,0,2,1:T(8,128)} %convolution_bitcast_fusion.7), channel_id=6, replica_groups=mesh['wide'=8,'narrow'=4] {'wide'}, use_global_device_ids=true, to_apply=%region_23.24.clone | all-reduce | flops 1966080 | bytes 11796480
  743.6 8.3 all-to-all-done.1
  781.9 147.2 %while.191 = (s32[]{:T(128)}, f32[16,1536]{1,0:T(8,128)S(1)}, f32[16,16,1536]{2,1,0:T(8,128)}, f32[16,16,1536]{2,1,0:T(8,128)}, f32[16,16,1536]{2,1,0:T(8,128)},...) while((s32[]{:T(128)}, f32[16,1536]{1,0:T(8,128)S(1)}, ...), condition=%wide.wide.region_29.30_spmd, body=%wide.wide.region_25.29_spmd.sunk | while | flops 79799312 | bytes 19867072 | solution.py:150
  929.1 33.9 all-gather.1
  963.0 32.5 all_gather.52
  996.1 47.4 %while.183 = (s32[]{:T(128)}, f32[16,16,1536]{2,1,0:T(8,128)S(1)}, f32[16,16,16]{2,1,0:T(8,128)}, f32[16,16,1536]{2,1,0:T(8,128)}, f32[16,1536]{1,0:T(8,128)S(1)...) while((s32[]{:T(128)}, f32[16,16,1536]{2,1,0:T(8,128)S(1)}, f32[16,16,16]{2,1,0:T(8,128)}, ...), condition=%wide.region_37.38_spmd, body=%wide.region_35.37_spmd.sunk | while | flops 1941506 | bytes 789797 | solution.py:165
  1053.6 10.9 all_to_all.41
  1068.3 10.9 all_to_all.42
  1080.5 54.7 %all-gather.11.cloned.1.call-done = bf16[32,4,20,768]{3,1,2,0:T(4,128)(2,1)} async-done(((bf16[4,4,20,768]{3,1,2,0:T(4,128)(2,1)}), bf16[32,4,20,768]{3,1,2,0:T(4,128)(2,1)}) %all-gather.11.cloned.1.call-update) | async-done | bytes 3932176 | tf_op jit(solution)/shard_map/all_gather | solution.py:255
  1135.3 16.5 fusion.113
  1151.8 54.2 %all-gather.13.cloned.1.call-done = bf16[32,4,20,768]{3,1,2,0:T(4,128)(2,1)} async-done(((bf16[4,4,20,768]{3,1,2,0:T(4,128)(2,1)}), bf16[32,4,20,768]{3,1,2,0:T(4,128)(2,1)}) %all-gather.13.cloned.1.call-update) | async-done | bytes 3932176 | tf_op jit(solution)/shard_map/all_gather | solution.py:255
  1205.9 8.8 fusion.110
  1214.8 7.9 convolution_bitcast_fusion.5
  1222.7 7.1 convolution_bitcast_fusion.6
  1229.8 602.5 %all-reduce.40 = (bf16[32,4,20,768]{3,0,2,1:T(8,128)(2,1)}, bf16[32,4,20,768]{3,0,2,1:T(8,128)(2,1)}) all-reduce(f32[32,4,20,768]{3,0,2,1:T(8,128)} %convolution_bitcast_fusion.6, f32[32,4,20,768]{3,0,2,1:T(8,128)} %convolution_bitcast_fusion.5), channel_id=7, replica_groups=mesh['wide'=8,'narrow'=4] {'wide'}, use_global_device_ids=true, to_apply=%region_43.44.clone | all-reduce | flops 3932160 | bytes 23592960
  1856.4 33.2 all_gather.57
  1903.2 44.8 %while.184 = (s32[]{:T(128)}, f32[16,16,1536]{2,1,0:T(8,128)S(1)}, f32[16,16,1536]{2,1,0:T(8,128)}, f32[16,1536]{1,0:T(8,128)S(1)}, f32[16,16]{1,0:T(8,128)}, /*...) while((s32[]{:T(128)}, f32[16,16,1536]{2,1,0:T(8,128)S(1)}, f32[16,16,1536]{2,1,0:T(8,128)}, ...), condition=%wide.region_50.51_spmd, body=%wide.region_48.50_spmd.sunk | while | flops 1941506 | bytes 986405 | solution.py:189
  1948.1 31.2 all-gather.2
  1979.3 7.1 while.188
  1991.7 251.1 %while.192 = (s32[]{:T(128)}, f32[16,1536]{1,0:T(8,128)S(1)}, f32[16,16,1536]{2,1,0:T(8,128)}, bf16[16,16,16]{1,2,0:T(8,128)(2,1)}, bf16[16,16,16]{1,2,0:T(8,128...) while((s32[]{:T(128)}, f32[16,1536]{1,0:T(8,128)S(1)}, ...), condition=%wide.wide.region_64.65_spmd, body=%wide.wide.region_54.64_spmd.sunk | while | flops 167462160 | bytes 31969480 | solution.py:226
  2268.4 11.5 all_to_all.43
  2281.9 34.1 all_gather.60
  2326.7 23.5 all-gather.15.cloned.1.call-done
  2350.2 8.8 fusion.103
  2360.3 7.1 convolution_bitcast_fusion.4
  2367.5 304.4 %all-reduce.41 = bf16[32,4,20,768]{3,0,2,1:T(8,128)(2,1)} all-reduce(f32[32,4,20,768]{3,0,2,1:T(8,128)} %convolution_bitcast_fusion.4), channel_id=9, replica_groups=mesh['wide'=8,'narrow'=4] {'wide'}, use_global_device_ids=true, to_apply=%region_67.68.clone | all-reduce | flops 1966080 | bytes 11796480
  2697.3 44.5 %while.185 = (s32[]{:T(128)}, f32[16,16,1536]{2,1,0:T(8,128)S(1)}, f32[16,16,1536]{2,1,0:T(8,128)}, f32[16,1536]{1,0:T(8,128)S(1)}, f32[16,16]{1,0:T(8,128)}, /*...) while((s32[]{:T(128)}, f32[16,16,1536]{2,1,0:T(8,128)S(1)}, f32[16,16,1536]{2,1,0:T(8,128)}, ...), condition=%wide.region_72.73_spmd, body=%wide.region_70.72_spmd.sunk | while | flops 1941506 | bytes 986405 | solution.py:189
  2741.9 31.5 all-gather.3
  2773.4 7.1 while.189
  2785.9 248.6 %while.193 = (s32[]{:T(128)}, f32[16,1536]{1,0:T(8,128)S(1)}, f32[16,16,1536]{2,1,0:T(8,128)}, bf16[16,16,16]{1,2,0:T(8,128)(2,1)}, bf16[16,16,16]{1,2,0:T(8,128...) while((s32[]{:T(128)}, f32[16,1536]{1,0:T(8,128)S(1)}, ...), condition=%wide.wide.region_86.87_spmd, body=%wide.wide.region_76.86_spmd.sunk | while | flops 167462160 | bytes 31182992 | solution.py:226
  3040.9 7.3 multiply_reduce_fusion.25
  3075.8 10.9 pad_maximum_fusion
  3086.8 28.2 copy.297
  3152.9 90.2 %reduce-scatter.31.cloned.1.call-done = f32[48,2]{1,0:T(8,128)} async-done(((f32[1536,2]{1,0:T(8,128)}), f32[48,2]{1,0:T(8,128)}) %reduce-scatter.31.cloned.1.call-update) | async-done | bytes 400
  3249.0 40.2 all-reduce.30
  3292.3 50.6 %reduce-scatter.29.cloned.1.call-done = f32[48,8]{1,0:T(8,128)} async-done(((f32[1536,8]{1,0:T(8,128)}), f32[48,8]{1,0:T(8,128)}) %reduce-scatter.29.cloned.1.call-update) | async-done | bytes 1552
  3344.3 98.2 %reduce-scatter.37.cloned.1.call-done = f32[48,32]{1,0:T(8,128)} async-done(((f32[1536,32]{1,0:T(8,128)}), f32[48,32]{1,0:T(8,128)}) %reduce-scatter.37.cloned.1.call-update) | async-done | bytes 6160
  3444.1 98.0 %reduce-scatter.33.cloned.1.call-done = f32[48,96]{1,0:T(8,128)} async-done(((f32[1536,96]{1,0:T(8,128)}), f32[48,96]{1,0:T(8,128)}) %reduce-scatter.33.cloned.1.call-update) | async-done | bytes 18448
  3543.7 331.1 %all-reduce.38.cloned.1.call-done = (f32[2,768,3072]{1,0,2:T(2,128)}, f32[2,1536,80]{2,0,1:T(2,128)}, f32[2,768,16]{1,2,0:T(8,128)}) async-done(((f32[2,768,3072]{1,0,2:T(2,128)}, f32[2,1536,80]{2,0,1:T(2,128)}, f32[2,768,16]{1,2,0:T(8,128)}), (f32[2,768,3072]{1,0,2:T(2,128)}, f32[2,1536,80]{2,0,1:T(2,128)}, f32[2,768,16]{1,2,0:T(8,128)})) %all-reduce.38.cloned.1.call-update) | async-done | bytes 19955728
  3879.6 137.9 %reduce-scatter.27.cloned.1.call-done = f32[2,48,768]{2,1,0:T(8,128)} async-done(((f32[2,1536,768]{2,1,0:T(8,128)}), f32[2,48,768]{2,1,0:T(8,128)}) %reduce-scatter.27.cloned.1.call-update) | async-done | bytes 294928 | tf_op jit(solution)/shard_map/reduce_scatter | solution.py:502
  (2729 shorter events, 1292.7 us)
Async XLA Ops:
  7.2 401.8 %all-gather.9.cloned.1.call-start = ((), (), s32[]{:S(2)}) async-start(), calls=%async_computation.15 | async-start | bytes 4423680 | tf_op jit(solution)/shard_map/all_gather | solution.py:255
  8.0 745.4 %copy-start.108 = (f32[768]{0:T(1024)}, f32[768]{0:T(1024)S(1)}, u32[]{:S(2)}) copy-start(f32[768]{0:T(1024)S(1)} %get-tuple-element.1962) | copy-start | bytes 9220
  16.3 13.0 collective-permute-start
  26.9 316.1 %copy-start.115 = (f32[768]{0:T(1024)}, f32[768]{0:T(1024)S(1)}, u32[]{:S(2)}) copy-start(f32[768]{0:T(1024)S(1)} %get-tuple-element.1961) | copy-start | bytes 9220
  272.9 47.3 %copy-start.33 = (f32[16,16,1536]{2,1,0:T(8,128)S(1)}, f32[16,16,1536]{2,1,0:T(8,128)}, u32[]{:S(2)}) copy-start(f32[16,16,1536]{2,1,0:T(8,128)} %get-tuple-element.1342) | copy-start | bytes 4718596
  326.8 426.3 %copy-start = (f32[256,768]{1,0:T(8,128)}, f32[256,768]{1,0:T(8,128)S(1)}, u32[]{:S(2)}) copy-start(f32[256,768]{1,0:T(8,128)S(1)} %get-tuple-element.2258) | copy-start | bytes 2359300
  342.4 409.5 %copy-start.190 = (s32[1024]{0:T(1024)}, s32[1024]{0:T(1024)S(1)}, u32[]{:S(2)}) copy-start(s32[1024]{0:T(1024)S(1)} %pad_clamp_fusion.1) | copy-start | bytes 12292
  343.0 400.5 %copy-start.218 = (pred[256]{0:T(512)(128)(4,1)}, pred[256]{0:T(512)(128)(4,1)S(1)}, u32[]{:S(2)}) copy-start(pred[256]{0:T(512)(128)(4,1)S(1)} %get-tuple-element.1965) | copy-start | bytes 772
  343.0 400.4 %copy-start.172 = (s32[1,1,256]{2,1,0:T(1,128)}, s32[1,1,256]{2,1,0:T(1,128)S(1)}, u32[]{:S(2)}) copy-start(s32[1,1,256]{2,1,0:T(1,128)S(1)} %get-tuple-element.2248) | copy-start | bytes 3076
  343.0 1551.0 %copy-start.175 = (s32[1,1,256]{2,1,0:T(1,128)}, s32[1,1,256]{2,1,0:T(1,128)S(1)}, u32[]{:S(2)}) copy-start(s32[1,1,256]{2,1,0:T(1,128)S(1)} %get-tuple-element.2247) | copy-start | bytes 3076
  343.2 81.6 %copy-start.49 = (bf16[256,768]{1,0:T(8,128)(2,1)}, bf16[256,768]{1,0:T(8,128)(2,1)S(1)}, u32[]{:S(2)}) copy-start(bf16[256,768]{1,0:T(8,128)(2,1)S(1)} %multiply_convert_fusion.7) | copy-start | bytes 1179652
  343.5 400.0 %copy-start.89 = (f32[256,16]{0,1:T(8,128)}, f32[256,16]{0,1:T(8,128)S(1)}, u32[]{:S(2)}) copy-start(f32[256,16]{0,1:T(8,128)S(1)} %get-tuple-element.2261) | copy-start | bytes 49156
  343.5 400.0 %copy-start.149 = (f32[256]{0:T(256)}, f32[256]{0:T(256)S(1)}, u32[]{:S(2)}) copy-start(f32[256]{0:T(256)S(1)} %get-tuple-element.2260) | copy-start | bytes 3076
  739.9 11.9 all-to-all-start.1
  743.4 391.9 %all-gather.11.cloned.1.call-start = ((), (), s32[]{:S(2)}) async-start(), calls=%async_computation.16 | async-start | bytes 4423680 | tf_op jit(solution)/shard_map/all_gather | solution.py:255
  759.2 3.5 collective-permute-start.1
  929.1 66.4 %copy-start.58 = (f32[16,1536]{1,0:T(8,128)S(1)}, f32[16,1536]{1,0:T(8,128)}, u32[]{:S(2)}) copy-start(f32[16,1536]{1,0:T(8,128)} %custom-call.1) | copy-start | bytes 294916
  1065.8 140.1 %all-gather.13.cloned.1.call-start = ((), (), s32[]{:S(2)}) async-start(), calls=%async_computation.17 | async-start | bytes 4423680 | tf_op jit(solution)/shard_map/all_gather | solution.py:255
  1066.3 827.8 %copy-start.91 = (f32[256,16]{0,1:T(8,128)}, f32[256,16]{0,1:T(8,128)S(1)}, u32[]{:S(2)}) copy-start(f32[256,16]{0,1:T(8,128)S(1)} %get-tuple-element.2268) | copy-start | bytes 49156
  1066.3 827.8 %copy-start.152 = (f32[256]{0:T(256)}, f32[256]{0:T(256)S(1)}, u32[]{:S(2)}) copy-start(f32[256]{0:T(256)S(1)} %get-tuple-element.2267) | copy-start | bytes 3076
  1066.4 827.7 %copy-start.169 = (f32[256]{0:T(256)}, f32[256]{0:T(256)S(1)}, u32[]{:S(2)}) copy-start(f32[256]{0:T(256)S(1)} %fusion.329) | copy-start | bytes 3076
  1835.1 12.1 all-to-all-start.5
  1847.1 42.5 %all-to-all-start.3 = ((bf16[4,80,768]{2,1,0:T(8,128)(2,1)}), bf16[4,80,768]{2,1,0:T(8,128)(2,1)}, u32[]{:S(2)}, u32[]{:S(2)}) async-start(bf16[4,80,768]{2,1,0:T(8,128)(2,1)} %copy.278), calls=%async_computation.3 | async-start | bytes 983040 | tf_op jit(solution)/shard_map/all_to_all | solution.py:251
  1851.3 498.9 %all-gather.15.cloned.1.call-start = ((), (), s32[]{:S(2)}) async-start(), calls=%async_computation.18 | async-start | bytes 4423680 | tf_op jit(solution)/shard_map/all_gather | solution.py:255
  2254.4 5.7 collective-permute-start.2
  2280.1 35.9 copy-start.208
  2280.2 36.5 copy-start.144
  2280.2 37.1 copy-start.213
  2280.2 37.7 copy-start.212
  2280.2 38.3 copy-start.211
  2280.2 38.8 copy-start.210
  2280.2 39.4 copy-start.209
  2281.2 41.2 %copy-start.92 = (f32[256,16]{0,1:T(8,128)S(1)}, f32[256,16]{0,1:T(8,128)}, u32[]{:S(2)}) copy-start(f32[256,16]{0,1:T(8,128)} %copy-done.91) | copy-start | bytes 49156
  2281.3 42.6 %copy-start.8 = (bf16[256,1536]{1,0:T(8,128)(2,1)S(1)}, bf16[256,1536]{1,0:T(8,128)(2,1)}, u32[]{:S(2)}) copy-start(bf16[256,1536]{1,0:T(8,128)(2,1)} %copy-done.6) | copy-start | bytes 2359300
  2281.3 42.6 %copy-start.119 = (bf16[256,48]{0,1:T(8,128)(2,1)S(1)}, bf16[256,48]{0,1:T(8,128)(2,1)}, u32[]{:S(2)}) copy-start(bf16[256,48]{0,1:T(8,128)(2,1)} %copy-done.118) | copy-start | bytes 73732
  2281.3 42.6 %copy-start.143 = (bf16[256,16]{0,1:T(8,128)(2,1)S(1)}, bf16[256,16]{0,1:T(8,128)(2,1)}, u32[]{:S(2)}) copy-start(bf16[256,16]{0,1:T(8,128)(2,1)} %copy-done.142) | copy-start | bytes 24580
  2674.2 11.9 all-to-all-start.7
  2677.7 472.4 %reduce-scatter.39.cloned.1.call-start = ((), (), s32[]{:S(2)}) async-start(), calls=%async_computation.25 | async-start | bytes 811008
  2697.1 454.5 %reduce-scatter.35.cloned.1.call-start = ((), (), s32[]{:S(2)}) async-start(), calls=%async_computation.23 | async-start | bytes 811008
  3049.7 193.4 %reduce-scatter.31.cloned.1.call-start = ((), (), s32[]{:S(2)}) async-start(), calls=%async_computation.21 | async-start | bytes 811008
  3052.0 290.9 %reduce-scatter.29.cloned.1.call-start = ((), (), s32[]{:S(2)}) async-start(), calls=%async_computation.20 | async-start | bytes 811008
  3056.0 386.6 %reduce-scatter.37.cloned.1.call-start = ((), (), s32[]{:S(2)}) async-start(), calls=%async_computation.24 | async-start | bytes 811008
  3067.1 6.0 collective-permute-start.3
  3068.4 473.7 %reduce-scatter.33.cloned.1.call-start = ((), (), s32[]{:S(2)}) async-start(), calls=%async_computation.22 | async-start | bytes 811008
  3070.9 803.9 %all-reduce.38.cloned.1.call-start = ((), (), s32[]{:S(2)}) async-start(), calls=%async_computation.26 | async-start | bytes 41091072
  3115.1 902.4 %reduce-scatter.27.cloned.1.call-start = ((), (), s32[]{:S(2)}) async-start(), calls=%async_computation.19 | async-start | bytes 9732096 | tf_op jit(solution)/shard_map/reduce_scatter | solution.py:502
  3145.7 98.8 %copy-start.71 = (bf16[256,1536]{1,0:T(8,128)(2,1)S(1)}, bf16[256,1536]{1,0:T(8,128)(2,1)}, u32[]{:S(2)}) copy-start(bf16[256,1536]{1,0:T(8,128)(2,1)} %copy-done.70) | copy-start | bytes 2359300
  3145.7 98.8 %copy-start.82 = (bf16[256,1536]{1,0:T(8,128)(2,1)S(1)}, bf16[256,1536]{1,0:T(8,128)(2,1)}, u32[]{:S(2)}) copy-start(bf16[256,1536]{1,0:T(8,128)(2,1)} %get-tuple-element.2221) | copy-start | bytes 2359300
  (295 other events, 926.8 us)
Sparse Core Ops, SparseCore 0:
  341.2 67.7 all-gather.8
  1066.0 69.2 all-gather.10
  1137.5 68.4 all-gather.12
  2281.4 68.7 all-gather.14
  2697.2 93.9 reduce-scatter.38
  3049.8 93.4 reduce-scatter.34
  3148.4 94.5 reduce-scatter.30
  3248.2 94.5 reduce-scatter.28
  3347.9 94.5 reduce-scatter.36
  3447.5 94.5 reduce-scatter.32
  3548.6 326.1 all-reduce.37
  3882.1 135.3 reduce-scatter.26
where the time goes:
time: 4060 us; the launch traced here: 4020 us
  blocking collectives  1570 us (39%)
  waiting for transfers between devices  1020 us (25%)
  local copies, waits for them, and re-layouts  705 us (17%)
  other arithmetic  372 us (9%)
  matrix products  304 us (7%)
    unnamed x4, blocking collectives  1250 us
    unnamed x19, waiting for transfers between devices  668 us
    all_gather x4, waiting for transfers between devices, spread(): return lax.all_gather(values, 'wide', axis=0, tiled=True)  198 us
    all_gather x4, blocking collectives, entering(): pieces = jax.tree.map(lambda part: lax.all_gather(part, axis), value)  143 us
    dot_general x96, matrix products, block_run(): jnp.dot(linked, inflow.reshape(size, -1), precision=TOP_PRECISION)  138 us
    reduce_scatter x1, waiting for transfers between devices, on_device(): lax.psum_scatter(stacked[9], ('wide', 'narrow'), scatter_dimension=1, til...  138 us
    all_gather x4, blocking collectives, carried_in(): lax.all_gather(part.astype(kind), axis)  130 us
    while x320, local copies, waits for them, and re-layouts  88.6 us
  transfers between devices with their start and end apart: 20, of which 15 were waited for; matrix products, arithmetic and copies ran while one was open for 12% of the time, Pallas kernels for 0%

commit v1 on v0

v1 whole, which is shorter than its diff:
```python
import functools

import jax
import jax.numpy as jnp
from jax import lax
from jax.experimental import pallas as pl
from jax.experimental.pallas import tpu as pltpu
from jax.sharding import PartitionSpec as P

EPS = 1e-05
CHUNKS = 8
LANES = 128
LOG2E = 1.4426950408889634
RESET = 1e9
MIB = 1024 * 1024
MESH = pl.DeviceIdType.MESH
VMEM = pltpu.VMEM


def to_steps(values):
    steps = values.shape[0] // CHUNKS
    return jnp.swapaxes(values.reshape((CHUNKS, steps) + values.shape[1:]), 0, 1)


def to_tokens(values):
    moved = jnp.swapaxes(values, 0, 1)
    return moved.reshape((-1,) + values.shape[2:])


def rms_scale(values, gain):
    return values * lax.rsqrt(jnp.mean(values * values, axis=-1, keepdims=True) + EPS) * gain


def rms_back(values, gain, grad):
    scale = lax.rsqrt(jnp.mean(values * values, axis=-1, keepdims=True) + EPS)
    weighted = grad * gain
    inner = jnp.mean(weighted * values, axis=-1, keepdims=True)
    return (
        scale * weighted - values * (scale * scale * scale) * inner,
        jnp.sum(grad * values * scale, axis=0),
    )


def dot_nn(left, right):
    return lax.dot_general(left, right, (((1,), (0,)), ((), ())), preferred_element_type=jnp.float32)


def dot_nt(left, right):
    return lax.dot_general(left, right, (((1,), (1,)), ((), ())), preferred_element_type=jnp.float32)


def dot_tn(left, right):
    return lax.dot_general(left, right, (((0,), (0,)), ((), ())), preferred_element_type=jnp.float32)


def passed_along(x, by):
    size = lax.axis_size("wide")
    return lax.ppermute(x, "wide", [(i, i + by) for i in range(size) if 0 <= i + by < size])


def with_rim(values, rim):
    count = rim.shape[0]
    tail = values[values.shape[0] - count :, : CHUNKS - 1]
    return jnp.concatenate([jnp.concatenate([rim[:, None], tail], axis=1), values], axis=0)


def keep_masks(starts, taps):
    extended = with_rim(starts[..., None], jnp.zeros((taps - 1, 1), jnp.float32))
    steps = starts.shape[0]
    alive = jnp.ones(starts.shape + (1,), jnp.float32)
    masks = []
    for offset in range(1, taps):
        back = taps - offset
        alive = alive * (1.0 - extended[back : back + steps])
        masks.append(alive)
    return jnp.broadcast_to(jnp.stack(masks), (taps - 1,) + starts.shape + (LANES,))


def rim_keep(starts, count):
    tail = 1.0 - starts[starts.shape[0] - count :, CHUNKS - 1]
    later = jnp.cumprod(tail[::-1])[::-1]
    return jnp.concatenate([later[1:], jnp.ones((1,), jnp.float32)])


def microseconds(count):
    return pl.CostEstimate(flops=int(count * 1.0e9), transcendentals=0, bytes_accessed=1000000)


def plain_call(kernel, grid, in_specs, out_specs, out_shapes, scratch, args, cost):
    return pl.pallas_call(
        kernel,
        grid=grid,
        in_specs=in_specs,
        out_specs=out_specs,
        out_shape=out_shapes,
        scratch_shapes=scratch,
        compiler_params=pltpu.CompilerParams(
            dimension_semantics=("arbitrary",), vmem_limit_bytes=48 * MIB
        ),
        cost_estimate=microseconds(cost),
    )(*args)


def shaped(shape, kind=jnp.float32):
    return jax.ShapeDtypeStruct(shape, kind)


def slab(steps, first=0):
    return pl.BlockSpec((steps, CHUNKS, LANES), lambda c: (0, 0, first + c))


def rows_of(count):
    return pl.BlockSpec((count, LANES), lambda c: (0, c))


def layer_rows(layer, count):
    return pl.BlockSpec((None, count, LANES), lambda c: (layer, 0, c))


def layer_columns(layer, count):
    return pl.BlockSpec((None, LANES, count), lambda c: (layer, c, 0))


def layer_whole(layer, shape):
    return pl.BlockSpec((None,) + shape, lambda c: (layer,) + (0,) * len(shape))


def whole(shape):
    return pl.BlockSpec(shape, lambda c: (0,) * len(shape))


ANYWHERE = pl.BlockSpec(memory_space=pl.ANY)


def spread_columns(selection_ref, first, states, out_ref):
    def one(step, carry):
        tile = selection_ref[step]
        for n in range(states):
            out_ref[step, n] = jnp.broadcast_to(tile[:, first + n : first + n + 1], (CHUNKS, LANES))
        return carry

    lax.fori_loop(0, selection_ref.shape[0], one, 0)


def rate_rows(rate):
    return [jnp.broadcast_to(rate[n : n + 1, :], (CHUNKS, LANES)) for n in range(rate.shape[0])]


def rates_of(decay_log):
    return -jnp.exp(decay_log) * LOG2E


def two_steps(ref, pair, lanes=slice(None)):
    both = ref[pl.ds(pl.multiple_of(pair * 2 * CHUNKS, 2 * CHUNKS), 2 * CHUNKS), lanes]
    both = both.astype(jnp.float32)
    return both[:CHUNKS], both[CHUNKS:]


def chunk_links(found, sizes, rates, reverse):
    place = lax.broadcasted_iota(jnp.int32, (CHUNKS, LANES), 0)
    if reverse:
        place = CHUNKS - 1 - place
    last = 0 if reverse else CHUNKS - 1

    def shifted(values, by):
        turned = pltpu.roll(values, CHUNKS - by if reverse else by, axis=0)
        return jnp.where(place >= by, turned, 0.0)

    lengths = [sizes]
    for by in (1, 2, 4):
        lengths.append(lengths[-1] + shifted(lengths[-1], by))
    links, totals = [], []
    for n, rate in enumerate(rates):
        level = found[n]
        for index, by in enumerate((1, 2, 4)):
            level = level + jnp.exp2(lengths[index] * rate) * shifted(level, by)
        links.append(shifted(level, 1))
        totals.append(level[last : last + 1])
    return links, totals, shifted(lengths[-1], 1), lengths[-1][last : last + 1]


def conv_slab(extended, step, mask_ref, kernel_ref, bias, taps):
    total = bias + kernel_ref[0:1, :] * extended[step + taps - 1]
    tiles = total.shape[1] // LANES
    for offset in range(1, taps):
        mask = mask_ref[offset - 1, step]
        mask = jnp.concatenate([mask] * tiles, axis=1) if tiles > 1 else mask
        total = total + kernel_ref[offset : offset + 1, :] * (
            extended[step + taps - 1 - offset] * mask
        )
    return total


def extend(value_ref, rim_ref, extended, taps):
    steps = value_ref.shape[0]
    place = lax.broadcasted_iota(jnp.int32, value_ref.shape[1:], 0)
    for j in range(taps - 1):
        turned = pltpu.roll(value_ref[steps - taps + 1 + j], 1, axis=0)
        extended[j] = jnp.where(place == 0, rim_ref[j : j + 1, :], turned)
    extended[taps - 1 :] = value_ref[...]


def front_kernel(dims, value_ref, rim_ref, mask_ref, reset_ref, conv_ref, conv_bias_ref, state_ref,
                 step_ref, step_bias_ref, decay_ref,
                 act_ref, selection_ref, size_ref, link_ref, link_size_ref, total_ref, total_size_ref,
                 extended, maps):
    taps, rank, states, steps, channels = dims
    extend(value_ref, rim_ref, extended, taps)
    bias = conv_bias_ref[...]

    def conv_pair(pair, carry):
        both = []
        for step in (2 * pair, 2 * pair + 1):
            both.append(jax.nn.silu(conv_slab(extended, step, mask_ref, conv_ref, bias, taps)))
        at = pl.ds(pl.multiple_of(pair * 2 * CHUNKS, 2 * CHUNKS), 2 * CHUNKS)
        act_ref[at, :] = jnp.concatenate(both, axis=0).astype(jnp.bfloat16)
        return carry

    lax.fori_loop(0, steps // 2, conv_pair, 0)
    selection = dot_nn(act_ref[...], state_ref[...])
    selection_ref[...] = selection.reshape(steps, CHUNKS, selection.shape[1])
    rank_low = selection[:, :rank].astype(jnp.bfloat16)

    def size_tile(c, carry):
        lanes = pl.ds(pl.multiple_of(c * 256, 256), 256)
        linear = dot_nn(rank_low, step_ref[:, lanes]) + step_bias_ref[:, lanes]
        size_ref[:, :, lanes] = jax.nn.softplus(linear).reshape(steps, CHUNKS, 256)
        return carry

    lax.fori_loop(0, channels // 256, size_tile, 0)
    spread_columns(selection_ref, rank, states, maps)

    def end_tile(c, carry):
        lanes = pl.ds(pl.multiple_of(c * LANES, LANES), LANES)
        rates = rate_rows(rates_of(decay_ref[:, lanes]))

        def one(pair, carry):
            levels, length = list(carry[:states]), carry[states]
            acts = two_steps(act_ref, pair, lanes)
            for half in (0, 1):
                step = 2 * pair + half
                size = size_ref[step, :, lanes]
                value = size * acts[half]
                size = size + reset_ref[step]
                for n in range(states):
                    levels[n] = jnp.exp2(size * rates[n]) * levels[n] + value * maps[step, n]
                length = length + size
            return tuple(levels) + (length,)

        zero = jnp.zeros((CHUNKS, LANES), jnp.float32)
        found = lax.fori_loop(0, steps // 2, one, (zero,) * (states + 1))
        links, totals, link_size, total_size = chunk_links(found, found[states], rates, False)
        link_size_ref[:, lanes] = link_size
        total_size_ref[:, lanes] = total_size
        for n in range(states):
            link_ref[n, :, lanes] = links[n]
            total_ref[n : n + 1, lanes] = totals[n]
        return carry

    lax.fori_loop(0, channels // LANES, end_tile, 0)


def mixer_front(layer, projected, rim, masks, reset, conv_weight, conv_bias, state_weight, step_weight,
                step_bias, decay_log):
    steps = projected.shape[0]
    channels = conv_weight.shape[2]
    taps, rank, states = conv_weight.shape[1], step_weight.shape[1], decay_log.shape[1]
    columns = state_weight.shape[2]
    value = pl.BlockSpec((steps, CHUNKS, channels), lambda c: (0, 0, 0))
    shapes = [
        shaped((steps * CHUNKS, channels), jnp.bfloat16),
        shaped((steps, CHUNKS, columns)),
        shaped((steps, CHUNKS, channels)),
        shaped((states, CHUNKS, channels)),
        shaped((CHUNKS, channels)),
        shaped((states, channels)),
        shaped((1, channels)),
    ]
    return plain_call(
        functools.partial(front_kernel, (taps, rank, states, steps, channels)),
        (1,),
        [value, whole(rim.shape), whole(masks.shape), whole(reset.shape),
         layer_whole(layer, conv_weight.shape[1:]), layer_whole(layer, conv_bias.shape[1:]),
         layer_whole(layer, state_weight.shape[1:]), layer_whole(layer, step_weight.shape[1:]),
         layer_whole(layer, step_bias.shape[1:]), layer_whole(layer, decay_log.shape[1:])],
        [whole(s.shape) for s in shapes],
        shapes,
        [VMEM((steps + taps - 1, CHUNKS, channels), jnp.float32),
         VMEM((steps, states, CHUNKS, LANES), jnp.float32)],
        (projected, rim, masks, reset, conv_weight, conv_bias, state_weight, step_weight, step_bias,
         decay_log),
        18,
    )


def run_kernel(dims, size_ref, act_ref, selection_ref, reset_ref, decay_ref, link_ref, link_size_ref,
               entering_ref, gate_ref, skip_ref, out_weight_ref, current_ref, norm_ref, router_ref, fill_ref,
               mixed_ref, gated_ref, begin_ref, middle_ref, routed_ref, logits_ref, outbound_ref,
               in_maps, out_maps):
    rank, states, steps, tiles = dims

    @pl.when(pl.program_id(0) == 0)
    def _():
        spread_columns(selection_ref, rank, states, in_maps)
        spread_columns(selection_ref, rank + states, states, out_maps)
        middle_ref[...] = current_ref[...]

    rates = rate_rows(rates_of(decay_ref[...]))
    link_size = link_size_ref[...]
    skip = skip_ref[...]
    begin = []
    for n in range(states):
        first = link_ref[n] + jnp.exp2(link_size * rates[n]) * entering_ref[n : n + 1, :]
        begin_ref[n] = first
        begin.append(first)

    def one(pair, carry):
        levels = list(carry)
        acts = two_steps(act_ref, pair)
        both = []
        for half in (0, 1):
            step = 2 * pair + half
            size = size_ref[step]
            value = size * acts[half]
            size = size + reset_ref[step]
            sums = [skip * acts[half], None]
            for n in range(states):
                levels[n] = jnp.exp2(size * rates[n]) * levels[n] + value * in_maps[step, n]
                term = out_maps[step, n] * levels[n]
                sums[n % 2] = term if sums[n % 2] is None else sums[n % 2] + term
            mixed = sums[0] + sums[1]
            mixed_ref[step] = mixed
            both.append(mixed * jax.nn.silu(gate_ref[step]))
        at = pl.ds(pl.multiple_of(pair * 2 * CHUNKS, 2 * CHUNKS), 2 * CHUNKS)
        gated_ref[at, :] = jnp.concatenate(both, axis=0).astype(jnp.bfloat16)
        return tuple(levels)

    lax.fori_loop(0, steps // 2, one, tuple(begin))
    middle_ref[...] += dot_nn(gated_ref[...], out_weight_ref[...])

    @pl.when(pl.program_id(0) == tiles - 1)
    def _():
        routed = rms_scale(middle_ref[...], norm_ref[...]).astype(jnp.bfloat16)
        routed_ref[...] = routed
        logits_ref[...] = dot_nn(routed, router_ref[...])
        outbound_ref[...] = dot_nn(fill_ref[...], routed).astype(jnp.bfloat16)


def mixer_run(layer, size, act, selection, reset, decay_log, link, link_size, entering, projected, skip_weight,
              out_weight, current, norm_expert, router, fill):
    steps, _, channels = size.shape
    tokens = steps * CHUNKS
    states, width, experts = decay_log.shape[1], current.shape[1], router.shape[2]
    rank = selection.shape[2] - 2 * states
    tiles = channels // LANES
    low = jnp.bfloat16
    maps = VMEM((steps, states, CHUNKS, LANES), jnp.float32)
    return plain_call(
        functools.partial(run_kernel, (rank, states, steps, tiles)),
        (tiles,),
        [slab(steps), rows_of(tokens), whole(selection.shape), whole(reset.shape),
         layer_rows(layer, states), slab(states), rows_of(CHUNKS), rows_of(states), slab(steps, tiles),
         layer_rows(layer, 1), layer_columns(layer, width), whole(current.shape),
         layer_whole(layer, (1, width)), layer_whole(layer, (width, experts)), whole(fill.shape)],
        [slab(steps), rows_of(tokens), slab(states), whole((tokens, width)), whole((tokens, width)),
         whole((tokens, experts)), whole((fill.shape[0], width))],
        [
            shaped((steps, CHUNKS, channels)),
            shaped((tokens, channels), low),
            shaped((states, CHUNKS, channels)),
            shaped((tokens, width)),
            shaped((tokens, width), low),
            shaped((tokens, experts)),
            shaped((fill.shape[0], width), low),
        ],
        [maps, maps],
        (size, act, selection, reset, decay_log, link, link_size, entering, projected, skip_weight, out_weight,
         current, norm_expert, router, fill),
        22,
    )


def turn_kernel(dims, grad_ref, out_weight_ref, gate_ref, mixed_ref, act_ref, gated_ref, size_ref,
                selection_ref, reset_ref, decay_ref,
                grad_y_ref, grad_gate_ref, grad_skip_ref, grad_out_ref, link_ref, link_size_ref, total_ref,
                total_size_ref, maps, held):
    rank, states, steps = dims

    @pl.when(pl.program_id(0) == 0)
    def _():
        spread_columns(selection_ref, rank + states, states, maps)

    grad = grad_ref[...]
    grad_out_ref[...] = dot_tn(gated_ref[...], grad).astype(jnp.bfloat16)
    held[...] = dot_nt(grad, out_weight_ref[...]).reshape(steps, CHUNKS, LANES)
    rates = rate_rows(rates_of(decay_ref[...]))

    def one(at, carry):
        levels, length, skip = list(carry[:states]), carry[states], carry[states + 1]
        pair = steps // 2 - 1 - at
        acts = two_steps(act_ref, pair)
        both = [None, None]
        for half in (1, 0):
            step = 2 * pair + half
            gate = gate_ref[step]
            share = jax.nn.sigmoid(gate)
            gated = held[step]
            grad_y = gated * (gate * share)
            both[half] = gated * mixed_ref[step] * (share * (1.0 + gate * (1.0 - share)))
            grad_y_ref[step] = grad_y
            skip = skip + grad_y * acts[half]
            size = size_ref[step] + reset_ref[step]
            for n in range(states):
                levels[n] = jnp.exp2(size * rates[n]) * (levels[n] + grad_y * maps[step, n])
            length = length + size
        rows = pl.ds(pl.multiple_of(pair * 2 * CHUNKS, 2 * CHUNKS), 2 * CHUNKS)
        grad_gate_ref[rows, :] = jnp.concatenate(both, axis=0).astype(jnp.bfloat16)
        return tuple(levels) + (length, skip)

    zero = jnp.zeros((CHUNKS, LANES), jnp.float32)
    found = lax.fori_loop(0, steps // 2, one, (zero,) * (states + 2))
    grad_skip_ref[...] = jnp.sum(found[states + 1], axis=0, keepdims=True)
    links, totals, link_size, total_size = chunk_links(found, found[states], rates, True)
    link_size_ref[...] = link_size
    total_size_ref[...] = total_size
    for n in range(states):
        link_ref[n] = links[n]
        total_ref[n : n + 1, :] = totals[n]


def mixer_turn(layer, grad_low, out_weight, projected, mixed, act, gated, size, selection, reset, decay_log):
    steps, _, channels = size.shape
    tokens = steps * CHUNKS
    states, width = decay_log.shape[1], grad_low.shape[1]
    rank = selection.shape[2] - 2 * states
    tiles = channels // LANES
    low = jnp.bfloat16
    return plain_call(
        functools.partial(turn_kernel, (rank, states, steps)),
        (tiles,),
        [whole(grad_low.shape), layer_columns(layer, width), slab(steps, tiles), slab(steps), rows_of(tokens),
         rows_of(tokens), slab(steps), whole(selection.shape), whole(reset.shape), layer_rows(layer, states)],
        [slab(steps), rows_of(tokens), rows_of(1), pl.BlockSpec((LANES, width), lambda c: (c, 0)),
         slab(states), rows_of(CHUNKS), rows_of(states), rows_of(1)],
        [
            shaped((steps, CHUNKS, channels)),
            shaped((tokens, channels), low),
            shaped((1, channels)),
            shaped((channels, width), low),
            shaped((states, CHUNKS, channels)),
            shaped((CHUNKS, channels)),
            shaped((states, channels)),
            shaped((1, channels)),
        ],
        [VMEM((steps, states, CHUNKS, LANES), jnp.float32), VMEM((steps, CHUNKS, LANES), jnp.float32)],
        (grad_low, out_weight, projected, mixed, act, gated, size, selection, reset, decay_log),
        14,
    )


def back_kernel(dims, size_ref, act_ref, grad_ref, decay_ref, selection_ref, reset_ref, begin_ref, link_ref,
                link_size_ref, entering_ref, step_ref, step_bias_ref, skip_ref,
                grad_act_ref, grad_decay_ref, grad_bias_ref, grad_step_ref, grad_selection_ref,
                in_maps, out_maps, levels, decays, grad_in, grad_out, grad_size, grad_rate, grad_rank):
    rank, states, steps, tiles = dims
    tokens = steps * CHUNKS

    @pl.when(pl.program_id(0) == 0)
    def _():
        spread_columns(selection_ref, rank, states, in_maps)
        spread_columns(selection_ref, rank + states, states, out_maps)
        grad_in[...] = jnp.zeros_like(grad_in)
        grad_out[...] = jnp.zeros_like(grad_out)
        grad_rank[...] = jnp.zeros_like(grad_rank)

    true_rates = -jnp.exp(decay_ref[...])
    rates = rate_rows(true_rates * LOG2E)
    skip = skip_ref[...]
    begin = []
    for n in range(states):
        levels[0, n] = begin_ref[n]
        begin.append(begin_ref[n])

    def ahead(pair, carry):
        now = list(carry)
        acts = two_steps(act_ref, pair)
        for half in (0, 1):
            step = 2 * pair + half
            size = size_ref[step]
            value = size * acts[half]
            size = size + reset_ref[step]
            for n in range(states):
                decay = jnp.exp2(size * rates[n])
                decays[step, n] = decay
                now[n] = decay * now[n] + value * in_maps[step, n]
                levels[step + 1, n] = now[n]
        return tuple(now)

    lax.fori_loop(0, steps // 2, ahead, tuple(begin))
    link_size = link_size_ref[...]
    tail = []
    for n in range(states):
        tail.append(link_ref[n] + jnp.exp2(link_size * rates[n]) * entering_ref[n : n + 1, :])
        grad_rate[n] = jnp.zeros((CHUNKS, LANES), jnp.float32)

    def retreat(at, carry):
        passed = list(carry)
        pair = steps // 2 - 1 - at
        acts = two_steps(act_ref, pair)
        for half in (1, 0):
            step = 2 * pair + half
            plain = size_ref[step]
            act = acts[half]
            grad = grad_ref[step]
            value = plain * act
            by_rate = jnp.zeros((CHUNKS, LANES), jnp.float32)
            by_input = jnp.zeros((CHUNKS, LANES), jnp.float32)
            for n in range(states):
                lanes = slice(n * LANES, (n + 1) * LANES)
                back = out_maps[step, n] * grad + passed[n]
                grad_out[step, :, lanes] += grad * levels[step + 1, n]
                grad_in[step, :, lanes] += back * value
                by_input = by_input + back * in_maps[step, n]
                passed[n] = decays[step, n] * back
                pull = passed[n] * levels[step, n]
                by_rate = by_rate + pull * rates[n]
                grad_rate[n] += pull * plain
            grad_size[step] = by_rate * (1.0 / LOG2E) + act * by_input
            grad_act_ref[step] = plain * by_input + grad * skip
        return tuple(passed)

    lax.fori_loop(0, steps // 2, retreat, tuple(tail))
    for n in range(states):
        grad_decay_ref[n : n + 1, :] = (
            jnp.sum(grad_rate[n], axis=0, keepdims=True) * true_rates[n : n + 1, :]
        )
    rank_low = selection_ref[...].reshape(tokens, selection_ref.shape[2])[:, :rank].astype(jnp.bfloat16)
    linear = dot_nn(rank_low, step_ref[...]) + step_bias_ref[...]
    grad_linear = grad_size[...].reshape(tokens, LANES) * jax.nn.sigmoid(linear)
    grad_bias_ref[...] = jnp.sum(grad_linear, axis=0, keepdims=True)
    grad_low = grad_linear.astype(jnp.bfloat16)
    grad_step_ref[...] = dot_tn(rank_low, grad_low)
    grad_rank[...] += dot_nt(grad_low, step_ref[...])

    @pl.when(pl.program_id(0) == tiles - 1)
    def _():
        size = states * LANES
        row = lax.broadcasted_iota(jnp.int32, (size, states), 0)
        column = lax.broadcasted_iota(jnp.int32, (size, states), 1)
        pick = ((row >= column * LANES) & (row < (column + 1) * LANES)).astype(jnp.float32)
        pick = pick.astype(jnp.bfloat16)
        found = [grad_rank[...]]
        for ref in (grad_in, grad_out):
            full = ref[...].reshape(tokens, size)
            high = full.astype(jnp.bfloat16)
            rest = (full - high.astype(jnp.float32)).astype(jnp.bfloat16)
            found.append(dot_nn(high, pick) + dot_nn(rest, pick))
        grad_selection_ref[...] = jnp.concatenate(found, axis=1).astype(jnp.bfloat16)


def mixer_back(layer, size, act, grad_y, decay_log, selection, reset, begin, link, link_size, entering,
               step_weight, step_bias, skip_weight):
    steps, _, channels = size.shape
    tokens = steps * CHUNKS
    states = decay_log.shape[1]
    columns = selection.shape[2]
    rank = columns - 2 * states
    tiles = channels // LANES
    f32 = jnp.float32
    maps = VMEM((steps, states, CHUNKS, LANES), f32)
    return plain_call(
        functools.partial(back_kernel, (rank, states, steps, tiles)),
        (tiles,),
        [slab(steps), rows_of(tokens), slab(steps), layer_rows(layer, states), whole(selection.shape),
         whole(reset.shape), slab(states), slab(states), rows_of(CHUNKS), rows_of(states),
         layer_rows(layer, rank), layer_rows(layer, 1), layer_rows(layer, 1)],
        [slab(steps), rows_of(states), rows_of(1), rows_of(rank), whole((tokens, columns))],
        [
            shaped((steps, CHUNKS, channels)),
            shaped((states, channels)),
            shaped((1, channels)),
            shaped((rank, channels)),
            shaped((tokens, columns), jnp.bfloat16),
        ],
        [maps, maps, VMEM((steps + 1, states, CHUNKS, LANES), f32), maps,
         VMEM((steps, CHUNKS, states * LANES), f32), VMEM((steps, CHUNKS, states * LANES), f32),
         VMEM((steps, CHUNKS, LANES), f32), VMEM((states, CHUNKS, LANES), f32), VMEM((tokens, rank), f32)],
        (size, act, grad_y, decay_log, selection, reset, begin, link, link_size, entering, step_weight,
         step_bias, skip_weight),
        35,
    )


def conv_back_kernel(dims, grad_act_ref, grad_selection_ref, state_ref, value_ref, rim_ref, mask_ref,
                     conv_ref, conv_bias_ref, act_ref, grad_step_ref, grad_decay_ref, grad_bias_ref,
                     grad_skip_ref, grad_value_ref, edge_ref, rim_grad_ref, channel_ref,
                     extended, passed):
    taps, states, steps = dims
    tokens = steps * CHUNKS
    extend(value_ref, rim_ref, extended, taps)
    bias = conv_bias_ref[...]
    grad_selection = grad_selection_ref[...]
    from_selection = dot_nt(grad_selection, state_ref[...]).reshape(steps, CHUNKS, LANES)
    passed[:steps] = grad_act_ref[...] + from_selection
    passed[steps:] = jnp.zeros((taps - 1, CHUNKS, LANES), jnp.float32)
    zero = jnp.zeros((CHUNKS, LANES), jnp.float32)

    def ahead(step, carry):
        convolved = conv_slab(extended, step, mask_ref, conv_ref, bias, taps)
        share = jax.nn.sigmoid(convolved)
        grad = passed[step] * (share * (1.0 + convolved * (1.0 - share)))
        passed[step] = grad
        new = [carry[0] + grad, carry[1] + grad * extended[step + taps - 1]]
        for offset in range(1, taps):
            kept = grad * mask_ref[offset - 1, step]
            new.append(carry[offset + 1] + kept * extended[step + taps - 1 - offset])
        return tuple(new)

    sums = lax.fori_loop(0, steps, ahead, (zero,) * (taps + 1), unroll=4)

    def reach(step, last):
        total = zero
        for offset in range(last):
            at = step + offset
            part = conv_ref[offset : offset + 1, :] * passed[at]
            if offset:
                part = part * mask_ref[offset - 1, at]
            total = total + part
        return total

    def back(pair, carry):
        both = [reach(2 * pair + half, taps) for half in (0, 1)]
        rows = pl.ds(pl.multiple_of(pair * 2 * CHUNKS, 2 * CHUNKS), 2 * CHUNKS)
        grad_value_ref[rows, :] = jnp.concatenate(both, axis=0).astype(jnp.bfloat16)
        return carry

    safe = (steps - taps + 1) // 2
    lax.fori_loop(0, safe, back, 0, unroll=2)
    place = lax.broadcasted_iota(jnp.int32, (CHUNKS, LANES), 0)
    ends = {}
    for j in range(taps - 1):
        before = zero
        for offset in range(taps - 1 - j, taps):
            at = j - taps + 1 + offset
            before = before + conv_ref[offset : offset + 1, :] * (
                passed[at] * mask_ref[offset - 1, at]
            )
        rim_grad_ref[j : j + 1, :] = before[0:1]
        ends[steps - taps + 1 + j] = jnp.where(
            place < CHUNKS - 1, pltpu.roll(before, CHUNKS - 1, axis=0), 0.0
        )
    for pair in range(safe, steps // 2):
        both = []
        for step in (2 * pair, 2 * pair + 1):
            total = reach(step, min(taps, steps - step))
            if step in ends:
                total = total + ends[step]
                j = step - steps + taps - 1
                edge_ref[j : j + 1, :] = total[CHUNKS - 1 : CHUNKS]
            both.append(total)
        grad_value_ref[2 * pair * CHUNKS : (2 * pair + 2) * CHUNKS, :] = jnp.concatenate(
            both, axis=0
        ).astype(jnp.bfloat16)
    small = jnp.zeros((CHUNKS, LANES), jnp.float32)
    rows = [jnp.sum(part, axis=0, keepdims=True) for part in sums[1:] + sums[:1]]
    rows += [grad_bias_ref[...], grad_skip_ref[...]]
    for index, row in enumerate(rows):
        small = jnp.where(place == index, row, small)
    grad_state = dot_tn(grad_selection, act_ref[...])
    parts = [grad_state, grad_step_ref[...], grad_decay_ref[...], small]
    used = sum(part.shape[0] for part in parts)
    parts.append(jnp.zeros((2 * LANES - used, LANES), jnp.float32))
    channel_ref[...] = jnp.concatenate(parts, axis=0).T.astype(jnp.bfloat16)


def mixer_conv_back(layer, grad_act, grad_selection, state_weight, projected, rim, masks, conv_weight,
                    conv_bias, act, grad_step, grad_decay, grad_bias, grad_skip):
    steps, _, channels = grad_act.shape
    tokens = steps * CHUNKS
    taps, columns = conv_weight.shape[1], state_weight.shape[2]
    states, rank = grad_decay.shape[0], grad_step.shape[0]
    tiles = channels // LANES
    f32 = jnp.float32
    return plain_call(
        functools.partial(conv_back_kernel, (taps, states, steps)),
        (tiles,),
        [slab(steps), whole(grad_selection.shape), layer_columns(layer, columns), slab(steps),
         rows_of(taps - 1), whole(masks.shape), layer_rows(layer, taps), layer_rows(layer, 1),
         rows_of(tokens), rows_of(rank), rows_of(states), rows_of(1), rows_of(1)],
        [rows_of(tokens), rows_of(taps - 1), rows_of(taps - 1),
         pl.BlockSpec((LANES, 2 * LANES), lambda c: (c, 0))],
        [
            shaped((tokens, channels), jnp.bfloat16),
            shaped((taps - 1, channels)),
            shaped((taps - 1, channels)),
            shaped((channels, 2 * LANES), jnp.bfloat16),
        ],
        [VMEM((steps + taps - 1, CHUNKS, LANES), f32), VMEM((steps + taps - 1, CHUNKS, LANES), f32)],
        (grad_act, grad_selection, state_weight, projected, rim, masks, conv_weight, conv_bias, act, grad_step,
         grad_decay, grad_bias, grad_skip),
        10,
    )


def link_kernel(layer, count, reverse, total_ref, size_ref, decay_ref, out_ref,
                mine, mine_length, near, near_length, both, both_length, far, far_length,
                send, recv, send_length, recv_length):
    here = lax.axis_index("wide")
    group = lax.axis_index("narrow")
    pairs = count // 2
    pair, side = here // 2, lax.rem(here, 2)
    partner = here + 1 - 2 * side
    others = [lax.rem(pair + k, pairs) for k in range(1, pairs)]
    f32 = jnp.float32
    barrier = pltpu.get_barrier_semaphore()
    pl.semaphore_signal(barrier, inc=1, device_id=(partner, group), device_id_type=MESH)
    for other in others:
        pl.semaphore_signal(barrier, inc=1, device_id=(2 * other + side, group), device_id_type=MESH)
    mine[...] = total_ref[...].astype(mine.dtype)
    mine_length[...] = size_ref[...]
    rate = rates_of(decay_ref[layer])
    pl.semaphore_wait(barrier, pairs)

    def hand(index, source, source_length, target, target_length, window):
        copies = []
        for src, dst, out, back in (
            (source, target, send, recv), (source_length, target_length, send_length, recv_length)):
            copies.append(pltpu.make_async_remote_copy(
                src_ref=src, dst_ref=dst, send_sem=out.at[index], recv_sem=back.at[index],
                device_id=(window, group), device_id_type=MESH))
            copies[-1].start()
        return copies

    first = hand(0, mine, mine_length, near, near_length, partner)
    for copy in first:
        copy.wait_recv()
    second_here = (side == 0) if reverse else (side == 1)
    own, own_length = total_ref[...], size_ref[...]
    met, met_length = near[...].astype(f32), near_length[...]
    late_length = jnp.where(second_here, own_length, met_length)
    early = jnp.where(second_here, met, own)
    late = jnp.where(second_here, own, met)
    both[...] = (jnp.exp2(late_length * rate) * early + late).astype(both.dtype)
    both_length[...] = own_length + met_length
    sent = []
    for k, other in enumerate(others):
        sent.append(hand(
            1 + k, both, both_length, far.at[pair], far_length.at[pair], 2 * other + side))
    for copies in sent:
        for copy in copies:
            copy.wait_recv()
    level = jnp.zeros(own.shape, f32)
    for at in range(pairs - 1, -1, -1) if reverse else range(pairs):
        valid = (pair < at) if reverse else (pair > at)
        step = jnp.exp2(far_length[at] * rate) * level + far[at].astype(f32)
        level = jnp.where(valid, step, level)
    step = jnp.exp2(met_length * rate) * level + met
    out_ref[...] = jnp.where(second_here, step, level)
    for copies in [first] + sent:
        for copy in copies:
            copy.wait_send()


def handed_on(layer, total, size, decay_log, reverse, identity):
    count = lax.axis_size("wide")
    pairs = count // 2
    states, channels = total.shape
    f32, low = jnp.float32, jnp.bfloat16
    dma = pltpu.SemaphoreType.DMA((pairs,))
    return pl.pallas_call(
        functools.partial(link_kernel, layer, count, reverse),
        out_shape=jax.ShapeDtypeStruct((states, channels), f32),
        in_specs=[pl.BlockSpec(memory_space=VMEM)] * 3,
        out_specs=pl.BlockSpec(memory_space=VMEM),
        scratch_shapes=[
            VMEM((states, channels), low),
            VMEM((1, channels), f32),
            VMEM((states, channels), low),
            VMEM((1, channels), f32),
            VMEM((states, channels), low),
            VMEM((1, channels), f32),
            VMEM((pairs, states, channels), low),
            VMEM((pairs, 1, channels), f32),
            dma, dma, dma, dma,
        ],
        compiler_params=pltpu.CompilerParams(
            collective_id=identity, has_side_effects=True, vmem_limit_bytes=16 * MIB
        ),
        cost_estimate=microseconds(12),
    )(total, size, decay_log)


def gelu_parts(values):
    bell = 0.5 * (1.0 + lax.erf(values * 0.7071067811865476))
    return bell


def expert_kernel(dims, backward, layer, *refs):
    count, groups, experts, block, share, width, hidden = dims
    if backward:
        (out_ref, perm_ref, up_hbm, down_hbm, pre_hbm, ret_ref, rows_hbm, low_hbm,
         arrived, rows, pre, low, part, got, final, landed, up, down,
         there_send, there_recv, gather_send, gather_recv, sum_send, sum_recv,
         back_send, back_recv, local) = refs
    else:
        (out_ref, perm_ref, up_hbm, down_hbm, ret_ref, rows_hbm, pre_hbm, low_hbm,
         arrived, rows, pre, low, part, got, final, landed, up, down,
         there_send, there_recv, gather_send, gather_recv, sum_send, sum_recv,
         back_send, back_recv, local) = refs
    here = lax.axis_index("wide")
    group = lax.axis_index("narrow")
    half = count // 2

    def window_of(position):
        position = lax.rem(position + 2 * count, count)
        upper = position // half
        return 2 * position * (1 - upper) + (2 * (count - 1 - position) + 1) * upper

    odd = lax.rem(here, 2)
    spot = (here // 2) * (1 - odd) + (count - 1 - here // 2) * odd
    ring = (window_of(spot + 1), window_of(spot - 1))
    peers = [lax.rem(group + k, groups) for k in range(1, groups)]

    loads = [
        pltpu.make_async_copy(up_hbm.at[layer], up, local.at[0]),
        pltpu.make_async_copy(down_hbm.at[layer], down, local.at[1]),
    ]
    if backward:
        loads.append(pltpu.make_async_copy(pre_hbm, pre, local.at[2]))
    for load in loads:
        load.start()

    barrier = pltpu.get_barrier_semaphore()
    for window in ring:
        pl.semaphore_signal(barrier, inc=1, device_id=(window, group), device_id_type=MESH)
    for peer in peers:
        pl.semaphore_signal(barrier, inc=1, device_id=(here, peer), device_id_type=MESH)
    pl.semaphore_wait(barrier, groups + 1)

    there = []
    for k, peer in enumerate(peers):
        there.append(pltpu.make_async_remote_copy(
            src_ref=out_ref.at[peer], dst_ref=arrived.at[group], send_sem=there_send.at[k],
            recv_sem=there_recv.at[k], device_id=(here, peer), device_id_type=MESH))
        there[-1].start()
    arrived[group] = out_ref[group]
    for copy in there:
        copy.wait_recv()
    flat = arrived[...].reshape(groups * block, width)
    own = dot_nn(perm_ref[...], flat).astype(jnp.bfloat16).reshape(experts, share, width)

    def span(window):
        return pl.ds(pl.multiple_of(window * share, 16), share)

    rows[:, span(here), :] = own

    def compute(windows):
        def one(e, carry):
            x = jnp.concatenate([rows[e, span(w), :] for w in windows], axis=0)
            if backward:
                grad_hidden = dot_nt(x, down[e])
                before = jnp.concatenate([pre[e, span(w), :] for w in windows], axis=0)
                slope = gelu_parts(before) + before * (
                    0.3989422804014327 * jnp.exp(-0.5 * before * before)
                )
                middle = (grad_hidden * slope).astype(jnp.bfloat16)
                y = dot_nt(middle, up[e])
            else:
                before = dot_nn(x, up[e])
                middle = (before * gelu_parts(before)).astype(jnp.bfloat16)
                y = dot_nn(middle, down[e])
            y = y.astype(jnp.bfloat16)
            for index, w in enumerate(windows):
                piece = slice(index * share, (index + 1) * share)
                if not backward:
                    pre[e, span(w), :] = before[piece]
                low[e, span(w), :] = middle[piece]
                part[e, span(w), :] = y[piece]
            return carry

        lax.fori_loop(0, experts, one, 0)

    cut = experts // 2
    halves = (pl.ds(0, cut), pl.ds(cut, experts - cut))
    gathers = []

    def parts_at(step):
        return [(way, sign, piece) for piece in (0, 1) for way, sign in ((0, 1), (1, -1))
                if step < half or piece == way]

    def hop(step, way, sign, piece):
        origin = window_of(spot - sign * (step - 1))
        return pltpu.make_async_remote_copy(
            src_ref=rows.at[halves[piece], span(origin), :], dst_ref=rows.at[halves[piece], span(origin), :],
            send_sem=gather_send.at[way, step - 1, piece], recv_sem=gather_recv.at[way, step - 1, piece],
            device_id=(ring[way], group), device_id_type=MESH)

    def pass_on(step, way, sign, piece):
        copy = hop(step, way, sign, piece)
        copy.start()
        gathers.append(copy)

    for way, sign, piece in parts_at(1):
        pass_on(1, way, sign, piece)
    for load in loads:
        load.wait()
    compute([here])
    for step in range(1, half + 1):
        for way, sign, piece in parts_at(step):
            hop(step, way, sign, piece).wait_recv()
            if step < half and (way, sign, piece) in parts_at(step + 1):
                pass_on(step + 1, way, sign, piece)
        if step < half:
            compute([window_of(spot - step), window_of(spot + step)])
        else:
            compute([window_of(spot + half)])

    saves = [
        pltpu.make_async_copy(rows, rows_hbm, local.at[3]),
        pltpu.make_async_copy(low, low_hbm, local.at[4]),
    ]
    if not backward:
        saves.append(pltpu.make_async_copy(pre, pre_hbm, local.at[2]))
    for save in saves:
        save.start()

    sums, last = [], {}
    for step in range(half):
        for which in (0, 1):
            for way, sign in ((0, 1), (1, -1)):
                if step == 0 and which != way:
                    continue
                window = window_of(spot + sign * (half - step))
                held = halves[which]
                if (way, which) in last:
                    last[way, which].wait_recv()
                    part[held, span(window), :] = (
                        part[held, span(window), :].astype(jnp.float32)
                        + got[way, step - 1, held].astype(jnp.float32)
                    ).astype(jnp.bfloat16)
                copy = pltpu.make_async_remote_copy(
                    src_ref=part.at[held, span(window), :], dst_ref=got.at[way, step, held],
                    send_sem=sum_send.at[way, step, which], recv_sem=sum_recv.at[way, step, which],
                    device_id=(ring[way], group), device_id_type=MESH)
                copy.start()
                sums.append(copy)
                last[way, which] = copy
    total = part[:, span(here), :].astype(jnp.float32)
    for way in (0, 1):
        for which in (0, 1):
            last[way, which].wait_recv()
        total = total + got[way, half - 1].astype(jnp.float32)
    packed = total.astype(jnp.bfloat16).reshape(experts * share, width)
    final[...] = dot_tn(perm_ref[...], packed).astype(jnp.bfloat16).reshape(groups, block, width)

    home = []
    for k, peer in enumerate(peers):
        home.append(pltpu.make_async_remote_copy(
            src_ref=final.at[peer], dst_ref=landed.at[group], send_sem=back_send.at[k],
            recv_sem=back_recv.at[k], device_id=(here, peer), device_id_type=MESH))
        home[-1].start()
    ret_ref[group] = final[group]
    for k, copy in enumerate(home):
        copy.wait_recv()
    for k in range(1, groups):
        source = lax.rem(group + groups - k, groups)
        ret_ref[source] = landed[source]
    for copy in there + gathers + sums + home:
        copy.wait_send()
    for save in saves:
        save.wait()


def expert_pass(outbound, perm, expert_up, expert_down, pre, layer, identity):
    count, groups = lax.axis_size("wide"), lax.axis_size("narrow")
    backward = pre is not None
    _, block, width = outbound.shape
    _, experts, _, hidden = expert_up.shape
    share = perm.shape[0] // experts
    half = count // 2
    total = count * share
    low, f32 = jnp.bfloat16, jnp.float32
    dims = (count, groups, experts, block, share, width, hidden)
    anywhere, inside = pl.BlockSpec(memory_space=pl.ANY), pl.BlockSpec(memory_space=VMEM)
    saved_rows = jax.ShapeDtypeStruct((experts, total, width), low)
    saved_low = jax.ShapeDtypeStruct((experts, total, hidden), low)
    saved_pre = jax.ShapeDtypeStruct((experts, total, hidden), f32)
    back = jax.ShapeDtypeStruct((groups, block, width), low)
    dma = pltpu.SemaphoreType.DMA
    args = (outbound, perm, expert_up, expert_down) + ((pre,) if backward else ())
    outs = [back, saved_rows] + ([] if backward else [saved_pre]) + [saved_low]
    return pl.pallas_call(
        functools.partial(expert_kernel, dims, backward, layer),
        out_shape=outs,
        in_specs=[inside, inside] + [anywhere] * (len(args) - 2),
        out_specs=[inside] + [anywhere] * (len(outs) - 1),
        scratch_shapes=[
            VMEM((groups, block, width), low),
            VMEM((experts, total, width), low),
            VMEM((experts, total, hidden), f32),
            VMEM((experts, total, hidden), low),
            VMEM((experts, total, width), low),
            VMEM((2, half, experts, share, width), low),
            VMEM((groups, block, width), low),
            VMEM((groups, block, width), low),
            VMEM((experts, width, hidden), low),
            VMEM((experts, hidden, width), low),
            dma((groups - 1,)), dma((groups - 1,)),
            dma((2, half, 2)), dma((2, half, 2)),
            dma((2, half, 2)), dma((2, half, 2)),
            dma((groups - 1,)), dma((groups - 1,)),
            dma((5,)),
        ],
        compiler_params=pltpu.CompilerParams(
            collective_id=identity, has_side_effects=True, vmem_limit_bytes=56 * MIB
        ),
        cost_estimate=microseconds(95),
    )(*args)


def expert_order(experts, groups, block, capacity):
    share = groups * capacity
    row = jnp.arange(experts * share, dtype=jnp.int32)
    expert, rest = row // share, row % share
    source = (rest // capacity) * block + expert * capacity + rest % capacity
    return (source[:, None] == jnp.arange(groups * block, dtype=jnp.int32)[None, :]).astype(jnp.bfloat16)


def sum_kernel(dims, *refs):
    count, lines, sizes, first_rows, width = dims
    total = len(sizes)
    arrays, out_ref = refs[:total], refs[total]
    (own, near, over, spun, spun_first, home, core_send, core_recv, load, over_send, over_recv,
     spin_send, spin_recv, spin_first_send, spin_first_recv, home_send, home_recv) = refs[total + 1 :]
    rows = sum(sizes)
    later = rows - first_rows
    here = lax.axis_index("wide")
    group = lax.axis_index("narrow")
    line, core = group // 2, lax.rem(group, 2)
    half = count // 2
    low, f32 = jnp.bfloat16, jnp.float32

    def window_of(position):
        position = lax.rem(position + 2 * count, count)
        upper = position // half
        return 2 * position * (1 - upper) + (2 * (count - 1 - position) + 1) * upper

    odd = lax.rem(here, 2)
    spot = (here // 2) * (1 - odd) + (count - 1 - here // 2) * odd
    ring = (window_of(spot + 1), window_of(spot - 1))
    peer = 2 * line + 1 - core
    lines_away = [lax.rem(line + k, lines) for k in range(1, lines)]

    barrier = pltpu.get_barrier_semaphore()
    for window in ring:
        pl.semaphore_signal(barrier, inc=1, device_id=(window, group), device_id_type=MESH)
    pl.semaphore_signal(barrier, inc=1, device_id=(here, peer), device_id_type=MESH)
    for other in lines_away:
        pl.semaphore_signal(barrier, inc=1, device_id=(here, 2 * other + core), device_id_type=MESH)
    pl.semaphore_wait(barrier, 2 + lines)

    order = [spot + half]
    for away in range(half - 1, 0, -1):
        order += [spot + away, spot - away]
    order = [window_of(position) for position in order + [spot]]
    sent, held = [], []
    for k, window in enumerate(order):
        held.append([])
        start = 0
        for i, size in enumerate(sizes):
            place = pl.ds(start, size)
            start += size
            copy = pltpu.make_async_remote_copy(
                src_ref=arrays[i].at[window, :, 1 - core], dst_ref=near.at[window, :, place],
                send_sem=core_send.at[k, i], recv_sem=core_recv.at[k, i],
                device_id=(here, peer), device_id_type=MESH)
            copy.start()
            mine = pltpu.make_async_copy(
                arrays[i].at[window, :, core], own.at[window, :, place], load.at[k, i])
            mine.start()
            sent.append(copy)
            held[-1].append((copy, mine))

    ahead, behind = pl.ds(0, first_rows), pl.ds(first_rows, later)
    cut_first = first_rows // 32 * 16
    cut_later = later // 32 * 16
    parts_first = (pl.ds(0, cut_first), pl.ds(cut_first, first_rows - cut_first))
    parts_later = (
        pl.ds(first_rows, cut_later), pl.ds(first_rows + cut_later, later - cut_later))
    parts_got = (pl.ds(0, cut_later), pl.ds(cut_later, later - cut_later))

    def meet(k):
        window = order[k]
        for copy, mine in held[k]:
            copy.wait_recv()
            mine.wait()

        def one(at, carry):
            place = pl.ds(pl.multiple_of(at * 16, 16), 16)
            for x in range(lines):
                own[window, x, place] = (
                    own[window, x, place].astype(f32) + near[window, x, place].astype(f32)
                ).astype(low)
            return carry

        lax.fori_loop(0, rows // 16, one, 0)
        for j, other in enumerate(lines_away):
            copy = pltpu.make_async_remote_copy(
                src_ref=own.at[window, other, ahead], dst_ref=over.at[j, window],
                send_sem=over_send.at[j, k], recv_sem=over_recv.at[j, k],
                device_id=(here, 2 * other + core), device_id_type=MESH)
            copy.start()
            sent.append(copy)
            crossing[k].append(copy)

    crossing = [[] for _ in order]

    def spin_later(step):
        for way, sign in ((0, 1), (1, -1)):
            window = window_of(spot + sign * (half - step))
            if step == 0:
                which, got_which = parts_later[way], parts_got[way]
            else:
                which, got_which = behind, pl.ds(0, later)
                add_which, add_got = (
                    (parts_later[way], parts_got[way]) if step == 1 else (which, got_which))
                turns[way][-1].wait_recv()
                own[window, :, add_which] = (
                    own[window, :, add_which].astype(f32)
                    + spun[way, step - 1, :, add_got].astype(f32)
                ).astype(low)
            copy = pltpu.make_async_remote_copy(
                src_ref=own.at[window, :, which], dst_ref=spun.at[way, step, :, got_which],
                send_sem=spin_send.at[way, step], recv_sem=spin_recv.at[way, step],
                device_id=(ring[way], group), device_id_type=MESH)
            copy.start()
            sent.append(copy)
            turns[way].append(copy)

    turns = ([], [])
    meet(0)
    spin_later(0)
    for step in range(1, half):
        meet(2 * step - 1)
        meet(2 * step)
        spin_later(step)
    meet(len(order) - 1)
    summed = own[here, :, behind].astype(f32)
    for way in (0, 1):
        turns[way][-1].wait_recv()
        summed = summed + spun[way, half - 1].astype(f32)
    own[here, :, behind] = summed.astype(low)
    homes = []
    for j, other in enumerate(lines_away):
        copy = pltpu.make_async_remote_copy(
            src_ref=own.at[here, other, behind], dst_ref=home.at[j],
            send_sem=home_send.at[j], recv_sem=home_recv.at[j],
            device_id=(here, 2 * other + core), device_id_type=MESH)
        copy.start()
        sent.append(copy)
        homes.append(copy)

    def cross(k):
        window = order[k]
        value = own[window, line, ahead].astype(f32)
        for j, copy in enumerate(crossing[k]):
            copy.wait_recv()
            value = value + over[j, window].astype(f32)
        return value

    first_turns = ([], [])

    def spin_first(step):
        for way, sign in ((0, 1), (1, -1)):
            k = 0 if step == 0 else 2 * step - 1 + way
            window = order[k]
            if step or way == 0:
                own[window, line, ahead] = cross(k).astype(low)
            if step == 0:
                which = parts_first[way]
            else:
                which = ahead
                add_which = parts_first[way] if step == 1 else which
                first_turns[way][-1].wait_recv()
                own[window, line, add_which] = (
                    own[window, line, add_which].astype(f32)
                    + spun_first[way, step - 1, add_which].astype(f32)
                ).astype(low)
            copy = pltpu.make_async_remote_copy(
                src_ref=own.at[window, line, which], dst_ref=spun_first.at[way, step, which],
                send_sem=spin_first_send.at[way, step], recv_sem=spin_first_recv.at[way, step],
                device_id=(ring[way], group), device_id_type=MESH)
            copy.start()
            sent.append(copy)
            first_turns[way].append(copy)

    for step in range(half):
        spin_first(step)
    summed = cross(len(order) - 1)
    for way in (0, 1):
        first_turns[way][-1].wait_recv()
        summed = summed + spun_first[way, half - 1].astype(f32)
    out_ref[ahead, :] = summed
    value = own[here, line, behind].astype(f32)
    for j, copy in enumerate(homes):
        copy.wait_recv()
        value = value + home[j].astype(f32)
    out_ref[behind, :] = value
    for copy in sent:
        copy.wait_send()


def summed_shares(arrays, identity):
    count, groups = lax.axis_size("wide"), lax.axis_size("narrow")
    lines, half = groups // 2, count // 2
    width = arrays[0].shape[2]
    if any(array.shape[1] % 16 for array in arrays):
        packed = jnp.concatenate(arrays, axis=1)
        arrays = [jnp.pad(packed, ((0, 0), (0, -packed.shape[1] % 16), (0, 0)))]
    sizes = tuple(array.shape[1] for array in arrays)
    rows = sum(sizes)
    first = max(32, rows * 11 // 20 // 16 * 16)
    later = rows - first
    low = jnp.bfloat16
    dma = pltpu.SemaphoreType.DMA
    return pl.pallas_call(
        functools.partial(sum_kernel, (count, lines, sizes, first, width)),
        out_shape=jax.ShapeDtypeStruct((rows, width), jnp.float32),
        in_specs=[ANYWHERE] * len(arrays),
        out_specs=pl.BlockSpec(memory_space=VMEM),
        scratch_shapes=[
            VMEM((count, lines, rows, width), low),
            VMEM((count, lines, rows, width), low),
            VMEM((lines - 1, count, first, width), low),
            VMEM((2, half, lines, later, width), low),
            VMEM((2, half, first, width), low),
            VMEM((lines - 1, later, width), low),
            dma((count, len(arrays))), dma((count, len(arrays))), dma((count, len(arrays))),
            dma((lines - 1, count)), dma((lines - 1, count)),
            dma((2, half)), dma((2, half)),
            dma((2, half)), dma((2, half)),
            dma((lines - 1,)), dma((lines - 1,)),
        ],
        compiler_params=pltpu.CompilerParams(
            collective_id=identity, has_side_effects=True, vmem_limit_bytes=56 * MIB
        ),
        cost_estimate=microseconds(60),
    )(*[array.reshape(count, lines, 2, array.shape[1], width) for array in arrays])


def weights_kernel(experts, *refs):
    first, second, (up_ref, down_ref) = refs[:4], refs[4:8], refs[8:]
    for layer, (rows, pre, hidden, grad) in enumerate((first, second)):
        @pl.when(pl.program_id(0) // experts == layer)
        def _():
            up_ref[...] = dot_tn(rows[...], pre[...])
            down_ref[...] = dot_tn(hidden[...], grad[...])


def expert_weights(kept):
    experts, total, width = kept[0][0].shape
    hidden = kept[0][1].shape[2]
    f32 = jnp.float32
    specs = []
    for layer in (0, 1):
        for columns in (width, hidden, hidden, width):
            if layer == 0:
                place = lambda i: (jnp.minimum(i, experts - 1), 0, 0)
            else:
                place = lambda i: (jnp.maximum(i - experts, 0), 0, 0)
            specs.append(pl.BlockSpec((None, total, columns), place))
    outs = [
        pl.BlockSpec((None, None, width, hidden), lambda i: (i // experts, i % experts, 0, 0)),
        pl.BlockSpec((None, None, hidden, width), lambda i: (i // experts, i % experts, 0, 0)),
    ]
    return plain_call(
        functools.partial(weights_kernel, experts),
        (2 * experts,),
        specs,
        outs,
        [shaped((2, experts, width, hidden), f32), shaped((2, experts, hidden, width), f32)],
        [],
        tuple(kept[0]) + tuple(kept[1]),
        15,
    )


def on_device(
    hidden,
    doc_start,
    expert_choice,
    slot_index,
    norm_mix,
    in_weight,
    conv_weight,
    conv_bias,
    state_weight,
    step_weight,
    step_bias,
    decay_log,
    skip_weight,
    out_weight,
    norm_expert,
    router,
    expert_up,
    expert_down,
    cotangent,
):
    layers = in_weight.shape[0]
    tokens = hidden.shape[1]
    width = hidden.shape[2]
    inner = skip_weight.shape[1]
    rank = step_weight.shape[1]
    states = decay_log.shape[1]
    experts = router.shape[2]
    taps = conv_weight.shape[1]
    steps = tokens // CHUNKS
    both = ("wide", "narrow")
    groups = lax.axis_size("narrow")
    devices = lax.axis_size("wide") * groups
    per_group = experts // groups
    capacity = max(2, 5 * tokens // (4 * experts))
    block = -(-per_group * capacity // 16) * 16
    low, f32 = jnp.bfloat16, jnp.float32
    starts = to_steps(doc_start[0]).astype(f32)
    masks = keep_masks(starts, taps)
    keep_mask = rim_keep(starts, taps - 1)[:, None]
    reset = jnp.broadcast_to((starts * RESET)[..., None], starts.shape + (LANES,))
    order = expert_order(per_group, groups, block, capacity)
    conv_bias, step_bias, skip_weight, norm_expert = (
        values[:, None, :] for values in (conv_bias, step_bias, skip_weight, norm_expert))
    current = to_steps(hidden[0]).reshape(tokens, width).astype(f32)
    saved = []

    def cube(values):
        return values.reshape(steps, CHUNKS, values.shape[-1])

    fills, onehots, keeps = [], [], []
    for layer in range(layers):
        chosen = to_steps(expert_choice[layer, 0]).reshape(tokens)
        slot_row = to_steps(slot_index[layer, 0]).reshape(tokens)
        kept = slot_row >= 0
        place = (chosen // per_group) * block + (chosen % per_group) * capacity + slot_row
        place = jnp.where(kept, place, -1)
        fills.append(
            (place[None, :] == jnp.arange(groups * block, dtype=jnp.int32)[:, None]).astype(low))
        onehots.append((chosen[:, None] == jnp.arange(experts, dtype=jnp.int32)[None, :]).astype(f32))
        keeps.append(kept.astype(f32)[:, None])

    for layer in range(layers):
        begin = current
        normed = rms_scale(current, norm_mix[layer]).astype(low)
        projected = cube(dot_nn(normed, in_weight[layer]))
        rim = passed_along(projected[steps - taps + 1 :, CHUNKS - 1, :inner] * keep_mask, 1)
        act, selection, size, link, link_size, total, total_size = mixer_front(
            layer, projected, rim, masks, reset, conv_weight, conv_bias, state_weight, step_weight, step_bias,
            decay_log)
        entering = handed_on(layer, total, total_size, decay_log, False, layer)
        mixed, gated, begins, middle, routed, logits, outbound = mixer_run(
            layer, size, act, selection, reset, decay_log, link, link_size, entering, projected, skip_weight,
            out_weight, current, norm_expert, router, fills[layer])
        returned, kept_rows, pre_act, hidden_low = expert_pass(
            outbound.reshape(groups, block, width), order, expert_up, expert_down, None, layer, 4 + layer)
        shares = jax.nn.softmax(logits, axis=-1)
        gate = jnp.sum(shares * onehots[layer], axis=1, keepdims=True)
        back_rows = dot_tn(fills[layer], returned.reshape(groups * block, width))
        current = middle + (keeps[layer] * gate) * back_rows
        saved.append(dict(
            begin=begin, normed=normed, projected=projected, rim=rim, act=act, selection=selection, size=size,
            begins=begins, mixed=mixed, gated=gated, middle=middle, routed=routed, shares=shares, gate=gate,
            kept_rows=kept_rows, pre_act=pre_act, hidden_low=hidden_low, back_rows=back_rows))
    output = to_tokens(cube(current.astype(low)))[None]
    grad = to_steps(cotangent[0]).reshape(tokens, width).astype(f32)
    packed = [None] * layers
    expert_kept = [None] * layers
    per_device = inner // devices
    norm_device = width // devices
    fold = width // (2 * LANES)
    spare = 160
    for layer in range(layers - 1, -1, -1):
        entry = saved[layer]
        fill, keep, gate = fills[layer], keeps[layer], entry["gate"]
        grad_rows_low = ((keep * gate) * grad).astype(low)
        grad_gate = keep * jnp.sum(grad * entry["back_rows"], axis=1, keepdims=True)
        outbound = dot_nn(fill, grad_rows_low).astype(low).reshape(groups, block, width)
        inbound, grad_rows, grad_pre = expert_pass(
            outbound, order, expert_up, expert_down, entry["pre_act"], layer, 6 + layer)
        expert_kept[layer] = (entry["kept_rows"], grad_pre, entry["hidden_low"], grad_rows)
        grad_sent = dot_tn(fill, inbound.reshape(groups * block, width))
        grad_logits_low = ((grad_gate * gate) * (onehots[layer] - entry["shares"])).astype(low)
        grad_router = dot_tn(entry["routed"], grad_logits_low)
        grad_routed = grad_sent + dot_nt(grad_logits_low, router[layer])
        grad_middle, grad_norm_expert = rms_back(entry["middle"], norm_expert[layer], grad_routed)
        grad = grad + grad_middle
        grad_low = grad.astype(low)
        grad_y, grad_igate, grad_skip, grad_out, link, link_size, total, total_size = mixer_turn(
            layer, grad_low, out_weight, entry["projected"], entry["mixed"], entry["act"], entry["gated"],
            entry["size"], entry["selection"], reset, decay_log)
        entering = handed_on(layer, total, total_size, decay_log, True, 2 + layer)
        grad_act, grad_decay, grad_bias, grad_step, grad_selection = mixer_back(
            layer, entry["size"], entry["act"], grad_y, decay_log, entry["selection"], reset,
            entry["begins"], link, link_size, entering, step_weight, step_bias, skip_weight)
        grad_value, edge, rim_grad, channel = mixer_conv_back(
            layer, grad_act, grad_selection, state_weight, entry["projected"], entry["rim"], masks, conv_weight,
            conv_bias, entry["act"], grad_step, grad_decay, grad_bias, grad_skip)
        edge = edge + passed_along(rim_grad, -1) * keep_mask
        grad_value = cube(grad_value).at[steps - taps + 1 :, CHUNKS - 1].set(edge.astype(low))
        grad_value = grad_value.reshape(tokens, inner)
        grad_projected = jnp.concatenate([grad_value, grad_igate], axis=1)
        grad_in = dot_tn(grad_projected, entry["normed"]).astype(low)
        grad_normed = dot_nt(grad_projected, in_weight[layer])
        grad_begin, grad_norm_mix = rms_back(entry["begin"], norm_mix[layer], grad_normed)
        grad = grad + grad_begin
        feature = jnp.concatenate(
            [grad_router, grad_norm_mix[:, None], grad_norm_expert.reshape(width, 1)], axis=1)
        feature = jnp.pad(
            feature.reshape(devices, norm_device, experts + 2).astype(low),
            ((0, 0), (0, per_device - norm_device), (spare, 2 * LANES - spare - experts - 2)))
        channel = channel.reshape(devices, per_device, 2 * LANES) + feature
        channel = jnp.swapaxes(channel.reshape(devices, fold, per_device // fold, 2 * LANES), 1, 2)
        packed[layer] = [
            grad_in.reshape(devices, -1, width),
            grad_out.reshape(devices, -1, width),
            channel.reshape(devices, -1, width),
        ]
    up_grads, down_grads = expert_weights(expert_kept)
    sums = summed_shares([part for parts in packed for part in parts], 8)
    bounds = [0]
    for part in packed[0]:
        bounds.append(bounds[-1] + part.shape[1])
    sums = sums[: layers * bounds[-1]].reshape(layers, bounds[-1], width)
    grad_in, grad_out, mine = (sums[:, bounds[i] : bounds[i + 1]] for i in range(3))
    mine = mine.reshape(layers, per_device // fold, fold, 2 * LANES)
    mine = jnp.swapaxes(mine, 1, 2).reshape(layers, per_device, 2 * LANES)
    feature = mine[:, :norm_device, spare : spare + experts + 2]
    fields = jnp.swapaxes(mine, 1, 2)
    bounds = [0]
    for count in (rank + 2 * states, rank, states, taps, 1, 1, 1):
        bounds.append(bounds[-1] + count)
    fields = [fields[:, bounds[i] : bounds[i + 1]] for i in range(7)]
    shared = (
        feature[:, :, experts],
        jnp.swapaxes(grad_in, 1, 2),
        fields[3],
        fields[4][:, 0],
        mine[:, :, : bounds[1]],
        fields[1],
        fields[5][:, 0],
        fields[2],
        fields[6][:, 0],
        grad_out,
        feature[:, :, experts + 1],
        feature[:, :, :experts],
    )
    output_grad = to_tokens(cube(grad))[None]
    return (output, output_grad, *shared, up_grads, down_grads)


def solution(mesh):
    both = ("wide", "narrow")
    placed = (
        P("narrow", "wide", None),
        P("narrow", "wide"),
        P(None, "narrow", "wide"),
        P(None, "narrow", "wide"),
    ) + (P(),) * 12 + (
        P(None, "narrow", None, "wide"),
        P(None, "narrow", "wide", None),
        P("narrow", "wide", None),
    )
    return jax.shard_map(
        on_device,
        mesh=mesh,
        in_specs=placed,
        out_specs=(
            P("narrow", "wide", None),
            P("narrow", "wide", None),
            P(None, both),
            P(None, None, both),
            P(None, None, both),
            P(None, both),
            P(None, both, None),
            P(None, None, both),
            P(None, both),
            P(None, None, both),
            P(None, both),
            P(None, both, None),
            P(None, both),
            P(None, both, None),
            P(None, "narrow", None, "wide"),
            P(None, "narrow", "wide", None),
        ),
        check_vma=False,
    )
```

time: 4060 us -> 856 us (0.21)
  blocking collectives: 1570 us -> 0 us
  waiting for transfers between devices: 1020 us -> 2.11 us
  Pallas kernels: 0 us -> 737 us
  local copies, waits for them, and re-layouts: 705 us -> 46.1 us
  other arithmetic: 372 us -> 14.4 us
  matrix products: 304 us -> 37.4 us
    unnamed x4 -> x0, blocking collectives: 1250 us -> none
    pallas_call x0 -> x20, Pallas kernels: none -> 737 us  [the longest x4 398 us: expert_pass(): pl.pallas_call(functools.partial(expert_kernel, dims, backward, layer), o...]
    unnamed x19 -> x0, waiting for transfers between devices: 668 us -> none
    all_gather x8 -> x0, blocking collectives: 273 us -> none  [the longest x4 143 us: entering(): pieces = jax.tree.map(lambda part: lax.all_gather(part, axis), value)]
    dot_general x138 -> x16, matrix products: 304 us -> 37.4 us  [the longest x8 15.6 us: dot_tn(): lax.dot_general(left, right, (((0,), (0,)), ((), ())), preferred_element_...]
    mul x388 -> x1, local copies, waits for them, and re-layouts: 239 us -> 0.08 us  [on_device(): starts * RESET]
    all_gather x4 -> x0, waiting for transfers between devices: 198 us -> none  [spread(): return lax.all_gather(values, 'wide', axis=0, tiled=True)]
    another operation x234 -> x13, local copies, waits for them, and re-layouts: 157 us -> 6.01 us  [the longest x2 5.26 us: summed_shares(): array.reshape(count, lines, 2, array.shape[1], width)]
  transfers between devices with their start and end apart: 20 -> 4, of which waited for: 15 -> 2; matrix products, arithmetic and copies ran while one was open for 12% -> 2% of each run, Pallas kernels for 0% -> 2%
where the time goes in v1:
time: 856 us; the launch traced here: 852 us
  Pallas kernels  737 us (86%)
  local copies, waits for them, and re-layouts  46.1 us (5%)
  matrix products  37.4 us (4%)
  other arithmetic  14.4 us (2%)
  starting transfers between devices  12.1 us (1%)
    pallas_call x4, Pallas kernels, expert_pass(): pl.pallas_call(functools.partial(expert_kernel, dims, backward, layer), o...  398 us
    pallas_call x11, Pallas kernels, plain_call(): pl.pallas_call(kernel, grid=grid, in_specs=in_specs, out_specs=out_specs,...  219 us
    pallas_call x1, Pallas kernels, summed_shares(): pl.pallas_call(functools.partial(sum_kernel, (count, lines, sizes, first,...  74.8 us
    pallas_call x4, Pallas kernels, handed_on(): pl.pallas_call(functools.partial(link_kernel, layer, count, reverse), out...  45.4 us
    unnamed x256, local copies, waits for them, and re-layouts  18.1 us
  transfers between devices with their start and end apart: 4, of which 2 were waited for; matrix products, arithmetic and copies ran while one was open for 2% of the time, Pallas kernels for 2%

profile of v1, /device:TPU:0, one launch (start us, length us, event | category | flops | bytes accessed | tf_op | source)
XLA Modules:
  0.0 852.3 jit_solution(15125946035427926512)
XLA Ops:
  1.7 1.4 slice_reduce_fusion.7
  3.7 4.2 fusion.4.value_ref.gate_ref
  8.0 1.6 copy-done.123
  11.5 5.4 collective-permute-start
  23.7 14.9 %shard_map.306 = (bf16[256,1536]{1,0:T(8,128)(2,1)S(1)}, f32[32,8,80]{2,1,0:T(8,128)S(1)}, f32[32,8,1536]{2,1,0:T(8,128)S(1)}, f32[16,8,1536]{2,1,0:T(8,128)S(1)...) custom-call(f32[32,8,3072]{2,1,0:T(8,128)} %copy-done.123, ...), custom_call_target="tpu_custom_call" | custom-call | flops 17999998976 | bytes 1000000 | tf_op jit(solution)/shard_map/pallas_call | solution.py:90
  38.7 10.5 %shard_map.307.entering_ref = f32[16,1536]{1,0:T(8,128)S(1)} custom-call(f32[16,1536]{1,0:T(8,128)S(1)} %get-tuple-element.123.total_ref, f32[1,1536]{1,0:T(1,128)S(1)} %get-tuple-element.124.size_ref, f32[2,16,1536]{2,1,0:T(8,128)S(1)} %copy-done.15), custom_call_target="tpu_custom_call" | custom-call | flops 12000000000 | bytes 1000000 | tf_op jit(solution)/shard_map/pallas_call | solution.py:770
  49.2 21.6 %shard_map.308 = (f32[32,8,1536]{2,1,0:T(8,128)}, bf16[256,1536]{1,0:T(8,128)(2,1)S(1)}, f32[16,8,1536]{2,1,0:T(8,128)S(1)}, f32[256,768]{1,0:T(8,128)S(1)}, bf1...) custom-call(f32[32,8,1536]{2,1,0:T(8,128)} %copy-done.32, ...), custom_call_target="tpu_custom_call" | custom-call | flops 22000001024 | bytes 1000000 | tf_op jit(solution)/shard_map/pallas_call | solution.py:90
  75.0 99.5 %shard_map.309 = (bf16[4,80,768]{2,1,0:T(8,128)(2,1)}, bf16[4,640,768]{2,1,0:T(8,128)(2,1)}, f32[4,640,384]{2,1,0:T(8,128)}, bf16[4,640,384]{2,1,0:T(8,128)(2,1)}) custom-call(bf16[4,80,768]{2,1,0:T(8,128)(2,1)} %bitcast.169, bf16[320,320]{1,0:T(8,128)(2,1)} %fusion.37.refs_1_, bf16[2,4,768,384]{3,2,1,0:T(8,128)(2,1)} %refs_2_.7, ...), custom_call_target="tpu_custom_call" | custom-call | flops 95000002560 | bytes 1000000 | tf_op jit(solution)/shard_map/pallas_call | solution.py:992
  174.6 2.4 multiply_reduce_fusion.11
  178.1 3.8 fusion.value_ref.gate_ref
  182.0 4.0 collective-permute-start.1
  187.4 14.9 %shard_map.310 = (bf16[256,1536]{1,0:T(8,128)(2,1)S(1)}, f32[32,8,80]{2,1,0:T(8,128)S(1)}, f32[32,8,1536]{2,1,0:T(8,128)S(1)}, f32[16,8,1536]{2,1,0:T(8,128)S(1)...) custom-call(f32[32,8,3072]{2,1,0:T(8,128)} %copy-done.124, ...), custom_call_target="tpu_custom_call" | custom-call | flops 17999998976 | bytes 1000000 | tf_op jit(solution)/shard_map/pallas_call | solution.py:90
  202.4 12.0 %shard_map.311.entering_ref = f32[16,1536]{1,0:T(8,128)S(1)} custom-call(f32[16,1536]{1,0:T(8,128)S(1)} %get-tuple-element.134.total_ref, f32[1,1536]{1,0:T(1,128)S(1)} %get-tuple-element.135.size_ref, f32[2,16,1536]{2,1,0:T(8,128)S(1)} %copy-done.15), custom_call_target="tpu_custom_call" | custom-call | flops 12000000000 | bytes 1000000 | tf_op jit(solution)/shard_map/pallas_call | solution.py:770
  214.4 21.6 %shard_map.312 = (f32[32,8,1536]{2,1,0:T(8,128)}, bf16[256,1536]{1,0:T(8,128)(2,1)S(1)}, f32[16,8,1536]{2,1,0:T(8,128)S(1)}, f32[256,768]{1,0:T(8,128)S(1)}, bf1...) custom-call(f32[32,8,1536]{2,1,0:T(8,128)} %copy-done.33, ...), custom_call_target="tpu_custom_call" | custom-call | flops 22000001024 | bytes 1000000 | tf_op jit(solution)/shard_map/pallas_call | solution.py:90
  239.9 99.2 %shard_map.313 = (bf16[4,80,768]{2,1,0:T(8,128)(2,1)}, bf16[4,640,768]{2,1,0:T(8,128)(2,1)}, f32[4,640,384]{2,1,0:T(8,128)}, bf16[4,640,384]{2,1,0:T(8,128)(2,1)}) custom-call(bf16[4,80,768]{2,1,0:T(8,128)(2,1)} %bitcast.168, bf16[320,320]{1,0:T(8,128)(2,1)} %fusion.37.refs_1_, bf16[2,4,768,384]{3,2,1,0:T(8,128)(2,1)} %refs_2_.7, ...), custom_call_target="tpu_custom_call" | custom-call | flops 95000002560 | bytes 1000000 | tf_op jit(solution)/shard_map/pallas_call | solution.py:992
  339.2 1.8 fusion.33
  341.0 1.5 convolution_convert_fusion.3
  342.5 99.1 %shard_map.314 = (bf16[4,80,768]{2,1,0:T(8,128)(2,1)}, bf16[4,640,768]{2,1,0:T(8,128)(2,1)}, bf16[4,640,384]{2,1,0:T(8,128)(2,1)}) custom-call(bf16[4,80,768]{2,1,0:T(8,128)(2,1)} %bitcast.194, bf16[320,320]{1,0:T(8,128)(2,1)} %fusion.37.refs_1_, bf16[2,4,768,384]{3,2,1,0:T(8,128)(2,1)} %refs_2_.7, bf16[2,4,384,768]{3,2,1,0:T(8,128)(2,1)} %refs_3_.7, ...), custom_call_target="tpu_custom_call" | custom-call | flops 95000002560 | bytes 1000000 | tf_op jit(solution)/shard_map/pallas_call | solution.py:992
  441.6 1.5 fusion.48
  443.8 1.5 fusion.97
  445.2 18.2 %shard_map.315 = (f32[32,8,1536]{2,1,0:T(8,128)S(1)}, bf16[256,1536]{1,0:T(8,128)(2,1)S(1)}, f32[1,1536]{1,0:T(1,128)S(1)}, bf16[1536,768]{1,0:T(8,128)(2,1)}, f...) custom-call(bf16[256,768]{1,0:T(8,128)(2,1)S(1)} %get-tuple-element.285.grad_, ...), custom_call_target="tpu_custom_call" | custom-call | flops 14000000000 | bytes 1000000 | tf_op jit(solution)/shard_map/pallas_call | solution.py:90
  463.4 11.2 %shard_map.316.entering_ref = f32[16,1536]{1,0:T(8,128)S(1)} custom-call(f32[16,1536]{1,0:T(8,128)S(1)} %get-tuple-element.148.total_ref, f32[1,1536]{1,0:T(1,128)S(1)} %get-tuple-element.149.size_ref, f32[2,16,1536]{2,1,0:T(8,128)S(1)} %copy-done.15), custom_call_target="tpu_custom_call" | custom-call | flops 12000000000 | bytes 1000000 | tf_op jit(solution)/shard_map/pallas_call | solution.py:770
  474.6 33.7 %shard_map.317 = (f32[32,8,1536]{2,1,0:T(8,128)S(1)}, f32[16,1536]{1,0:T(8,128)S(1)}, f32[1,1536]{1,0:T(1,128)S(1)}, f32[48,1536]{1,0:T(8,128)S(1)}, bf16[256,80]{1,0:T(8,128)(2,1)S(1)}) custom-call(f32[32,8,1536]{2,1,0:T(8,128)} %copy-done.33, bf16[256,1536]{1,0:T(8,128)(2,1)S(1)} %copy-done.39, f32[32,8,1536]{2,1,0:T(8,128)} %copy-done.35, ...), custom_call_target="tpu_custom_call" | custom-call | flops 35000000512 | bytes 1000000 | tf_op jit(solution)/shard_map/pallas_call | solution.py:90
  508.4 11.4 %shard_map.318 = (bf16[256,1536]{1,0:T(8,128)(2,1)S(1)}, f32[3,1536]{1,0:T(4,128)S(1)}, f32[3,1536]{1,0:T(4,128)S(1)}, bf16[1536,256]{1,0:T(8,128)(2,1)S(1)}) custom-call(f32[32,8,1536]{2,1,0:T(8,128)S(1)} %get-tuple-element.150.grad_act_ref, bf16[256,80]{1,0:T(8,128)(2,1)S(1)} %get-tuple-element.151.grad_selection_ref, ...), custom_call_target="tpu_custom_call" | custom-call | flops 10000000000 | bytes 1000000 | tf_op jit(solution)/shard_map/pallas_call | solution.py:90
  519.8 1.4 collective-permute-start.2
  524.3 1.4 collective-permute-done.2
  525.8 1.6 scatter.6
  527.4 5.2 multiply_reduce_fusion.1
  532.7 3.7 convolution_convert_fusion
  538.3 100.7 %shard_map.319 = (bf16[4,80,768]{2,1,0:T(8,128)(2,1)}, bf16[4,640,768]{2,1,0:T(8,128)(2,1)}, bf16[4,640,384]{2,1,0:T(8,128)(2,1)}) custom-call(bf16[4,80,768]{2,1,0:T(8,128)(2,1)} %bitcast.193, bf16[320,320]{1,0:T(8,128)(2,1)} %fusion.37.refs_1_, bf16[2,4,768,384]{3,2,1,0:T(8,128)(2,1)} %refs_2_.7, bf16[2,4,384,768]{3,2,1,0:T(8,128)(2,1)} %refs_3_.7, ...), custom_call_target="tpu_custom_call" | custom-call | flops 95000002560 | bytes 1000000 | tf_op jit(solution)/shard_map/pallas_call | solution.py:992
  639.1 1.4 fusion.51
  642.8 18.1 %shard_map.320 = (f32[32,8,1536]{2,1,0:T(8,128)S(1)}, bf16[256,1536]{1,0:T(8,128)(2,1)S(1)}, f32[1,1536]{1,0:T(1,128)S(1)}, bf16[1536,768]{1,0:T(8,128)(2,1)}, f...) custom-call(bf16[256,768]{1,0:T(8,128)(2,1)S(1)} %get-tuple-element.281.grad_, ...), custom_call_target="tpu_custom_call" | custom-call | flops 14000000000 | bytes 1000000 | tf_op jit(solution)/shard_map/pallas_call | solution.py:90
  661.0 11.8 %shard_map.321.entering_ref = f32[16,1536]{1,0:T(8,128)S(1)} custom-call(f32[16,1536]{1,0:T(8,128)S(1)} %get-tuple-element.168.total_ref, f32[1,1536]{1,0:T(1,128)S(1)} %get-tuple-element.169.size_ref, f32[2,16,1536]{2,1,0:T(8,128)S(1)} %copy-done.15), custom_call_target="tpu_custom_call" | custom-call | flops 12000000000 | bytes 1000000 | tf_op jit(solution)/shard_map/pallas_call | solution.py:770
  672.9 33.8 %shard_map.322 = (f32[32,8,1536]{2,1,0:T(8,128)S(1)}, f32[16,1536]{1,0:T(8,128)S(1)}, f32[1,1536]{1,0:T(1,128)S(1)}, f32[48,1536]{1,0:T(8,128)S(1)}, bf16[256,80]{1,0:T(8,128)(2,1)S(1)}) custom-call(f32[32,8,1536]{2,1,0:T(8,128)} %copy-done.32, bf16[256,1536]{1,0:T(8,128)(2,1)S(1)} %copy-done.37, f32[32,8,1536]{2,1,0:T(8,128)} %copy-done.34, ...), custom_call_target="tpu_custom_call" | custom-call | flops 35000000512 | bytes 1000000 | tf_op jit(solution)/shard_map/pallas_call | solution.py:90
  706.7 11.5 %shard_map.323 = (bf16[256,1536]{1,0:T(8,128)(2,1)S(1)}, f32[3,1536]{1,0:T(4,128)S(1)}, f32[3,1536]{1,0:T(4,128)S(1)}, bf16[1536,256]{1,0:T(8,128)(2,1)S(1)}) custom-call(f32[32,8,1536]{2,1,0:T(8,128)S(1)} %get-tuple-element.170.grad_act_ref, bf16[256,80]{1,0:T(8,128)(2,1)S(1)} %get-tuple-element.171.grad_selection_ref, ...), custom_call_target="tpu_custom_call" | custom-call | flops 10000000000 | bytes 1000000 | tf_op jit(solution)/shard_map/pallas_call | solution.py:90
  719.1 1.3 collective-permute-start.3
  720.8 1.2 fusion.29
  722.6 1.5 copy-done.30
  724.1 1.5 copy-done.31
  725.7 19.1 %shard_map.325 = (f32[2,4,768,384]{3,2,1,0:T(8,128)}, f32[2,4,384,768]{3,2,1,0:T(8,128)}) custom-call(bf16[4,640,768]{2,1,0:T(8,128)(2,1)} %get-tuple-element.186.refs_0_, bf16[4,640,384]{2,1,0:T(8,128)(2,1)S(1)} %copy-done.31, bf16[4,640,384]{2,1,0:T(8,128)(2,1)S(1)} %copy-done.29, bf16[4,640,768]{2,1,0:T(8,128)(2,1)} %get-tuple-element.189.refs_3_, ...), custom_call_target="tpu_custom_call" | custom-call | flops 15000000512 | bytes 1000000 | tf_op jit(solution)/shard_map/pallas_call | solution.py:90
  746.4 2.7 copy.144
  749.0 3.4 reshape_reshape.23.refs_5_
  752.7 5.0 multiply_reduce_fusion.3
  757.7 4.0 convolution_convert_fusion.1
  763.8 1.9 reshape_reshape.20.refs_2_
  765.7 74.8 %shard_map.324 = f32[320,768]{1,0:T(8,128)} custom-call(bf16[8,2,2,96,768]{4,3,2,1,0:T(8,128)(2,1)} %bitcast.205, bf16[8,2,2,48,768]{4,3,2,1,0:T(8,128)(2,1)} %bitcast.207, bf16[8,2,2,16,768]{4,3,2,1,0:T(8,128)(2,1)} %reshape_reshape.20.refs_2_, bf16[8,2,2,96,768]{4,3,2,1,0:T(8,128)(2,1)} %bitcast.204, bf16[8,2,2,48,768]{4,3,2,1,0:T(8,128)(2,1)} %bitcast.206, ...), custom_call_target="tpu_custom_call" | custom-call | flops 60000002048 | bytes 1000000 | tf_op jit(solution)/shard_map/pallas_call | solution.py:1226
  841.6 1.9 slice_bitcast_fusion
  845.8 1.7 slice.208
  (359 shorter events, 42.4 us)
Async XLA Ops:
  3.6 15.6 %copy-start.76 = (f32[2,768]{1,0:T(2,128)S(1)}, f32[2,768]{1,0:T(2,128)}, u32[]{:S(2)}) copy-start(f32[2,768]{1,0:T(2,128)} %param.37) | copy-start | bytes 18436
  3.7 16.8 %copy-start.60 = (bf16[1,256,768]{2,1,0:T(8,128)(2,1)S(1)}, bf16[1,256,768]{2,1,0:T(8,128)(2,1)}, u32[]{:S(2)}) copy-start(bf16[1,256,768]{2,1,0:T(8,128)(2,1)} %param.23) | copy-start | bytes 1179652
  7.9 14.2 %copy-start.93 = (f32[2,1536]{1,0:T(2,128)S(1)}, f32[2,1536]{1,0:T(2,128)}, u32[]{:S(2)}) copy-start(f32[2,1536]{1,0:T(2,128)} %param.33) | copy-start | bytes 36868
  7.9 14.3 %copy-start.94 = (f32[2,1536]{1,0:T(2,128)S(1)}, f32[2,1536]{1,0:T(2,128)}, u32[]{:S(2)}) copy-start(f32[2,1536]{1,0:T(2,128)} %param.35) | copy-start | bytes 36868
  7.9 14.3 %copy-start.66 = (bf16[2,768,16]{1,2,0:T(8,128)(2,1)S(1)}, bf16[2,768,16]{1,2,0:T(8,128)(2,1)}, u32[]{:S(2)}) copy-start(bf16[2,768,16]{1,2,0:T(8,128)(2,1)} %param.38) | copy-start | bytes 147460
  11.5 12.0 %collective-permute-start = (f32[3,1536]{1,0:T(4,128)}, f32[3,1536]{1,0:T(4,128)S(1)}, u32[]{:S(2)}, u32[]{:S(2)}) collective-permute-start(f32[3,1536]{1,0:T(4,128)} %fusion.65), channel_id=1, source_target_pairs={{0,4},{4,8},{8,12},{12,16},{16,20},{20,24},{24,28},{1,5},{5,9},{9,... | collective-permute-start | bytes 55304 | tf_op jit(solution)/shard_map/ppermute | solution.py:58
  17.5 57.2 %copy-start.88 = (s32[256]{0:T(256)}, s32[256]{0:T(256)S(1)}, u32[]{:S(2)}) copy-start(s32[256]{0:T(256)S(1)} %reshape.528) | copy-start | bytes 3076
  17.7 56.7 %copy-start.81 = (s32[256]{0:T(256)}, s32[256]{0:T(256)S(1)}, u32[]{:S(2)}) copy-start(s32[256]{0:T(256)S(1)} %reshape.529) | copy-start | bytes 3076
  23.4 15.2 %copy-start.17 = (f32[3,1536]{1,0:T(4,128)}, f32[3,1536]{1,0:T(4,128)S(1)}, u32[]{:S(2)}) copy-start(f32[3,1536]{1,0:T(4,128)S(1)} %collective-permute-done.rim_ref) | copy-start | bytes 55300
  23.6 484.8 %copy-start.8 = (f32[3,32,8,128]{3,2,1,0:T(8,128)}, f32[3,32,8,128]{3,2,1,0:T(8,128)S(1)}, u32[]{:S(2)}) copy-start(f32[3,32,8,128]{3,2,1,0:T(8,128)S(1)} %broadcast_in_dim.21.mask_ref) | copy-start | bytes 1179652
  74.1 100.5 %copy-start.4 = (f32[256,16]{1,0:T(8,128)}, f32[256,16]{1,0:T(8,128)S(1)}, u32[]{:S(2)}) copy-start(f32[256,16]{1,0:T(8,128)S(1)} %get-tuple-element.126) | copy-start | bytes 49156
  74.1 100.5 %copy-start.2 = (f32[256,768]{1,0:T(8,128)}, f32[256,768]{1,0:T(8,128)S(1)}, u32[]{:S(2)}) copy-start(f32[256,768]{1,0:T(8,128)S(1)} %get-tuple-element.125) | copy-start | bytes 2359300
  74.7 99.9 %copy-start.105 = (f32[256]{0:T(256)}, f32[256]{0:T(256)S(1)}, u32[]{:S(2)}) copy-start(f32[256]{0:T(256)S(1)} %select_reduce_fusion.1) | copy-start | bytes 3076
  74.7 99.9 %copy-start.103 = (f32[256]{0:T(256)}, f32[256]{0:T(256)S(1)}, u32[]{:S(2)}) copy-start(f32[256]{0:T(256)S(1)} %broadcast_select_fusion.1) | copy-start | bytes 3076
  75.0 99.6 %copy-start.72 = (s32[256]{0:T(256)S(1)}, s32[256]{0:T(256)}, u32[]{:S(2)}) copy-start(s32[256]{0:T(256)} %copy-done.71) | copy-start | bytes 3076
  177.0 25.3 %copy-start.57 = (f32[256,768]{1,0:T(8,128)}, f32[256,768]{1,0:T(8,128)S(1)}, u32[]{:S(2)}) copy-start(f32[256,768]{1,0:T(8,128)S(1)} %get-tuple-element.288.current_ref) | copy-start | bytes 2359300
  182.0 5.4 collective-permute-start.1
  202.4 242.9 %copy-start.50 = (f32[32,8,80]{2,1,0:T(8,128)}, f32[32,8,80]{2,1,0:T(8,128)S(1)}, u32[]{:S(2)}) copy-start(f32[32,8,80]{2,1,0:T(8,128)S(1)} %get-tuple-element.131.selection_ref) | copy-start | bytes 245764
  214.4 25.3 %copy-start.84 = (s32[256]{0:T(256)S(1)}, s32[256]{0:T(256)}, u32[]{:S(2)}) copy-start(s32[256]{0:T(256)} %copy-done.83) | copy-start | bytes 3076
  237.7 101.4 %copy-start.6 = (f32[256,16]{1,0:T(8,128)}, f32[256,16]{1,0:T(8,128)S(1)}, u32[]{:S(2)}) copy-start(f32[256,16]{1,0:T(8,128)S(1)} %get-tuple-element.137) | copy-start | bytes 49156
  237.7 101.4 %copy-start.23 = (bf16[256,768]{1,0:T(8,128)(2,1)}, bf16[256,768]{1,0:T(8,128)(2,1)S(1)}, u32[]{:S(2)}) copy-start(bf16[256,768]{1,0:T(8,128)(2,1)S(1)} %get-tuple-element.185) | copy-start | bytes 1179652
  239.4 99.7 %copy-start.79 = (f32[256]{0:T(256)}, f32[256]{0:T(256)S(1)}, u32[]{:S(2)}) copy-start(f32[256]{0:T(256)S(1)} %reduce_max.19) | copy-start | bytes 3076
  239.7 99.5 %copy-start.97 = (f32[256]{0:T(256)}, f32[256]{0:T(256)S(1)}, u32[]{:S(2)}) copy-start(f32[256]{0:T(256)S(1)} %fusion.63) | copy-start | bytes 3076
  239.9 99.2 %copy-start.52 = (f32[8,32,768]{2,1,0:T(8,128)S(1)}, f32[8,32,768]{2,1,0:T(8,128)}, u32[]{:S(2)}) copy-start(f32[8,32,768]{2,1,0:T(8,128)} %convert.39) | copy-start | bytes 2359300
  239.9 99.2 %copy-start.75 = (s32[256]{0:T(256)S(1)}, s32[256]{0:T(256)}, u32[]{:S(2)}) copy-start(s32[256]{0:T(256)} %copy-done.74) | copy-start | bytes 3076
  342.5 100.6 %copy-start.1 = (f32[256,768]{1,0:T(8,128)S(1)}, f32[256,768]{1,0:T(8,128)}, u32[]{:S(2)}) copy-start(f32[256,768]{1,0:T(8,128)} %copy-done) | copy-start | bytes 2359300
  342.5 100.6 %copy-start.7 = (f32[256,16]{1,0:T(8,128)S(1)}, f32[256,16]{1,0:T(8,128)}, u32[]{:S(2)}) copy-start(f32[256,16]{1,0:T(8,128)} %copy-done.6) | copy-start | bytes 49156
  342.5 100.6 %copy-start.67 = (bf16[2,768,16]{1,2,0:T(8,128)(2,1)S(1)}, bf16[2,768,16]{1,2,0:T(8,128)(2,1)}, u32[]{:S(2)}) copy-start(bf16[2,768,16]{1,2,0:T(8,128)(2,1)} %param.38) | copy-start | bytes 147460
  342.5 100.6 %copy-start.69 = (f32[768]{0:T(1024)S(1)}, f32[768]{0:T(1024)}, u32[]{:S(2)}) copy-start(f32[768]{0:T(1024)} %get-tuple-element.274) | copy-start | bytes 9220
  342.5 100.6 %copy-start.80 = (f32[256]{0:T(256)S(1)}, f32[256]{0:T(256)}, u32[]{:S(2)}) copy-start(f32[256]{0:T(256)} %copy-done.79) | copy-start | bytes 3076
  342.5 100.6 %copy-start.85 = (s32[256]{0:T(256)S(1)}, s32[256]{0:T(256)}, u32[]{:S(2)}) copy-start(s32[256]{0:T(256)} %copy-done.83) | copy-start | bytes 3076
  342.5 100.6 %copy-start.98 = (f32[256]{0:T(256)S(1)}, f32[256]{0:T(256)}, u32[]{:S(2)}) copy-start(f32[256]{0:T(256)} %copy-done.97) | copy-start | bytes 3076
  342.5 100.6 %copy-start.100 = (f32[256]{0:T(256)S(1)}, f32[256]{0:T(256)}, u32[]{:S(2)}) copy-start(f32[256]{0:T(256)} %get-tuple-element.302) | copy-start | bytes 3076
  519.8 5.9 collective-permute-start.2
  538.2 102.3 %copy-start.89 = (s32[256]{0:T(256)S(1)}, s32[256]{0:T(256)}, u32[]{:S(2)}) copy-start(s32[256]{0:T(256)} %copy-done.88) | copy-start | bytes 3076
  538.2 102.3 %copy-start.106 = (f32[256]{0:T(256)S(1)}, f32[256]{0:T(256)}, u32[]{:S(2)}) copy-start(f32[256]{0:T(256)} %copy-done.105) | copy-start | bytes 3076
  538.2 102.3 %copy-start.3 = (f32[256,768]{1,0:T(8,128)S(1)}, f32[256,768]{1,0:T(8,128)}, u32[]{:S(2)}) copy-start(f32[256,768]{1,0:T(8,128)} %copy-done.2) | copy-start | bytes 2359300
  538.3 102.3 %copy-start.5 = (f32[256,16]{1,0:T(8,128)S(1)}, f32[256,16]{1,0:T(8,128)}, u32[]{:S(2)}) copy-start(f32[256,16]{1,0:T(8,128)} %copy-done.4) | copy-start | bytes 49156
  538.3 102.3 %copy-start.68 = (bf16[2,768,16]{1,2,0:T(8,128)(2,1)S(1)}, bf16[2,768,16]{1,2,0:T(8,128)(2,1)}, u32[]{:S(2)}) copy-start(bf16[2,768,16]{1,2,0:T(8,128)(2,1)} %param.38) | copy-start | bytes 147460
  538.3 102.3 %copy-start.70 = (f32[768]{0:T(1024)S(1)}, f32[768]{0:T(1024)}, u32[]{:S(2)}) copy-start(f32[768]{0:T(1024)} %get-tuple-element.273) | copy-start | bytes 9220
  538.3 102.3 %copy-start.78 = (f32[256]{0:T(256)S(1)}, f32[256]{0:T(256)}, u32[]{:S(2)}) copy-start(f32[256]{0:T(256)} %copy-done.77) | copy-start | bytes 3076
  538.3 102.3 %copy-start.82 = (s32[256]{0:T(256)S(1)}, s32[256]{0:T(256)}, u32[]{:S(2)}) copy-start(s32[256]{0:T(256)} %copy-done.81) | copy-start | bytes 3076
  538.3 102.3 %copy-start.96 = (f32[256]{0:T(256)S(1)}, f32[256]{0:T(256)}, u32[]{:S(2)}) copy-start(f32[256]{0:T(256)} %copy-done.95) | copy-start | bytes 3076
  538.3 102.3 %copy-start.99 = (f32[256]{0:T(256)S(1)}, f32[256]{0:T(256)}, u32[]{:S(2)}) copy-start(f32[256]{0:T(256)} %get-tuple-element.298) | copy-start | bytes 3076
  672.9 33.8 %copy-start.9 = (f32[3,32,8,128]{3,2,1,0:T(8,128)S(1)}, f32[3,32,8,128]{3,2,1,0:T(8,128)}, u32[]{:S(2)}) copy-start(f32[3,32,8,128]{3,2,1,0:T(8,128)} %copy-done.8) | copy-start | bytes 1179652
  672.9 33.8 %copy-start.18 = (f32[3,1536]{1,0:T(4,128)S(1)}, f32[3,1536]{1,0:T(4,128)}, u32[]{:S(2)}) copy-start(f32[3,1536]{1,0:T(4,128)} %copy-done.17) | copy-start | bytes 55300
  719.1 33.3 %collective-permute-start.3 = (f32[3,1536]{1,0:T(4,128)S(1)}, f32[3,1536]{1,0:T(4,128)S(1)}, u32[]{:S(2)}, u32[]{:S(2)}) collective-permute-start(f32[3,1536]{1,0:T(4,128)S(1)} %get-tuple-element.178), channel_id=1, source_target_pairs={{4,0},{8,4},{12,8},{16,12},{20,16},{24,20},{28,24},{5,1},{9,5},{13... | collective-permute-start | bytes 55304 | tf_op jit(solution)/shard_map/ppermute | solution.py:58
  725.7 19.1 %copy-start.22 = (bf16[256,768]{1,0:T(8,128)(2,1)S(1)}, bf16[256,768]{1,0:T(8,128)(2,1)}, u32[]{:S(2)}) copy-start(bf16[256,768]{1,0:T(8,128)(2,1)} %copy-done.21) | copy-start | bytes 1179652
  (81 other events, 449.4 us)

commit v2 on v1

--- a/solution.py
+++ b/solution.py
@@ -83,7 +83,7 @@
 
 
 def microseconds(count):
-    return pl.CostEstimate(flops=int(count * 1.0e9), transcendentals=0, bytes_accessed=1000000)
+    return pl.CostEstimate(flops=int(count * 1.5e8), transcendentals=0, bytes_accessed=10000)
 
 
 def plain_call(kernel, grid, in_specs, out_specs, out_shapes, scratch, args, cost):
@@ -95,7 +95,7 @@
         out_shape=out_shapes,
         scratch_shapes=scratch,
         compiler_params=pltpu.CompilerParams(
-            dimension_semantics=("arbitrary",), vmem_limit_bytes=48 * MIB
+            dimension_semantics=("arbitrary",), vmem_limit_bytes=60 * MIB
         ),
         cost_estimate=microseconds(cost),
     )(*args)
@@ -139,7 +139,7 @@
             out_ref[step, n] = jnp.broadcast_to(tile[:, first + n : first + n + 1], (CHUNKS, LANES))
         return carry
 
-    lax.fori_loop(0, selection_ref.shape[0], one, 0)
+    lax.fori_loop(0, selection_ref.shape[0], one, 0, unroll=8)
 
 
 def rate_rows(rate):
@@ -248,7 +248,7 @@
             return tuple(levels) + (length,)
 
         zero = jnp.zeros((CHUNKS, LANES), jnp.float32)
-        found = lax.fori_loop(0, steps // 2, one, (zero,) * (states + 1))
+        found = lax.fori_loop(0, steps // 2, one, (zero,) * (states + 1), unroll=2)
         links, totals, link_size, total_size = chunk_links(found, found[states], rates, False)
         link_size_ref[:, lanes] = link_size
         total_size_ref[:, lanes] = total_size
@@ -335,7 +335,7 @@
         gated_ref[at, :] = jnp.concatenate(both, axis=0).astype(jnp.bfloat16)
         return tuple(levels)
 
-    lax.fori_loop(0, steps // 2, one, tuple(begin))
+    lax.fori_loop(0, steps // 2, one, tuple(begin), unroll=2)
     middle_ref[...] += dot_nn(gated_ref[...], out_weight_ref[...])
 
     @pl.when(pl.program_id(0) == tiles - 1)
@@ -418,7 +418,7 @@
         return tuple(levels) + (length, skip)
 
     zero = jnp.zeros((CHUNKS, LANES), jnp.float32)
-    found = lax.fori_loop(0, steps // 2, one, (zero,) * (states + 2))
+    found = lax.fori_loop(0, steps // 2, one, (zero,) * (states + 2), unroll=2)
     grad_skip_ref[...] = jnp.sum(found[states + 1], axis=0, keepdims=True)
     links, totals, link_size, total_size = chunk_links(found, found[states], rates, True)
     link_size_ref[...] = link_size
@@ -461,7 +461,7 @@
 def back_kernel(dims, size_ref, act_ref, grad_ref, decay_ref, selection_ref, reset_ref, begin_ref, link_ref,
                 link_size_ref, entering_ref, step_ref, step_bias_ref, skip_ref,
                 grad_act_ref, grad_decay_ref, grad_bias_ref, grad_step_ref, grad_selection_ref,
-                in_maps, out_maps, levels, decays, grad_in, grad_out, grad_size, grad_rate, grad_rank):
+                in_maps, out_maps, levels, decays, grad_in, grad_out, grad_size, grad_rate, grad_all):
     rank, states, steps, tiles = dims
     tokens = steps * CHUNKS
 
@@ -471,7 +471,6 @@
         spread_columns(selection_ref, rank + states, states, out_maps)
         grad_in[...] = jnp.zeros_like(grad_in)
         grad_out[...] = jnp.zeros_like(grad_out)
-        grad_rank[...] = jnp.zeros_like(grad_rank)
 
     true_rates = -jnp.exp(decay_ref[...])
     rates = rate_rows(true_rates * LOG2E)
@@ -496,7 +495,7 @@
                 levels[step + 1, n] = now[n]
         return tuple(now)
 
-    lax.fori_loop(0, steps // 2, ahead, tuple(begin))
+    lax.fori_loop(0, steps // 2, ahead, tuple(begin), unroll=2)
     link_size = link_size_ref[...]
     tail = []
     for n in range(states):
@@ -529,27 +528,29 @@
             grad_act_ref[step] = plain * by_input + grad * skip
         return tuple(passed)
 
-    lax.fori_loop(0, steps // 2, retreat, tuple(tail))
+    lax.fori_loop(0, steps // 2, retreat, tuple(tail), unroll=2)
     for n in range(states):
         grad_decay_ref[n : n + 1, :] = (
             jnp.sum(grad_rate[n], axis=0, keepdims=True) * true_rates[n : n + 1, :]
         )
-    rank_low = selection_ref[...].reshape(tokens, selection_ref.shape[2])[:, :rank].astype(jnp.bfloat16)
-    linear = dot_nn(rank_low, step_ref[...]) + step_bias_ref[...]
-    grad_linear = grad_size[...].reshape(tokens, LANES) * jax.nn.sigmoid(linear)
-    grad_bias_ref[...] = jnp.sum(grad_linear, axis=0, keepdims=True)
-    grad_low = grad_linear.astype(jnp.bfloat16)
-    grad_step_ref[...] = dot_tn(rank_low, grad_low)
-    grad_rank[...] += dot_nt(grad_low, step_ref[...])
+    tile = pl.program_id(0)
+    grad_all[:, pl.ds(pl.multiple_of(tile * LANES, LANES), LANES)] = grad_size[...].reshape(tokens, LANES)
 
     @pl.when(pl.program_id(0) == tiles - 1)
     def _():
+        rank_low = selection_ref[...].reshape(tokens, selection_ref.shape[2])[:, :rank].astype(jnp.bfloat16)
+        linear = dot_nn(rank_low, step_ref[...]) + step_bias_ref[...]
+        grad_linear = grad_all[...] * jax.nn.sigmoid(linear)
+        grad_bias_ref[...] = jnp.sum(grad_linear, axis=0, keepdims=True)
+        grad_low = grad_linear.astype(jnp.bfloat16)
+        grad_step_ref[...] = dot_tn(rank_low, grad_low)
+        grad_rank = dot_nt(grad_low, step_ref[...])
         size = states * LANES
         row = lax.broadcasted_iota(jnp.int32, (size, states), 0)
         column = lax.broadcasted_iota(jnp.int32, (size, states), 1)
         pick = ((row >= column * LANES) & (row < (column + 1) * LANES)).astype(jnp.float32)
         pick = pick.astype(jnp.bfloat16)
-        found = [grad_rank[...]]
+        found = [grad_rank]
         for ref in (grad_in, grad_out):
             full = ref[...].reshape(tokens, size)
             high = full.astype(jnp.bfloat16)
@@ -573,8 +574,9 @@
         (tiles,),
         [slab(steps), rows_of(tokens), slab(steps), layer_rows(layer, states), whole(selection.shape),
          whole(reset.shape), slab(states), slab(states), rows_of(CHUNKS), rows_of(states),
-         layer_rows(layer, rank), layer_rows(layer, 1), layer_rows(layer, 1)],
-        [slab(steps), rows_of(states), rows_of(1), rows_of(rank), whole((tokens, columns))],
+         layer_whole(layer, (rank, channels)), layer_whole(layer, (1, channels)), layer_rows(layer, 1)],
+        [slab(steps), rows_of(states), whole((1, channels)), whole((rank, channels)),
+         whole((tokens, columns))],
         [
             shaped((steps, CHUNKS, channels)),
             shaped((states, channels)),
@@ -584,7 +586,7 @@
         ],
         [maps, maps, VMEM((steps + 1, states, CHUNKS, LANES), f32), maps,
          VMEM((steps, CHUNKS, states * LANES), f32), VMEM((steps, CHUNKS, states * LANES), f32),
-         VMEM((steps, CHUNKS, LANES), f32), VMEM((states, CHUNKS, LANES), f32), VMEM((tokens, rank), f32)],
+         VMEM((steps, CHUNKS, LANES), f32), VMEM((states, CHUNKS, LANES), f32), VMEM((tokens, channels), f32)],
         (size, act, grad_y, decay_log, selection, reset, begin, link, link_size, entering, step_weight,
          step_bias, skip_weight),
         35,
@@ -784,58 +786,59 @@
             dma, dma, dma, dma,
         ],
         compiler_params=pltpu.CompilerParams(
-            collective_id=identity, has_side_effects=True, vmem_limit_bytes=16 * MIB
+            collective_id=identity, has_side_effects=True, vmem_limit_bytes=60 * MIB
         ),
         cost_estimate=microseconds(12),
     )(total, size, decay_log)
 
 
-def gelu_parts(values):
-    bell = 0.5 * (1.0 + lax.erf(values * 0.7071067811865476))
-    return bell
-
-
-def expert_kernel(dims, backward, layer, *refs):
-    count, groups, experts, block, share, width, hidden = dims
+def bell(values):
+    return 0.5 * (1.0 + lax.erf(values * 0.7071067811865476))
+
+
+def expert_kernel(dims, backward, *refs):
+    count, groups, members, block, share, width, hidden = dims
+    folded = folds(width, hidden)
+    out_ref, perm_ref, *refs = refs
+    weight_refs, refs = (refs[:1], refs[1:]) if folded else (refs[:2], refs[2:])
     if backward:
-        (out_ref, perm_ref, up_hbm, down_hbm, pre_hbm, ret_ref, rows_hbm, low_hbm,
-         arrived, rows, pre, low, part, got, final, landed, up, down,
-         there_send, there_recv, gather_send, gather_recv, sum_send, sum_recv,
-         back_send, back_recv, local) = refs
+        pre_hbm, ret_ref, rows_hbm, low_hbm, *scratch = refs
     else:
-        (out_ref, perm_ref, up_hbm, down_hbm, ret_ref, rows_hbm, pre_hbm, low_hbm,
-         arrived, rows, pre, low, part, got, final, landed, up, down,
-         there_send, there_recv, gather_send, gather_recv, sum_send, sum_recv,
-         back_send, back_recv, local) = refs
+        ret_ref, rows_hbm, pre_hbm, low_hbm, *scratch = refs
+    (arrived, own, rows, pre, low, part, got, final, landed, up, down, total,
+     there_send, there_recv, row_send, row_recv, sum_send, sum_recv, back_send, back_recv, local) = scratch
+    f32, bf16 = jnp.float32, jnp.bfloat16
     here = lax.axis_index("wide")
     group = lax.axis_index("narrow")
-    half = count // 2
-
-    def window_of(position):
-        position = lax.rem(position + 2 * count, count)
-        upper = position // half
-        return 2 * position * (1 - upper) + (2 * (count - 1 - position) + 1) * upper
-
-    odd = lax.rem(here, 2)
-    spot = (here // 2) * (1 - odd) + (count - 1 - here // 2) * odd
-    ring = (window_of(spot + 1), window_of(spot - 1))
+    quads = count // members
+    quad, member = here // members, lax.rem(here, members)
     peers = [lax.rem(group + k, groups) for k in range(1, groups)]
 
-    loads = [
-        pltpu.make_async_copy(up_hbm.at[layer], up, local.at[0]),
-        pltpu.make_async_copy(down_hbm.at[layer], down, local.at[1]),
-    ]
+    fold = max(folded, 1)
+    loads = [pltpu.make_async_copy(weight_refs[0].at[:, pl.ds(0, width)], up, local.at[0])]
+    for f in range(folded):
+        loads.append(pltpu.make_async_copy(
+            weight_refs[0].at[:, pl.ds(width + f * hidden, hidden)],
+            down.at[:, :, pl.ds(f * hidden, hidden)], local.at[1 + f]))
+    if not folded:
+        loads.append(pltpu.make_async_copy(weight_refs[1], down, local.at[1]))
     if backward:
-        loads.append(pltpu.make_async_copy(pre_hbm, pre, local.at[2]))
+        loads.append(pltpu.make_async_copy(pre_hbm, pre, local.at[1 + fold]))
     for load in loads:
         load.start()
 
+    def window_at(away, turn):
+        return lax.rem(quad + away, quads) * members + lax.rem(member + turn, members)
+
     barrier = pltpu.get_barrier_semaphore()
-    for window in ring:
-        pl.semaphore_signal(barrier, inc=1, device_id=(window, group), device_id_type=MESH)
     for peer in peers:
         pl.semaphore_signal(barrier, inc=1, device_id=(here, peer), device_id_type=MESH)
-    pl.semaphore_wait(barrier, groups + 1)
+    for away in range(quads):
+        for turn in range(members):
+            if away or turn:
+                pl.semaphore_signal(
+                    barrier, inc=1, device_id=(window_at(away, turn), group), device_id_type=MESH)
+    pl.semaphore_wait(barrier, groups - 1 + count - 1)
 
     there = []
     for k, peer in enumerate(peers):
@@ -847,111 +850,115 @@
     for copy in there:
         copy.wait_recv()
     flat = arrived[...].reshape(groups * block, width)
-    own = dot_nn(perm_ref[...], flat).astype(jnp.bfloat16).reshape(experts, share, width)
+    own[...] = dot_nn(perm_ref[...], flat).astype(bf16).reshape(members, share, width)
 
     def span(window):
         return pl.ds(pl.multiple_of(window * share, 16), share)
 
-    rows[:, span(here), :] = own
+    sent = []
+
+    def carry(away, turn):
+        window = window_at(away, turn)
+        copy = pltpu.make_async_remote_copy(
+            src_ref=own.at[lax.rem(member + turn, members)], dst_ref=rows.at[span(here), :],
+            send_sem=row_send.at[away, turn], recv_sem=row_recv.at[away, turn],
+            device_id=(window, group), device_id_type=MESH)
+        copy.start()
+        sent.append(copy)
+
+    for turn in range(members):
+        for away in list(range(1, quads)) + [0]:
+            if away or turn:
+                carry(away, turn)
+    rows[span(here), :] = own[member]
+
+    def arrive(away, turn):
+        window = lax.rem(quad + quads - away, quads) * members + lax.rem(member + members - turn, members)
+        pltpu.make_async_remote_copy(
+            src_ref=own.at[member], dst_ref=rows.at[span(window), :],
+            send_sem=row_send.at[away, turn], recv_sem=row_recv.at[away, turn],
+            device_id=(window, group), device_id_type=MESH).wait_recv()
+        return window
 
     def compute(windows):
-        def one(e, carry):
-            x = jnp.concatenate([rows[e, span(w), :] for w in windows], axis=0)
+        size = len(windows) * share
+
+        def one(s, carry):
+            x = jnp.concatenate([rows[span(w), :] for w in windows], axis=0)
             if backward:
-                grad_hidden = dot_nt(x, down[e])
-                before = jnp.concatenate([pre[e, span(w), :] for w in windows], axis=0)
-                slope = gelu_parts(before) + before * (
-                    0.3989422804014327 * jnp.exp(-0.5 * before * before)
-                )
-                middle = (grad_hidden * slope).astype(jnp.bfloat16)
-                y = dot_nt(middle, up[e])
+                grad_hidden = dot_nt(x, down[s])
+                before = jnp.concatenate([pre[s, span(w), :] for w in windows], axis=0)
+                slope = bell(before) + before * (0.3989422804014327 * jnp.exp(-0.5 * before * before))
+                middle = (grad_hidden * slope).astype(bf16)
+                y = dot_nt(middle, up[s])
             else:
-                before = dot_nn(x, up[e])
-                middle = (before * gelu_parts(before)).astype(jnp.bfloat16)
-                y = dot_nn(middle, down[e])
-            y = y.astype(jnp.bfloat16)
+                before = dot_nn(x, up[s])
+                middle = (before * bell(before)).astype(bf16)
+                y = dot_nn(middle, down[s])
             for index, w in enumerate(windows):
                 piece = slice(index * share, (index + 1) * share)
                 if not backward:
-                    pre[e, span(w), :] = before[piece]
-                low[e, span(w), :] = middle[piece]
-                part[e, span(w), :] = y[piece]
+                    pre[s, span(w), :] = before[piece]
+                low[s, span(w), :] = middle[piece]
+
+            @pl.when(s == 0)
+            def _():
+                total[:size] = y
+
+            @pl.when(s > 0)
+            def _():
+                total[:size] += y
+
             return carry
 
-        lax.fori_loop(0, experts, one, 0)
-
-    cut = experts // 2
-    halves = (pl.ds(0, cut), pl.ds(cut, experts - cut))
-    gathers = []
-
-    def parts_at(step):
-        return [(way, sign, piece) for piece in (0, 1) for way, sign in ((0, 1), (1, -1))
-                if step < half or piece == way]
-
-    def hop(step, way, sign, piece):
-        origin = window_of(spot - sign * (step - 1))
-        return pltpu.make_async_remote_copy(
-            src_ref=rows.at[halves[piece], span(origin), :], dst_ref=rows.at[halves[piece], span(origin), :],
-            send_sem=gather_send.at[way, step - 1, piece], recv_sem=gather_recv.at[way, step - 1, piece],
-            device_id=(ring[way], group), device_id_type=MESH)
-
-    def pass_on(step, way, sign, piece):
-        copy = hop(step, way, sign, piece)
+        lax.fori_loop(0, members, one, 0)
+        for index, w in enumerate(windows):
+            part[w] = total[index * share : (index + 1) * share].astype(bf16)
+
+    def give_back(away, turn, window):
+        copy = pltpu.make_async_remote_copy(
+            src_ref=part.at[window], dst_ref=got.at[here],
+            send_sem=sum_send.at[away, turn], recv_sem=sum_recv.at[away, turn],
+            device_id=(window, group), device_id_type=MESH)
         copy.start()
-        gathers.append(copy)
-
-    for way, sign, piece in parts_at(1):
-        pass_on(1, way, sign, piece)
+        sent.append(copy)
+
     for load in loads:
         load.wait()
-    compute([here])
-    for step in range(1, half + 1):
-        for way, sign, piece in parts_at(step):
-            hop(step, way, sign, piece).wait_recv()
-            if step < half and (way, sign, piece) in parts_at(step + 1):
-                pass_on(step + 1, way, sign, piece)
-        if step < half:
-            compute([window_of(spot - step), window_of(spot + step)])
-        else:
-            compute([window_of(spot + half)])
+    windows = [here] + [arrive(0, turn) for turn in range(1, members)]
+    compute(windows)
+    for turn in range(1, members):
+        give_back(0, turn, windows[turn])
+    got[here] = part[here]
+    for away in range(1, quads):
+        for first in range(0, members, 2):
+            windows = [arrive(away, turn) for turn in (first, first + 1)]
+            compute(windows)
+            for turn in (first, first + 1):
+                give_back(away, turn, windows[turn - first])
 
     saves = [
-        pltpu.make_async_copy(rows, rows_hbm, local.at[3]),
-        pltpu.make_async_copy(low, low_hbm, local.at[4]),
+        pltpu.make_async_copy(rows, rows_hbm, local.at[2 + fold]),
+        pltpu.make_async_copy(low, low_hbm, local.at[3 + fold]),
     ]
     if not backward:
-        saves.append(pltpu.make_async_copy(pre, pre_hbm, local.at[2]))
+        saves.append(pltpu.make_async_copy(pre, pre_hbm, local.at[1 + fold]))
     for save in saves:
         save.start()
 
-    sums, last = [], {}
-    for step in range(half):
-        for which in (0, 1):
-            for way, sign in ((0, 1), (1, -1)):
-                if step == 0 and which != way:
-                    continue
-                window = window_of(spot + sign * (half - step))
-                held = halves[which]
-                if (way, which) in last:
-                    last[way, which].wait_recv()
-                    part[held, span(window), :] = (
-                        part[held, span(window), :].astype(jnp.float32)
-                        + got[way, step - 1, held].astype(jnp.float32)
-                    ).astype(jnp.bfloat16)
-                copy = pltpu.make_async_remote_copy(
-                    src_ref=part.at[held, span(window), :], dst_ref=got.at[way, step, held],
-                    send_sem=sum_send.at[way, step, which], recv_sem=sum_recv.at[way, step, which],
-                    device_id=(ring[way], group), device_id_type=MESH)
-                copy.start()
-                sums.append(copy)
-                last[way, which] = copy
-    total = part[:, span(here), :].astype(jnp.float32)
-    for way in (0, 1):
-        for which in (0, 1):
-            last[way, which].wait_recv()
-        total = total + got[way, half - 1].astype(jnp.float32)
-    packed = total.astype(jnp.bfloat16).reshape(experts * share, width)
-    final[...] = dot_tn(perm_ref[...], packed).astype(jnp.bfloat16).reshape(groups, block, width)
+    for away in range(quads):
+        for turn in range(members):
+            if away or turn:
+                window = window_at(away, turn)
+                pltpu.make_async_remote_copy(
+                    src_ref=part.at[here], dst_ref=got.at[window],
+                    send_sem=sum_send.at[away, turn], recv_sem=sum_recv.at[away, turn],
+                    device_id=(window, group), device_id_type=MESH).wait_recv()
+    summed = got[pl.ds(0, members)].astype(f32)
+    for q in range(1, quads):
+        summed = summed + got[pl.ds(q * members, members)].astype(f32)
+    packed = summed.astype(bf16).reshape(members * share, width)
+    final[...] = dot_tn(perm_ref[...], packed).astype(bf16).reshape(groups, block, width)
 
     home = []
     for k, peer in enumerate(peers):
@@ -960,61 +967,60 @@
             recv_sem=back_recv.at[k], device_id=(here, peer), device_id_type=MESH))
         home[-1].start()
     ret_ref[group] = final[group]
-    for k, copy in enumerate(home):
+    for copy in home:
         copy.wait_recv()
     for k in range(1, groups):
         source = lax.rem(group + groups - k, groups)
         ret_ref[source] = landed[source]
-    for copy in there + gathers + sums + home:
+    for copy in there + sent + home:
         copy.wait_send()
     for save in saves:
         save.wait()
 
 
-def expert_pass(outbound, perm, expert_up, expert_down, pre, layer, identity):
+def expert_pass(outbound, perm, weights, pre, identity):
     count, groups = lax.axis_size("wide"), lax.axis_size("narrow")
     backward = pre is not None
     _, block, width = outbound.shape
-    _, experts, _, hidden = expert_up.shape
-    share = perm.shape[0] // experts
-    half = count // 2
+    members, _, hidden = weights[0].shape
+    share = perm.shape[0] // members
+    quads = count // members
     total = count * share
     low, f32 = jnp.bfloat16, jnp.float32
-    dims = (count, groups, experts, block, share, width, hidden)
-    anywhere, inside = pl.BlockSpec(memory_space=pl.ANY), pl.BlockSpec(memory_space=VMEM)
-    saved_rows = jax.ShapeDtypeStruct((experts, total, width), low)
-    saved_low = jax.ShapeDtypeStruct((experts, total, hidden), low)
-    saved_pre = jax.ShapeDtypeStruct((experts, total, hidden), f32)
-    back = jax.ShapeDtypeStruct((groups, block, width), low)
+    dims = (count, groups, members, block, share, width, hidden)
+    inside = pl.BlockSpec(memory_space=VMEM)
+    args = (outbound, perm) + tuple(weights) + ((pre,) if backward else ())
+    outs = [shaped((groups, block, width), low), shaped((total, width), low)]
+    outs += ([] if backward else [shaped((members, total, hidden))]) + [shaped((members, total, hidden), low)]
     dma = pltpu.SemaphoreType.DMA
-    args = (outbound, perm, expert_up, expert_down) + ((pre,) if backward else ())
-    outs = [back, saved_rows] + ([] if backward else [saved_pre]) + [saved_low]
     return pl.pallas_call(
-        functools.partial(expert_kernel, dims, backward, layer),
+        functools.partial(expert_kernel, dims, backward),
         out_shape=outs,
-        in_specs=[inside, inside] + [anywhere] * (len(args) - 2),
-        out_specs=[inside] + [anywhere] * (len(outs) - 1),
+        in_specs=[inside, inside] + [ANYWHERE] * (len(args) - 2),
+        out_specs=[inside] + [ANYWHERE] * (len(outs) - 1),
         scratch_shapes=[
             VMEM((groups, block, width), low),
-            VMEM((experts, total, width), low),
-            VMEM((experts, total, hidden), f32),
-            VMEM((experts, total, hidden), low),
-            VMEM((experts, total, width), low),
-            VMEM((2, half, experts, share, width), low),
+            VMEM((members, share, width), low),
+            VMEM((total, width), low),
+            VMEM((members, total, hidden), f32),
+            VMEM((members, total, hidden), low),
+            VMEM((count, share, width), low),
+            VMEM((count, share, width), low),
             VMEM((groups, block, width), low),
             VMEM((groups, block, width), low),
-            VMEM((experts, width, hidden), low),
-            VMEM((experts, hidden, width), low),
+            VMEM((members, width, hidden), low),
+            VMEM((members, hidden, width), low),
+            VMEM((members * share, width), f32),
             dma((groups - 1,)), dma((groups - 1,)),
-            dma((2, half, 2)), dma((2, half, 2)),
-            dma((2, half, 2)), dma((2, half, 2)),
+            dma((quads, members)), dma((quads, members)),
+            dma((quads, members)), dma((quads, members)),
             dma((groups - 1,)), dma((groups - 1,)),
-            dma((5,)),
+            dma((4 + max(folds(width, hidden), 1),)),
         ],
         compiler_params=pltpu.CompilerParams(
-            collective_id=identity, has_side_effects=True, vmem_limit_bytes=56 * MIB
+            collective_id=identity, has_side_effects=True, vmem_limit_bytes=60 * MIB
         ),
-        cost_estimate=microseconds(95),
+        cost_estimate=microseconds(65),
     )(*args)
 
 
@@ -1024,6 +1030,113 @@
     expert, rest = row // share, row % share
     source = (rest // capacity) * block + expert * capacity + rest % capacity
     return (source[:, None] == jnp.arange(groups * block, dtype=jnp.int32)[None, :]).astype(jnp.bfloat16)
+
+
+def between_members(arrays):
+    count, members = lax.axis_size("wide"), arrays[0].shape[0]
+    quads = [list(range(first, first + members)) for first in range(0, count, members)]
+    return [
+        lax.all_to_all(values, "wide", split_axis=0, concat_axis=0, tiled=True, axis_index_groups=quads)
+        for values in arrays
+    ]
+
+
+def folds(width, hidden):
+    return 0 if hidden % LANES else width // hidden
+
+
+def pack_kernel(up_ref, down_ref, out_ref):
+    width, hidden = up_ref.shape
+    out_ref[:width] = up_ref[...]
+    for f in range(width // hidden):
+        out_ref[width + f * hidden : width + (f + 1) * hidden] = down_ref[:, f * hidden : (f + 1) * hidden]
+
+
+def packed_weights(layer, up, down):
+    _, experts, width, hidden = up.shape
+    if not folds(width, hidden):
+        return [up[layer], down[layer]]
+    return [plain_call(
+        pack_kernel,
+        (experts,),
+        [pl.BlockSpec((None, None, width, hidden), lambda e: (layer, e, 0, 0)),
+         pl.BlockSpec((None, None, hidden, width), lambda e: (layer, e, 0, 0))],
+        pl.BlockSpec((None, 2 * width, hidden), lambda e: (e, 0, 0)),
+        shaped((experts, 2 * width, hidden), up.dtype),
+        [],
+        (up, down),
+        4,
+    )]
+
+
+def weights_kernel(rows_ref, pre_ref, hidden_ref, grad_ref, *out_refs):
+    width, hidden = rows_ref.shape[1], pre_ref.shape[1]
+    low = jnp.bfloat16
+    up = dot_tn(rows_ref[...], pre_ref[...]).astype(low)
+    down = dot_tn(hidden_ref[...], grad_ref[...]).astype(low)
+    if len(out_refs) == 2:
+        out_refs[0][...], out_refs[1][...] = up, down
+        return
+    out_refs[0][:width] = up
+    for f in range(width // hidden):
+        out_refs[0][width + f * hidden : width + (f + 1) * hidden] = down[:, f * hidden : (f + 1) * hidden]
+
+
+def expert_weights(rows, pre, hidden_rows, grad_rows):
+    total, width = rows.shape
+    members, _, hidden = pre.shape
+    slices = pl.BlockSpec((None, total, hidden), lambda s: (s, 0, 0))
+    sizes = [(2 * width, hidden)] if folds(width, hidden) else [(width, hidden), (hidden, width)]
+    return plain_call(
+        weights_kernel,
+        (members,),
+        [whole((total, width)), slices, slices, whole((total, width))],
+        [pl.BlockSpec((None,) + size, lambda s: (s, 0, 0)) for size in sizes],
+        [shaped((members,) + size, jnp.bfloat16) for size in sizes],
+        [],
+        (rows, pre, hidden_rows, grad_rows),
+        6,
+    )
+
+
+def widen_kernel(experts, *refs):
+    up_ref, down_ref = refs[-2:]
+    refs = refs[:-2]
+    width, hidden = up_ref.shape
+    for layer in (0, 1):
+        @pl.when(pl.program_id(0) // experts == layer)
+        def _():
+            if len(refs) == 4:
+                up_ref[...] = refs[2 * layer][...].astype(jnp.float32)
+                down_ref[...] = refs[2 * layer + 1][...].astype(jnp.float32)
+                return
+            up_ref[...] = refs[layer][:width].astype(jnp.float32)
+            for f in range(width // hidden):
+                down_ref[:, f * hidden : (f + 1) * hidden] = refs[layer][
+                    width + f * hidden : width + (f + 1) * hidden].astype(jnp.float32)
+
+
+def widened(first, second, width, hidden):
+    experts = first[0].shape[0]
+    specs = []
+    for layer, arrays in enumerate((first, second)):
+        for array in arrays:
+            if layer == 0:
+                place = lambda i: (jnp.minimum(i, experts - 1), 0, 0)
+            else:
+                place = lambda i: (jnp.maximum(i - experts, 0), 0, 0)
+            specs.append(pl.BlockSpec((None,) + array.shape[1:], place))
+    return plain_call(
+        functools.partial(widen_kernel, experts),
+        (2 * experts,),
+        specs,
+        [pl.BlockSpec((None, None, width, hidden), lambda i: (i // experts, i % experts, 0, 0)),
+         pl.BlockSpec((None, None, hidden, width), lambda i: (i // experts, i % experts, 0, 0))],
+        [shaped((2, experts, width, hidden)), shaped((2, experts, hidden, width))],
+        [],
+        tuple(first) + tuple(second),
+        9,
+    )
 
 
 def sum_kernel(dims, *refs):
@@ -1242,47 +1355,10 @@
             dma((lines - 1,)), dma((lines - 1,)),
         ],
         compiler_params=pltpu.CompilerParams(
-            collective_id=identity, has_side_effects=True, vmem_limit_bytes=56 * MIB
+            collective_id=identity, has_side_effects=True, vmem_limit_bytes=60 * MIB
         ),
         cost_estimate=microseconds(60),
     )(*[array.reshape(count, lines, 2, array.shape[1], width) for array in arrays])
-
-
-def weights_kernel(experts, *refs):
-    first, second, (up_ref, down_ref) = refs[:4], refs[4:8], refs[8:]
-    for layer, (rows, pre, hidden, grad) in enumerate((first, second)):
-        @pl.when(pl.program_id(0) // experts == layer)
-        def _():
-            up_ref[...] = dot_tn(rows[...], pre[...])
-            down_ref[...] = dot_tn(hidden[...], grad[...])
-
-
-def expert_weights(kept):
-    experts, total, width = kept[0][0].shape
-    hidden = kept[0][1].shape[2]
-    f32 = jnp.float32
-    specs = []
-    for layer in (0, 1):
-        for columns in (width, hidden, hidden, width):
-            if layer == 0:
-                place = lambda i: (jnp.minimum(i, experts - 1), 0, 0)
-            else:
-                place = lambda i: (jnp.maximum(i - experts, 0), 0, 0)
-            specs.append(pl.BlockSpec((None, total, columns), place))
-    outs = [
-        pl.BlockSpec((None, None, width, hidden), lambda i: (i // experts, i % experts, 0, 0)),
-        pl.BlockSpec((None, None, hidden, width), lambda i: (i // experts, i % experts, 0, 0)),
-    ]
-    return plain_call(
-        functools.partial(weights_kernel, experts),
-        (2 * experts,),
-        specs,
-        outs,
-        [shaped((2, experts, width, hidden), f32), shaped((2, experts, hidden, width), f32)],
-        [],
-        tuple(kept[0]) + tuple(kept[1]),
-        15,
-    )
 
 
 def on_device(
@@ -1347,20 +1423,32 @@
         onehots.append((chosen[:, None] == jnp.arange(experts, dtype=jnp.int32)[None, :]).astype(f32))
         keeps.append(kept.astype(f32)[:, None])
 
+    tail = passed_along(hidden[0, tokens - taps + 1 :] * keep_mask.astype(low), 1)
+    weights = [None] * layers
+    ready, tail = lax.optimization_barrier((packed_weights(0, expert_up, expert_down), tail))
+    weights[0] = between_members(ready)
     for layer in range(layers):
         begin = current
         normed = rms_scale(current, norm_mix[layer]).astype(low)
         projected = cube(dot_nn(normed, in_weight[layer]))
-        rim = passed_along(projected[steps - taps + 1 :, CHUNKS - 1, :inner] * keep_mask, 1)
+        if layer == 0:
+            before = rms_scale(tail.astype(f32), norm_mix[layer]).astype(low)
+            rim = dot_nn(before, in_weight[layer, :, :inner])
+        else:
+            rim = passed_along(projected[steps - taps + 1 :, CHUNKS - 1, :inner] * keep_mask, 1)
         act, selection, size, link, link_size, total, total_size = mixer_front(
             layer, projected, rim, masks, reset, conv_weight, conv_bias, state_weight, step_weight, step_bias,
             decay_log)
         entering = handed_on(layer, total, total_size, decay_log, False, layer)
+        if layer + 1 < layers:
+            ready, entering = lax.optimization_barrier(
+                (packed_weights(layer + 1, expert_up, expert_down), entering))
+            weights[layer + 1] = between_members(ready)
         mixed, gated, begins, middle, routed, logits, outbound = mixer_run(
             layer, size, act, selection, reset, decay_log, link, link_size, entering, projected, skip_weight,
             out_weight, current, norm_expert, router, fills[layer])
         returned, kept_rows, pre_act, hidden_low = expert_pass(
-            outbound.reshape(groups, block, width), order, expert_up, expert_down, None, layer, 4 + layer)
+            outbound.reshape(groups, block, width), order, weights[layer], None, 4 + layer)
         shares = jax.nn.softmax(logits, axis=-1)
         gate = jnp.sum(shares * onehots[layer], axis=1, keepdims=True)
         back_rows = dot_tn(fills[layer], returned.reshape(groups * block, width))
@@ -1372,7 +1460,7 @@
     output = to_tokens(cube(current.astype(low)))[None]
     grad = to_steps(cotangent[0]).reshape(tokens, width).astype(f32)
     packed = [None] * layers
-    expert_kept = [None] * layers
+    expert_grads = [None] * layers
     per_device = inner // devices
     norm_device = width // devices
     fold = width // (2 * LANES)
@@ -1384,8 +1472,8 @@
         grad_gate = keep * jnp.sum(grad * entry["back_rows"], axis=1, keepdims=True)
         outbound = dot_nn(fill, grad_rows_low).astype(low).reshape(groups, block, width)
         inbound, grad_rows, grad_pre = expert_pass(
-            outbound, order, expert_up, expert_down, entry["pre_act"], layer, 6 + layer)
-        expert_kept[layer] = (entry["kept_rows"], grad_pre, entry["hidden_low"], grad_rows)
+            outbound, order, weights[layer], entry["pre_act"], 6 + layer)
+        ready = expert_weights(entry["kept_rows"], grad_pre, entry["hidden_low"], grad_rows)
         grad_sent = dot_tn(fill, inbound.reshape(groups * block, width))
         grad_logits_low = ((grad_gate * gate) * (onehots[layer] - entry["shares"])).astype(low)
         grad_router = dot_tn(entry["routed"], grad_logits_low)
@@ -1397,6 +1485,8 @@
             layer, grad_low, out_weight, entry["projected"], entry["mixed"], entry["act"], entry["gated"],
             entry["size"], entry["selection"], reset, decay_log)
         entering = handed_on(layer, total, total_size, decay_log, True, 2 + layer)
+        ready, entering = lax.optimization_barrier((ready, entering))
+        expert_grads[layer] = between_members(ready)
         grad_act, grad_decay, grad_bias, grad_step, grad_selection = mixer_back(
             layer, entry["size"], entry["act"], grad_y, decay_log, entry["selection"], reset,
             entry["begins"], link, link_size, entering, step_weight, step_bias, skip_weight)
@@ -1423,7 +1513,7 @@
             grad_out.reshape(devices, -1, width),
             channel.reshape(devices, -1, width),
         ]
-    up_grads, down_grads = expert_weights(expert_kept)
+    up_grads, down_grads = widened(*expert_grads, width, expert_up.shape[3])
     sums = summed_shares([part for parts in packed for part in parts], 8)
     bounds = [0]
     for part in packed[0]:

time: 856 us -> 779 us (0.910)
  Pallas kernels: 737 us -> 626 us
  starting transfers between devices: 12.1 us -> 29.4 us
  local copies, waits for them, and re-layouts: 46.1 us -> 31.5 us
  waiting for transfers between devices: 2.11 us -> 13.3 us
  other arithmetic: 14.4 us -> 23.2 us
    pallas_call x4, Pallas kernels: 398 us -> 255 us  [expert_pass(): pl.pallas_call(functools.partial(expert_kernel, dims, backward), out_shap...]
    pallas_call x4, Pallas kernels: 45.4 us -> 79.4 us  [handed_on(): pl.pallas_call(functools.partial(link_kernel, layer, count, reverse), out...]
    all_to_all x0 -> x4, starting transfers between devices: none -> 20.5 us  [between_members(): lax.all_to_all(values, 'wide', split_axis=0, concat_axis=0, tiled=True, a...]
    unnamed x256 -> x180, local copies, waits for them, and re-layouts: 18.1 us -> 5.98 us
    ppermute x4, waiting for transfers between devices: 2.11 us -> 13.3 us  [passed_along(): lax.ppermute(x, 'wide', [(i, i + by) for i in range(size) if 0 <= i + by...]
    pallas_call x11 -> x15, Pallas kernels: 219 us -> 216 us  [plain_call(): pl.pallas_call(kernel, grid=grid, in_specs=in_specs, out_specs=out_specs,...]
  transfers between devices with their start and end apart: 4 -> 8, of which waited for: 2 -> 2; matrix products, arithmetic and copies ran while one was open for 2% -> 11% of each run, Pallas kernels for 2% -> 58%
where the time goes in v2:
time: 779 us; the launch traced here: 771 us
  Pallas kernels  626 us (80%)
  matrix products  45.2 us (6%)
  local copies, waits for them, and re-layouts  31.5 us (4%)
  starting transfers between devices  29.4 us (4%)
  other arithmetic  23.2 us (3%)
  waiting for transfers between devices  13.3 us (2%)
    pallas_call x4, Pallas kernels, expert_pass(): pl.pallas_call(functools.partial(expert_kernel, dims, backward), out_shap...  255 us
    pallas_call x15, Pallas kernels, plain_call(): pl.pallas_call(kernel, grid=grid, in_specs=in_specs, out_specs=out_specs,...  216 us
    pallas_call x4, Pallas kernels, handed_on(): pl.pallas_call(functools.partial(link_kernel, layer, count, reverse), out...  79.4 us
    pallas_call x1, Pallas kernels, summed_shares(): pl.pallas_call(functools.partial(sum_kernel, (count, lines, sizes, first,...  75.2 us
    all_to_all x4, starting transfers between devices, between_members(): lax.all_to_all(values, 'wide', split_axis=0, concat_axis=0, tiled=True, a...  20.5 us
    dot_general x8, matrix products, dot_tn(): lax.dot_general(left, right, (((0,), (0,)), ((), ())), preferred_element_...  17.7 us
  transfers between devices with their start and end apart: 8, of which 2 were waited for; matrix products, arithmetic and copies ran while one was open for 11% of the time, Pallas kernels for 58%

profile of v2, /device:TPU:0, one launch (start us, length us, event | category | flops | bytes accessed | tf_op | source)
XLA Modules:
  0.0 771.0 jit_solution(6508376614396417499)
XLA Ops:
  2.7 4.9 collective-permute-start
  7.6 5.0 shard_map.306
  12.7 5.1 all-to-all-start
  20.7 5.0 shard_map.308
  26.3 5.7 fusion.4.value_ref.gate_ref
  32.1 2.7 fusion.12.rim_ref
  36.5 13.8 %shard_map.307 = (bf16[256,1536]{1,0:T(8,128)(2,1)}, f32[32,8,80]{2,1,0:T(8,128)}, f32[32,8,1536]{2,1,0:T(8,128)}, f32[16,8,1536]{2,1,0:T(8,128)}, f32[8,1536]{1...) custom-call(f32[32,8,3072]{2,1,0:T(8,128)} %fusion.4.value_ref.gate_ref, f32[3,1536]{1,0:T(4,128)} %fusion.12.rim_ref, ...), custom_call_target="tpu_custom_call" | custom-call | flops 2700000000 | bytes 10000 | tf_op jit(solution)/shard_map/pallas_call | solution.py:90
  50.4 29.2 %shard_map.309.entering_ref = f32[16,1536]{1,0:T(8,128)} custom-call(f32[16,1536]{1,0:T(8,128)} %get-tuple-element.132.total_ref, f32[1,1536]{1,0:T(1,128)} %get-tuple-element.133.size_ref, f32[2,16,1536]{2,1,0:T(8,128)} %decay_ref.23), custom_call_target="tpu_custom_call" | custom-call | flops 1800000000 | bytes 10000 | tf_op jit(solution)/shard_map/pallas_call | solution.py:772
  79.7 5.3 all-to-all-start.1
  91.6 18.6 %shard_map.310 = (f32[32,8,1536]{2,1,0:T(8,128)}, bf16[256,1536]{1,0:T(8,128)(2,1)}, f32[16,8,1536]{2,1,0:T(8,128)}, f32[256,768]{1,0:T(8,128)}, bf16[256,768]{1...) custom-call(f32[32,8,1536]{2,1,0:T(8,128)} %get-tuple-element.127.size_ref, ...), custom_call_target="tpu_custom_call" | custom-call | flops 3300000000 | bytes 10000 | tf_op jit(solution)/shard_map/pallas_call | solution.py:90
  113.5 71.5 %shard_map.311 = (bf16[4,80,768]{2,1,0:T(8,128)(2,1)}, bf16[640,768]{1,0:T(8,128)(2,1)}, f32[4,640,384]{2,1,0:T(8,128)}, bf16[4,640,384]{2,1,0:T(8,128)(2,1)}) custom-call(bf16[4,80,768]{2,1,0:T(8,128)(2,1)} %bitcast.206, bf16[320,320]{1,0:T(8,128)(2,1)} %fusion.40.refs_1_, bf16[4,1536,384]{2,1,0:T(8,128)(2,1)} %all-to-all-done.refs_2_), custom_call_target="tpu_custom_call" | custom-call | flops 9749999616 | bytes 10000 | tf_op jit(solution)/shard_map/pallas_call | solution.py:996
  185.1 3.0 multiply_reduce_fusion.11
  188.7 3.8 fusion.value_ref.gate_ref
  192.7 1.5 collective-permute-start.1
  196.1 13.8 %shard_map.312 = (bf16[256,1536]{1,0:T(8,128)(2,1)}, f32[32,8,80]{2,1,0:T(8,128)}, f32[32,8,1536]{2,1,0:T(8,128)}, f32[16,8,1536]{2,1,0:T(8,128)}, f32[8,1536]{1...) custom-call(f32[32,8,3072]{2,1,0:T(8,128)} %copy-done, f32[3,1536]{1,0:T(4,128)} %copy-done.30, ...), custom_call_target="tpu_custom_call" | custom-call | flops 2700000000 | bytes 10000 | tf_op jit(solution)/shard_map/pallas_call | solution.py:90
  209.9 17.7 %shard_map.313.entering_ref = f32[16,1536]{1,0:T(8,128)} custom-call(f32[16,1536]{1,0:T(8,128)} %get-tuple-element.145.total_ref, f32[1,1536]{1,0:T(1,128)} %get-tuple-element.146.size_ref, f32[2,16,1536]{2,1,0:T(8,128)} %decay_ref.23), custom_call_target="tpu_custom_call" | custom-call | flops 1800000000 | bytes 10000 | tf_op jit(solution)/shard_map/pallas_call | solution.py:772
  227.6 18.6 %shard_map.314 = (f32[32,8,1536]{2,1,0:T(8,128)}, bf16[256,1536]{1,0:T(8,128)(2,1)}, f32[16,8,1536]{2,1,0:T(8,128)}, f32[256,768]{1,0:T(8,128)}, bf16[256,768]{1...) custom-call(f32[32,8,1536]{2,1,0:T(8,128)} %get-tuple-element.140.size_ref, ...), custom_call_target="tpu_custom_call" | custom-call | flops 3300000000 | bytes 10000 | tf_op jit(solution)/shard_map/pallas_call | solution.py:90
  251.3 60.5 %shard_map.315 = (bf16[4,80,768]{2,1,0:T(8,128)(2,1)}, bf16[640,768]{1,0:T(8,128)(2,1)}, f32[4,640,384]{2,1,0:T(8,128)}, bf16[4,640,384]{2,1,0:T(8,128)(2,1)}) custom-call(bf16[4,80,768]{2,1,0:T(8,128)(2,1)} %bitcast.205, bf16[320,320]{1,0:T(8,128)(2,1)} %fusion.40.refs_1_, bf16[4,1536,384]{2,1,0:T(8,128)(2,1)} %all-to-all-done.1.refs_2_), custom_call_target="tpu_custom_call" | custom-call | flops 9749999616 | bytes 10000 | tf_op jit(solution)/shard_map/pallas_call | solution.py:996
  311.8 1.8 fusion.36
  315.7 63.9 %shard_map.316 = (bf16[4,80,768]{2,1,0:T(8,128)(2,1)}, bf16[640,768]{1,0:T(8,128)(2,1)}, bf16[4,640,384]{2,1,0:T(8,128)(2,1)}) custom-call(bf16[4,80,768]{2,1,0:T(8,128)(2,1)} %bitcast.187, bf16[320,320]{1,0:T(8,128)(2,1)} %fusion.40.refs_1_, bf16[4,1536,384]{2,1,0:T(8,128)(2,1)} %all-to-all-done.1.refs_2_, f32[4,640,384]{2,1,0:T(8,128)} %get-tuple-element.152.refs_3_), custom_call_target="tpu_custom_call" | custom-call | flops 9749999616 | bytes 10000 | tf_op jit(solution)/shard_map/pallas_call | solution.py:996
  381.2 1.8 multiply_reduce_fusion
  383.1 1.5 fusion.106
  384.5 16.7 %shard_map.317 = (f32[32,8,1536]{2,1,0:T(8,128)}, bf16[256,1536]{1,0:T(8,128)(2,1)}, f32[1,1536]{1,0:T(1,128)}, bf16[1536,768]{1,0:T(8,128)(2,1)}, f32[16,8,1536...) custom-call(bf16[256,768]{1,0:T(8,128)(2,1)} %get-tuple-element.301.grad_ref, ...), custom_call_target="tpu_custom_call" | custom-call | flops 2100000000 | bytes 10000 | tf_op jit(solution)/shard_map/pallas_call | solution.py:90
  401.3 15.9 %shard_map.319.entering_ref = f32[16,1536]{1,0:T(8,128)} custom-call(f32[16,1536]{1,0:T(8,128)} %get-tuple-element.164.total_ref, f32[1,1536]{1,0:T(1,128)} %get-tuple-element.165.size_ref, f32[2,16,1536]{2,1,0:T(8,128)} %decay_ref.23), custom_call_target="tpu_custom_call" | custom-call | flops 1800000000 | bytes 10000 | tf_op jit(solution)/shard_map/pallas_call | solution.py:772
  417.2 8.3 %shard_map.318 = bf16[4,1536,384]{2,1,0:T(8,128)(2,1)} custom-call(bf16[640,768]{1,0:T(8,128)(2,1)} %get-tuple-element.160.rows_ref, bf16[4,640,384]{2,1,0:T(8,128)(2,1)} %get-tuple-element.161.pre_ref, bf16[4,640,384]{2,1,0:T(8,128)(2,1)} %get-tuple-element.162.hidden_ref, bf16[640,768]{1,0:T(8,128)(2,1)} %get-tuple-element.163.grad_ref), custom_call_target="tpu_custom_call" | custom-call | flops 900000000 | bytes 10000 | tf_op jit(solution)/shard_map/pallas_call | solution.py:90
  425.5 5.0 all-to-all-start.3
  430.4 26.6 %shard_map.320 = (f32[32,8,1536]{2,1,0:T(8,128)}, f32[16,1536]{1,0:T(8,128)}, f32[1,1536]{1,0:T(1,128)}, f32[48,1536]{1,0:T(8,128)}, bf16[256,80]{1,0:T(8,128)(2,1)}) custom-call(f32[32,8,1536]{2,1,0:T(8,128)} %get-tuple-element.140.size_ref, bf16[256,1536]{1,0:T(8,128)(2,1)} %get-tuple-element.141.act_ref, f32[32,8,1536]{2,1,0:T(8,128)} %get-tuple-element.156.grad_ref, ...), custom_call_target="tpu_custom_call" | custom-call | flops 5249999872 | bytes 10000 | tf_op jit(solution)/shard_map/pallas_call | solution.py:90
  457.1 13.3 %shard_map.321 = (bf16[256,1536]{1,0:T(8,128)(2,1)}, f32[3,1536]{1,0:T(4,128)}, f32[3,1536]{1,0:T(4,128)}, bf16[1536,256]{1,0:T(8,128)(2,1)}) custom-call(f32[32,8,1536]{2,1,0:T(8,128)} %get-tuple-element.167.grad_act_ref, bf16[256,80]{1,0:T(8,128)(2,1)} %get-tuple-element.168.grad_selection_ref, bf16[2,1536,80]{2,1,0:T(8,128)(2,1)} %copy.117.state_ref, ...), custom_call_target="tpu_custom_call" | custom-call | flops 1500000000 | bytes 10000 | tf_op jit(solution)/shard_map/pallas_call | solution.py:90
  471.7 12.7 %collective-permute-done.2 = f32[3,1536]{1,0:T(4,128)S(1)} collective-permute-done((f32[3,1536]{1,0:T(4,128)}, f32[3,1536]{1,0:T(4,128)S(1)}, u32[]{:S(2)}, u32[]{:S(2)}) %collective-permute-start.2) | collective-permute-done | bytes 18464 | tf_op jit(solution)/shard_map/ppermute | solution.py:58
  485.2 1.6 scatter.6
  486.8 4.2 multiply_reduce_fusion.1
  492.9 59.6 %shard_map.322 = (bf16[4,80,768]{2,1,0:T(8,128)(2,1)}, bf16[640,768]{1,0:T(8,128)(2,1)}, bf16[4,640,384]{2,1,0:T(8,128)(2,1)}) custom-call(bf16[4,80,768]{2,1,0:T(8,128)(2,1)} %bitcast.186, bf16[320,320]{1,0:T(8,128)(2,1)} %fusion.40.refs_1_, bf16[4,1536,384]{2,1,0:T(8,128)(2,1)} %all-to-all-done.refs_2_, f32[4,640,384]{2,1,0:T(8,128)} %get-tuple-element.177.refs_3_), custom_call_target="tpu_custom_call" | custom-call | flops 9749999616 | bytes 10000 | tf_op jit(solution)/shard_map/pallas_call | solution.py:996
  552.5 8.4 %shard_map.324 = bf16[4,1536,384]{2,1,0:T(8,128)(2,1)} custom-call(bf16[640,768]{1,0:T(8,128)(2,1)} %get-tuple-element.185.rows_ref, bf16[4,640,384]{2,1,0:T(8,128)(2,1)} %get-tuple-element.186.pre_ref, bf16[4,640,384]{2,1,0:T(8,128)(2,1)} %get-tuple-element.187.hidden_ref, bf16[640,768]{1,0:T(8,128)(2,1)} %get-tuple-element.188.grad_ref), custom_call_target="tpu_custom_call" | custom-call | flops 900000000 | bytes 10000 | tf_op jit(solution)/shard_map/pallas_call | solution.py:90
  563.5 16.3 %shard_map.323 = (f32[32,8,1536]{2,1,0:T(8,128)}, bf16[256,1536]{1,0:T(8,128)(2,1)}, f32[1,1536]{1,0:T(1,128)}, bf16[1536,768]{1,0:T(8,128)(2,1)}, f32[16,8,1536...) custom-call(bf16[256,768]{1,0:T(8,128)(2,1)} %get-tuple-element.297.grad_ref, ...), custom_call_target="tpu_custom_call" | custom-call | flops 2100000000 | bytes 10000 | tf_op jit(solution)/shard_map/pallas_call | solution.py:90
  579.8 16.6 %shard_map.325.entering_ref = f32[16,1536]{1,0:T(8,128)} custom-call(f32[16,1536]{1,0:T(8,128)} %get-tuple-element.189.total_ref, f32[1,1536]{1,0:T(1,128)} %get-tuple-element.190.size_ref, f32[2,16,1536]{2,1,0:T(8,128)} %decay_ref.23), custom_call_target="tpu_custom_call" | custom-call | flops 1800000000 | bytes 10000 | tf_op jit(solution)/shard_map/pallas_call | solution.py:772
  596.5 5.1 all-to-all-start.2
  604.4 26.5 %shard_map.326 = (f32[32,8,1536]{2,1,0:T(8,128)}, f32[16,1536]{1,0:T(8,128)}, f32[1,1536]{1,0:T(1,128)}, f32[48,1536]{1,0:T(8,128)}, bf16[256,80]{1,0:T(8,128)(2,1)}) custom-call(f32[32,8,1536]{2,1,0:T(8,128)} %get-tuple-element.127.size_ref, bf16[256,1536]{1,0:T(8,128)(2,1)} %get-tuple-element.128.act_ref, f32[32,8,1536]{2,1,0:T(8,128)} %get-tuple-element.181.grad_ref, ...), custom_call_target="tpu_custom_call" | custom-call | flops 5249999872 | bytes 10000 | tf_op jit(solution)/shard_map/pallas_call | solution.py:90
  630.9 13.3 %shard_map.327 = (bf16[256,1536]{1,0:T(8,128)(2,1)}, f32[3,1536]{1,0:T(4,128)}, f32[3,1536]{1,0:T(4,128)}, bf16[1536,256]{1,0:T(8,128)(2,1)}) custom-call(f32[32,8,1536]{2,1,0:T(8,128)} %get-tuple-element.192.grad_act_ref, bf16[256,80]{1,0:T(8,128)(2,1)} %get-tuple-element.193.grad_selection_ref, bf16[2,1536,80]{2,1,0:T(8,128)(2,1)} %copy.117.state_ref, ...), custom_call_target="tpu_custom_call" | custom-call | flops 1500000000 | bytes 10000 | tf_op jit(solution)/shard_map/pallas_call | solution.py:90
  647.0 5.1 convolution_convert_fusion
  654.0 1.9 reshape_reshape.23.refs_5_
  657.1 1.6 scatter.9
  658.7 5.5 multiply_reduce_fusion.3
  665.4 1.7 reshape_reshape.20.refs_2_
  667.1 5.2 convolution_convert_fusion.1
  672.3 75.2 %shard_map.328 = f32[320,768]{1,0:T(8,128)} custom-call(bf16[8,2,2,96,768]{4,3,2,1,0:T(8,128)(2,1)} %bitcast.208, bf16[8,2,2,48,768]{4,3,2,1,0:T(8,128)(2,1)} %bitcast.198, bf16[8,2,2,16,768]{4,3,2,1,0:T(8,128)(2,1)} %reshape_reshape.20.refs_2_, bf16[8,2,2,96,768]{4,3,2,1,0:T(8,128)(2,1)} %bitcast.207, bf16[8,2,2,48,768]{4,3,2,1,0:T(8,128)(2,1)} %bitcast.197, ...), custom_call_target="tpu_custom_call" | custom-call | flops 8999999488 | bytes 10000 | tf_op jit(solution)/shard_map/pallas_call | solution.py:1339
  749.4 1.7 slice.212
  751.1 1.8 add_bitcast_fusion
  759.0 11.7 %shard_map.329 = (f32[2,4,768,384]{3,2,1,0:T(8,128)}, f32[2,4,384,768]{3,2,1,0:T(8,128)}) custom-call(bf16[4,1536,384]{2,1,0:T(8,128)(2,1)} %all-to-all-done.2.refs_0_, bf16[4,1536,384]{2,1,0:T(8,128)(2,1)} %all-to-all-done.3.refs_1_), custom_call_target="tpu_custom_call" | custom-call | flops 1350000000 | bytes 10000 | tf_op jit(solution)/shard_map/pallas_call | solution.py:90
  (298 shorter events, 52.6 us)
Async XLA Ops:
  2.7 9.9 %collective-permute-start = (bf16[3,768]{1,0:T(4,128)(2,1)S(1)}, bf16[3,768]{1,0:T(4,128)(2,1)S(1)}, u32[]{:S(2)}, u32[]{:S(2)}) collective-permute-start(bf16[3,768]{1,0:T(4,128)(2,1)S(1)} %bitcast_multiply_fusion.4), channel_id=1, source_target_pairs={{0,4},{4,8},{8,12},{12,16},{16,20},{20,24},{24,28},{1,5},{5,9},{9,... | collective-permute-start | bytes 13832 | tf_op jit(solution)/shard_map/ppermute | solution.py:58
  12.6 6.9 copy-start.17
  12.7 67.0 %all-to-all-start = ((bf16[4,1536,384]{2,1,0:T(8,128)(2,1)}), bf16[4,1536,384]{2,1,0:T(8,128)(2,1)}, u32[]{:S(2)}, u32[]{:S(2)}) async-start(bf16[4,1536,384]{2,1,0:T(8,128)(2,1)} %shard_map.306), calls=%async_computation | async-start | bytes 9437184 | tf_op jit(solution)/shard_map/all_to_all | solution.py:1039
  25.7 162.9 %copy-start.45 = (f32[768]{0:T(1024)}, f32[768]{0:T(1024)S(1)}, u32[]{:S(2)}) copy-start(f32[768]{0:T(1024)S(1)} %get-tuple-element.291) | copy-start | bytes 9220
  79.6 7.4 copy-start.50
  79.6 8.7 %copy-start.20 = (bf16[2,768,16]{1,2,0:T(8,128)(2,1)S(1)}, bf16[2,768,16]{1,2,0:T(8,128)(2,1)}, u32[]{:S(2)}) copy-start(bf16[2,768,16]{1,2,0:T(8,128)(2,1)} %param.38) | copy-start | bytes 147460
  79.7 171.7 %all-to-all-start.1 = ((bf16[4,1536,384]{2,1,0:T(8,128)(2,1)}), bf16[4,1536,384]{2,1,0:T(8,128)(2,1)}, u32[]{:S(2)}, u32[]{:S(2)}) async-start(bf16[4,1536,384]{2,1,0:T(8,128)(2,1)} %shard_map.308), calls=%async_computation.1 | async-start | bytes 9437184 | tf_op jit(solution)/shard_map/all_to_all | solution.py:1039
  87.9 25.5 %copy-start.43 = (s32[256]{0:T(256)}, s32[256]{0:T(256)S(1)}, u32[]{:S(2)}) copy-start(s32[256]{0:T(256)S(1)} %reshape.551) | copy-start | bytes 3076
  88.1 24.2 %copy-start.38 = (s32[256]{0:T(256)}, s32[256]{0:T(256)S(1)}, u32[]{:S(2)}) copy-start(s32[256]{0:T(256)S(1)} %reshape.552) | copy-start | bytes 3076
  88.3 160.0 %copy-start.41 = (s32[256]{0:T(256)}, s32[256]{0:T(256)S(1)}, u32[]{:S(2)}) copy-start(s32[256]{0:T(256)S(1)} %reshape.556) | copy-start | bytes 3076
  89.3 103.3 %copy-start.68 = (f32[3]{0:T(128)}, f32[3]{0:T(128)S(1)}, u32[]{:S(2)}) copy-start(f32[3]{0:T(128)S(1)} %pad_maximum_fusion.6) | copy-start | bytes 40
  89.4 95.7 %copy-start.26 = (s32[256]{0:T(256)}, s32[256]{0:T(256)S(1)}, u32[]{:S(2)}) copy-start(s32[256]{0:T(256)S(1)} %fusion.99) | copy-start | bytes 3076
  89.4 224.9 %copy-start.28 = (s32[256]{0:T(256)}, s32[256]{0:T(256)S(1)}, u32[]{:S(2)}) copy-start(s32[256]{0:T(256)S(1)} %fusion.98) | copy-start | bytes 3076
  111.2 73.9 %copy-start.33 = (f32[256]{0:T(256)}, f32[256]{0:T(256)S(1)}, u32[]{:S(2)}) copy-start(f32[256]{0:T(256)S(1)} %reduce_max.18) | copy-start | bytes 3076
  112.3 72.8 %copy-start.51 = (f32[256]{0:T(256)}, f32[256]{0:T(256)S(1)}, u32[]{:S(2)}) copy-start(f32[256]{0:T(256)S(1)} %fusion.64) | copy-start | bytes 3076
  113.5 71.6 %copy-start.63 = (f32[256]{0:T(256)}, f32[256]{0:T(256)S(1)}, u32[]{:S(2)}) copy-start(f32[256]{0:T(256)S(1)} %select_reduce_fusion.1) | copy-start | bytes 3076
  113.5 71.6 %copy-start.59 = (f32[256]{0:T(256)}, f32[256]{0:T(256)S(1)}, u32[]{:S(2)}) copy-start(f32[256]{0:T(256)S(1)} %broadcast_select_fusion.1) | copy-start | bytes 3076
  113.5 71.6 %copy-start.4 = (f32[256,768]{1,0:T(8,128)S(1)}, f32[256,768]{1,0:T(8,128)}, u32[]{:S(2)}) copy-start(f32[256,768]{1,0:T(8,128)} %get-tuple-element.135) | copy-start | bytes 2359300
  192.7 2.8 collective-permute-start.1
  247.2 64.6 %copy-start.36 = (f32[256]{0:T(256)}, f32[256]{0:T(256)S(1)}, u32[]{:S(2)}) copy-start(f32[256]{0:T(256)S(1)} %reduce_max.19) | copy-start | bytes 3076
  248.3 63.5 %copy-start.54 = (f32[256]{0:T(256)}, f32[256]{0:T(256)S(1)}, u32[]{:S(2)}) copy-start(f32[256]{0:T(256)S(1)} %fusion.66) | copy-start | bytes 3076
  315.7 64.0 %copy-start.29 = (s32[256]{0:T(256)S(1)}, s32[256]{0:T(256)}, u32[]{:S(2)}) copy-start(s32[256]{0:T(256)} %copy-done.28) | copy-start | bytes 3076
  315.7 65.4 %copy-start.1 = (f32[256,768]{1,0:T(8,128)S(1)}, f32[256,768]{1,0:T(8,128)}, u32[]{:S(2)}) copy-start(f32[256,768]{1,0:T(8,128)} %get-tuple-element.147) | copy-start | bytes 2359300
  315.7 65.4 %copy-start.10 = (f32[256,16]{1,0:T(8,128)S(1)}, f32[256,16]{1,0:T(8,128)}, u32[]{:S(2)}) copy-start(f32[256,16]{1,0:T(8,128)} %get-tuple-element.148) | copy-start | bytes 49156
  425.5 171.0 %all-to-all-start.3 = ((bf16[4,1536,384]{2,1,0:T(8,128)(2,1)}), bf16[4,1536,384]{2,1,0:T(8,128)(2,1)}, u32[]{:S(2)}, u32[]{:S(2)}) async-start(bf16[4,1536,384]{2,1,0:T(8,128)(2,1)} %shard_map.318), calls=%async_computation.3 | async-start | bytes 9437184 | tf_op jit(solution)/shard_map/all_to_all | solution.py:1039
  457.0 14.7 %copy-start.75 = (f32[256]{0:T(256)S(1)}, f32[256]{0:T(256)}, u32[]{:S(2)}) copy-start(f32[256]{0:T(256)} %get-tuple-element.305) | copy-start | bytes 3076
  457.0 27.4 %copy-start.69 = (f32[3]{0:T(128)S(1)}, f32[3]{0:T(128)}, u32[]{:S(2)}) copy-start(f32[3]{0:T(128)} %copy-done.68) | copy-start | bytes 40
  457.0 29.8 %copy-start.7 = (f32[256,768]{1,0:T(8,128)S(1)}, f32[256,768]{1,0:T(8,128)}, u32[]{:S(2)}) copy-start(f32[256,768]{1,0:T(8,128)} %copy-done.6) | copy-start | bytes 2359300
  457.0 29.8 %copy-start.46 = (f32[768]{0:T(1024)S(1)}, f32[768]{0:T(1024)}, u32[]{:S(2)}) copy-start(f32[768]{0:T(1024)} %copy-done.45) | copy-start | bytes 9220
  457.0 29.8 %copy-start.78 = (f32[256]{0:T(256)S(1)}, f32[256]{0:T(256)}, u32[]{:S(2)}) copy-start(f32[256]{0:T(256)} %copy-done.77) | copy-start | bytes 3076
  457.0 29.8 %copy-start.83 = (bf16[256,1536]{1,0:T(8,128)(2,1)S(1)}, bf16[256,1536]{1,0:T(8,128)(2,1)}, u32[]{:S(2)}) copy-start(bf16[256,1536]{1,0:T(8,128)(2,1)} %get-tuple-element.176) | copy-start | bytes 2359300
  470.4 14.0 %collective-permute-start.2 = (f32[3,1536]{1,0:T(4,128)}, f32[3,1536]{1,0:T(4,128)S(1)}, u32[]{:S(2)}, u32[]{:S(2)}) collective-permute-start(f32[3,1536]{1,0:T(4,128)} %get-tuple-element.175), channel_id=1, source_target_pairs={{4,0},{8,4},{12,8},{16,12},{20,16},{24,20},{28,24},{5,1},{9,5},{13... | collective-permute-start | bytes 55304 | tf_op jit(solution)/shard_map/ppermute | solution.py:58
  552.4 8.5 %copy-start.44 = (s32[256]{0:T(256)S(1)}, s32[256]{0:T(256)}, u32[]{:S(2)}) copy-start(s32[256]{0:T(256)} %copy-done.43) | copy-start | bytes 3076
  552.4 8.5 %copy-start.64 = (f32[256]{0:T(256)S(1)}, f32[256]{0:T(256)}, u32[]{:S(2)}) copy-start(f32[256]{0:T(256)} %copy-done.63) | copy-start | bytes 3076
  552.4 8.5 %copy-start.18 = (bf16[4,80,768]{2,1,0:T(8,128)(2,1)S(1)}, bf16[4,80,768]{2,1,0:T(8,128)(2,1)}, u32[]{:S(2)}) copy-start(bf16[4,80,768]{2,1,0:T(8,128)(2,1)} %get-tuple-element.178) | copy-start | bytes 1474564
  552.5 8.9 %copy-start.5 = (f32[256,768]{1,0:T(8,128)S(1)}, f32[256,768]{1,0:T(8,128)}, u32[]{:S(2)}) copy-start(f32[256,768]{1,0:T(8,128)} %get-tuple-element.135) | copy-start | bytes 2359300
  552.5 8.9 %copy-start.9 = (f32[256,16]{1,0:T(8,128)S(1)}, f32[256,16]{1,0:T(8,128)}, u32[]{:S(2)}) copy-start(f32[256,16]{1,0:T(8,128)} %get-tuple-element.136) | copy-start | bytes 49156
  552.5 8.9 %copy-start.21 = (bf16[2,768,16]{1,2,0:T(8,128)(2,1)S(1)}, bf16[2,768,16]{1,2,0:T(8,128)(2,1)}, u32[]{:S(2)}) copy-start(bf16[2,768,16]{1,2,0:T(8,128)(2,1)} %param.38) | copy-start | bytes 147460
  552.5 8.9 %copy-start.25 = (f32[768]{0:T(1024)S(1)}, f32[768]{0:T(1024)}, u32[]{:S(2)}) copy-start(f32[768]{0:T(1024)} %get-tuple-element.289) | copy-start | bytes 9220
  552.5 8.9 %copy-start.34 = (f32[256]{0:T(256)S(1)}, f32[256]{0:T(256)}, u32[]{:S(2)}) copy-start(f32[256]{0:T(256)} %copy-done.33) | copy-start | bytes 3076
  552.5 8.9 %copy-start.39 = (s32[256]{0:T(256)S(1)}, s32[256]{0:T(256)}, u32[]{:S(2)}) copy-start(s32[256]{0:T(256)} %copy-done.38) | copy-start | bytes 3076
  552.5 8.9 %copy-start.52 = (f32[256]{0:T(256)S(1)}, f32[256]{0:T(256)}, u32[]{:S(2)}) copy-start(f32[256]{0:T(256)} %copy-done.51) | copy-start | bytes 3076
  596.5 162.6 %all-to-all-start.2 = ((bf16[4,1536,384]{2,1,0:T(8,128)(2,1)}), bf16[4,1536,384]{2,1,0:T(8,128)(2,1)}, u32[]{:S(2)}, u32[]{:S(2)}) async-start(bf16[4,1536,384]{2,1,0:T(8,128)(2,1)} %shard_map.324), calls=%async_computation.2 | async-start | bytes 9437184 | tf_op jit(solution)/shard_map/all_to_all | solution.py:1039
  630.9 16.0 %copy-start.47 = (f32[768]{0:T(1024)S(1)}, f32[768]{0:T(1024)}, u32[]{:S(2)}) copy-start(f32[768]{0:T(1024)} %copy-done.45) | copy-start | bytes 9220
  630.9 16.0 %copy-start.79 = (f32[256]{0:T(256)S(1)}, f32[256]{0:T(256)}, u32[]{:S(2)}) copy-start(f32[256]{0:T(256)} %copy-done.77) | copy-start | bytes 3076
  644.2 12.0 %collective-permute-start.3 = (f32[3,1536]{1,0:T(4,128)}, f32[3,1536]{1,0:T(4,128)}, u32[]{:S(2)}, u32[]{:S(2)}) collective-permute-start(f32[3,1536]{1,0:T(4,128)} %get-tuple-element.200), channel_id=1, source_target_pairs={{4,0},{8,4},{12,8},{16,12},{20,16},{24,20},{28,24},{5,1},{9,5},{13... | collective-permute-start | bytes 55304 | tf_op jit(solution)/shard_map/ppermute | solution.py:58
  672.3 78.8 %copy-start.72 = (f32[256]{0:T(256)S(1)}, f32[256]{0:T(256)}, u32[]{:S(2)}) copy-start(f32[256]{0:T(256)} %multiply_multiply_fusion) | copy-start | bytes 3076
  751.1 7.1 copy-start.14
  (47 other events, 220.6 us)

commit v3 on v2

--- a/solution.py
+++ b/solution.py
@@ -86,7 +86,7 @@
     return pl.CostEstimate(flops=int(count * 1.5e8), transcendentals=0, bytes_accessed=10000)
 
 
-def plain_call(kernel, grid, in_specs, out_specs, out_shapes, scratch, args, cost):
+def plain_call(kernel, grid, in_specs, out_specs, out_shapes, scratch, args, cost, aliases=None):
     return pl.pallas_call(
         kernel,
         grid=grid,
@@ -94,6 +94,7 @@
         out_specs=out_specs,
         out_shape=out_shapes,
         scratch_shapes=scratch,
+        input_output_aliases=aliases or {},
         compiler_params=pltpu.CompilerParams(
             dimension_semantics=("arbitrary",), vmem_limit_bytes=60 * MIB
         ),
@@ -203,7 +204,7 @@
 def front_kernel(dims, value_ref, rim_ref, mask_ref, reset_ref, conv_ref, conv_bias_ref, state_ref,
                  step_ref, step_bias_ref, decay_ref,
                  act_ref, selection_ref, size_ref, link_ref, link_size_ref, total_ref, total_size_ref,
-                 extended, maps):
+                 extended, maps, sized, pushed):
     taps, rank, states, steps, channels = dims
     extend(value_ref, rim_ref, extended, taps)
     bias = conv_bias_ref[...]
@@ -233,22 +234,19 @@
     def end_tile(c, carry):
         lanes = pl.ds(pl.multiple_of(c * LANES, LANES), LANES)
         rates = rate_rows(rates_of(decay_ref[:, lanes]))
-
-        def one(pair, carry):
-            levels, length = list(carry[:states]), carry[states]
-            acts = two_steps(act_ref, pair, lanes)
-            for half in (0, 1):
-                step = 2 * pair + half
-                size = size_ref[step, :, lanes]
-                value = size * acts[half]
-                size = size + reset_ref[step]
-                for n in range(states):
-                    levels[n] = jnp.exp2(size * rates[n]) * levels[n] + value * maps[step, n]
-                length = length + size
-            return tuple(levels) + (length,)
+        size = size_ref[:, :, lanes]
+        pushed[...] = size * act_ref[:, lanes].astype(jnp.float32).reshape(size.shape)
+        sized[...] = size + reset_ref[...]
+
+        def one(step, carry):
+            size, value = sized[step], pushed[step]
+            new = []
+            for n in range(states):
+                new.append(jnp.exp2(size * rates[n]) * carry[n] + value * maps[step, n])
+            return tuple(new) + (carry[states] + size,)
 
         zero = jnp.zeros((CHUNKS, LANES), jnp.float32)
-        found = lax.fori_loop(0, steps // 2, one, (zero,) * (states + 1), unroll=2)
+        found = lax.fori_loop(0, steps, one, (zero,) * (states + 1), unroll=4)
         links, totals, link_size, total_size = chunk_links(found, found[states], rates, False)
         link_size_ref[:, lanes] = link_size
         total_size_ref[:, lanes] = total_size
@@ -286,7 +284,8 @@
         [whole(s.shape) for s in shapes],
         shapes,
         [VMEM((steps + taps - 1, CHUNKS, channels), jnp.float32),
-         VMEM((steps, states, CHUNKS, LANES), jnp.float32)],
+         VMEM((steps, states, CHUNKS, LANES), jnp.float32),
+         VMEM((steps, CHUNKS, LANES), jnp.float32), VMEM((steps, CHUNKS, LANES), jnp.float32)],
         (projected, rim, masks, reset, conv_weight, conv_bias, state_weight, step_weight, step_bias,
          decay_log),
         18,
@@ -296,7 +295,7 @@
 def run_kernel(dims, size_ref, act_ref, selection_ref, reset_ref, decay_ref, link_ref, link_size_ref,
                entering_ref, gate_ref, skip_ref, out_weight_ref, current_ref, norm_ref, router_ref, fill_ref,
                mixed_ref, gated_ref, begin_ref, middle_ref, routed_ref, logits_ref, outbound_ref,
-               in_maps, out_maps):
+               in_maps, out_maps, sized, pushed):
     rank, states, steps, tiles = dims
 
     @pl.when(pl.program_id(0) == 0)
@@ -314,28 +313,28 @@
         begin_ref[n] = first
         begin.append(first)
 
-    def one(pair, carry):
-        levels = list(carry)
-        acts = two_steps(act_ref, pair)
-        both = []
-        for half in (0, 1):
-            step = 2 * pair + half
-            size = size_ref[step]
-            value = size * acts[half]
-            size = size + reset_ref[step]
-            sums = [skip * acts[half], None]
-            for n in range(states):
-                levels[n] = jnp.exp2(size * rates[n]) * levels[n] + value * in_maps[step, n]
-                term = out_maps[step, n] * levels[n]
-                sums[n % 2] = term if sums[n % 2] is None else sums[n % 2] + term
-            mixed = sums[0] + sums[1]
-            mixed_ref[step] = mixed
-            both.append(mixed * jax.nn.silu(gate_ref[step]))
-        at = pl.ds(pl.multiple_of(pair * 2 * CHUNKS, 2 * CHUNKS), 2 * CHUNKS)
-        gated_ref[at, :] = jnp.concatenate(both, axis=0).astype(jnp.bfloat16)
-        return tuple(levels)
-
-    lax.fori_loop(0, steps // 2, one, tuple(begin), unroll=2)
+    size = size_ref[...]
+    act = act_ref[...].astype(jnp.float32).reshape(size.shape)
+    pushed[...] = size * act
+    sized[...] = size + reset_ref[...]
+
+    def one(step, carry):
+        size, value = sized[step], pushed[step]
+        new = []
+        sums = [None, None]
+        for n in range(states):
+            level = jnp.exp2(size * rates[n]) * carry[n] + value * in_maps[step, n]
+            new.append(level)
+            term = out_maps[step, n] * level
+            sums[n % 2] = term if sums[n % 2] is None else sums[n % 2] + term
+        mixed_ref[step] = sums[0] + sums[1]
+        return tuple(new)
+
+    lax.fori_loop(0, steps, one, tuple(begin), unroll=4)
+    mixed = mixed_ref[...] + skip * act
+    mixed_ref[...] = mixed
+    gated = mixed * jax.nn.silu(gate_ref[...])
+    gated_ref[...] = gated.reshape(steps * CHUNKS, LANES).astype(jnp.bfloat16)
     middle_ref[...] += dot_nn(gated_ref[...], out_weight_ref[...])
 
     @pl.when(pl.program_id(0) == tiles - 1)
@@ -373,7 +372,7 @@
             shaped((tokens, experts)),
             shaped((fill.shape[0], width), low),
         ],
-        [maps, maps],
+        [maps, maps] + [VMEM((steps, CHUNKS, LANES), jnp.float32)] * 2,
         (size, act, selection, reset, decay_log, link, link_size, entering, projected, skip_weight, out_weight,
          current, norm_expert, router, fill),
         22,
@@ -383,7 +382,7 @@
 def turn_kernel(dims, grad_ref, out_weight_ref, gate_ref, mixed_ref, act_ref, gated_ref, size_ref,
                 selection_ref, reset_ref, decay_ref,
                 grad_y_ref, grad_gate_ref, grad_skip_ref, grad_out_ref, link_ref, link_size_ref, total_ref,
-                total_size_ref, maps, held):
+                total_size_ref, maps, sized):
     rank, states, steps = dims
 
     @pl.when(pl.program_id(0) == 0)
@@ -392,34 +391,28 @@
 
     grad = grad_ref[...]
     grad_out_ref[...] = dot_tn(gated_ref[...], grad).astype(jnp.bfloat16)
-    held[...] = dot_nt(grad, out_weight_ref[...]).reshape(steps, CHUNKS, LANES)
+    gated = dot_nt(grad, out_weight_ref[...]).reshape(steps, CHUNKS, LANES)
+    gate = gate_ref[...]
+    share = jax.nn.sigmoid(gate)
+    grad_y = gated * (gate * share)
+    grad_y_ref[...] = grad_y
+    grad_gate = gated * mixed_ref[...] * (share * (1.0 + gate * (1.0 - share)))
+    grad_gate_ref[...] = grad_gate.reshape(steps * CHUNKS, LANES).astype(jnp.bfloat16)
+    by_skip = grad_y * act_ref[...].astype(jnp.float32).reshape(steps, CHUNKS, LANES)
+    grad_skip_ref[...] = jnp.sum(jnp.sum(by_skip, axis=0), axis=0, keepdims=True)
+    sized[...] = size_ref[...] + reset_ref[...]
     rates = rate_rows(rates_of(decay_ref[...]))
 
     def one(at, carry):
-        levels, length, skip = list(carry[:states]), carry[states], carry[states + 1]
-        pair = steps // 2 - 1 - at
-        acts = two_steps(act_ref, pair)
-        both = [None, None]
-        for half in (1, 0):
-            step = 2 * pair + half
-            gate = gate_ref[step]
-            share = jax.nn.sigmoid(gate)
-            gated = held[step]
-            grad_y = gated * (gate * share)
-            both[half] = gated * mixed_ref[step] * (share * (1.0 + gate * (1.0 - share)))
-            grad_y_ref[step] = grad_y
-            skip = skip + grad_y * acts[half]
-            size = size_ref[step] + reset_ref[step]
-            for n in range(states):
-                levels[n] = jnp.exp2(size * rates[n]) * (levels[n] + grad_y * maps[step, n])
-            length = length + size
-        rows = pl.ds(pl.multiple_of(pair * 2 * CHUNKS, 2 * CHUNKS), 2 * CHUNKS)
-        grad_gate_ref[rows, :] = jnp.concatenate(both, axis=0).astype(jnp.bfloat16)
-        return tuple(levels) + (length, skip)
+        step = steps - 1 - at
+        size, grad_y = sized[step], grad_y_ref[step]
+        new = []
+        for n in range(states):
+            new.append(jnp.exp2(size * rates[n]) * (carry[n] + grad_y * maps[step, n]))
+        return tuple(new) + (carry[states] + size,)
 
     zero = jnp.zeros((CHUNKS, LANES), jnp.float32)
-    found = lax.fori_loop(0, steps // 2, one, (zero,) * (states + 2), unroll=2)
-    grad_skip_ref[...] = jnp.sum(found[states + 1], axis=0, keepdims=True)
+    found = lax.fori_loop(0, steps, one, (zero,) * (states + 1), unroll=4)
     links, totals, link_size, total_size = chunk_links(found, found[states], rates, True)
     link_size_ref[...] = link_size
     total_size_ref[...] = total_size
@@ -440,11 +433,12 @@
         (tiles,),
         [whole(grad_low.shape), layer_columns(layer, width), slab(steps, tiles), slab(steps), rows_of(tokens),
          rows_of(tokens), slab(steps), whole(selection.shape), whole(reset.shape), layer_rows(layer, states)],
-        [slab(steps), rows_of(tokens), rows_of(1), pl.BlockSpec((LANES, width), lambda c: (c, 0)),
+        [slab(steps), pl.BlockSpec((tokens, LANES), lambda c: (0, tiles + c)), rows_of(1),
+         pl.BlockSpec((LANES, width), lambda c: (c, 0)),
          slab(states), rows_of(CHUNKS), rows_of(states), rows_of(1)],
         [
             shaped((steps, CHUNKS, channels)),
-            shaped((tokens, channels), low),
+            shaped((tokens, 2 * channels), low),
             shaped((1, channels)),
             shaped((channels, width), low),
             shaped((states, CHUNKS, channels)),
@@ -461,7 +455,7 @@
 def back_kernel(dims, size_ref, act_ref, grad_ref, decay_ref, selection_ref, reset_ref, begin_ref, link_ref,
                 link_size_ref, entering_ref, step_ref, step_bias_ref, skip_ref,
                 grad_act_ref, grad_decay_ref, grad_bias_ref, grad_step_ref, grad_selection_ref,
-                in_maps, out_maps, levels, decays, grad_in, grad_out, grad_size, grad_rate, grad_all):
+                in_maps, out_maps, levels, decays, grad_in, grad_out, grad_size, grad_rate, grad_all, sized, pushed, acted):
     rank, states, steps, tiles = dims
     tokens = steps * CHUNKS
 
@@ -480,22 +474,24 @@
         levels[0, n] = begin_ref[n]
         begin.append(begin_ref[n])
 
-    def ahead(pair, carry):
-        now = list(carry)
-        acts = two_steps(act_ref, pair)
-        for half in (0, 1):
-            step = 2 * pair + half
-            size = size_ref[step]
-            value = size * acts[half]
-            size = size + reset_ref[step]
-            for n in range(states):
-                decay = jnp.exp2(size * rates[n])
-                decays[step, n] = decay
-                now[n] = decay * now[n] + value * in_maps[step, n]
-                levels[step + 1, n] = now[n]
-        return tuple(now)
-
-    lax.fori_loop(0, steps // 2, ahead, tuple(begin), unroll=2)
+    size = size_ref[...]
+    act = act_ref[...].astype(jnp.float32).reshape(size.shape)
+    acted[...] = act
+    pushed[...] = size * act
+    sized[...] = size + reset_ref[...]
+
+    def ahead(step, carry):
+        size, value = sized[step], pushed[step]
+        new = []
+        for n in range(states):
+            decay = jnp.exp2(size * rates[n])
+            decays[step, n] = decay
+            level = decay * carry[n] + value * in_maps[step, n]
+            levels[step + 1, n] = level
+            new.append(level)
+        return tuple(new)
+
+    lax.fori_loop(0, steps, ahead, tuple(begin), unroll=4)
     link_size = link_size_ref[...]
     tail = []
     for n in range(states):
@@ -503,32 +499,27 @@
         grad_rate[n] = jnp.zeros((CHUNKS, LANES), jnp.float32)
 
     def retreat(at, carry):
-        passed = list(carry)
-        pair = steps // 2 - 1 - at
-        acts = two_steps(act_ref, pair)
-        for half in (1, 0):
-            step = 2 * pair + half
-            plain = size_ref[step]
-            act = acts[half]
-            grad = grad_ref[step]
-            value = plain * act
-            by_rate = jnp.zeros((CHUNKS, LANES), jnp.float32)
-            by_input = jnp.zeros((CHUNKS, LANES), jnp.float32)
-            for n in range(states):
-                lanes = slice(n * LANES, (n + 1) * LANES)
-                back = out_maps[step, n] * grad + passed[n]
-                grad_out[step, :, lanes] += grad * levels[step + 1, n]
-                grad_in[step, :, lanes] += back * value
-                by_input = by_input + back * in_maps[step, n]
-                passed[n] = decays[step, n] * back
-                pull = passed[n] * levels[step, n]
-                by_rate = by_rate + pull * rates[n]
-                grad_rate[n] += pull * plain
-            grad_size[step] = by_rate * (1.0 / LOG2E) + act * by_input
-            grad_act_ref[step] = plain * by_input + grad * skip
-        return tuple(passed)
-
-    lax.fori_loop(0, steps // 2, retreat, tuple(tail), unroll=2)
+        step = steps - 1 - at
+        plain, act, grad, value = size_ref[step], acted[step], grad_ref[step], pushed[step]
+        by_rate = jnp.zeros((CHUNKS, LANES), jnp.float32)
+        by_input = jnp.zeros((CHUNKS, LANES), jnp.float32)
+        new = []
+        for n in range(states):
+            lanes = slice(n * LANES, (n + 1) * LANES)
+            back = out_maps[step, n] * grad + carry[n]
+            grad_out[step, :, lanes] += grad * levels[step + 1, n]
+            grad_in[step, :, lanes] += back * value
+            by_input = by_input + back * in_maps[step, n]
+            passed = decays[step, n] * back
+            new.append(passed)
+            pull = passed * levels[step, n]
+            by_rate = by_rate + pull * rates[n]
+            grad_rate[n] += pull * plain
+        grad_size[step] = by_rate * (1.0 / LOG2E) + act * by_input
+        grad_act_ref[step] = plain * by_input + grad * skip
+        return tuple(new)
+
+    lax.fori_loop(0, steps, retreat, tuple(tail), unroll=2)
     for n in range(states):
         grad_decay_ref[n : n + 1, :] = (
             jnp.sum(grad_rate[n], axis=0, keepdims=True) * true_rates[n : n + 1, :]
@@ -586,7 +577,8 @@
         ],
         [maps, maps, VMEM((steps + 1, states, CHUNKS, LANES), f32), maps,
          VMEM((steps, CHUNKS, states * LANES), f32), VMEM((steps, CHUNKS, states * LANES), f32),
-         VMEM((steps, CHUNKS, LANES), f32), VMEM((states, CHUNKS, LANES), f32), VMEM((tokens, channels), f32)],
+         VMEM((steps, CHUNKS, LANES), f32), VMEM((states, CHUNKS, LANES), f32), VMEM((tokens, channels), f32)]
+        + [VMEM((steps, CHUNKS, LANES), f32)] * 3,
         (size, act, grad_y, decay_log, selection, reset, begin, link, link_size, entering, step_weight,
          step_bias, skip_weight),
         35,
@@ -595,7 +587,7 @@
 
 def conv_back_kernel(dims, grad_act_ref, grad_selection_ref, state_ref, value_ref, rim_ref, mask_ref,
                      conv_ref, conv_bias_ref, act_ref, grad_step_ref, grad_decay_ref, grad_bias_ref,
-                     grad_skip_ref, grad_value_ref, edge_ref, rim_grad_ref, channel_ref,
+                     grad_skip_ref, half_ref, grad_value_ref, edge_ref, rim_grad_ref, channel_ref,
                      extended, passed):
     taps, states, steps = dims
     tokens = steps * CHUNKS
@@ -676,7 +668,7 @@
 
 
 def mixer_conv_back(layer, grad_act, grad_selection, state_weight, projected, rim, masks, conv_weight,
-                    conv_bias, act, grad_step, grad_decay, grad_bias, grad_skip):
+                    conv_bias, act, grad_step, grad_decay, grad_bias, grad_skip, halved):
     steps, _, channels = grad_act.shape
     tokens = steps * CHUNKS
     taps, columns = conv_weight.shape[1], state_weight.shape[2]
@@ -688,19 +680,20 @@
         (tiles,),
         [slab(steps), whole(grad_selection.shape), layer_columns(layer, columns), slab(steps),
          rows_of(taps - 1), whole(masks.shape), layer_rows(layer, taps), layer_rows(layer, 1),
-         rows_of(tokens), rows_of(rank), rows_of(states), rows_of(1), rows_of(1)],
+         rows_of(tokens), rows_of(rank), rows_of(states), rows_of(1), rows_of(1), ANYWHERE],
         [rows_of(tokens), rows_of(taps - 1), rows_of(taps - 1),
          pl.BlockSpec((LANES, 2 * LANES), lambda c: (c, 0))],
         [
-            shaped((tokens, channels), jnp.bfloat16),
+            shaped((tokens, 2 * channels), jnp.bfloat16),
             shaped((taps - 1, channels)),
             shaped((taps - 1, channels)),
             shaped((channels, 2 * LANES), jnp.bfloat16),
         ],
         [VMEM((steps + taps - 1, CHUNKS, LANES), f32), VMEM((steps + taps - 1, CHUNKS, LANES), f32)],
         (grad_act, grad_selection, state_weight, projected, rim, masks, conv_weight, conv_bias, act, grad_step,
-         grad_decay, grad_bias, grad_skip),
+         grad_decay, grad_bias, grad_skip, halved),
         10,
+        {13: 0},
     )
 
 
@@ -798,13 +791,10 @@
 
 def expert_kernel(dims, backward, *refs):
     count, groups, members, block, share, width, hidden = dims
-    folded = folds(width, hidden)
-    out_ref, perm_ref, *refs = refs
-    weight_refs, refs = (refs[:1], refs[1:]) if folded else (refs[:2], refs[2:])
     if backward:
-        pre_hbm, ret_ref, rows_hbm, low_hbm, *scratch = refs
+        out_ref, perm_ref, up_hbm, down_hbm, pre_hbm, ret_ref, rows_hbm, low_hbm, *scratch = refs
     else:
-        ret_ref, rows_hbm, pre_hbm, low_hbm, *scratch = refs
+        out_ref, perm_ref, up_hbm, down_hbm, ret_ref, rows_hbm, pre_hbm, low_hbm, *scratch = refs
     (arrived, own, rows, pre, low, part, got, final, landed, up, down, total,
      there_send, there_recv, row_send, row_recv, sum_send, sum_recv, back_send, back_recv, local) = scratch
     f32, bf16 = jnp.float32, jnp.bfloat16
@@ -812,18 +802,19 @@
     group = lax.axis_index("narrow")
     quads = count // members
     quad, member = here // members, lax.rem(here, members)
-    peers = [lax.rem(group + k, groups) for k in range(1, groups)]
-
-    fold = max(folded, 1)
-    loads = [pltpu.make_async_copy(weight_refs[0].at[:, pl.ds(0, width)], up, local.at[0])]
-    for f in range(folded):
-        loads.append(pltpu.make_async_copy(
-            weight_refs[0].at[:, pl.ds(width + f * hidden, hidden)],
-            down.at[:, :, pl.ds(f * hidden, hidden)], local.at[1 + f]))
-    if not folded:
-        loads.append(pltpu.make_async_copy(weight_refs[1], down, local.at[1]))
+    lines = groups // 2
+    line, core = group // 2, lax.rem(group, 2)
+    near_group = group + 1 - 2 * core
+    others = [(2 * away + c, 2 * lax.rem(line + away, lines) + c) for away in range(1, lines) for c in (0, 1)]
+    early = 2 * (share // groups) // 16 * 16
+    head, tail = pl.ds(0, early), pl.ds(early, share - early)
+
+    loads = [
+        pltpu.make_async_copy(up_hbm, up, local.at[0]),
+        pltpu.make_async_copy(down_hbm, down, local.at[1]),
+    ]
     if backward:
-        loads.append(pltpu.make_async_copy(pre_hbm, pre, local.at[1 + fold]))
+        loads.append(pltpu.make_async_copy(pre_hbm, pre, local.at[2]))
     for load in loads:
         load.start()
 
@@ -831,7 +822,7 @@
         return lax.rem(quad + away, quads) * members + lax.rem(member + turn, members)
 
     barrier = pltpu.get_barrier_semaphore()
-    for peer in peers:
+    for peer in [near_group] + [other for _, other in others]:
         pl.semaphore_signal(barrier, inc=1, device_id=(here, peer), device_id_type=MESH)
     for away in range(quads):
         for turn in range(members):
@@ -841,43 +832,72 @@
     pl.semaphore_wait(barrier, groups - 1 + count - 1)
 
     there = []
-    for k, peer in enumerate(peers):
-        there.append(pltpu.make_async_remote_copy(
-            src_ref=out_ref.at[peer], dst_ref=arrived.at[group], send_sem=there_send.at[k],
-            recv_sem=there_recv.at[k], device_id=(here, peer), device_id_type=MESH))
-        there[-1].start()
-    arrived[group] = out_ref[group]
-    for copy in there:
-        copy.wait_recv()
-    flat = arrived[...].reshape(groups * block, width)
-    own[...] = dot_nn(perm_ref[...], flat).astype(bf16).reshape(members, share, width)
-
-    def span(window):
-        return pl.ds(pl.multiple_of(window * share, 16), share)
+
+    def hand_over(k, source, target, send, recv):
+        if k:
+            place, peer = others[k - 1]
+            away = place // 2
+            landing, signal = (lines - away) * 2 + core, 2 * away - 1 + core
+        else:
+            peer, landing, signal = near_group, core, 0
+        copy = pltpu.make_async_remote_copy(
+            src_ref=source, dst_ref=target.at[landing], send_sem=send.at[k], recv_sem=recv.at[signal],
+            device_id=(here, peer), device_id_type=MESH)
+        copy.start()
+        return copy
+
+    def taken(k, target, send, recv):
+        pltpu.make_async_remote_copy(
+            src_ref=out_ref.at[group], dst_ref=target.at[0], send_sem=send.at[k], recv_sem=recv.at[k],
+            device_id=(here, near_group), device_id_type=MESH).wait_recv()
+
+    there = [hand_over(0, out_ref.at[near_group], arrived, there_send, there_recv)]
+    for k, (_, other) in enumerate(others):
+        there.append(hand_over(1 + k, out_ref.at[other], arrived, there_send, there_recv))
+    arrived[core] = out_ref[group]
+
+    def span(window, part=None):
+        start, size = (0, share) if part is None else ((0, early), (early, share - early))[part]
+        return pl.ds(pl.multiple_of(window * share + start, 16), size)
 
     sent = []
-
-    def carry(away, turn):
+    ways = [(away, turn) for turn in range(members) for away in list(range(1, quads)) + [0] if away or turn]
+
+    def carry(away, turn, part):
         window = window_at(away, turn)
         copy = pltpu.make_async_remote_copy(
-            src_ref=own.at[lax.rem(member + turn, members)], dst_ref=rows.at[span(here), :],
-            send_sem=row_send.at[away, turn], recv_sem=row_recv.at[away, turn],
+            src_ref=own.at[lax.rem(member + turn, members), (head, tail)[part]],
+            dst_ref=rows.at[span(here, part), :],
+            send_sem=row_send.at[away, turn, part], recv_sem=row_recv.at[away, turn, part],
             device_id=(window, group), device_id_type=MESH)
         copy.start()
         sent.append(copy)
 
-    for turn in range(members):
-        for away in list(range(1, quads)) + [0]:
-            if away or turn:
-                carry(away, turn)
+    taken(0, arrived, there_send, there_recv)
+    order = perm_ref[...].reshape(members, share, groups * block)
+    first = arrived[pl.ds(0, 2)].reshape(2 * block, width)
+    own[:, head] = dot_nn(
+        order[:, :early, : 2 * block].reshape(members * early, 2 * block), first
+    ).astype(bf16).reshape(members, early, width)
+    for away, turn in ways:
+        carry(away, turn, 0)
+    for k in range(1, groups - 1):
+        taken(k, arrived, there_send, there_recv)
+    own[:, tail] = dot_nn(
+        order[:, early:].reshape(members * (share - early), groups * block),
+        arrived[...].reshape(groups * block, width),
+    ).astype(bf16).reshape(members, share - early, width)
+    for away, turn in ways:
+        carry(away, turn, 1)
     rows[span(here), :] = own[member]
 
     def arrive(away, turn):
         window = lax.rem(quad + quads - away, quads) * members + lax.rem(member + members - turn, members)
-        pltpu.make_async_remote_copy(
-            src_ref=own.at[member], dst_ref=rows.at[span(window), :],
-            send_sem=row_send.at[away, turn], recv_sem=row_recv.at[away, turn],
-            device_id=(window, group), device_id_type=MESH).wait_recv()
+        for part in (0, 1):
+            pltpu.make_async_remote_copy(
+                src_ref=own.at[member, (head, tail)[part]], dst_ref=rows.at[span(window, part), :],
+                send_sem=row_send.at[away, turn, part], recv_sem=row_recv.at[away, turn, part],
+                device_id=(window, group), device_id_type=MESH).wait_recv()
         return window
 
     def compute(windows):
@@ -915,63 +935,81 @@
         for index, w in enumerate(windows):
             part[w] = total[index * share : (index + 1) * share].astype(bf16)
 
-    def give_back(away, turn, window):
+    def give_back(away, turn, window, part):
         copy = pltpu.make_async_remote_copy(
-            src_ref=part.at[window], dst_ref=got.at[here],
-            send_sem=sum_send.at[away, turn], recv_sem=sum_recv.at[away, turn],
+            src_ref=part_rows(window, part), dst_ref=got.at[here, (head, tail)[part]],
+            send_sem=sum_send.at[away, turn, part], recv_sem=sum_recv.at[away, turn, part],
             device_id=(window, group), device_id_type=MESH)
         copy.start()
         sent.append(copy)
+
+    def part_rows(window, which):
+        return part.at[window, (head, tail)[which]]
 
     for load in loads:
         load.wait()
     windows = [here] + [arrive(0, turn) for turn in range(1, members)]
     compute(windows)
-    for turn in range(1, members):
-        give_back(0, turn, windows[turn])
+    for which in (1, 0):
+        for turn in range(1, members):
+            give_back(0, turn, windows[turn], which)
     got[here] = part[here]
+    late = []
     for away in range(1, quads):
         for first in range(0, members, 2):
             windows = [arrive(away, turn) for turn in (first, first + 1)]
             compute(windows)
             for turn in (first, first + 1):
-                give_back(away, turn, windows[turn - first])
+                give_back(away, turn, windows[turn - first], 1)
+                late.append((away, turn, windows[turn - first]))
+    for away, turn, window in late:
+        give_back(away, turn, window, 0)
 
     saves = [
-        pltpu.make_async_copy(rows, rows_hbm, local.at[2 + fold]),
-        pltpu.make_async_copy(low, low_hbm, local.at[3 + fold]),
+        pltpu.make_async_copy(rows, rows_hbm, local.at[3]),
+        pltpu.make_async_copy(low, low_hbm, local.at[4]),
     ]
     if not backward:
-        saves.append(pltpu.make_async_copy(pre, pre_hbm, local.at[1 + fold]))
+        saves.append(pltpu.make_async_copy(pre, pre_hbm, local.at[2]))
     for save in saves:
         save.start()
 
-    for away in range(quads):
-        for turn in range(members):
-            if away or turn:
-                window = window_at(away, turn)
-                pltpu.make_async_remote_copy(
-                    src_ref=part.at[here], dst_ref=got.at[window],
-                    send_sem=sum_send.at[away, turn], recv_sem=sum_recv.at[away, turn],
-                    device_id=(window, group), device_id_type=MESH).wait_recv()
-    summed = got[pl.ds(0, members)].astype(f32)
-    for q in range(1, quads):
-        summed = summed + got[pl.ds(q * members, members)].astype(f32)
-    packed = summed.astype(bf16).reshape(members * share, width)
-    final[...] = dot_tn(perm_ref[...], packed).astype(bf16).reshape(groups, block, width)
-
+    def returned(which):
+        for away, turn in ways:
+            window = window_at(away, turn)
+            pltpu.make_async_remote_copy(
+                src_ref=part_rows(here, which), dst_ref=got.at[window, (head, tail)[which]],
+                send_sem=sum_send.at[away, turn, which], recv_sem=sum_recv.at[away, turn, which],
+                device_id=(window, group), device_id_type=MESH).wait_recv()
+        place = (head, tail)[which]
+        summed = got[pl.ds(0, members), place].astype(f32)
+        for q in range(1, quads):
+            summed = summed + got[pl.ds(q * members, members), place].astype(f32)
+        return summed.astype(bf16)
+
+    later = returned(1)
+    rest = groups - 2
+    final[pl.ds(2, rest)] = dot_tn(
+        order[:, early:, 2 * block :].reshape(members * (share - early), rest * block),
+        later.reshape(members * (share - early), width),
+    ).astype(bf16).reshape(rest, block, width)
     home = []
-    for k, peer in enumerate(peers):
-        home.append(pltpu.make_async_remote_copy(
-            src_ref=final.at[peer], dst_ref=landed.at[group], send_sem=back_send.at[k],
-            recv_sem=back_recv.at[k], device_id=(here, peer), device_id_type=MESH))
-        home[-1].start()
-    ret_ref[group] = final[group]
-    for copy in home:
-        copy.wait_recv()
-    for k in range(1, groups):
-        source = lax.rem(group + groups - k, groups)
-        ret_ref[source] = landed[source]
+    for k, (place, _) in enumerate(others):
+        home.append(hand_over(1 + k, final.at[place], landed, back_send, back_recv))
+    sooner = returned(0)
+    final[pl.ds(0, 2)] = (
+        dot_tn(order[:, :early, : 2 * block].reshape(members * early, 2 * block),
+               sooner.reshape(members * early, width))
+        + dot_tn(order[:, early:, : 2 * block].reshape(members * (share - early), 2 * block),
+                 later.reshape(members * (share - early), width))
+    ).astype(bf16).reshape(2, block, width)
+    home.append(hand_over(0, final.at[1 - core], landed, back_send, back_recv))
+    ret_ref[group] = final[core]
+    for k in range(groups - 1):
+        taken(k, landed, back_send, back_recv)
+    ret_ref[near_group] = landed[1 - core]
+    for place, other in others:
+        ret_ref[other] = landed[place]
     for copy in there + sent + home:
         copy.wait_send()
     for save in saves:
@@ -1012,10 +1050,10 @@
             VMEM((members, hidden, width), low),
             VMEM((members * share, width), f32),
             dma((groups - 1,)), dma((groups - 1,)),
-            dma((quads, members)), dma((quads, members)),
-            dma((quads, members)), dma((quads, members)),
+            dma((quads, members, 2)), dma((quads, members, 2)),
+            dma((quads, members, 2)), dma((quads, members, 2)),
             dma((groups - 1,)), dma((groups - 1,)),
-            dma((4 + max(folds(width, hidden), 1),)),
+            dma((5,)),
         ],
         compiler_params=pltpu.CompilerParams(
             collective_id=identity, has_side_effects=True, vmem_limit_bytes=60 * MIB
@@ -1041,32 +1079,35 @@
     ]
 
 
+def slice_kernel(layer, from_ref, to_ref, held, got, put):
+    count = held.shape[0]
+    incoming = [pltpu.make_async_copy(from_ref.at[layer, e], held.at[e], got.at[e]) for e in range(count)]
+    outgoing = [pltpu.make_async_copy(held.at[e], to_ref.at[e], put.at[e]) for e in range(count)]
+    for copy in incoming:
+        copy.start()
+    for into, out in zip(incoming, outgoing):
+        into.wait()
+        out.start()
+    for out in outgoing:
+        out.wait()
+
+
+def layer_of(values, layer):
+    shape = values.shape[1:]
+    return pl.pallas_call(
+        functools.partial(slice_kernel, layer),
+        out_shape=shaped(shape, values.dtype),
+        in_specs=[ANYWHERE],
+        out_specs=ANYWHERE,
+        scratch_shapes=[
+            VMEM(shape, values.dtype), pltpu.SemaphoreType.DMA(shape[:1]), pltpu.SemaphoreType.DMA(shape[:1])],
+        compiler_params=pltpu.CompilerParams(vmem_limit_bytes=60 * MIB),
+        cost_estimate=microseconds(2),
+    )(values)
+
+
 def folds(width, hidden):
     return 0 if hidden % LANES else width // hidden
-
-
-def pack_kernel(up_ref, down_ref, out_ref):
-    width, hidden = up_ref.shape
-    out_ref[:width] = up_ref[...]
-    for f in range(width // hidden):
-        out_ref[width + f * hidden : width + (f + 1) * hidden] = down_ref[:, f * hidden : (f + 1) * hidden]
-
-
-def packed_weights(layer, up, down):
-    _, experts, width, hidden = up.shape
-    if not folds(width, hidden):
-        return [up[layer], down[layer]]
-    return [plain_call(
-        pack_kernel,
-        (experts,),
-        [pl.BlockSpec((None, None, width, hidden), lambda e: (layer, e, 0, 0)),
-         pl.BlockSpec((None, None, hidden, width), lambda e: (layer, e, 0, 0))],
-        pl.BlockSpec((None, 2 * width, hidden), lambda e: (e, 0, 0)),
-        shaped((experts, 2 * width, hidden), up.dtype),
-        [],
-        (up, down),
-        4,
-    )]
 
 
 def weights_kernel(rows_ref, pre_ref, hidden_ref, grad_ref, *out_refs):
@@ -1233,15 +1274,18 @@
             window = window_of(spot + sign * (half - step))
             if step == 0:
                 which, got_which = parts_later[way], parts_got[way]
+                if not (later - cut_later if way else cut_later):
+                    continue
             else:
                 which, got_which = behind, pl.ds(0, later)
                 add_which, add_got = (
                     (parts_later[way], parts_got[way]) if step == 1 else (which, got_which))
-                turns[way][-1].wait_recv()
-                own[window, :, add_which] = (
-                    own[window, :, add_which].astype(f32)
-                    + spun[way, step - 1, :, add_got].astype(f32)
-                ).astype(low)
+                if turns[way]:
+                    turns[way][-1].wait_recv()
+                    own[window, :, add_which] = (
+                        own[window, :, add_which].astype(f32)
+                        + spun[way, step - 1, :, add_got].astype(f32)
+                    ).astype(low)
             copy = pltpu.make_async_remote_copy(
                 src_ref=own.at[window, :, which], dst_ref=spun.at[way, step, :, got_which],
                 send_sem=spin_send.at[way, step], recv_sem=spin_recv.at[way, step],
@@ -1249,29 +1293,6 @@
             copy.start()
             sent.append(copy)
             turns[way].append(copy)
-
-    turns = ([], [])
-    meet(0)
-    spin_later(0)
-    for step in range(1, half):
-        meet(2 * step - 1)
-        meet(2 * step)
-        spin_later(step)
-    meet(len(order) - 1)
-    summed = own[here, :, behind].astype(f32)
-    for way in (0, 1):
-        turns[way][-1].wait_recv()
-        summed = summed + spun[way, half - 1].astype(f32)
-    own[here, :, behind] = summed.astype(low)
-    homes = []
-    for j, other in enumerate(lines_away):
-        copy = pltpu.make_async_remote_copy(
-            src_ref=own.at[here, other, behind], dst_ref=home.at[j],
-            send_sem=home_send.at[j], recv_sem=home_recv.at[j],
-            device_id=(here, 2 * other + core), device_id_type=MESH)
-        copy.start()
-        sent.append(copy)
-        homes.append(copy)
 
     def cross(k):
         window = order[k]
@@ -1307,8 +1328,31 @@
             sent.append(copy)
             first_turns[way].append(copy)
 
-    for step in range(half):
-        spin_first(step)
+    turns = ([], [])
+    meet(0)
+    spin_later(0)
+    for step in range(1, half):
+        meet(2 * step - 1)
+        meet(2 * step)
+        spin_first(step - 1)
+        spin_later(step)
+    meet(len(order) - 1)
+    spin_first(half - 1)
+    summed = own[here, :, behind].astype(f32)
+    for way in (0, 1):
+        turns[way][-1].wait_recv()
+        summed = summed + spun[way, half - 1].astype(f32)
+    own[here, :, behind] = summed.astype(low)
+    homes = []
+    for j, other in enumerate(lines_away):
+        copy = pltpu.make_async_remote_copy(
+            src_ref=own.at[here, other, behind], dst_ref=home.at[j],
+            send_sem=home_send.at[j], recv_sem=home_recv.at[j],
+            device_id=(here, 2 * other + core), device_id_type=MESH)
+        copy.start()
+        sent.append(copy)
+        homes.append(copy)
+
     summed = cross(len(order) - 1)
     for way in (0, 1):
         first_turns[way][-1].wait_recv()
@@ -1359,6 +1403,161 @@
         ),
         cost_estimate=microseconds(60),
     )(*[array.reshape(count, lines, 2, array.shape[1], width) for array in arrays])
+
+
+def inward_kernel(dims, grad_ref, weight_ref, edge_ref, handed_ref, normed_ref, begin_ref, gain_ref, passed_ref,
+                  out_ref, channel_ref, router_ref, expert_ref, packed_ref, new_ref, rows, features):
+    blocks, wide, tall, held, fold, marks, spare, steps = dims
+    owners, count, _ = packed_ref.shape
+    f32, low = jnp.float32, jnp.bfloat16
+    step = pl.program_id(0)
+    tokens = grad_ref.shape[0]
+    last = edge_ref.shape[0]
+    value = lax.rem(step, blocks) < blocks // 2
+    place = lax.broadcasted_iota(jnp.int32, grad_ref.shape, 0)
+    block = grad_ref[...].astype(f32)
+    edge = edge_ref[...] + handed_ref[...]
+    for j in range(last):
+        row = (steps - last + j) * CHUNKS + CHUNKS - 1
+        block = jnp.where(jnp.logical_and(place == row, value), edge[j : j + 1], block)
+    block = block.astype(low)
+
+    @pl.when(step == 0)
+    def _():
+        new_ref[...] = jnp.zeros_like(new_ref)
+        rows[...] = jnp.zeros_like(rows)
+
+    @pl.when(step < blocks)
+    def _():
+        new_ref[...] += dot_nt(block, weight_ref[...])
+
+    @pl.when(step == blocks - 1)
+    def _():
+        grad, norm_grad = rms_back(begin_ref[...], gain_ref[...], new_ref[...])
+        new_ref[...] = passed_ref[...] + grad
+        experts = router_ref.shape[1]
+        lane = lax.broadcasted_iota(jnp.int32, (experts, 2 * LANES), 1)
+        row = lax.broadcasted_iota(jnp.int32, (experts, 2 * LANES), 0)
+        pick = (lane == row + spare).astype(f32).astype(low)
+        lane = lax.broadcasted_iota(jnp.int32, (2, 2 * LANES), 1)
+        row = lax.broadcasted_iota(jnp.int32, (2, 2 * LANES), 0)
+        pick_norms = (lane == row + spare + experts).astype(f32).astype(low)
+        norms = jnp.concatenate([norm_grad[None], expert_ref[...]], axis=0).astype(low)
+        features[...] = dot_nn(router_ref[...].astype(low), pick) + dot_tn(norms, pick_norms)
+
+    @pl.when(step >= blocks)
+    def _():
+        grad = dot_tn(block, normed_ref[...])
+        passed = out_ref[...]
+        channel = channel_ref[...].astype(f32)
+        start = pl.multiple_of((step - blocks) * owners * marks, 8)
+        mine = features[pl.ds(start, owners * marks), :]
+        thin = held // fold
+        whole_tiles = not any(size % 16 for size in (wide, tall, thin))
+        target = packed_ref if whole_tiles else rows
+        kind = target.dtype
+        for k in range(owners):
+            target[k, :wide] = grad[k * wide : (k + 1) * wide].astype(kind)
+            target[k, wide : wide + tall] = passed[k * tall : (k + 1) * tall].astype(kind)
+            small = channel[k * held : (k + 1) * held]
+            extra = mine[k * marks : (k + 1) * marks]
+            small = small + jnp.concatenate([extra, jnp.zeros((held - marks, 2 * LANES), f32)], axis=0)
+            for f in range(fold):
+                target[k, wide + tall : wide + tall + thin, f * 2 * LANES : (f + 1) * 2 * LANES] = small[
+                    f * thin : (f + 1) * thin].astype(kind)
+            if whole_tiles and count > wide + tall + thin:
+                packed_ref[k, wide + tall + thin :] = jnp.zeros((count - wide - tall - thin, grad.shape[1]), kind)
+        if not whole_tiles:
+            packed_ref[...] = rows[...].astype(low)
+
+
+def mixer_inward(layer, grad_projected, in_weight, edge, handed, normed, begin, gain, passed, grad_out, channel,
+                 grad_router, grad_expert, devices, spare):
+    tokens, columns = grad_projected.shape
+    width = normed.shape[1]
+    wide, tall = columns // devices, grad_out.shape[0] // devices
+    held, marks = channel.shape[0] // devices, width // devices
+    fold = width // (2 * LANES)
+    count = wide + tall + held // fold
+    count += -count % 16
+    owners = 1
+    while owners * wide % LANES:
+        owners *= 2
+    blocks = devices // owners
+    span = owners * wide
+    taps = edge.shape[0]
+    inner = edge.shape[1] // span
+
+    def at(i):
+        return jnp.maximum(i - blocks, 0)
+
+    return plain_call(
+        functools.partial(inward_kernel, (blocks, wide, tall, held, fold, marks, spare, tokens // CHUNKS)),
+        (2 * blocks,),
+        [pl.BlockSpec((tokens, span), lambda i: (0, i % blocks)),
+         pl.BlockSpec((None, width, span), lambda i: (layer, 0, jnp.minimum(i, blocks - 1))),
+         pl.BlockSpec((taps, span), lambda i: (0, jnp.minimum(i % blocks, inner - 1))),
+         pl.BlockSpec((taps, span), lambda i: (0, jnp.minimum(i % blocks, inner - 1))),
+         whole(normed.shape), whole(begin.shape), layer_whole(layer, (1, width)), whole(passed.shape),
+         pl.BlockSpec((owners * tall, width), lambda i: (at(i), 0)),
+         pl.BlockSpec((owners * held, 2 * LANES), lambda i: (at(i), 0)),
+         whole(grad_router.shape), whole(grad_expert.shape)],
+        [pl.BlockSpec((owners, count, width), lambda i: (at(i), 0, 0)), whole((tokens, width))],
+        [shaped((devices, count, width), jnp.bfloat16), shaped((tokens, width))],
+        [VMEM((owners, count, width), jnp.float32), VMEM((width, 2 * LANES), jnp.float32)],
+        (grad_projected, in_weight, edge, handed, normed, begin, gain, passed, grad_out, channel, grad_router,
+         grad_expert),
+        9,
+    )
+
+
+def unfold_kernel(dims, *refs):
+    layers, wide, tall, held, fold, marks, spare, sizes = dims
+    inputs, outs = refs[:layers], refs[layers:]
+    (in_ref, out_ref, state_ref, step_ref, decay_ref, conv_ref, conv_bias_ref, step_bias_ref, skip_ref,
+     router_ref, mix_ref, expert_ref) = outs
+    thin = held // fold
+    for layer in range(layers):
+        whole_rows = inputs[layer][...].astype(jnp.float32)
+        in_ref[layer] = whole_rows[:wide]
+        out_ref[layer] = whole_rows[wide : wide + tall]
+        mine = whole_rows[wide + tall : wide + tall + thin]
+        channel = jnp.concatenate(
+            [mine[:, f * 2 * LANES : (f + 1) * 2 * LANES] for f in range(fold)], axis=0)
+        state_ref[layer] = channel[:, : sizes[0]]
+        turned = channel.T
+        bounds = [0]
+        for size in sizes:
+            bounds.append(bounds[-1] + size)
+        pieces = [turned[bounds[i] : bounds[i + 1]] for i in range(7)]
+        step_ref[layer] = pieces[1]
+        decay_ref[layer] = pieces[2]
+        conv_ref[layer] = pieces[3]
+        conv_bias_ref[layer : layer + 1] = pieces[4]
+        step_bias_ref[layer : layer + 1] = pieces[5]
+        skip_ref[layer : layer + 1] = pieces[6]
+        experts = router_ref.shape[1]
+        router_ref[layer] = turned[spare : spare + experts, :marks]
+        mix_ref[layer : layer + 1] = turned[spare + experts : spare + experts + 1, :marks]
+        expert_ref[layer : layer + 1] = turned[spare + experts + 1 : spare + experts + 2, :marks]
+
+
+def unfolded(sums, wide, tall, held, marks, experts, spare, sizes):
+    layers, width = len(sums), sums[0].shape[1]
+    fold = width // (2 * LANES)
+    shapes = [
+        (wide, width), (tall, width), (held, sizes[0]), (sizes[1], held), (sizes[2], held), (sizes[3], held),
+        (held,), (held,), (held,), (experts, marks), (marks,), (marks,),
+    ]
+    inside = pl.BlockSpec(memory_space=VMEM)
+    return pl.pallas_call(
+        functools.partial(unfold_kernel, (layers, wide, tall, held, fold, marks, spare, sizes)),
+        out_shape=[shaped((layers,) + shape) for shape in shapes],
+        in_specs=[inside] * layers,
+        out_specs=[inside] * len(shapes),
+        compiler_params=pltpu.CompilerParams(vmem_limit_bytes=60 * MIB),
+        cost_estimate=microseconds(3),
+    )(*sums)
 
 
 def on_device(
@@ -1403,8 +1602,8 @@
     keep_mask = rim_keep(starts, taps - 1)[:, None]
     reset = jnp.broadcast_to((starts * RESET)[..., None], starts.shape + (LANES,))
     order = expert_order(per_group, groups, block, capacity)
-    conv_bias, step_bias, skip_weight, norm_expert = (
-        values[:, None, :] for values in (conv_bias, step_bias, skip_weight, norm_expert))
+    norm_mix, conv_bias, step_bias, skip_weight, norm_expert = (
+        values[:, None, :] for values in (norm_mix, conv_bias, step_bias, skip_weight, norm_expert))
     current = to_steps(hidden[0]).reshape(tokens, width).astype(f32)
     saved = []
 
@@ -1425,8 +1624,8 @@
 
     tail = passed_along(hidden[0, tokens - taps + 1 :] * keep_mask.astype(low), 1)
     weights = [None] * layers
-    ready, tail = lax.optimization_barrier((packed_weights(0, expert_up, expert_down), tail))
-    weights[0] = between_members(ready)
+    ready, tail = lax.optimization_barrier((layer_of(expert_up, 0), tail))
+    weights[0] = between_members([ready])
     for layer in range(layers):
         begin = current
         normed = rms_scale(current, norm_mix[layer]).astype(low)
@@ -1439,14 +1638,18 @@
         act, selection, size, link, link_size, total, total_size = mixer_front(
             layer, projected, rim, masks, reset, conv_weight, conv_bias, state_weight, step_weight, step_bias,
             decay_log)
+        if layer == 0:
+            total, fills, order = lax.optimization_barrier((total, fills, order))
+        total, ready = lax.optimization_barrier((total, layer_of(expert_down, layer)))
         entering = handed_on(layer, total, total_size, decay_log, False, layer)
-        if layer + 1 < layers:
-            ready, entering = lax.optimization_barrier(
-                (packed_weights(layer + 1, expert_up, expert_down), entering))
-            weights[layer + 1] = between_members(ready)
+        ready, entering = lax.optimization_barrier((ready, entering))
+        weights[layer] += between_members([ready])
         mixed, gated, begins, middle, routed, logits, outbound = mixer_run(
             layer, size, act, selection, reset, decay_log, link, link_size, entering, projected, skip_weight,
             out_weight, current, norm_expert, router, fills[layer])
+        if layer + 1 < layers:
+            ready, outbound = lax.optimization_barrier((layer_of(expert_up, layer + 1), outbound))
+            weights[layer + 1] = between_members([ready])
         returned, kept_rows, pre_act, hidden_low = expert_pass(
             outbound.reshape(groups, block, width), order, weights[layer], None, 4 + layer)
         shares = jax.nn.softmax(logits, axis=-1)
@@ -1459,11 +1662,10 @@
             kept_rows=kept_rows, pre_act=pre_act, hidden_low=hidden_low, back_rows=back_rows))
     output = to_tokens(cube(current.astype(low)))[None]
     grad = to_steps(cotangent[0]).reshape(tokens, width).astype(f32)
-    packed = [None] * layers
+    sums = [None] * layers
     expert_grads = [None] * layers
     per_device = inner // devices
     norm_device = width // devices
-    fold = width // (2 * LANES)
     spare = 160
     for layer in range(layers - 1, -1, -1):
         entry = saved[layer]
@@ -1490,58 +1692,28 @@
         grad_act, grad_decay, grad_bias, grad_step, grad_selection = mixer_back(
             layer, entry["size"], entry["act"], grad_y, decay_log, entry["selection"], reset,
             entry["begins"], link, link_size, entering, step_weight, step_bias, skip_weight)
-        grad_value, edge, rim_grad, channel = mixer_conv_back(
+        grad_projected, edge, rim_grad, channel = mixer_conv_back(
             layer, grad_act, grad_selection, state_weight, entry["projected"], entry["rim"], masks, conv_weight,
-            conv_bias, entry["act"], grad_step, grad_decay, grad_bias, grad_skip)
-        edge = edge + passed_along(rim_grad, -1) * keep_mask
-        grad_value = cube(grad_value).at[steps - taps + 1 :, CHUNKS - 1].set(edge.astype(low))
-        grad_value = grad_value.reshape(tokens, inner)
-        grad_projected = jnp.concatenate([grad_value, grad_igate], axis=1)
-        grad_in = dot_tn(grad_projected, entry["normed"]).astype(low)
-        grad_normed = dot_nt(grad_projected, in_weight[layer])
-        grad_begin, grad_norm_mix = rms_back(entry["begin"], norm_mix[layer], grad_normed)
-        grad = grad + grad_begin
-        feature = jnp.concatenate(
-            [grad_router, grad_norm_mix[:, None], grad_norm_expert.reshape(width, 1)], axis=1)
-        feature = jnp.pad(
-            feature.reshape(devices, norm_device, experts + 2).astype(low),
-            ((0, 0), (0, per_device - norm_device), (spare, 2 * LANES - spare - experts - 2)))
-        channel = channel.reshape(devices, per_device, 2 * LANES) + feature
-        channel = jnp.swapaxes(channel.reshape(devices, fold, per_device // fold, 2 * LANES), 1, 2)
-        packed[layer] = [
-            grad_in.reshape(devices, -1, width),
-            grad_out.reshape(devices, -1, width),
-            channel.reshape(devices, -1, width),
-        ]
+            conv_bias, entry["act"], grad_step, grad_decay, grad_bias, grad_skip, grad_igate)
+        handed = passed_along(rim_grad, -1) * keep_mask
+        blocks, grad = mixer_inward(
+            layer, grad_projected, in_weight, edge, handed, entry["normed"], entry["begin"], norm_mix, grad,
+            grad_out, channel, grad_router, grad_norm_expert.reshape(1, width), devices, spare)
+        if layer:
+            blocks, grad = lax.optimization_barrier((blocks, grad))
+            rows = blocks.shape[1]
+            sums[layer] = lax.psum_scatter(
+                blocks.reshape(devices * rows, width), both, scatter_dimension=0, tiled=True)
+        else:
+            sums[layer] = summed_shares([blocks], 8)
+    (grad_in, grad_out, grad_state, grad_step, grad_decay, grad_conv, grad_conv_bias, grad_step_bias, grad_skip,
+     grad_router, grad_norm_mix, grad_norm_expert) = unfolded(
+        sums, 2 * inner // devices, per_device, per_device, norm_device, experts, spare,
+        (rank + 2 * states, rank, states, taps, 1, 1, 1))
+    shared = (
+        grad_norm_mix, jnp.swapaxes(grad_in, 1, 2), grad_conv, grad_conv_bias, grad_state, grad_step,
+        grad_step_bias, grad_decay, grad_skip, grad_out, grad_norm_expert, jnp.swapaxes(grad_router, 1, 2))
     up_grads, down_grads = widened(*expert_grads, width, expert_up.shape[3])
-    sums = summed_shares([part for parts in packed for part in parts], 8)
-    bounds = [0]
-    for part in packed[0]:
-        bounds.append(bounds[-1] + part.shape[1])
-    sums = sums[: layers * bounds[-1]].reshape(layers, bounds[-1], width)
-    grad_in, grad_out, mine = (sums[:, bounds[i] : bounds[i + 1]] for i in range(3))
-    mine = mine.reshape(layers, per_device // fold, fold, 2 * LANES)
-    mine = jnp.swapaxes(mine, 1, 2).reshape(layers, per_device, 2 * LANES)
-    feature = mine[:, :norm_device, spare : spare + experts + 2]
-    fields = jnp.swapaxes(mine, 1, 2)
-    bounds = [0]
-    for count in (rank + 2 * states, rank, states, taps, 1, 1, 1):
-        bounds.append(bounds[-1] + count)
-    fields = [fields[:, bounds[i] : bounds[i + 1]] for i in range(7)]
-    shared = (
-        feature[:, :, experts],
-        jnp.swapaxes(grad_in, 1, 2),
-        fields[3],
-        fields[4][:, 0],
-        mine[:, :, : bounds[1]],
-        fields[1],
-        fields[5][:, 0],
-        fields[2],
-        fields[6][:, 0],
-        grad_out,
-        feature[:, :, experts + 1],
-        feature[:, :, :experts],
-    )
     output_grad = to_tokens(cube(grad))[None]
     return (output, output_grad, *shared, up_grads, down_grads)
 

time: 779 us -> 747 us (0.959)
  Pallas kernels: 626 us -> 593 us
  matrix products: 45.2 us -> 28.2 us
  local copies, waits for them, and re-layouts: 31.5 us -> 17 us
  between operations: 2.31 us -> 15.3 us
  starting transfers between devices: 29.4 us -> 41.8 us
  waiting for transfers between devices: 13.3 us -> 22.9 us
    pallas_call x1, Pallas kernels: 75.2 us -> 43.7 us  [summed_shares(): pl.pallas_call(functools.partial(sum_kernel, (count, lines, sizes, first,...]
    pallas_call x15, Pallas kernels: 216 us -> 240 us  [plain_call(): pl.pallas_call(kernel, grid=grid, in_specs=in_specs, out_specs=out_specs,...]
    pallas_call x4, Pallas kernels: 255 us -> 236 us  [expert_pass(): pl.pallas_call(functools.partial(expert_kernel, dims, backward), out_shap...]
    pallas_call x4, Pallas kernels: 79.4 us -> 60.9 us  [handed_on(): pl.pallas_call(functools.partial(link_kernel, layer, count, reverse), out...]
    pallas_call x0 -> x5, Pallas kernels: none -> 12.3 us  [the longest x4 10.2 us: layer_of(): pl.pallas_call(functools.partial(slice_kernel, layer), out_shape=shaped(s...]
    all_to_all x4 -> x6, starting transfers between devices: 20.5 us -> 30.8 us  [between_members(): lax.all_to_all(values, 'wide', split_axis=0, concat_axis=0, tiled=True, a...]
    dot_general x4 -> x2, matrix products: 12.6 us -> 2.56 us  [dot_nt(): lax.dot_general(left, right, (((1,), (1,)), ((), ())), preferred_element_...]
    dot_general x8 -> x6, matrix products: 17.7 us -> 10.6 us  [dot_tn(): lax.dot_general(left, right, (((0,), (0,)), ((), ())), preferred_element_...]
  transfers between devices with their start and end apart: 8 -> 11, of which waited for: 2 -> 4; matrix products, arithmetic and copies ran while one was open for 11% -> 7% of each run, Pallas kernels for 58% -> 60%
where the time goes in v3:
time: 747 us; the launch traced here: 737 us
  Pallas kernels  593 us (79%)
  starting transfers between devices  41.8 us (6%)
  matrix products  28.2 us (4%)
  waiting for transfers between devices  22.9 us (3%)
  other arithmetic  18.9 us (3%)
  local copies, waits for them, and re-layouts  17 us (2%)
  between operations  15.3 us (2%)
    pallas_call x15, Pallas kernels, plain_call(): pl.pallas_call(kernel, grid=grid, in_specs=in_specs, out_specs=out_specs,...  240 us
    pallas_call x4, Pallas kernels, expert_pass(): pl.pallas_call(functools.partial(expert_kernel, dims, backward), out_shap...  236 us
    pallas_call x4, Pallas kernels, handed_on(): pl.pallas_call(functools.partial(link_kernel, layer, count, reverse), out...  60.9 us
    pallas_call x1, Pallas kernels, summed_shares(): pl.pallas_call(functools.partial(sum_kernel, (count, lines, sizes, first,...  43.7 us
    all_to_all x6, starting transfers between devices, between_members(): lax.all_to_all(values, 'wide', split_axis=0, concat_axis=0, tiled=True, a...  30.8 us
    ppermute x4, waiting for transfers between devices, passed_along(): lax.ppermute(x, 'wide', [(i, i + by) for i in range(size) if 0 <= i + by...  18.9 us
    dot_general x5, matrix products, dot_nn(): lax.dot_general(left, right, (((1,), (0,)), ((), ())), preferred_element_...  15 us
  transfers between devices with their start and end apart: 11, of which 4 were waited for; matrix products, arithmetic and copies ran while one was open for 7% of the time, Pallas kernels for 60%

profile of v3, /device:TPU:0, one launch (start us, length us, event | category | flops | bytes accessed | tf_op | source)
XLA Modules:
  0.0 736.9 jit_solution(3668065091696074983)
XLA Ops:
  9.3 4.9 collective-permute-start
  15.1 2.5 shard_map.306
  20.0 3.8 all-to-all-start
  26.2 2.5 shard_map.308
  31.6 5.7 fusion.2.value_ref.gate_ref
  37.4 2.7 fusion.6.rim_ref
  41.8 14.0 %shard_map.307 = (bf16[256,1536]{1,0:T(8,128)(2,1)}, f32[32,8,80]{2,1,0:T(8,128)}, f32[32,8,1536]{2,1,0:T(8,128)}, f32[16,8,1536]{2,1,0:T(8,128)}, f32[8,1536]{1...) custom-call(f32[32,8,3072]{2,1,0:T(8,128)} %fusion.2.value_ref.gate_ref, f32[3,1536]{1,0:T(4,128)} %fusion.6.rim_ref, ...), custom_call_target="tpu_custom_call" | custom-call | flops 2700000000 | bytes 10000 | tf_op jit(solution)/shard_map/pallas_call | solution.py:90
  55.9 13.3 %shard_map.309.entering_ref = f32[16,1536]{1,0:T(8,128)} custom-call(f32[16,1536]{1,0:T(8,128)} %get-tuple-element.139.total_ref, f32[1,1536]{1,0:T(1,128)} %get-tuple-element.140.size_ref, f32[2,16,1536]{2,1,0:T(8,128)} %decay_ref.23), custom_call_target="tpu_custom_call" | custom-call | flops 1800000000 | bytes 10000 | tf_op jit(solution)/shard_map/pallas_call | solution.py:765
  69.2 4.5 all-to-all-start.1
  73.7 2.1 copy.88
  77.9 2.5 shard_map.311
  80.5 18.4 %shard_map.310 = (f32[32,8,1536]{2,1,0:T(8,128)}, bf16[256,1536]{1,0:T(8,128)(2,1)}, f32[16,8,1536]{2,1,0:T(8,128)}, f32[256,768]{1,0:T(8,128)}, bf16[256,768]{1...) custom-call(f32[32,8,1536]{2,1,0:T(8,128)} %get-tuple-element.131.size_ref, ...), custom_call_target="tpu_custom_call" | custom-call | flops 3300000000 | bytes 10000 | tf_op jit(solution)/shard_map/pallas_call | solution.py:90
  99.1 4.8 all-to-all-start.2
  105.7 70.9 %shard_map.312 = (bf16[4,80,768]{2,1,0:T(8,128)(2,1)}, bf16[640,768]{1,0:T(8,128)(2,1)}, f32[4,640,384]{2,1,0:T(8,128)}, bf16[4,640,384]{2,1,0:T(8,128)(2,1)}) custom-call(bf16[4,80,768]{2,1,0:T(8,128)(2,1)} %bitcast.145, bf16[320,320]{1,0:T(8,128)(2,1)} %fusion.14.refs_1_, bf16[4,768,384]{2,1,0:T(8,128)(2,1)} %copy-done.9, ...), custom_call_target="tpu_custom_call" | custom-call | flops 9749999616 | bytes 10000 | tf_op jit(solution)/shard_map/pallas_call | solution.py:1034
  176.7 2.9 multiply_reduce_fusion.7
  179.8 4.0 fusion.value_ref.gate_ref
  184.6 3.5 collective-permute-start.1
  188.1 2.6 shard_map.314
  190.7 14.0 %shard_map.313 = (bf16[256,1536]{1,0:T(8,128)(2,1)}, f32[32,8,80]{2,1,0:T(8,128)}, f32[32,8,1536]{2,1,0:T(8,128)}, f32[16,8,1536]{2,1,0:T(8,128)}, f32[8,1536]{1...) custom-call(f32[32,8,3072]{2,1,0:T(8,128)} %copy-done, f32[3,1536]{1,0:T(4,128)} %collective-permute-done.1.rim_ref, ...), custom_call_target="tpu_custom_call" | custom-call | flops 2700000000 | bytes 10000 | tf_op jit(solution)/shard_map/pallas_call | solution.py:90
  204.7 14.6 %shard_map.315.entering_ref = f32[16,1536]{1,0:T(8,128)} custom-call(f32[16,1536]{1,0:T(8,128)} %get-tuple-element.158.total_ref, f32[1,1536]{1,0:T(1,128)} %get-tuple-element.159.size_ref, f32[2,16,1536]{2,1,0:T(8,128)} %decay_ref.23), custom_call_target="tpu_custom_call" | custom-call | flops 1800000000 | bytes 10000 | tf_op jit(solution)/shard_map/pallas_call | solution.py:765
  219.3 5.2 all-to-all-start.3
  224.6 18.4 %shard_map.316 = (f32[32,8,1536]{2,1,0:T(8,128)}, bf16[256,1536]{1,0:T(8,128)(2,1)}, f32[16,8,1536]{2,1,0:T(8,128)}, f32[256,768]{1,0:T(8,128)}, bf16[256,768]{1...) custom-call(f32[32,8,1536]{2,1,0:T(8,128)} %get-tuple-element.151.size_ref, ...), custom_call_target="tpu_custom_call" | custom-call | flops 3300000000 | bytes 10000 | tf_op jit(solution)/shard_map/pallas_call | solution.py:90
  247.6 3.7 all-to-all-done.3.refs_3_
  251.3 53.0 %shard_map.317 = (bf16[4,80,768]{2,1,0:T(8,128)(2,1)}, bf16[640,768]{1,0:T(8,128)(2,1)}, f32[4,640,384]{2,1,0:T(8,128)}, bf16[4,640,384]{2,1,0:T(8,128)(2,1)}) custom-call(bf16[4,80,768]{2,1,0:T(8,128)(2,1)} %bitcast.146, bf16[320,320]{1,0:T(8,128)(2,1)} %fusion.14.refs_1_, bf16[4,768,384]{2,1,0:T(8,128)(2,1)} %all-to-all-done.2.refs_2_, ...), custom_call_target="tpu_custom_call" | custom-call | flops 9749999616 | bytes 10000 | tf_op jit(solution)/shard_map/pallas_call | solution.py:1034
  304.4 1.9 fusion.10
  308.9 55.3 %shard_map.318 = (bf16[4,80,768]{2,1,0:T(8,128)(2,1)}, bf16[640,768]{1,0:T(8,128)(2,1)}, bf16[4,640,384]{2,1,0:T(8,128)(2,1)}) custom-call(bf16[4,80,768]{2,1,0:T(8,128)(2,1)} %bitcast.132, bf16[320,320]{1,0:T(8,128)(2,1)} %fusion.14.refs_1_, bf16[4,768,384]{2,1,0:T(8,128)(2,1)} %all-to-all-done.2.refs_2_, bf16[4,384,768]{2,1,0:T(8,128)(2,1)} %all-to-all-done.3.refs_3_, ...), custom_call_target="tpu_custom_call" | custom-call | flops 9749999616 | bytes 10000 | tf_op jit(solution)/shard_map/pallas_call | solution.py:1034
  364.2 1.8 multiply_reduce_fusion.4
  367.8 15.9 %shard_map.319 = (f32[32,8,1536]{2,1,0:T(8,128)}, bf16[256,3072]{1,0:T(8,128)(2,1)}, f32[1,1536]{1,0:T(1,128)}, bf16[1536,768]{1,0:T(8,128)(2,1)}, f32[16,8,1536...) custom-call(bf16[256,768]{1,0:T(8,128)(2,1)} %get-tuple-element.258.grad_ref, ...), custom_call_target="tpu_custom_call" | custom-call | flops 2100000000 | bytes 10000 | tf_op jit(solution)/shard_map/pallas_call | solution.py:90
  383.7 13.5 %shard_map.321.entering_ref = f32[16,1536]{1,0:T(8,128)} custom-call(f32[16,1536]{1,0:T(8,128)} %get-tuple-element.180.total_ref, f32[1,1536]{1,0:T(1,128)} %get-tuple-element.181.size_ref, f32[2,16,1536]{2,1,0:T(8,128)} %decay_ref.23), custom_call_target="tpu_custom_call" | custom-call | flops 1800000000 | bytes 10000 | tf_op jit(solution)/shard_map/pallas_call | solution.py:765
  397.2 8.4 %shard_map.320 = bf16[4,1536,384]{2,1,0:T(8,128)(2,1)} custom-call(bf16[640,768]{1,0:T(8,128)(2,1)} %get-tuple-element.176.rows_ref, bf16[4,640,384]{2,1,0:T(8,128)(2,1)} %get-tuple-element.177.pre_ref, bf16[4,640,384]{2,1,0:T(8,128)(2,1)} %get-tuple-element.178.hidden_ref, bf16[640,768]{1,0:T(8,128)(2,1)} %get-tuple-element.179.grad_ref), custom_call_target="tpu_custom_call" | custom-call | flops 900000000 | bytes 10000 | tf_op jit(solution)/shard_map/pallas_call | solution.py:90
  405.7 5.1 all-to-all-start.5
  411.4 27.1 %shard_map.322 = (f32[32,8,1536]{2,1,0:T(8,128)}, f32[16,1536]{1,0:T(8,128)}, f32[1,1536]{1,0:T(1,128)}, f32[48,1536]{1,0:T(8,128)}, bf16[256,80]{1,0:T(8,128)(2,1)}) custom-call(f32[32,8,1536]{2,1,0:T(8,128)} %get-tuple-element.151.size_ref, bf16[256,1536]{1,0:T(8,128)(2,1)} %get-tuple-element.152.act_ref, f32[32,8,1536]{2,1,0:T(8,128)} %get-tuple-element.172.grad_ref, ...), custom_call_target="tpu_custom_call" | custom-call | flops 5249999872 | bytes 10000 | tf_op jit(solution)/shard_map/pallas_call | solution.py:90
  438.5 13.2 %shard_map.323 = (bf16[256,3072]{1,0:T(8,128)(2,1)}, f32[3,1536]{1,0:T(4,128)}, f32[3,1536]{1,0:T(4,128)}, bf16[1536,256]{1,0:T(8,128)(2,1)}) custom-call(f32[32,8,1536]{2,1,0:T(8,128)} %get-tuple-element.183.grad_act_ref, bf16[256,80]{1,0:T(8,128)(2,1)} %get-tuple-element.184.grad_selection_ref, ...), custom_call_target="tpu_custom_call", output_to_operand_aliasing={{0}: (13, {})} | custom-call | flops 1500000000 | bytes 10000 | tf_op jit(solution)/shard_map/pallas_call | solution.py:90
  454.9 9.8 %collective-permute-done.2 = f32[3,1536]{1,0:T(4,128)S(1)} collective-permute-done((f32[3,1536]{1,0:T(4,128)}, f32[3,1536]{1,0:T(4,128)S(1)}, u32[]{:S(2)}, u32[]{:S(2)}) %collective-permute-start.2) | collective-permute-done | bytes 18464 | tf_op jit(solution)/shard_map/ppermute | solution.py:58
  465.4 17.1 %shard_map.324 = (bf16[32,160,768]{2,1,0:T(8,128)(2,1)}, f32[256,768]{1,0:T(8,128)}) custom-call(bf16[256,3072]{1,0:T(8,128)(2,1)} %get-tuple-element.190.grad_ref, bf16[2,768,3072]{2,1,0:T(8,128)(2,1)} %weight_ref.3, f32[3,1536]{1,0:T(4,128)} %get-tuple-element.191.edge_ref, f32[3,1536]{1,0:T(4,128)} %broadcast_multiply_fusion.1.handed_ref, ...), custom_call_target="tpu_custom_call" | custom-call | flops 1350000000 | bytes 10000 | tf_op jit(solution)/shard_map/pallas_call | solution.py:90
  484.9 56.4 %shard_map.325 = (bf16[4,80,768]{2,1,0:T(8,128)(2,1)}, bf16[640,768]{1,0:T(8,128)(2,1)}, bf16[4,640,384]{2,1,0:T(8,128)(2,1)}) custom-call(bf16[4,80,768]{2,1,0:T(8,128)(2,1)} %bitcast.133, bf16[320,320]{1,0:T(8,128)(2,1)} %fusion.14.refs_1_, bf16[4,768,384]{2,1,0:T(8,128)(2,1)} %copy-done.9, bf16[4,384,768]{2,1,0:T(8,128)(2,1)} %all-to-all-done.1.refs_3_, ...), custom_call_target="tpu_custom_call" | custom-call | flops 9749999616 | bytes 10000 | tf_op jit(solution)/shard_map/pallas_call | solution.py:1034
  541.3 8.4 %shard_map.327 = bf16[4,1536,384]{2,1,0:T(8,128)(2,1)} custom-call(bf16[640,768]{1,0:T(8,128)(2,1)} %get-tuple-element.205.rows_ref, bf16[4,640,384]{2,1,0:T(8,128)(2,1)} %get-tuple-element.206.pre_ref, bf16[4,640,384]{2,1,0:T(8,128)(2,1)} %get-tuple-element.207.hidden_ref, bf16[640,768]{1,0:T(8,128)(2,1)} %get-tuple-element.208.grad_ref), custom_call_target="tpu_custom_call" | custom-call | flops 900000000 | bytes 10000 | tf_op jit(solution)/shard_map/pallas_call | solution.py:90
  554.1 16.1 %shard_map.326 = (f32[32,8,1536]{2,1,0:T(8,128)}, bf16[256,3072]{1,0:T(8,128)(2,1)}, f32[1,1536]{1,0:T(1,128)}, bf16[1536,768]{1,0:T(8,128)(2,1)}, f32[16,8,1536...) custom-call(bf16[256,768]{1,0:T(8,128)(2,1)} %get-tuple-element.256.grad_ref, ...), custom_call_target="tpu_custom_call" | custom-call | flops 2100000000 | bytes 10000 | tf_op jit(solution)/shard_map/pallas_call | solution.py:90
  570.2 19.6 %shard_map.328.entering_ref = f32[16,1536]{1,0:T(8,128)} custom-call(f32[16,1536]{1,0:T(8,128)} %get-tuple-element.209.total_ref, f32[1,1536]{1,0:T(1,128)} %get-tuple-element.210.size_ref, f32[2,16,1536]{2,1,0:T(8,128)} %decay_ref.23), custom_call_target="tpu_custom_call" | custom-call | flops 1800000000 | bytes 10000 | tf_op jit(solution)/shard_map/pallas_call | solution.py:765
  589.8 7.4 %all-to-all-start.4 = ((bf16[4,1536,384]{2,1,0:T(8,128)(2,1)}), bf16[4,1536,384]{2,1,0:T(8,128)(2,1)}, u32[]{:S(2)}, u32[]{:S(2)}) async-start(bf16[4,1536,384]{2,1,0:T(8,128)(2,1)} %shard_map.327), calls=%async_computation.5 | async-start | bytes 9437184 | tf_op jit(solution)/shard_map/all_to_all | solution.py:1077
  599.4 27.1 %shard_map.329 = (f32[32,8,1536]{2,1,0:T(8,128)}, f32[16,1536]{1,0:T(8,128)}, f32[1,1536]{1,0:T(1,128)}, f32[48,1536]{1,0:T(8,128)}, bf16[256,80]{1,0:T(8,128)(2,1)}) custom-call(f32[32,8,1536]{2,1,0:T(8,128)} %get-tuple-element.131.size_ref, bf16[256,1536]{1,0:T(8,128)(2,1)} %get-tuple-element.132.act_ref, f32[32,8,1536]{2,1,0:T(8,128)} %get-tuple-element.201.grad_ref, ...), custom_call_target="tpu_custom_call" | custom-call | flops 5249999872 | bytes 10000 | tf_op jit(solution)/shard_map/pallas_call | solution.py:90
  626.5 13.3 %shard_map.330 = (bf16[256,3072]{1,0:T(8,128)(2,1)}, f32[3,1536]{1,0:T(4,128)}, f32[3,1536]{1,0:T(4,128)}, bf16[1536,256]{1,0:T(8,128)(2,1)}) custom-call(f32[32,8,1536]{2,1,0:T(8,128)} %get-tuple-element.212.grad_act_ref, bf16[256,80]{1,0:T(8,128)(2,1)} %get-tuple-element.213.grad_selection_ref, ...), custom_call_target="tpu_custom_call", output_to_operand_aliasing={{0}: (13, {})} | custom-call | flops 1500000000 | bytes 10000 | tf_op jit(solution)/shard_map/pallas_call | solution.py:90
  643.0 9.0 %collective-permute-done.3 = f32[3,1536]{1,0:T(4,128)S(1)} collective-permute-done((f32[3,1536]{1,0:T(4,128)}, f32[3,1536]{1,0:T(4,128)S(1)}, u32[]{:S(2)}, u32[]{:S(2)}) %collective-permute-start.3) | collective-permute-done | bytes 18464 | tf_op jit(solution)/shard_map/ppermute | solution.py:58
  652.7 17.2 %shard_map.331 = (bf16[32,160,768]{2,1,0:T(8,128)(2,1)}, f32[256,768]{1,0:T(8,128)}) custom-call(bf16[256,3072]{1,0:T(8,128)(2,1)} %get-tuple-element.219.grad_ref, bf16[2,768,3072]{2,1,0:T(8,128)(2,1)} %weight_ref.3, f32[3,1536]{1,0:T(4,128)} %get-tuple-element.220.edge_ref, f32[3,1536]{1,0:T(4,128)} %broadcast_multiply_fusion.handed_ref, ...), custom_call_target="tpu_custom_call" | custom-call | flops 1350000000 | bytes 10000 | tf_op jit(solution)/shard_map/pallas_call | solution.py:90
  669.9 2.3 copy.70
  672.2 43.7 %shard_map.332.refs_0_ = f32[160,768]{1,0:T(8,128)} custom-call(bf16[8,2,2,160,768]{4,3,2,1,0:T(8,128)(2,1)} %bitcast.144), custom_call_target="tpu_custom_call" | custom-call | flops 8999999488 | bytes 10000 | tf_op jit(solution)/shard_map/pallas_call | solution.py:1383
  715.9 11.8 %shard_map.334 = (f32[2,4,768,384]{3,2,1,0:T(8,128)}, f32[2,4,384,768]{3,2,1,0:T(8,128)}) custom-call(bf16[4,1536,384]{2,1,0:T(8,128)(2,1)} %all-to-all-done.4.refs_0_, bf16[4,1536,384]{2,1,0:T(8,128)(2,1)} %all-to-all-done.5.refs_1_), custom_call_target="tpu_custom_call" | custom-call | flops 1350000000 | bytes 10000 | tf_op jit(solution)/shard_map/pallas_call | solution.py:90
  727.7 2.1 shard_map.333
  (205 shorter events, 43.5 us)
Async XLA Ops:
  9.3 10.7 %collective-permute-start = (bf16[3,768]{1,0:T(4,128)(2,1)S(1)}, bf16[3,768]{1,0:T(4,128)(2,1)S(1)}, u32[]{:S(2)}, u32[]{:S(2)}) collective-permute-start(bf16[3,768]{1,0:T(4,128)(2,1)S(1)} %bitcast_multiply_fusion.4), channel_id=1, source_target_pairs={{0,4},{4,8},{8,12},{12,16},{16,20},{20,24},{24,28},{1,5},{5,9},{9,... | collective-permute-start | bytes 13832 | tf_op jit(solution)/shard_map/ppermute | solution.py:58
  17.6 6.3 copy-start.15
  19.4 9.9 %copy-start.39 = (s32[256]{0:T(256)}, s32[256]{0:T(256)S(1)}, u32[]{:S(2)}) copy-start(s32[256]{0:T(256)S(1)} %reshape.423) | copy-start | bytes 3076
  19.6 85.5 %copy-start.22 = (s32[256]{0:T(256)}, s32[256]{0:T(256)S(1)}, u32[]{:S(2)}) copy-start(s32[256]{0:T(256)S(1)} %reshape.421) | copy-start | bytes 3076
  19.8 85.1 %copy-start.26 = (s32[256]{0:T(256)}, s32[256]{0:T(256)S(1)}, u32[]{:S(2)}) copy-start(s32[256]{0:T(256)S(1)} %reshape.422) | copy-start | bytes 3076
  19.9 9.4 %copy-start.29 = (s32[256]{0:T(256)}, s32[256]{0:T(256)S(1)}, u32[]{:S(2)}) copy-start(s32[256]{0:T(256)S(1)} %reshape.424) | copy-start | bytes 3076
  20.0 49.2 %all-to-all-start = ((bf16[4,768,384]{2,1,0:T(8,128)(2,1)}), bf16[4,768,384]{2,1,0:T(8,128)(2,1)S(1)}, u32[]{:S(2)}, u32[]{:S(2)}) async-start(bf16[4,768,384]{2,1,0:T(8,128)(2,1)} %shard_map.306), calls=%async_computation | async-start | bytes 4718592 | tf_op jit(solution)/shard_map/all_to_all | solution.py:1077
  69.1 6.7 copy-start.19
  69.1 7.3 copy-start.33
  69.1 7.9 %copy-start.17 = (bf16[2,768,16]{1,2,0:T(8,128)(2,1)S(1)}, bf16[2,768,16]{1,2,0:T(8,128)(2,1)}, u32[]{:S(2)}) copy-start(bf16[2,768,16]{1,2,0:T(8,128)(2,1)} %param.34) | copy-start | bytes 147460
  69.2 8.8 %copy-start.9 = (bf16[4,768,384]{2,1,0:T(8,128)(2,1)}, bf16[4,768,384]{2,1,0:T(8,128)(2,1)S(1)}, u32[]{:S(2)}) copy-start(bf16[4,768,384]{2,1,0:T(8,128)(2,1)S(1)} %all-to-all-done.refs_2_) | copy-start | bytes 7077892
  69.2 30.0 %all-to-all-start.1 = ((bf16[4,384,768]{2,1,0:T(8,128)(2,1)}), bf16[4,384,768]{2,1,0:T(8,128)(2,1)}, u32[]{:S(2)}, u32[]{:S(2)}) async-start(bf16[4,384,768]{2,1,0:T(8,128)(2,1)} %shard_map.308), calls=%async_computation.1 | async-start | bytes 4718592 | tf_op jit(solution)/shard_map/all_to_all | solution.py:1077
  98.9 5.7 copy-start.10
  99.1 120.2 %all-to-all-start.2 = ((bf16[4,768,384]{2,1,0:T(8,128)(2,1)}), bf16[4,768,384]{2,1,0:T(8,128)(2,1)}, u32[]{:S(2)}, u32[]{:S(2)}) async-start(bf16[4,768,384]{2,1,0:T(8,128)(2,1)} %shard_map.311), calls=%async_computation.2 | async-start | bytes 4718592 | tf_op jit(solution)/shard_map/all_to_all | solution.py:1077
  105.7 70.9 %copy-start.35 = (f32[256]{0:T(256)}, f32[256]{0:T(256)S(1)}, u32[]{:S(2)}) copy-start(f32[256]{0:T(256)S(1)} %broadcast_select_fusion.1) | copy-start | bytes 3076
  105.7 70.9 %copy-start.3 = (f32[256,768]{1,0:T(8,128)S(1)}, f32[256,768]{1,0:T(8,128)}, u32[]{:S(2)}) copy-start(f32[256,768]{1,0:T(8,128)} %get-tuple-element.143) | copy-start | bytes 2359300
  105.7 70.9 %copy-start.6 = (bf16[320,256]{1,0:T(8,128)(2,1)S(1)}, bf16[320,256]{1,0:T(8,128)(2,1)}, u32[]{:S(2)}) copy-start(bf16[320,256]{1,0:T(8,128)(2,1)} %fusion.23.fill_ref) | copy-start | bytes 491524
  179.6 4.2 copy-start.1
  179.7 4.1 copy-start.43
  183.8 6.9 copy-start
  184.6 6.0 collective-permute-start.1
  219.3 5.2 copy-start.16
  219.3 32.0 %all-to-all-start.3 = ((bf16[4,384,768]{2,1,0:T(8,128)(2,1)}), bf16[4,384,768]{2,1,0:T(8,128)(2,1)}, u32[]{:S(2)}, u32[]{:S(2)}) async-start(bf16[4,384,768]{2,1,0:T(8,128)(2,1)} %shard_map.314), calls=%async_computation.3 | async-start | bytes 4718592 | tf_op jit(solution)/shard_map/all_to_all | solution.py:1077
  224.6 20.5 %copy-start.30 = (s32[256]{0:T(256)S(1)}, s32[256]{0:T(256)}, u32[]{:S(2)}) copy-start(s32[256]{0:T(256)} %copy-done.29) | copy-start | bytes 3076
  251.3 53.0 %copy-start.7 = (bf16[320,256]{1,0:T(8,128)(2,1)S(1)}, bf16[320,256]{1,0:T(8,128)(2,1)}, u32[]{:S(2)}) copy-start(bf16[320,256]{1,0:T(8,128)(2,1)} %fusion.24.fill_ref) | copy-start | bytes 491524
  251.3 54.9 %copy-start.40 = (s32[256]{0:T(256)S(1)}, s32[256]{0:T(256)}, u32[]{:S(2)}) copy-start(s32[256]{0:T(256)} %copy-done.39) | copy-start | bytes 3076
  308.9 55.3 %copy-start.2 = (f32[256,768]{1,0:T(8,128)S(1)}, f32[256,768]{1,0:T(8,128)}, u32[]{:S(2)}) copy-start(f32[256,768]{1,0:T(8,128)} %get-tuple-element.162) | copy-start | bytes 2359300
  405.7 5.1 copy-start.21
  405.7 184.2 %all-to-all-start.5 = ((bf16[4,1536,384]{2,1,0:T(8,128)(2,1)}), bf16[4,1536,384]{2,1,0:T(8,128)(2,1)}, u32[]{:S(2)}, u32[]{:S(2)}) async-start(bf16[4,1536,384]{2,1,0:T(8,128)(2,1)} %shard_map.320), calls=%async_computation.6 | async-start | bytes 9437184 | tf_op jit(solution)/shard_map/all_to_all | solution.py:1077
  410.7 316.9 %reduce-scatter.2.cloned.1.call-start = ((), (), s32[]{:S(2)}) async-start(), calls=%async_computation.7 | async-start | bytes 8110080 | tf_op jit(solution)/shard_map/reduce_scatter | solution.py:1705
  438.5 14.5 %copy-start.51 = (bf16[256,768]{1,0:T(8,128)(2,1)S(1)}, bf16[256,768]{1,0:T(8,128)(2,1)}, u32[]{:S(2)}) copy-start(bf16[256,768]{1,0:T(8,128)(2,1)} %get-tuple-element.195) | copy-start | bytes 1179652
  438.5 26.1 %copy-start.44 = (f32[3]{0:T(128)S(1)}, f32[3]{0:T(128)}, u32[]{:S(2)}) copy-start(f32[3]{0:T(128)} %pad_maximum_fusion) | copy-start | bytes 40
  451.8 12.9 %collective-permute-start.2 = (f32[3,1536]{1,0:T(4,128)}, f32[3,1536]{1,0:T(4,128)S(1)}, u32[]{:S(2)}, u32[]{:S(2)}) collective-permute-start(f32[3,1536]{1,0:T(4,128)} %get-tuple-element.192), channel_id=1, source_target_pairs={{4,0},{8,4},{12,8},{16,12},{20,16},{24,20},{28,24},{5,1},{9,5},{13... | collective-permute-start | bytes 55304 | tf_op jit(solution)/shard_map/ppermute | solution.py:58
  541.3 8.4 %copy-start.8 = (f32[256,768]{1,0:T(8,128)S(1)}, f32[256,768]{1,0:T(8,128)}, u32[]{:S(2)}) copy-start(f32[256,768]{1,0:T(8,128)} %get-tuple-element.274) | copy-start | bytes 2359300
  541.3 8.6 %copy-start.23 = (s32[256]{0:T(256)S(1)}, s32[256]{0:T(256)}, u32[]{:S(2)}) copy-start(s32[256]{0:T(256)} %copy-done.22) | copy-start | bytes 3076
  541.3 8.6 %copy-start.38 = (f32[256]{0:T(256)S(1)}, f32[256]{0:T(256)}, u32[]{:S(2)}) copy-start(f32[256]{0:T(256)} %copy-done.37) | copy-start | bytes 3076
  541.3 8.6 %copy-start.25 = (f32[256]{0:T(256)S(1)}, f32[256]{0:T(256)}, u32[]{:S(2)}) copy-start(f32[256]{0:T(256)} %copy-done.24) | copy-start | bytes 3076
  541.3 8.6 %copy-start.27 = (s32[256]{0:T(256)S(1)}, s32[256]{0:T(256)}, u32[]{:S(2)}) copy-start(s32[256]{0:T(256)} %copy-done.26) | copy-start | bytes 3076
  541.3 9.9 %copy-start.4 = (f32[256,768]{1,0:T(8,128)S(1)}, f32[256,768]{1,0:T(8,128)}, u32[]{:S(2)}) copy-start(f32[256,768]{1,0:T(8,128)} %get-tuple-element.143) | copy-start | bytes 2359300
  589.8 8.8 %copy-start.13 = (bf16[8,32,768]{2,0,1:T(8,128)(2,1)S(1)}, bf16[8,32,768]{2,0,1:T(8,128)(2,1)}, u32[]{:S(2)}) copy-start(bf16[8,32,768]{2,0,1:T(8,128)(2,1)} %get-tuple-element.263) | copy-start | bytes 1179652
  589.8 126.1 %all-to-all-start.4 = ((bf16[4,1536,384]{2,1,0:T(8,128)(2,1)}), bf16[4,1536,384]{2,1,0:T(8,128)(2,1)}, u32[]{:S(2)}, u32[]{:S(2)}) async-start(bf16[4,1536,384]{2,1,0:T(8,128)(2,1)} %shard_map.327), calls=%async_computation.5 | async-start | bytes 9437184 | tf_op jit(solution)/shard_map/all_to_all | solution.py:1077
  626.4 14.7 %copy-start.11 = (f32[256,16]{1,0:T(8,128)S(1)}, f32[256,16]{1,0:T(8,128)}, u32[]{:S(2)}) copy-start(f32[256,16]{1,0:T(8,128)} %get-tuple-element.144) | copy-start | bytes 49156
  626.5 14.7 %copy-start.28 = (s32[256]{0:T(256)S(1)}, s32[256]{0:T(256)}, u32[]{:S(2)}) copy-start(s32[256]{0:T(256)} %copy-done.26) | copy-start | bytes 3076
  626.5 14.7 %copy-start.42 = (f32[256]{0:T(256)S(1)}, f32[256]{0:T(256)}, u32[]{:S(2)}) copy-start(f32[256]{0:T(256)} %copy-done.41) | copy-start | bytes 3076
  626.5 14.7 %copy-start.49 = (f32[256]{0:T(256)S(1)}, f32[256]{0:T(256)}, u32[]{:S(2)}) copy-start(f32[256]{0:T(256)} %copy-done.48) | copy-start | bytes 3076
  626.5 14.7 %copy-start.50 = (bf16[256,768]{1,0:T(8,128)(2,1)S(1)}, bf16[256,768]{1,0:T(8,128)(2,1)}, u32[]{:S(2)}) copy-start(bf16[256,768]{1,0:T(8,128)(2,1)} %get-tuple-element.224) | copy-start | bytes 1179652
  626.5 25.5 %copy-start.45 = (f32[3]{0:T(128)S(1)}, f32[3]{0:T(128)}, u32[]{:S(2)}) copy-start(f32[3]{0:T(128)} %pad_maximum_fusion) | copy-start | bytes 40
  639.8 12.2 %collective-permute-start.3 = (f32[3,1536]{1,0:T(4,128)}, f32[3,1536]{1,0:T(4,128)S(1)}, u32[]{:S(2)}, u32[]{:S(2)}) collective-permute-start(f32[3,1536]{1,0:T(4,128)} %get-tuple-element.221), channel_id=1, source_target_pairs={{4,0},{8,4},{12,8},{16,12},{20,16},{24,20},{28,24},{5,1},{9,5},{13... | collective-permute-start | bytes 55304 | tf_op jit(solution)/shard_map/ppermute | solution.py:58
  (15 other events, 32.1 us)
Sparse Core Ops, SparseCore 0:
  482.7 141.6 reduce-scatter.1

commit v4 on v3

--- a/solution.py
+++ b/solution.py
@@ -58,28 +58,79 @@
     return lax.ppermute(x, "wide", [(i, i + by) for i in range(size) if 0 <= i + by < size])
 
 
-def with_rim(values, rim):
-    count = rim.shape[0]
-    tail = values[values.shape[0] - count :, : CHUNKS - 1]
-    return jnp.concatenate([jnp.concatenate([rim[:, None], tail], axis=1), values], axis=0)
-
-
-def keep_masks(starts, taps):
-    extended = with_rim(starts[..., None], jnp.zeros((taps - 1, 1), jnp.float32))
-    steps = starts.shape[0]
-    alive = jnp.ones(starts.shape + (1,), jnp.float32)
-    masks = []
-    for offset in range(1, taps):
-        back = taps - offset
-        alive = alive * (1.0 - extended[back : back + steps])
-        masks.append(alive)
-    return jnp.broadcast_to(jnp.stack(masks), (taps - 1,) + starts.shape + (LANES,))
-
-
-def rim_keep(starts, count):
-    tail = 1.0 - starts[starts.shape[0] - count :, CHUNKS - 1]
+def tables_kernel(dims, doc_ref, choice_ref, slot_ref, reset_ref, mask_ref, *outs):
+    layers, taps, per_group, block, capacity = dims
+    tokens = doc_ref.shape[1]
+    steps = tokens // CHUNKS
+    f32, low = jnp.float32, jnp.bfloat16
+    fills, onehots, keeps = outs[:layers], outs[layers : 2 * layers], outs[2 * layers :]
+    rows = [doc_ref[...]] + [choice_ref[l] for l in range(layers)] + [slot_ref[l] for l in range(layers)]
+    rows = jnp.concatenate([row.astype(f32) for row in rows], axis=0)
+    rows = jnp.concatenate([rows, jnp.zeros((CHUNKS - rows.shape[0], tokens), f32)], axis=0).astype(low)
+    place = lax.broadcasted_iota(jnp.int32, (tokens, tokens), 1)
+    token = (place & (CHUNKS - 1)) * steps + lax.shift_right_logical(place, 3)
+    order = (lax.broadcasted_iota(jnp.int32, (tokens, tokens), 0) == token).astype(f32).astype(low)
+    along = dot_nn(rows, order)
+    down = lax.dot_general(order, rows, (((0,), (1,)), ((), ())), preferred_element_type=f32)
+
+    starts = jnp.broadcast_to(down[:, 0:1], (tokens, LANES)).reshape(steps, CHUNKS, LANES)
+    reset_ref[...] = starts * RESET
+    chunk = lax.broadcasted_iota(jnp.int32, (CHUNKS, LANES), 0)
+    mask_ref[0] = 1.0 - starts
+    for offset in range(2, taps):
+        mask_ref[offset - 1, offset - 1 :] = mask_ref[offset - 2, offset - 1 :] * (
+            1.0 - starts[: steps - offset + 1])
+        for i in range(offset - 1):
+            before = jnp.where(chunk == 0, 0.0, pltpu.roll(starts[steps - offset + 1 + i], 1, axis=0))
+            mask_ref[offset - 1, i] = mask_ref[offset - 2, i] * (1.0 - before)
+
+    for l in range(layers):
+        chosen, slot = along[1 + l : 2 + l], along[1 + layers + l : 2 + layers + l]
+        group = jnp.floor((chosen + 0.5) * (1.0 / per_group))
+        spot = group * block + (chosen - group * per_group) * capacity + slot
+        spot = jnp.where(slot >= 0.0, spot, -1.0).astype(jnp.int32)
+        fills[l][...] = (
+            lax.broadcasted_iota(jnp.int32, fills[l].shape, 0) == spot).astype(f32).astype(low)
+        picked = down[:, 1 + l : 2 + l].astype(jnp.int32)
+        onehots[l][...] = (lax.broadcasted_iota(jnp.int32, onehots[l].shape, 1) == picked).astype(f32)
+        keeps[l][...] = jnp.where(down[:, 1 + layers + l : 2 + layers + l] >= 0.0, 1.0, 0.0)
+
+
+def tables(doc_start, expert_choice, slot_index, taps, experts, groups, block, capacity):
+    layers = expert_choice.shape[0]
+    tokens = doc_start.shape[1]
+    steps = tokens // CHUNKS
+    f32 = jnp.float32
+    shapes = [shaped((steps, CHUNKS, LANES)), shaped((taps - 1, steps, CHUNKS, LANES))]
+    shapes += [shaped((groups * block, tokens), jnp.bfloat16)] * layers
+    shapes += [shaped((tokens, experts))] * layers + [shaped((tokens, 1))] * layers
+    inside = pl.BlockSpec(memory_space=VMEM)
+    reset, masks, *rest = pl.pallas_call(
+        functools.partial(tables_kernel, (layers, taps, experts // groups, block, capacity)),
+        out_shape=shapes,
+        in_specs=[inside] * 3,
+        out_specs=[inside] * len(shapes),
+        compiler_params=pltpu.CompilerParams(vmem_limit_bytes=60 * MIB),
+        cost_estimate=microseconds(3),
+    )(doc_start, expert_choice, slot_index)
+    return reset, masks, rest[:layers], rest[layers : 2 * layers], rest[2 * layers :]
+
+
+def rim_keep(doc_start, count):
+    tail = 1.0 - doc_start[doc_start.shape[0] - count :].astype(jnp.float32)
     later = jnp.cumprod(tail[::-1])[::-1]
     return jnp.concatenate([later[1:], jnp.ones((1,), jnp.float32)])
+
+
+TILE = 2 * LANES
+
+
+def each_part(body):
+    def one(at, carry):
+        body(pl.ds(pl.multiple_of(at * LANES, LANES), LANES))
+        return carry
+
+    lax.fori_loop(0, TILE // LANES, one, 0)
 
 
 def microseconds(count):
@@ -107,19 +158,19 @@
 
 
 def slab(steps, first=0):
-    return pl.BlockSpec((steps, CHUNKS, LANES), lambda c: (0, 0, first + c))
+    return pl.BlockSpec((steps, CHUNKS, TILE), lambda c: (0, 0, first + c))
 
 
 def rows_of(count):
-    return pl.BlockSpec((count, LANES), lambda c: (0, c))
+    return pl.BlockSpec((count, TILE), lambda c: (0, c))
 
 
 def layer_rows(layer, count):
-    return pl.BlockSpec((None, count, LANES), lambda c: (layer, 0, c))
+    return pl.BlockSpec((None, count, TILE), lambda c: (layer, 0, c))
 
 
 def layer_columns(layer, count):
-    return pl.BlockSpec((None, LANES, count), lambda c: (layer, c, 0))
+    return pl.BlockSpec((None, TILE, count), lambda c: (layer, c, 0))
 
 
 def layer_whole(layer, shape):
@@ -295,7 +346,7 @@
 def run_kernel(dims, size_ref, act_ref, selection_ref, reset_ref, decay_ref, link_ref, link_size_ref,
                entering_ref, gate_ref, skip_ref, out_weight_ref, current_ref, norm_ref, router_ref, fill_ref,
                mixed_ref, gated_ref, begin_ref, middle_ref, routed_ref, logits_ref, outbound_ref,
-               in_maps, out_maps, sized, pushed):
+               in_maps, out_maps, pushed):
     rank, states, steps, tiles = dims
 
     @pl.when(pl.program_id(0) == 0)
@@ -304,37 +355,38 @@
         spread_columns(selection_ref, rank + states, states, out_maps)
         middle_ref[...] = current_ref[...]
 
-    rates = rate_rows(rates_of(decay_ref[...]))
-    link_size = link_size_ref[...]
-    skip = skip_ref[...]
-    begin = []
-    for n in range(states):
-        first = link_ref[n] + jnp.exp2(link_size * rates[n]) * entering_ref[n : n + 1, :]
-        begin_ref[n] = first
-        begin.append(first)
-
     size = size_ref[...]
     act = act_ref[...].astype(jnp.float32).reshape(size.shape)
     pushed[...] = size * act
-    sized[...] = size + reset_ref[...]
-
-    def one(step, carry):
-        size, value = sized[step], pushed[step]
-        new = []
-        sums = [None, None]
+
+    def scan(lanes):
+        rates = rate_rows(rates_of(decay_ref[:, lanes]))
+        link_size = link_size_ref[:, lanes]
+        begin = []
         for n in range(states):
-            level = jnp.exp2(size * rates[n]) * carry[n] + value * in_maps[step, n]
-            new.append(level)
-            term = out_maps[step, n] * level
-            sums[n % 2] = term if sums[n % 2] is None else sums[n % 2] + term
-        mixed_ref[step] = sums[0] + sums[1]
-        return tuple(new)
-
-    lax.fori_loop(0, steps, one, tuple(begin), unroll=4)
-    mixed = mixed_ref[...] + skip * act
+            first = link_ref[n, :, lanes] + jnp.exp2(link_size * rates[n]) * entering_ref[n : n + 1, lanes]
+            begin_ref[n, :, lanes] = first
+            begin.append(first)
+
+        def one(step, carry):
+            size, value = size_ref[step, :, lanes] + reset_ref[step], pushed[step, :, lanes]
+            new = []
+            sums = [None, None]
+            for n in range(states):
+                level = jnp.exp2(size * rates[n]) * carry[n] + value * in_maps[step, n]
+                new.append(level)
+                term = out_maps[step, n] * level
+                sums[n % 2] = term if sums[n % 2] is None else sums[n % 2] + term
+            mixed_ref[step, :, lanes] = sums[0] + sums[1]
+            return tuple(new)
+
+        lax.fori_loop(0, steps, one, tuple(begin), unroll=4)
+
+    each_part(scan)
+    mixed = mixed_ref[...] + skip_ref[...] * act
     mixed_ref[...] = mixed
     gated = mixed * jax.nn.silu(gate_ref[...])
-    gated_ref[...] = gated.reshape(steps * CHUNKS, LANES).astype(jnp.bfloat16)
+    gated_ref[...] = gated.reshape(steps * CHUNKS, TILE).astype(jnp.bfloat16)
     middle_ref[...] += dot_nn(gated_ref[...], out_weight_ref[...])
 
     @pl.when(pl.program_id(0) == tiles - 1)
@@ -351,7 +403,7 @@
     tokens = steps * CHUNKS
     states, width, experts = decay_log.shape[1], current.shape[1], router.shape[2]
     rank = selection.shape[2] - 2 * states
-    tiles = channels // LANES
+    tiles = channels // TILE
     low = jnp.bfloat16
     maps = VMEM((steps, states, CHUNKS, LANES), jnp.float32)
     return plain_call(
@@ -372,7 +424,7 @@
             shaped((tokens, experts)),
             shaped((fill.shape[0], width), low),
         ],
-        [maps, maps] + [VMEM((steps, CHUNKS, LANES), jnp.float32)] * 2,
+        [maps, maps, VMEM((steps, CHUNKS, TILE), jnp.float32)],
         (size, act, selection, reset, decay_log, link, link_size, entering, projected, skip_weight, out_weight,
          current, norm_expert, router, fill),
         22,
@@ -382,7 +434,7 @@
 def turn_kernel(dims, grad_ref, out_weight_ref, gate_ref, mixed_ref, act_ref, gated_ref, size_ref,
                 selection_ref, reset_ref, decay_ref,
                 grad_y_ref, grad_gate_ref, grad_skip_ref, grad_out_ref, link_ref, link_size_ref, total_ref,
-                total_size_ref, maps, sized):
+                total_size_ref, maps):
     rank, states, steps = dims
 
     @pl.when(pl.program_id(0) == 0)
@@ -391,34 +443,37 @@
 
     grad = grad_ref[...]
     grad_out_ref[...] = dot_tn(gated_ref[...], grad).astype(jnp.bfloat16)
-    gated = dot_nt(grad, out_weight_ref[...]).reshape(steps, CHUNKS, LANES)
+    gated = dot_nt(grad, out_weight_ref[...]).reshape(steps, CHUNKS, TILE)
     gate = gate_ref[...]
     share = jax.nn.sigmoid(gate)
     grad_y = gated * (gate * share)
     grad_y_ref[...] = grad_y
     grad_gate = gated * mixed_ref[...] * (share * (1.0 + gate * (1.0 - share)))
-    grad_gate_ref[...] = grad_gate.reshape(steps * CHUNKS, LANES).astype(jnp.bfloat16)
-    by_skip = grad_y * act_ref[...].astype(jnp.float32).reshape(steps, CHUNKS, LANES)
+    grad_gate_ref[...] = grad_gate.reshape(steps * CHUNKS, TILE).astype(jnp.bfloat16)
+    by_skip = grad_y * act_ref[...].astype(jnp.float32).reshape(steps, CHUNKS, TILE)
     grad_skip_ref[...] = jnp.sum(jnp.sum(by_skip, axis=0), axis=0, keepdims=True)
-    sized[...] = size_ref[...] + reset_ref[...]
-    rates = rate_rows(rates_of(decay_ref[...]))
-
-    def one(at, carry):
-        step = steps - 1 - at
-        size, grad_y = sized[step], grad_y_ref[step]
-        new = []
+
+    def scan(lanes):
+        rates = rate_rows(rates_of(decay_ref[:, lanes]))
+
+        def one(at, carry):
+            step = steps - 1 - at
+            size, grad_y = size_ref[step, :, lanes] + reset_ref[step], grad_y_ref[step, :, lanes]
+            new = []
+            for n in range(states):
+                new.append(jnp.exp2(size * rates[n]) * (carry[n] + grad_y * maps[step, n]))
+            return tuple(new) + (carry[states] + size,)
+
+        zero = jnp.zeros((CHUNKS, LANES), jnp.float32)
+        found = lax.fori_loop(0, steps, one, (zero,) * (states + 1), unroll=4)
+        links, totals, link_size, total_size = chunk_links(found, found[states], rates, True)
+        link_size_ref[:, lanes] = link_size
+        total_size_ref[:, lanes] = total_size
         for n in range(states):
-            new.append(jnp.exp2(size * rates[n]) * (carry[n] + grad_y * maps[step, n]))
-        return tuple(new) + (carry[states] + size,)
-
-    zero = jnp.zeros((CHUNKS, LANES), jnp.float32)
-    found = lax.fori_loop(0, steps, one, (zero,) * (states + 1), unroll=4)
-    links, totals, link_size, total_size = chunk_links(found, found[states], rates, True)
-    link_size_ref[...] = link_size
-    total_size_ref[...] = total_size
-    for n in range(states):
-        link_ref[n] = links[n]
-        total_ref[n : n + 1, :] = totals[n]
+            link_ref[n, :, lanes] = links[n]
+            total_ref[n : n + 1, lanes] = totals[n]
+
+    each_part(scan)
 
 
 def mixer_turn(layer, grad_low, out_weight, projected, mixed, act, gated, size, selection, reset, decay_log):
@@ -426,15 +481,15 @@
     tokens = steps * CHUNKS
     states, width = decay_log.shape[1], grad_low.shape[1]
     rank = selection.shape[2] - 2 * states
-    tiles = channels // LANES
+    tiles = channels // TILE
     low = jnp.bfloat16
     return plain_call(
         functools.partial(turn_kernel, (rank, states, steps)),
         (tiles,),
         [whole(grad_low.shape), layer_columns(layer, width), slab(steps, tiles), slab(steps), rows_of(tokens),
          rows_of(tokens), slab(steps), whole(selection.shape), whole(reset.shape), layer_rows(layer, states)],
-        [slab(steps), pl.BlockSpec((tokens, LANES), lambda c: (0, tiles + c)), rows_of(1),
-         pl.BlockSpec((LANES, width), lambda c: (c, 0)),
+        [slab(steps), pl.BlockSpec((tokens, TILE), lambda c: (0, tiles + c)), rows_of(1),
+         pl.BlockSpec((TILE, width), lambda c: (c, 0)),
          slab(states), rows_of(CHUNKS), rows_of(states), rows_of(1)],
         [
             shaped((steps, CHUNKS, channels)),
@@ -446,7 +501,7 @@
             shaped((states, channels)),
             shaped((1, channels)),
         ],
-        [VMEM((steps, states, CHUNKS, LANES), jnp.float32), VMEM((steps, CHUNKS, LANES), jnp.float32)],
+        [VMEM((steps, states, CHUNKS, LANES), jnp.float32)],
         (grad_low, out_weight, projected, mixed, act, gated, size, selection, reset, decay_log),
         14,
     )
@@ -455,7 +510,7 @@
 def back_kernel(dims, size_ref, act_ref, grad_ref, decay_ref, selection_ref, reset_ref, begin_ref, link_ref,
                 link_size_ref, entering_ref, step_ref, step_bias_ref, skip_ref,
                 grad_act_ref, grad_decay_ref, grad_bias_ref, grad_step_ref, grad_selection_ref,
-                in_maps, out_maps, levels, decays, grad_in, grad_out, grad_size, grad_rate, grad_all, sized, pushed, acted):
+                in_maps, out_maps, levels, decays, grad_in, grad_out, grad_size, grad_rate, grad_all, pushed, acted):
     rank, states, steps, tiles = dims
     tokens = steps * CHUNKS
 
@@ -466,66 +521,71 @@
         grad_in[...] = jnp.zeros_like(grad_in)
         grad_out[...] = jnp.zeros_like(grad_out)
 
-    true_rates = -jnp.exp(decay_ref[...])
-    rates = rate_rows(true_rates * LOG2E)
     skip = skip_ref[...]
-    begin = []
-    for n in range(states):
-        levels[0, n] = begin_ref[n]
-        begin.append(begin_ref[n])
-
     size = size_ref[...]
     act = act_ref[...].astype(jnp.float32).reshape(size.shape)
     acted[...] = act
     pushed[...] = size * act
-    sized[...] = size + reset_ref[...]
-
-    def ahead(step, carry):
-        size, value = sized[step], pushed[step]
-        new = []
+
+    def scan(lanes):
+        true_rates = -jnp.exp(decay_ref[:, lanes])
+        rates = rate_rows(true_rates * LOG2E)
+        begin = []
         for n in range(states):
-            decay = jnp.exp2(size * rates[n])
-            decays[step, n] = decay
-            level = decay * carry[n] + value * in_maps[step, n]
-            levels[step + 1, n] = level
-            new.append(level)
-        return tuple(new)
-
-    lax.fori_loop(0, steps, ahead, tuple(begin), unroll=4)
-    link_size = link_size_ref[...]
-    tail = []
-    for n in range(states):
-        tail.append(link_ref[n] + jnp.exp2(link_size * rates[n]) * entering_ref[n : n + 1, :])
-        grad_rate[n] = jnp.zeros((CHUNKS, LANES), jnp.float32)
-
-    def retreat(at, carry):
-        step = steps - 1 - at
-        plain, act, grad, value = size_ref[step], acted[step], grad_ref[step], pushed[step]
-        by_rate = jnp.zeros((CHUNKS, LANES), jnp.float32)
-        by_input = jnp.zeros((CHUNKS, LANES), jnp.float32)
-        new = []
+            levels[0, n] = begin_ref[n, :, lanes]
+            begin.append(begin_ref[n, :, lanes])
+
+        def ahead(step, carry):
+            size, value = size_ref[step, :, lanes] + reset_ref[step], pushed[step, :, lanes]
+            new = []
+            for n in range(states):
+                decay = jnp.exp2(size * rates[n])
+                decays[step, n] = decay
+                level = decay * carry[n] + value * in_maps[step, n]
+                levels[step + 1, n] = level
+                new.append(level)
+            return tuple(new)
+
+        lax.fori_loop(0, steps, ahead, tuple(begin), unroll=4)
+        link_size = link_size_ref[:, lanes]
+        tail = []
         for n in range(states):
-            lanes = slice(n * LANES, (n + 1) * LANES)
-            back = out_maps[step, n] * grad + carry[n]
-            grad_out[step, :, lanes] += grad * levels[step + 1, n]
-            grad_in[step, :, lanes] += back * value
-            by_input = by_input + back * in_maps[step, n]
-            passed = decays[step, n] * back
-            new.append(passed)
-            pull = passed * levels[step, n]
-            by_rate = by_rate + pull * rates[n]
-            grad_rate[n] += pull * plain
-        grad_size[step] = by_rate * (1.0 / LOG2E) + act * by_input
-        grad_act_ref[step] = plain * by_input + grad * skip
-        return tuple(new)
-
-    lax.fori_loop(0, steps, retreat, tuple(tail), unroll=2)
-    for n in range(states):
-        grad_decay_ref[n : n + 1, :] = (
-            jnp.sum(grad_rate[n], axis=0, keepdims=True) * true_rates[n : n + 1, :]
-        )
+            tail.append(
+                link_ref[n, :, lanes] + jnp.exp2(link_size * rates[n]) * entering_ref[n : n + 1, lanes])
+            grad_rate[n] = jnp.zeros((CHUNKS, LANES), jnp.float32)
+
+        def retreat(at, carry):
+            step = steps - 1 - at
+            plain, act, grad, value = (
+                ref[step, :, lanes] for ref in (size_ref, acted, grad_ref, pushed))
+            by_rate = jnp.zeros((CHUNKS, LANES), jnp.float32)
+            by_input = jnp.zeros((CHUNKS, LANES), jnp.float32)
+            new = []
+            for n in range(states):
+                spot = slice(n * LANES, (n + 1) * LANES)
+                back = out_maps[step, n] * grad + carry[n]
+                grad_out[step, :, spot] += grad * levels[step + 1, n]
+                grad_in[step, :, spot] += back * value
+                by_input = by_input + back * in_maps[step, n]
+                passed = decays[step, n] * back
+                new.append(passed)
+                pull = passed * levels[step, n]
+                by_rate = by_rate + pull * rates[n]
+                grad_rate[n] += pull * plain
+            grad_size[step, :, lanes] = by_rate * (1.0 / LOG2E) + act * by_input
+            grad_act_ref[step, :, lanes] = plain * by_input
+            return tuple(new)
+
+        lax.fori_loop(0, steps, retreat, tuple(tail), unroll=2)
+        for n in range(states):
+            grad_decay_ref[n : n + 1, lanes] = (
+                jnp.sum(grad_rate[n], axis=0, keepdims=True) * true_rates[n : n + 1, :]
+            )
+
+    each_part(scan)
+    grad_act_ref[...] += grad_ref[...] * skip
     tile = pl.program_id(0)
-    grad_all[:, pl.ds(pl.multiple_of(tile * LANES, LANES), LANES)] = grad_size[...].reshape(tokens, LANES)
+    grad_all[:, pl.ds(pl.multiple_of(tile * TILE, TILE), TILE)] = grad_size[...].reshape(tokens, TILE)
 
     @pl.when(pl.program_id(0) == tiles - 1)
     def _():
@@ -557,7 +617,7 @@
     states = decay_log.shape[1]
     columns = selection.shape[2]
     rank = columns - 2 * states
-    tiles = channels // LANES
+    tiles = channels // TILE
     f32 = jnp.float32
     maps = VMEM((steps, states, CHUNKS, LANES), f32)
     return plain_call(
@@ -577,8 +637,8 @@
         ],
         [maps, maps, VMEM((steps + 1, states, CHUNKS, LANES), f32), maps,
          VMEM((steps, CHUNKS, states * LANES), f32), VMEM((steps, CHUNKS, states * LANES), f32),
-         VMEM((steps, CHUNKS, LANES), f32), VMEM((states, CHUNKS, LANES), f32), VMEM((tokens, channels), f32)]
-        + [VMEM((steps, CHUNKS, LANES), f32)] * 3,
+         VMEM((steps, CHUNKS, TILE), f32), VMEM((states, CHUNKS, LANES), f32), VMEM((tokens, channels), f32)]
+        + [VMEM((steps, CHUNKS, TILE), f32)] * 2,
         (size, act, grad_y, decay_log, selection, reset, begin, link, link_size, entering, step_weight,
          step_bias, skip_weight),
         35,
@@ -590,14 +650,17 @@
                      grad_skip_ref, half_ref, grad_value_ref, edge_ref, rim_grad_ref, channel_ref,
                      extended, passed):
     taps, states, steps = dims
-    tokens = steps * CHUNKS
+    lanes = grad_act_ref.shape[2]
     extend(value_ref, rim_ref, extended, taps)
     bias = conv_bias_ref[...]
     grad_selection = grad_selection_ref[...]
-    from_selection = dot_nt(grad_selection, state_ref[...]).reshape(steps, CHUNKS, LANES)
+    from_selection = dot_nt(grad_selection, state_ref[...]).reshape(steps, CHUNKS, lanes)
     passed[:steps] = grad_act_ref[...] + from_selection
-    passed[steps:] = jnp.zeros((taps - 1, CHUNKS, LANES), jnp.float32)
-    zero = jnp.zeros((CHUNKS, LANES), jnp.float32)
+    passed[steps:] = jnp.zeros((taps - 1, CHUNKS, lanes), jnp.float32)
+    zero = jnp.zeros((CHUNKS, lanes), jnp.float32)
+
+    def keep(offset, step):
+        return jnp.concatenate([mask_ref[offset - 1, step]] * (lanes // LANES), axis=1)
 
     def ahead(step, carry):
         convolved = conv_slab(extended, step, mask_ref, conv_ref, bias, taps)
@@ -606,11 +669,11 @@
         passed[step] = grad
         new = [carry[0] + grad, carry[1] + grad * extended[step + taps - 1]]
         for offset in range(1, taps):
-            kept = grad * mask_ref[offset - 1, step]
+            kept = grad * keep(offset, step)
             new.append(carry[offset + 1] + kept * extended[step + taps - 1 - offset])
         return tuple(new)
 
-    sums = lax.fori_loop(0, steps, ahead, (zero,) * (taps + 1), unroll=4)
+    sums = lax.fori_loop(0, steps, ahead, (zero,) * (taps + 1), unroll=2)
 
     def reach(step, last):
         total = zero
@@ -618,7 +681,7 @@
             at = step + offset
             part = conv_ref[offset : offset + 1, :] * passed[at]
             if offset:
-                part = part * mask_ref[offset - 1, at]
+                part = part * keep(offset, at)
             total = total + part
         return total
 
@@ -630,14 +693,14 @@
 
     safe = (steps - taps + 1) // 2
     lax.fori_loop(0, safe, back, 0, unroll=2)
-    place = lax.broadcasted_iota(jnp.int32, (CHUNKS, LANES), 0)
+    place = lax.broadcasted_iota(jnp.int32, (CHUNKS, lanes), 0)
     ends = {}
     for j in range(taps - 1):
         before = zero
         for offset in range(taps - 1 - j, taps):
             at = j - taps + 1 + offset
             before = before + conv_ref[offset : offset + 1, :] * (
-                passed[at] * mask_ref[offset - 1, at]
+                passed[at] * keep(offset, at)
             )
         rim_grad_ref[j : j + 1, :] = before[0:1]
         ends[steps - taps + 1 + j] = jnp.where(
@@ -655,7 +718,7 @@
         grad_value_ref[2 * pair * CHUNKS : (2 * pair + 2) * CHUNKS, :] = jnp.concatenate(
             both, axis=0
         ).astype(jnp.bfloat16)
-    small = jnp.zeros((CHUNKS, LANES), jnp.float32)
+    small = jnp.zeros((CHUNKS, lanes), jnp.float32)
     rows = [jnp.sum(part, axis=0, keepdims=True) for part in sums[1:] + sums[:1]]
     rows += [grad_bias_ref[...], grad_skip_ref[...]]
     for index, row in enumerate(rows):
@@ -663,7 +726,7 @@
     grad_state = dot_tn(grad_selection, act_ref[...])
     parts = [grad_state, grad_step_ref[...], grad_decay_ref[...], small]
     used = sum(part.shape[0] for part in parts)
-    parts.append(jnp.zeros((2 * LANES - used, LANES), jnp.float32))
+    parts.append(jnp.zeros((2 * LANES - used, lanes), jnp.float32))
     channel_ref[...] = jnp.concatenate(parts, axis=0).T.astype(jnp.bfloat16)
 
 
@@ -673,23 +736,34 @@
     tokens = steps * CHUNKS
     taps, columns = conv_weight.shape[1], state_weight.shape[2]
     states, rank = grad_decay.shape[0], grad_step.shape[0]
-    tiles = channels // LANES
+    lanes = 2 * LANES
     f32 = jnp.float32
+
+    def cubes(count):
+        return pl.BlockSpec((count, CHUNKS, lanes), lambda c: (0, 0, c))
+
+    def rows(count):
+        return pl.BlockSpec((count, lanes), lambda c: (0, c))
+
+    def weight_rows(count):
+        return pl.BlockSpec((None, count, lanes), lambda c: (layer, 0, c))
+
     return plain_call(
         functools.partial(conv_back_kernel, (taps, states, steps)),
-        (tiles,),
-        [slab(steps), whole(grad_selection.shape), layer_columns(layer, columns), slab(steps),
-         rows_of(taps - 1), whole(masks.shape), layer_rows(layer, taps), layer_rows(layer, 1),
-         rows_of(tokens), rows_of(rank), rows_of(states), rows_of(1), rows_of(1), ANYWHERE],
-        [rows_of(tokens), rows_of(taps - 1), rows_of(taps - 1),
-         pl.BlockSpec((LANES, 2 * LANES), lambda c: (c, 0))],
+        (channels // lanes,),
+        [cubes(steps), whole(grad_selection.shape),
+         pl.BlockSpec((None, lanes, columns), lambda c: (layer, c, 0)), cubes(steps),
+         rows(taps - 1), whole(masks.shape), weight_rows(taps), weight_rows(1),
+         rows(tokens), rows(rank), rows(states), rows(1), rows(1), ANYWHERE],
+        [rows(tokens), rows(taps - 1), rows(taps - 1),
+         pl.BlockSpec((lanes, 2 * LANES), lambda c: (c, 0))],
         [
             shaped((tokens, 2 * channels), jnp.bfloat16),
             shaped((taps - 1, channels)),
             shaped((taps - 1, channels)),
             shaped((channels, 2 * LANES), jnp.bfloat16),
         ],
-        [VMEM((steps + taps - 1, CHUNKS, LANES), f32), VMEM((steps + taps - 1, CHUNKS, LANES), f32)],
+        [VMEM((steps + taps - 1, CHUNKS, lanes), f32), VMEM((steps + taps - 1, CHUNKS, lanes), f32)],
         (grad_act, grad_selection, state_weight, projected, rim, masks, conv_weight, conv_bias, act, grad_step,
          grad_decay, grad_bias, grad_skip, halved),
         10,
@@ -697,9 +771,9 @@
     )
 
 
-def link_kernel(layer, count, reverse, total_ref, size_ref, decay_ref, out_ref,
-                mine, mine_length, near, near_length, both, both_length, far, far_length,
-                send, recv, send_length, recv_length):
+def hand_on(layer, count, reverse, total_ref, size_ref, decay_ref, out_ref, scratch, between, after):
+    (mine, mine_length, near, near_length, both, both_length, far, far_length,
+     send, recv, send_length, recv_length) = scratch
     here = lax.axis_index("wide")
     group = lax.axis_index("narrow")
     pairs = count // 2
@@ -727,6 +801,7 @@
         return copies
 
     first = hand(0, mine, mine_length, near, near_length, partner)
+    between()
     for copy in first:
         copy.wait_recv()
     second_here = (side == 0) if reverse else (side == 1)
@@ -741,6 +816,7 @@
     for k, other in enumerate(others):
         sent.append(hand(
             1 + k, both, both_length, far.at[pair], far_length.at[pair], 2 * other + side))
+    after()
     for copies in sent:
         for copy in copies:
             copy.wait_recv()
@@ -756,45 +832,152 @@
             copy.wait_send()
 
 
-def handed_on(layer, total, size, decay_log, reverse, identity):
-    count = lax.axis_size("wide")
+LINK_REFS = 12
+
+
+def link_scratch(count, states, channels):
     pairs = count // 2
-    states, channels = total.shape
     f32, low = jnp.float32, jnp.bfloat16
     dma = pltpu.SemaphoreType.DMA((pairs,))
+    return [
+        VMEM((states, channels), low), VMEM((1, channels), f32),
+        VMEM((states, channels), low), VMEM((1, channels), f32),
+        VMEM((states, channels), low), VMEM((1, channels), f32),
+        VMEM((pairs, states, channels), low), VMEM((pairs, 1, channels), f32),
+        dma, dma, dma, dma,
+    ]
+
+
+def link_call(kernel, total, size, decay_log, beside, out_shapes, scratch, identity):
+    states, channels = total.shape
+    inside = pl.BlockSpec(memory_space=VMEM)
     return pl.pallas_call(
-        functools.partial(link_kernel, layer, count, reverse),
-        out_shape=jax.ShapeDtypeStruct((states, channels), f32),
-        in_specs=[pl.BlockSpec(memory_space=VMEM)] * 3,
-        out_specs=pl.BlockSpec(memory_space=VMEM),
-        scratch_shapes=[
-            VMEM((states, channels), low),
-            VMEM((1, channels), f32),
-            VMEM((states, channels), low),
-            VMEM((1, channels), f32),
-            VMEM((states, channels), low),
-            VMEM((1, channels), f32),
-            VMEM((pairs, states, channels), low),
-            VMEM((pairs, 1, channels), f32),
-            dma, dma, dma, dma,
-        ],
+        kernel,
+        out_shape=[shaped((states, channels))] + out_shapes,
+        in_specs=[inside] * 3 + [ANYWHERE] * len(beside),
+        out_specs=[inside] + [ANYWHERE] * len(out_shapes),
+        scratch_shapes=link_scratch(lax.axis_size("wide"), states, channels) + scratch,
         compiler_params=pltpu.CompilerParams(
             collective_id=identity, has_side_effects=True, vmem_limit_bytes=60 * MIB
         ),
         cost_estimate=microseconds(12),
-    )(total, size, decay_log)
+    )(total, size, decay_log, *beside)
+
+
+def ahead_kernel(layer, count, wanted, total_ref, size_ref, decay_ref, *refs):
+    arrays = len(wanted)
+    sources, out_ref, targets = refs[:arrays], refs[arrays], refs[arrays + 1 : 2 * arrays + 1]
+    scratch, (*held, got, put) = refs[2 * arrays + 1 :][:LINK_REFS], refs[2 * arrays + 1 + LINK_REFS :]
+    into = [
+        pltpu.make_async_copy(sources[i].at[wanted[i]], held[i], got.at[i]) for i in range(arrays)]
+    out = [pltpu.make_async_copy(held[i], targets[i], put.at[i]) for i in range(arrays)]
+    for copy in into:
+        copy.start()
+
+    def after():
+        for i in range(arrays):
+            into[i].wait()
+            out[i].start()
+
+    hand_on(layer, count, False, total_ref, size_ref, decay_ref, out_ref, scratch, lambda: None, after)
+    for copy in out:
+        copy.wait()
+
+
+def handed_ahead(layer, total, size, decay_log, wanted, identity):
+    shapes = [array.shape[1:] for array, _ in wanted]
+    dma = pltpu.SemaphoreType.DMA((len(wanted),))
+    return link_call(
+        functools.partial(ahead_kernel, layer, lax.axis_size("wide"), tuple(which for _, which in wanted)),
+        total, size, decay_log, [array for array, _ in wanted],
+        [shaped(shape, array.dtype) for shape, (array, _) in zip(shapes, wanted)],
+        [VMEM(shape, array.dtype) for shape, (array, _) in zip(shapes, wanted)] + [dma, dma],
+        identity)
+
+
+def behind_kernel(layer, count, total_ref, size_ref, decay_ref, rows_hbm, pre_hbm, hidden_hbm, grad_hbm,
+                  out_ref, *refs):
+    outs = len(refs) - LINK_REFS - 6
+    outs //= 2
+    targets, scratch = refs[:outs], refs[outs : outs + LINK_REFS]
+    rows, pre, hidden_rows, grad, *found = refs[outs + LINK_REFS : -2]
+    got, put = refs[-2:]
+    members, _, hidden = pre.shape
+    width = rows.shape[1]
+    low = jnp.bfloat16
+    loads = [
+        pltpu.make_async_copy(source, target, got.at[i])
+        for i, (source, target) in enumerate(
+            ((rows_hbm, rows), (pre_hbm, pre), (hidden_hbm, hidden_rows), (grad_hbm, grad)))
+    ]
+    for load in loads:
+        load.start()
+    stores = [
+        [pltpu.make_async_copy(found[i].at[s], targets[i].at[s], put.at[i, s]) for i in range(outs)]
+        for s in range(members)
+    ]
+
+    def weights(s):
+        up = dot_tn(rows[...], pre[s]).astype(low)
+        down = dot_tn(hidden_rows[s], grad[...]).astype(low)
+        if outs == 2:
+            found[0][s], found[1][s] = up, down
+        else:
+            found[0][s, :width] = up
+            for f in range(width // hidden):
+                found[0][s, width + f * hidden : width + (f + 1) * hidden] = down[
+                    :, f * hidden : (f + 1) * hidden]
+        for store in stores[s]:
+            store.start()
+
+    def between():
+        for load in loads:
+            load.wait()
+        weights(0)
+
+    def after():
+        for s in range(1, members):
+            weights(s)
+
+    hand_on(layer, count, True, total_ref, size_ref, decay_ref, out_ref, scratch, between, after)
+    for pair in stores:
+        for store in pair:
+            store.wait()
+
+
+def handed_back(layer, total, size, decay_log, rows, pre, hidden_rows, grad_rows, identity):
+    members, _, hidden = pre.shape
+    width = rows.shape[1]
+    low = jnp.bfloat16
+    sizes = [(2 * width, hidden)] if folds(width, hidden) else [(width, hidden), (hidden, width)]
+    shapes = [(members,) + size for size in sizes]
+    return link_call(
+        functools.partial(behind_kernel, layer, lax.axis_size("wide")),
+        total, size, decay_log, [rows, pre, hidden_rows, grad_rows],
+        [shaped(shape, low) for shape in shapes],
+        [VMEM(array.shape, low) for array in (rows, pre, hidden_rows, grad_rows)]
+        + [VMEM(shape, low) for shape in shapes]
+        + [pltpu.SemaphoreType.DMA((4,)), pltpu.SemaphoreType.DMA((len(shapes), members))],
+        identity)
 
 
 def bell(values):
     return 0.5 * (1.0 + lax.erf(values * 0.7071067811865476))
 
 
-def expert_kernel(dims, backward, *refs):
+def expert_kernel(dims, backward, beside, which, *refs):
     count, groups, members, block, share, width, hidden = dims
+    out_ref, perm_ref, up_hbm, down_hbm, *refs = refs
     if backward:
-        out_ref, perm_ref, up_hbm, down_hbm, pre_hbm, ret_ref, rows_hbm, low_hbm, *scratch = refs
-    else:
-        out_ref, perm_ref, up_hbm, down_hbm, ret_ref, rows_hbm, pre_hbm, low_hbm, *scratch = refs
+        pre_hbm, *refs = refs
+    if beside:
+        next_hbm, *refs = refs
+    ret_ref, rows_hbm, *refs = refs
+    if not backward:
+        pre_hbm, *refs = refs
+    low_hbm, *scratch = refs
+    if beside:
+        met_hbm, *scratch, leaving, met, next_send, next_recv, next_local = scratch
     (arrived, own, rows, pre, low, part, got, final, landed, up, down, total,
      there_send, there_recv, row_send, row_recv, sum_send, sum_recv, back_send, back_recv, local) = scratch
     f32, bf16 = jnp.float32, jnp.bfloat16
@@ -817,6 +1000,10 @@
         loads.append(pltpu.make_async_copy(pre_hbm, pre, local.at[2]))
     for load in loads:
         load.start()
+    if beside:
+        source = next_hbm if which is None else next_hbm.at[which]
+        next_load = pltpu.make_async_copy(source, leaving, next_local.at[0])
+        next_load.start()
 
     def window_at(away, turn):
         return lax.rem(quad + away, quads) * members + lax.rem(member + turn, members)
@@ -890,6 +1077,21 @@
     for away, turn in ways:
         carry(away, turn, 1)
     rows[span(here), :] = own[member]
+    beside_copies = []
+
+    def send_beside(turns):
+        for turn in turns if beside else ():
+            copy = pltpu.make_async_remote_copy(
+                src_ref=leaving.at[lax.rem(member + turn, members)], dst_ref=met.at[member],
+                send_sem=next_send.at[turn], recv_sem=next_recv.at[turn],
+                device_id=(window_at(0, turn), group), device_id_type=MESH)
+            copy.start()
+            beside_copies.append(copy)
+
+    if beside:
+        next_load.wait()
+        met[member] = leaving[member]
+    send_beside([1])
 
     def arrive(away, turn):
         window = lax.rem(quad + quads - away, quads) * members + lax.rem(member + members - turn, members)
@@ -964,6 +1166,7 @@
                 late.append((away, turn, windows[turn - first]))
     for away, turn, window in late:
         give_back(away, turn, window, 0)
+    send_beside(range(2, members))
 
     saves = [
         pltpu.make_async_copy(rows, rows_hbm, local.at[3]),
@@ -1010,13 +1213,18 @@
     ret_ref[near_group] = landed[1 - core]
     for place, other in others:
         ret_ref[other] = landed[place]
-    for copy in there + sent + home:
+    if beside:
+        for copy in beside_copies:
+            copy.wait_recv()
+        saves.append(pltpu.make_async_copy(met, met_hbm, next_local.at[1]))
+        saves[-1].start()
+    for copy in there + sent + home + beside_copies:
         copy.wait_send()
     for save in saves:
         save.wait()
 
 
-def expert_pass(outbound, perm, weights, pre, identity):
+def expert_pass(outbound, perm, weights, pre, identity, beside=None, which=None):
     count, groups = lax.axis_size("wide"), lax.axis_size("narrow")
     backward = pre is not None
     _, block, width = outbound.shape
@@ -1028,11 +1236,17 @@
     dims = (count, groups, members, block, share, width, hidden)
     inside = pl.BlockSpec(memory_space=VMEM)
     args = (outbound, perm) + tuple(weights) + ((pre,) if backward else ())
+    args += () if beside is None else (beside,)
     outs = [shaped((groups, block, width), low), shaped((total, width), low)]
     outs += ([] if backward else [shaped((members, total, hidden))]) + [shaped((members, total, hidden), low)]
     dma = pltpu.SemaphoreType.DMA
+    more = []
+    if beside is not None:
+        shape = beside.shape[-3:]
+        outs.append(shaped(shape, low))
+        more = [VMEM(shape, low), VMEM(shape, low), dma((members,)), dma((members,)), dma((2,))]
     return pl.pallas_call(
-        functools.partial(expert_kernel, dims, backward),
+        functools.partial(expert_kernel, dims, backward, beside is not None, which),
         out_shape=outs,
         in_specs=[inside, inside] + [ANYWHERE] * (len(args) - 2),
         out_specs=[inside] + [ANYWHERE] * (len(outs) - 1),
@@ -1054,7 +1268,7 @@
             dma((quads, members, 2)), dma((quads, members, 2)),
             dma((groups - 1,)), dma((groups - 1,)),
             dma((5,)),
-        ],
+        ] + more,
         compiler_params=pltpu.CompilerParams(
             collective_id=identity, has_side_effects=True, vmem_limit_bytes=60 * MIB
         ),
@@ -1110,73 +1324,34 @@
     return 0 if hidden % LANES else width // hidden
 
 
-def weights_kernel(rows_ref, pre_ref, hidden_ref, grad_ref, *out_refs):
-    width, hidden = rows_ref.shape[1], pre_ref.shape[1]
-    low = jnp.bfloat16
-    up = dot_tn(rows_ref[...], pre_ref[...]).astype(low)
-    down = dot_tn(hidden_ref[...], grad_ref[...]).astype(low)
-    if len(out_refs) == 2:
-        out_refs[0][...], out_refs[1][...] = up, down
+def widen_kernel(arrays, *refs):
+    refs, (up_ref, down_ref) = refs[:arrays], refs[-2:]
+    width, hidden = up_ref.shape
+    if arrays == 2:
+        up_ref[...] = refs[0][...].astype(jnp.float32)
+        down_ref[...] = refs[1][...].astype(jnp.float32)
         return
-    out_refs[0][:width] = up
+    up_ref[...] = refs[0][:width].astype(jnp.float32)
     for f in range(width // hidden):
-        out_refs[0][width + f * hidden : width + (f + 1) * hidden] = down[:, f * hidden : (f + 1) * hidden]
-
-
-def expert_weights(rows, pre, hidden_rows, grad_rows):
-    total, width = rows.shape
-    members, _, hidden = pre.shape
-    slices = pl.BlockSpec((None, total, hidden), lambda s: (s, 0, 0))
-    sizes = [(2 * width, hidden)] if folds(width, hidden) else [(width, hidden), (hidden, width)]
+        down_ref[:, f * hidden : (f + 1) * hidden] = refs[0][
+            width + f * hidden : width + (f + 1) * hidden].astype(jnp.float32)
+
+
+def widened(layer, layers, arrays, width, hidden, held):
+    experts = arrays[0].shape[0]
+    count = len(arrays)
     return plain_call(
-        weights_kernel,
-        (members,),
-        [whole((total, width)), slices, slices, whole((total, width))],
-        [pl.BlockSpec((None,) + size, lambda s: (s, 0, 0)) for size in sizes],
-        [shaped((members,) + size, jnp.bfloat16) for size in sizes],
+        functools.partial(widen_kernel, count),
+        (experts,),
+        [pl.BlockSpec((None,) + array.shape[1:], lambda e: (e, 0, 0)) for array in arrays]
+        + [ANYWHERE] * len(held),
+        [pl.BlockSpec((None, None, width, hidden), lambda e: (layer, e, 0, 0)),
+         pl.BlockSpec((None, None, hidden, width), lambda e: (layer, e, 0, 0))],
+        [shaped((layers, experts, width, hidden)), shaped((layers, experts, hidden, width))],
         [],
-        (rows, pre, hidden_rows, grad_rows),
-        6,
-    )
-
-
-def widen_kernel(experts, *refs):
-    up_ref, down_ref = refs[-2:]
-    refs = refs[:-2]
-    width, hidden = up_ref.shape
-    for layer in (0, 1):
-        @pl.when(pl.program_id(0) // experts == layer)
-        def _():
-            if len(refs) == 4:
-                up_ref[...] = refs[2 * layer][...].astype(jnp.float32)
-                down_ref[...] = refs[2 * layer + 1][...].astype(jnp.float32)
-                return
-            up_ref[...] = refs[layer][:width].astype(jnp.float32)
-            for f in range(width // hidden):
-                down_ref[:, f * hidden : (f + 1) * hidden] = refs[layer][
-                    width + f * hidden : width + (f + 1) * hidden].astype(jnp.float32)
-
-
-def widened(first, second, width, hidden):
-    experts = first[0].shape[0]
-    specs = []
-    for layer, arrays in enumerate((first, second)):
-        for array in arrays:
-            if layer == 0:
-                place = lambda i: (jnp.minimum(i, experts - 1), 0, 0)
-            else:
-                place = lambda i: (jnp.maximum(i - experts, 0), 0, 0)
-            specs.append(pl.BlockSpec((None,) + array.shape[1:], place))
-    return plain_call(
-        functools.partial(widen_kernel, experts),
-        (2 * experts,),
-        specs,
-        [pl.BlockSpec((None, None, width, hidden), lambda i: (i // experts, i % experts, 0, 0)),
-         pl.BlockSpec((None, None, hidden, width), lambda i: (i // experts, i % experts, 0, 0))],
-        [shaped((2, experts, width, hidden)), shaped((2, experts, hidden, width))],
-        [],
-        tuple(first) + tuple(second),
-        9,
+        tuple(arrays) + tuple(held),
+        60,
+        {count + k: k for k in range(len(held))},
     )
 
 
@@ -1406,21 +1581,27 @@
 
 
 def inward_kernel(dims, grad_ref, weight_ref, edge_ref, handed_ref, normed_ref, begin_ref, gain_ref, passed_ref,
-                  out_ref, channel_ref, router_ref, expert_ref, packed_ref, new_ref, rows, features):
+                  out_ref, channel_ref, router_ref, expert_ref, packed_ref, new_ref, rows, features, held_block):
     blocks, wide, tall, held, fold, marks, spare, steps = dims
     owners, count, _ = packed_ref.shape
     f32, low = jnp.float32, jnp.bfloat16
     step = pl.program_id(0)
     tokens = grad_ref.shape[0]
     last = edge_ref.shape[0]
-    value = lax.rem(step, blocks) < blocks // 2
-    place = lax.broadcasted_iota(jnp.int32, grad_ref.shape, 0)
-    block = grad_ref[...].astype(f32)
-    edge = edge_ref[...] + handed_ref[...]
-    for j in range(last):
-        row = (steps - last + j) * CHUNKS + CHUNKS - 1
-        block = jnp.where(jnp.logical_and(place == row, value), edge[j : j + 1], block)
-    block = block.astype(low)
+    edited = (last + 1) // 2 * 2 * CHUNKS
+    held_block[...] = grad_ref[...]
+
+    @pl.when(lax.rem(step, blocks) < blocks // 2)
+    def _():
+        edge = edge_ref[...] + handed_ref[...]
+        ends = grad_ref[tokens - edited :, :].astype(f32)
+        place = lax.broadcasted_iota(jnp.int32, ends.shape, 0)
+        for j in range(last):
+            row = edited - (last - j) * CHUNKS + CHUNKS - 1
+            ends = jnp.where(place == row, edge[j : j + 1], ends)
+        held_block[tokens - edited :, :] = ends.astype(low)
+
+    block = held_block[...]
 
     @pl.when(step == 0)
     def _():
@@ -1480,9 +1661,7 @@
     fold = width // (2 * LANES)
     count = wide + tall + held // fold
     count += -count % 16
-    owners = 1
-    while owners * wide % LANES:
-        owners *= 2
+    owners = width // wide
     blocks = devices // owners
     span = owners * wide
     taps = edge.shape[0]
@@ -1504,7 +1683,8 @@
          whole(grad_router.shape), whole(grad_expert.shape)],
         [pl.BlockSpec((owners, count, width), lambda i: (at(i), 0, 0)), whole((tokens, width))],
         [shaped((devices, count, width), jnp.bfloat16), shaped((tokens, width))],
-        [VMEM((owners, count, width), jnp.float32), VMEM((width, 2 * LANES), jnp.float32)],
+        [VMEM((owners, count, width), jnp.float32), VMEM((width, 2 * LANES), jnp.float32),
+         VMEM((tokens, span), jnp.bfloat16)],
         (grad_projected, in_weight, edge, handed, normed, begin, gain, passed, grad_out, channel, grad_router,
          grad_expert),
         9,
@@ -1597,10 +1777,7 @@
     capacity = max(2, 5 * tokens // (4 * experts))
     block = -(-per_group * capacity // 16) * 16
     low, f32 = jnp.bfloat16, jnp.float32
-    starts = to_steps(doc_start[0]).astype(f32)
-    masks = keep_masks(starts, taps)
-    keep_mask = rim_keep(starts, taps - 1)[:, None]
-    reset = jnp.broadcast_to((starts * RESET)[..., None], starts.shape + (LANES,))
+    keep_mask = rim_keep(doc_start[0], taps - 1)[:, None]
     order = expert_order(per_group, groups, block, capacity)
     norm_mix, conv_bias, step_bias, skip_weight, norm_expert = (
         values[:, None, :] for values in (norm_mix, conv_bias, step_bias, skip_weight, norm_expert))
@@ -1610,22 +1787,13 @@
     def cube(values):
         return values.reshape(steps, CHUNKS, values.shape[-1])
 
-    fills, onehots, keeps = [], [], []
-    for layer in range(layers):
-        chosen = to_steps(expert_choice[layer, 0]).reshape(tokens)
-        slot_row = to_steps(slot_index[layer, 0]).reshape(tokens)
-        kept = slot_row >= 0
-        place = (chosen // per_group) * block + (chosen % per_group) * capacity + slot_row
-        place = jnp.where(kept, place, -1)
-        fills.append(
-            (place[None, :] == jnp.arange(groups * block, dtype=jnp.int32)[:, None]).astype(low))
-        onehots.append((chosen[:, None] == jnp.arange(experts, dtype=jnp.int32)[None, :]).astype(f32))
-        keeps.append(kept.astype(f32)[:, None])
-
     tail = passed_along(hidden[0, tokens - taps + 1 :] * keep_mask.astype(low), 1)
     weights = [None] * layers
-    ready, tail = lax.optimization_barrier((layer_of(expert_up, 0), tail))
+    ready, tail, slot_index = lax.optimization_barrier((layer_of(expert_up, 0), tail, slot_index))
     weights[0] = between_members([ready])
+    reset, masks, fills, onehots, keeps = tables(
+        doc_start, expert_choice, slot_index, taps, experts, groups, block, capacity)
+
     for layer in range(layers):
         begin = current
         normed = rms_scale(current, norm_mix[layer]).astype(low)
@@ -1639,19 +1807,17 @@
             layer, projected, rim, masks, reset, conv_weight, conv_bias, state_weight, step_weight, step_bias,
             decay_log)
         if layer == 0:
-            total, fills, order = lax.optimization_barrier((total, fills, order))
-        total, ready = lax.optimization_barrier((total, layer_of(expert_down, layer)))
-        entering = handed_on(layer, total, total_size, decay_log, False, layer)
-        ready, entering = lax.optimization_barrier((ready, entering))
+            total, order = lax.optimization_barrier((total, order))
+        entering, ready = handed_ahead(layer, total, total_size, decay_log, [(expert_down, layer)], layer)
         weights[layer] += between_members([ready])
         mixed, gated, begins, middle, routed, logits, outbound = mixer_run(
             layer, size, act, selection, reset, decay_log, link, link_size, entering, projected, skip_weight,
             out_weight, current, norm_expert, router, fills[layer])
-        if layer + 1 < layers:
-            ready, outbound = lax.optimization_barrier((layer_of(expert_up, layer + 1), outbound))
-            weights[layer + 1] = between_members([ready])
-        returned, kept_rows, pre_act, hidden_low = expert_pass(
-            outbound.reshape(groups, block, width), order, weights[layer], None, 4 + layer)
+        returned, kept_rows, pre_act, hidden_low, *following = expert_pass(
+            outbound.reshape(groups, block, width), order, weights[layer], None, 4 + layer,
+            expert_up if layer + 1 < layers else None, layer + 1)
+        if following:
+            weights[layer + 1] = following
         shares = jax.nn.softmax(logits, axis=-1)
         gate = jnp.sum(shares * onehots[layer], axis=1, keepdims=True)
         back_rows = dot_tn(fills[layer], returned.reshape(groups * block, width))
@@ -1663,6 +1829,7 @@
     output = to_tokens(cube(current.astype(low)))[None]
     grad = to_steps(cotangent[0]).reshape(tokens, width).astype(f32)
     sums = [None] * layers
+    wide_grads = ()
     expert_grads = [None] * layers
     per_device = inner // devices
     norm_device = width // devices
@@ -1675,7 +1842,6 @@
         outbound = dot_nn(fill, grad_rows_low).astype(low).reshape(groups, block, width)
         inbound, grad_rows, grad_pre = expert_pass(
             outbound, order, weights[layer], entry["pre_act"], 6 + layer)
-        ready = expert_weights(entry["kept_rows"], grad_pre, entry["hidden_low"], grad_rows)
         grad_sent = dot_tn(fill, inbound.reshape(groups * block, width))
         grad_logits_low = ((grad_gate * gate) * (onehots[layer] - entry["shares"])).astype(low)
         grad_router = dot_tn(entry["routed"], grad_logits_low)
@@ -1686,8 +1852,9 @@
         grad_y, grad_igate, grad_skip, grad_out, link, link_size, total, total_size = mixer_turn(
             layer, grad_low, out_weight, entry["projected"], entry["mixed"], entry["act"], entry["gated"],
             entry["size"], entry["selection"], reset, decay_log)
-        entering = handed_on(layer, total, total_size, decay_log, True, 2 + layer)
-        ready, entering = lax.optimization_barrier((ready, entering))
+        entering, *ready = handed_back(
+            layer, total, total_size, decay_log, entry["kept_rows"], grad_pre, entry["hidden_low"], grad_rows,
+            2 + layer)
         expert_grads[layer] = between_members(ready)
         grad_act, grad_decay, grad_bias, grad_step, grad_selection = mixer_back(
             layer, entry["size"], entry["act"], grad_y, decay_log, entry["selection"], reset,
@@ -1696,6 +1863,9 @@
             layer, grad_act, grad_selection, state_weight, entry["projected"], entry["rim"], masks, conv_weight,
             conv_bias, entry["act"], grad_step, grad_decay, grad_bias, grad_skip, grad_igate)
         handed = passed_along(rim_grad, -1) * keep_mask
+        if layer + 1 < layers:
+            wide_grads = widened(layer + 1, layers, expert_grads[layer + 1], width, expert_up.shape[3], wide_grads)
+            handed, *wide_grads = lax.optimization_barrier((handed, *wide_grads))
         blocks, grad = mixer_inward(
             layer, grad_projected, in_weight, edge, handed, entry["normed"], entry["begin"], norm_mix, grad,
             grad_out, channel, grad_router, grad_norm_expert.reshape(1, width), devices, spare)
@@ -1713,7 +1883,7 @@
     shared = (
         grad_norm_mix, jnp.swapaxes(grad_in, 1, 2), grad_conv, grad_conv_bias, grad_state, grad_step,
         grad_step_bias, grad_decay, grad_skip, grad_out, grad_norm_expert, jnp.swapaxes(grad_router, 1, 2))
-    up_grads, down_grads = widened(*expert_grads, width, expert_up.shape[3])
+    up_grads, down_grads = widened(0, layers, expert_grads[0], width, expert_up.shape[3], wide_grads)
     output_grad = to_tokens(cube(grad))[None]
     return (output, output_grad, *shared, up_grads, down_grads)
 

time: 747 us -> 699 us (0.936)
  Pallas kernels: 593 us -> 540 us
  waiting for transfers between devices: 22.9 us -> 35.7 us
    pallas_call x15 -> x14, Pallas kernels: 240 us -> 196 us  [plain_call(): pl.pallas_call(kernel, grid=grid, in_specs=in_specs, out_specs=out_specs,...]
    ppermute x4, waiting for transfers between devices: 18.9 us -> 31.3 us  [passed_along(): lax.ppermute(x, 'wide', [(i, i + by) for i in range(size) if 0 <= i + by...]
    pallas_call x4 -> x1, Pallas kernels: 10.2 us -> 2.53 us  [layer_of(): pl.pallas_call(functools.partial(slice_kernel, layer), out_shape=shaped(s...]
    all_to_all x6 -> x5, starting transfers between devices: 30.8 us -> 24.1 us  [between_members(): lax.all_to_all(values, 'wide', split_axis=0, concat_axis=0, tiled=True, a...]
    pallas_call x8 -> x9, Pallas kernels: 296 us -> 291 us  [the longest x4 233 us: expert_pass(): pl.pallas_call(functools.partial(expert_kernel, dims, backward, beside is...]
  transfers between devices with their start and end apart: 11 -> 10, of which waited for: 4 -> 4; matrix products, arithmetic and copies ran while one was open for 7% -> 6% of each run, Pallas kernels for 60% -> 45%
where the time goes in v4:
time: 699 us; the launch traced here: 692 us
  Pallas kernels  540 us (77%)
  starting transfers between devices  39.2 us (6%)
  waiting for transfers between devices  35.7 us (5%)
  matrix products  27.1 us (4%)
  other arithmetic  18.8 us (3%)
  local copies, waits for them, and re-layouts  16.8 us (2%)
  between operations  15.2 us (2%)
    pallas_call x4, Pallas kernels, expert_pass(): pl.pallas_call(functools.partial(expert_kernel, dims, backward, beside is...  233 us
    pallas_call x14, Pallas kernels, plain_call(): pl.pallas_call(kernel, grid=grid, in_specs=in_specs, out_specs=out_specs,...  196 us
    pallas_call x4, Pallas kernels, link_call(): pl.pallas_call(kernel, out_shape=[shaped((states, channels))] + out_shape...  56.3 us
    pallas_call x1, Pallas kernels, summed_shares(): pl.pallas_call(functools.partial(sum_kernel, (count, lines, sizes, first,...  47.6 us
    ppermute x4, waiting for transfers between devices, passed_along(): lax.ppermute(x, 'wide', [(i, i + by) for i in range(size) if 0 <= i + by...  31.3 us
    all_to_all x5, starting transfers between devices, between_members(): lax.all_to_all(values, 'wide', split_axis=0, concat_axis=0, tiled=True, a...  24.1 us
    ppermute x4, starting transfers between devices, passed_along(): lax.ppermute(x, 'wide', [(i, i + by) for i in range(size) if 0 <= i + by...  15 us
    dot_general x5, matrix products, dot_nn(): lax.dot_general(left, right, (((1,), (0,)), ((), ())), preferred_element_...  15 us
  transfers between devices with their start and end apart: 10, of which 4 were waited for; matrix products, arithmetic and copies ran while one was open for 6% of the time, Pallas kernels for 45%

profile of v4, /device:TPU:0, one launch (start us, length us, event | category | flops | bytes accessed | tf_op | source)
XLA Modules:
  0.0 692.3 jit_solution(3850260568654259781)
XLA Ops:
  9.2 5.5 collective-permute-start
  14.6 2.5 shard_map.306
  17.2 3.8 all-to-all-start
  25.4 5.8 fusion.2.value_ref.gate_ref
  31.2 2.3 shard_map.307
  34.3 2.7 fusion.6.rim_ref
  37.0 14.0 %shard_map.308 = (bf16[256,1536]{1,0:T(8,128)(2,1)}, f32[32,8,80]{2,1,0:T(8,128)}, f32[32,8,1536]{2,1,0:T(8,128)}, f32[16,8,1536]{2,1,0:T(8,128)}, f32[8,1536]{1...) custom-call(f32[32,8,3072]{2,1,0:T(8,128)} %fusion.2.value_ref.gate_ref, f32[3,1536]{1,0:T(4,128)} %fusion.6.rim_ref, ...), custom_call_target="tpu_custom_call" | custom-call | flops 2700000000 | bytes 10000 | tf_op jit(solution)/shard_map/pallas_call | solution.py:141
  51.0 13.2 %shard_map.309 = (f32[16,1536]{1,0:T(8,128)}, bf16[4,384,768]{2,1,0:T(8,128)(2,1)}) custom-call(f32[16,1536]{1,0:T(8,128)} %get-tuple-element.147.total_ref, f32[1,1536]{1,0:T(1,128)} %get-tuple-element.148.size_ref, f32[2,16,1536]{2,1,0:T(8,128)} %decay_ref.23, bf16[2,4,384,768]{3,2,1,0:T(8,128)(2,1)} %refs_0_.3), custom_call_target="tpu_custom_call" | custom-call | flops 1800000000 | bytes 10000 | tf_op jit(solution)/shard_map/pallas_call | solution.py:854
  64.2 4.8 all-to-all-start.1
  73.4 1.7 copy.54.router_ref
  75.9 15.7 %shard_map.310 = (f32[32,8,1536]{2,1,0:T(8,128)}, bf16[256,1536]{1,0:T(8,128)(2,1)}, f32[16,8,1536]{2,1,0:T(8,128)}, f32[256,768]{1,0:T(8,128)}, bf16[256,768]{1...) custom-call(f32[32,8,1536]{2,1,0:T(8,128)} %get-tuple-element.141.size_ref, ...), custom_call_target="tpu_custom_call" | custom-call | flops 3300000000 | bytes 10000 | tf_op jit(solution)/shard_map/pallas_call | solution.py:141
  95.2 66.9 %shard_map.311 = (bf16[4,80,768]{2,1,0:T(8,128)(2,1)}, bf16[640,768]{1,0:T(8,128)(2,1)}, f32[4,640,384]{2,1,0:T(8,128)}, bf16[4,640,384]{2,1,0:T(8,128)(2,1)}, bf16[4,768,384]{2,1,0:T(8,128)(2,1)}) custom-call(bf16[4,80,768]{2,1,0:T(8,128)(2,1)} %bitcast.122, bf16[320,320]{1,0:T(8,128)(2,1)} %fusion.14.refs_1_, bf16[4,768,384]{2,1,0:T(8,128)(2,1)} %copy-done.11, ...), custom_call_target="tpu_custom_call" | custom-call | flops 9749999616 | bytes 10000 | tf_op jit(solution)/shard_map/pallas_call | solution.py:1248
  162.1 2.9 multiply_reduce_fusion.7
  166.3 3.9 fusion.value_ref.gate_ref
  170.4 7.0 %collective-permute-start.1 = (f32[3,1536]{1,0:T(4,128)S(1)}, f32[3,1536]{1,0:T(4,128)S(1)}, u32[]{:S(2)}, u32[]{:S(2)}) collective-permute-start(f32[3,1536]{1,0:T(4,128)S(1)} %fusion.27), channel_id=1, source_target_pairs={{0,4},{4,8},{8,12},{12,16},{16,20},{20,24},{24,28},{1,5},{5,9},{9,... | collective-permute-start | bytes 55304 | tf_op jit(solution)/shard_map/ppermute | solution.py:58
  177.3 1.5 collective-permute-done.1.rim_ref
  179.4 14.0 %shard_map.312 = (bf16[256,1536]{1,0:T(8,128)(2,1)}, f32[32,8,80]{2,1,0:T(8,128)}, f32[32,8,1536]{2,1,0:T(8,128)}, f32[16,8,1536]{2,1,0:T(8,128)}, f32[8,1536]{1...) custom-call(f32[32,8,3072]{2,1,0:T(8,128)} %copy-done, f32[3,1536]{1,0:T(4,128)} %copy-done.35, ...), custom_call_target="tpu_custom_call" | custom-call | flops 2700000000 | bytes 10000 | tf_op jit(solution)/shard_map/pallas_call | solution.py:141
  193.5 12.4 %shard_map.313 = (f32[16,1536]{1,0:T(8,128)}, bf16[4,384,768]{2,1,0:T(8,128)(2,1)}) custom-call(f32[16,1536]{1,0:T(8,128)} %get-tuple-element.165.total_ref, f32[1,1536]{1,0:T(1,128)} %get-tuple-element.166.size_ref, f32[2,16,1536]{2,1,0:T(8,128)} %decay_ref.23, bf16[2,4,384,768]{3,2,1,0:T(8,128)(2,1)} %refs_0_.3), custom_call_target="tpu_custom_call" | custom-call | flops 1800000000 | bytes 10000 | tf_op jit(solution)/shard_map/pallas_call | solution.py:854
  206.0 5.2 all-to-all-start.2
  211.3 15.7 %shard_map.314 = (f32[32,8,1536]{2,1,0:T(8,128)}, bf16[256,1536]{1,0:T(8,128)(2,1)}, f32[16,8,1536]{2,1,0:T(8,128)}, f32[256,768]{1,0:T(8,128)}, bf16[256,768]{1...) custom-call(f32[32,8,1536]{2,1,0:T(8,128)} %get-tuple-element.160.size_ref, ...), custom_call_target="tpu_custom_call" | custom-call | flops 3300000000 | bytes 10000 | tf_op jit(solution)/shard_map/pallas_call | solution.py:141
  231.6 4.3 all-to-all-done.2.refs_3_
  236.0 52.9 %shard_map.315 = (bf16[4,80,768]{2,1,0:T(8,128)(2,1)}, bf16[640,768]{1,0:T(8,128)(2,1)}, f32[4,640,384]{2,1,0:T(8,128)}, bf16[4,640,384]{2,1,0:T(8,128)(2,1)}) custom-call(bf16[4,80,768]{2,1,0:T(8,128)(2,1)} %bitcast.121, bf16[320,320]{1,0:T(8,128)(2,1)} %fusion.14.refs_1_, bf16[4,768,384]{2,1,0:T(8,128)(2,1)} %get-tuple-element.174.refs_2_, ...), custom_call_target="tpu_custom_call" | custom-call | flops 9749999616 | bytes 10000 | tf_op jit(solution)/shard_map/pallas_call | solution.py:1248
  289.0 1.8 fusion.10
  291.1 1.4 convolution_convert_fusion.1
  293.9 55.3 %shard_map.316 = (bf16[4,80,768]{2,1,0:T(8,128)(2,1)}, bf16[640,768]{1,0:T(8,128)(2,1)}, bf16[4,640,384]{2,1,0:T(8,128)(2,1)}) custom-call(bf16[4,80,768]{2,1,0:T(8,128)(2,1)} %bitcast.111, bf16[320,320]{1,0:T(8,128)(2,1)} %fusion.14.refs_1_, bf16[4,768,384]{2,1,0:T(8,128)(2,1)} %get-tuple-element.174.refs_2_, bf16[4,384,768]{2,1,0:T(8,128)(2,1)} %all-to-all-done.2.refs_3_, ...), custom_call_target="tpu_custom_call" | custom-call | flops 9749999616 | bytes 10000 | tf_op jit(solution)/shard_map/pallas_call | solution.py:1248
  349.2 1.8 multiply_reduce_fusion.4
  351.1 1.7 fusion.55
  352.8 13.1 %shard_map.317 = (f32[32,8,1536]{2,1,0:T(8,128)}, bf16[256,3072]{1,0:T(8,128)(2,1)}, f32[1,1536]{1,0:T(1,128)}, bf16[1536,768]{1,0:T(8,128)(2,1)}, f32[16,8,1536...) custom-call(bf16[256,768]{1,0:T(8,128)(2,1)} %get-tuple-element.270.grad_ref, ...), custom_call_target="tpu_custom_call" | custom-call | flops 2100000000 | bytes 10000 | tf_op jit(solution)/shard_map/pallas_call | solution.py:141
  365.9 14.7 %shard_map.318 = (f32[16,1536]{1,0:T(8,128)}, bf16[4,1536,384]{2,1,0:T(8,128)(2,1)}) custom-call(f32[16,1536]{1,0:T(8,128)} %get-tuple-element.185.total_ref, f32[1,1536]{1,0:T(1,128)} %get-tuple-element.186.size_ref, f32[2,16,1536]{2,1,0:T(8,128)} %decay_ref.23, bf16[640,768]{1,0:T(8,128)(2,1)} %get-tuple-element.187.rows_hbm, ...), custom_call_target="tpu_custom_call" | custom-call | flops 1800000000 | bytes 10000 | tf_op jit(solution)/shard_map/pallas_call | solution.py:854
  380.6 5.0 all-to-all-start.3
  386.3 26.9 %shard_map.319 = (f32[32,8,1536]{2,1,0:T(8,128)}, f32[16,1536]{1,0:T(8,128)}, f32[1,1536]{1,0:T(1,128)}, f32[48,1536]{1,0:T(8,128)}, bf16[256,80]{1,0:T(8,128)(2,1)}) custom-call(f32[32,8,1536]{2,1,0:T(8,128)} %get-tuple-element.160.size_ref, bf16[256,1536]{1,0:T(8,128)(2,1)} %get-tuple-element.161.act_ref, f32[32,8,1536]{2,1,0:T(8,128)} %get-tuple-element.181.grad_ref, ...), custom_call_target="tpu_custom_call" | custom-call | flops 5249999872 | bytes 10000 | tf_op jit(solution)/shard_map/pallas_call | solution.py:141
  413.2 9.1 %shard_map.320 = (bf16[256,3072]{1,0:T(8,128)(2,1)}, f32[3,1536]{1,0:T(4,128)}, f32[3,1536]{1,0:T(4,128)}, bf16[1536,256]{1,0:T(8,128)(2,1)}) custom-call(f32[32,8,1536]{2,1,0:T(8,128)} %get-tuple-element.192.grad_act_ref, bf16[256,80]{1,0:T(8,128)(2,1)} %get-tuple-element.193.grad_selection_ref, ...), custom_call_target="tpu_custom_call", output_to_operand_aliasing={{0}: (13, {})} | custom-call | flops 1500000000 | bytes 10000 | tf_op jit(solution)/shard_map/pallas_call | solution.py:141
  425.4 14.2 %collective-permute-done.2 = f32[3,1536]{1,0:T(4,128)S(1)} collective-permute-done((f32[3,1536]{1,0:T(4,128)}, f32[3,1536]{1,0:T(4,128)S(1)}, u32[]{:S(2)}, u32[]{:S(2)}) %collective-permute-start.2) | collective-permute-done | bytes 18464 | tf_op jit(solution)/shard_map/ppermute | solution.py:58
  440.2 13.0 %shard_map.321 = (bf16[32,160,768]{2,1,0:T(8,128)(2,1)}, f32[256,768]{1,0:T(8,128)}) custom-call(bf16[256,3072]{1,0:T(8,128)(2,1)} %get-tuple-element.199.grad_ref, bf16[2,768,3072]{2,1,0:T(8,128)(2,1)} %weight_ref.3, f32[3,1536]{1,0:T(4,128)} %get-tuple-element.200.edge_ref, f32[3,1536]{1,0:T(4,128)} %broadcast_multiply_fusion.1.handed_ref, ...), custom_call_target="tpu_custom_call" | custom-call | flops 1350000000 | bytes 10000 | tf_op jit(solution)/shard_map/pallas_call | solution.py:141
  456.6 57.4 %shard_map.322 = (bf16[4,80,768]{2,1,0:T(8,128)(2,1)}, bf16[640,768]{1,0:T(8,128)(2,1)}, bf16[4,640,384]{2,1,0:T(8,128)(2,1)}) custom-call(bf16[4,80,768]{2,1,0:T(8,128)(2,1)} %bitcast.112, bf16[320,320]{1,0:T(8,128)(2,1)} %fusion.14.refs_1_, bf16[4,768,384]{2,1,0:T(8,128)(2,1)} %copy-done.11, bf16[4,384,768]{2,1,0:T(8,128)(2,1)} %all-to-all-done.1.refs_3_, ...), custom_call_target="tpu_custom_call" | custom-call | flops 9749999616 | bytes 10000 | tf_op jit(solution)/shard_map/pallas_call | solution.py:1248
  514.0 1.6 multiply_reduce_fusion
  516.9 13.0 %shard_map.323 = (f32[32,8,1536]{2,1,0:T(8,128)}, bf16[256,3072]{1,0:T(8,128)(2,1)}, f32[1,1536]{1,0:T(1,128)}, bf16[1536,768]{1,0:T(8,128)(2,1)}, f32[16,8,1536...) custom-call(bf16[256,768]{1,0:T(8,128)(2,1)} %get-tuple-element.268.grad_ref, ...), custom_call_target="tpu_custom_call" | custom-call | flops 2100000000 | bytes 10000 | tf_op jit(solution)/shard_map/pallas_call | solution.py:141
  529.9 16.0 %shard_map.324 = (f32[16,1536]{1,0:T(8,128)}, bf16[4,1536,384]{2,1,0:T(8,128)(2,1)}) custom-call(f32[16,1536]{1,0:T(8,128)} %get-tuple-element.214.total_ref, f32[1,1536]{1,0:T(1,128)} %get-tuple-element.215.size_ref, f32[2,16,1536]{2,1,0:T(8,128)} %decay_ref.23, bf16[640,768]{1,0:T(8,128)(2,1)} %get-tuple-element.216.rows_hbm, ...), custom_call_target="tpu_custom_call" | custom-call | flops 1800000000 | bytes 10000 | tf_op jit(solution)/shard_map/pallas_call | solution.py:854
  546.0 5.3 all-to-all-start.4
  552.1 26.9 %shard_map.325 = (f32[32,8,1536]{2,1,0:T(8,128)}, f32[16,1536]{1,0:T(8,128)}, f32[1,1536]{1,0:T(1,128)}, f32[48,1536]{1,0:T(8,128)}, bf16[256,80]{1,0:T(8,128)(2,1)}) custom-call(f32[32,8,1536]{2,1,0:T(8,128)} %get-tuple-element.141.size_ref, bf16[256,1536]{1,0:T(8,128)(2,1)} %get-tuple-element.142.act_ref, f32[32,8,1536]{2,1,0:T(8,128)} %get-tuple-element.210.grad_ref, ...), custom_call_target="tpu_custom_call" | custom-call | flops 5249999872 | bytes 10000 | tf_op jit(solution)/shard_map/pallas_call | solution.py:141
  579.1 9.2 %shard_map.326 = (bf16[256,3072]{1,0:T(8,128)(2,1)}, f32[3,1536]{1,0:T(4,128)}, f32[3,1536]{1,0:T(4,128)}, bf16[1536,256]{1,0:T(8,128)(2,1)}) custom-call(f32[32,8,1536]{2,1,0:T(8,128)} %get-tuple-element.221.grad_act_ref, bf16[256,80]{1,0:T(8,128)(2,1)} %get-tuple-element.222.grad_selection_ref, ...), custom_call_target="tpu_custom_call", output_to_operand_aliasing={{0}: (13, {})} | custom-call | flops 1500000000 | bytes 10000 | tf_op jit(solution)/shard_map/pallas_call | solution.py:141
  591.3 15.6 %collective-permute-done.3 = f32[3,1536]{1,0:T(4,128)S(1)} collective-permute-done((f32[3,1536]{1,0:T(4,128)}, f32[3,1536]{1,0:T(4,128)S(1)}, u32[]{:S(2)}, u32[]{:S(2)}) %collective-permute-start.3) | collective-permute-done | bytes 18464 | tf_op jit(solution)/shard_map/ppermute | solution.py:58
  607.6 6.4 shard_map.327
  614.0 12.8 %shard_map.328 = (bf16[32,160,768]{2,1,0:T(8,128)(2,1)}, f32[256,768]{1,0:T(8,128)}) custom-call(bf16[256,3072]{1,0:T(8,128)(2,1)} %get-tuple-element.228.grad_ref, bf16[2,768,3072]{2,1,0:T(8,128)(2,1)} %weight_ref.3, f32[3,1536]{1,0:T(4,128)} %get-tuple-element.229.edge_ref, f32[3,1536]{1,0:T(4,128)} %broadcast_multiply_fusion.handed_ref, ...), custom_call_target="tpu_custom_call" | custom-call | flops 1350000000 | bytes 10000 | tf_op jit(solution)/shard_map/pallas_call | solution.py:141
  626.8 2.3 copy.70
  629.1 47.6 %shard_map.329.refs_0_ = f32[160,768]{1,0:T(8,128)} custom-call(bf16[8,2,2,160,768]{4,3,2,1,0:T(8,128)(2,1)} %bitcast.120), custom_call_target="tpu_custom_call" | custom-call | flops 8999999488 | bytes 10000 | tf_op jit(solution)/shard_map/pallas_call | solution.py:1558
  676.7 6.4 shard_map.331
  683.1 2.1 shard_map.330
  (163 shorter events, 37.6 us)
Async XLA Ops:
  8.3 6.3 copy-start.45
  9.2 8.1 %collective-permute-start = (bf16[3,768]{1,0:T(4,128)(2,1)S(1)}, bf16[3,768]{1,0:T(4,128)(2,1)}, u32[]{:S(2)}, u32[]{:S(2)}) collective-permute-start(bf16[3,768]{1,0:T(4,128)(2,1)S(1)} %bitcast_multiply_fusion.4), channel_id=1, source_target_pairs={{0,4},{4,8},{8,12},{12,16},{16,20},{20,24},{24,28},{1,5},{5,9},{9,... | collective-permute-start | bytes 13832 | tf_op jit(solution)/shard_map/ppermute | solution.py:58
  17.2 3.9 copy-start.37
  17.2 4.5 copy-start.38
  17.2 5.1 copy-start.24
  17.2 6.2 copy-start.12
  17.2 6.3 copy-start.33
  17.2 47.0 %all-to-all-start = ((bf16[4,768,384]{2,1,0:T(8,128)(2,1)}), bf16[4,768,384]{2,1,0:T(8,128)(2,1)S(1)}, u32[]{:S(2)}, u32[]{:S(2)}) async-start(bf16[4,768,384]{2,1,0:T(8,128)(2,1)} %shard_map.306), calls=%async_computation | async-start | bytes 4718592 | tf_op jit(solution)/shard_map/all_to_all | solution.py:1291
  24.1 10.2 %copy-start.30 = (f32[768]{0:T(1024)}, f32[768]{0:T(1024)S(1)}, u32[]{:S(2)}) copy-start(f32[768]{0:T(1024)S(1)} %get-tuple-element.267) | copy-start | bytes 9220
  64.2 10.9 %copy-start.11 = (bf16[4,768,384]{2,1,0:T(8,128)(2,1)}, bf16[4,768,384]{2,1,0:T(8,128)(2,1)S(1)}, u32[]{:S(2)}) copy-start(bf16[4,768,384]{2,1,0:T(8,128)(2,1)S(1)} %all-to-all-done.refs_2_) | copy-start | bytes 7077892
  64.2 30.9 %all-to-all-start.1 = ((bf16[4,384,768]{2,1,0:T(8,128)(2,1)}), bf16[4,384,768]{2,1,0:T(8,128)(2,1)}, u32[]{:S(2)}, u32[]{:S(2)}) async-start(bf16[4,384,768]{2,1,0:T(8,128)(2,1)} %get-tuple-element.158), calls=%async_computation.1 | async-start | bytes 4718592 | tf_op jit(solution)/shard_map/all_to_all | solution.py:1291
  75.9 94.4 %copy-start.41 = (f32[3]{0:T(128)}, f32[3]{0:T(128)S(1)}, u32[]{:S(2)}) copy-start(f32[3]{0:T(128)S(1)} %pad_maximum_fusion) | copy-start | bytes 40
  75.9 17.8 %copy-start.15 = (f32[256,16]{1,0:T(8,128)S(1)}, f32[256,16]{1,0:T(8,128)}, u32[]{:S(2)}) copy-start(f32[256,16]{1,0:T(8,128)} %get-tuple-element.154) | copy-start | bytes 49156
  75.9 19.1 %copy-start.22 = (f32[256,1]{1,0:T(8,128)S(1)}, f32[256,1]{1,0:T(8,128)}, u32[]{:S(2)}) copy-start(f32[256,1]{1,0:T(8,128)} %get-tuple-element.152) | copy-start | bytes 3076
  95.0 67.1 %copy-start.20 = (f32[256,1]{1,0:T(8,128)}, f32[256,1]{1,0:T(8,128)S(1)}, u32[]{:S(2)}) copy-start(f32[256,1]{1,0:T(8,128)S(1)} %copy.55) | copy-start | bytes 3076
  95.2 67.0 %copy-start.39 = (f32[256]{0:T(256)}, f32[256]{0:T(256)S(1)}, u32[]{:S(2)}) copy-start(f32[256]{0:T(256)S(1)} %multiply_reduce_fusion.12) | copy-start | bytes 3076
  95.2 66.9 %copy-start.3 = (f32[256,768]{1,0:T(8,128)S(1)}, f32[256,768]{1,0:T(8,128)}, u32[]{:S(2)}) copy-start(f32[256,768]{1,0:T(8,128)} %get-tuple-element.151) | copy-start | bytes 2359300
  95.2 66.9 %copy-start.8 = (bf16[320,256]{1,0:T(8,128)(2,1)S(1)}, bf16[320,256]{1,0:T(8,128)(2,1)}, u32[]{:S(2)}) copy-start(bf16[320,256]{1,0:T(8,128)(2,1)} %get-tuple-element.150.fill_ref) | copy-start | bytes 491524
  95.2 69.9 %copy-start.31 = (f32[768]{0:T(1024)S(1)}, f32[768]{0:T(1024)}, u32[]{:S(2)}) copy-start(f32[768]{0:T(1024)} %copy-done.30) | copy-start | bytes 9220
  95.2 69.9 %copy-start.36 = (f32[768]{0:T(1024)S(1)}, f32[768]{0:T(1024)}, u32[]{:S(2)}) copy-start(f32[768]{0:T(1024)} %get-tuple-element.266) | copy-start | bytes 9220
  95.2 69.9 %copy-start.44 = (f32[256]{0:T(256)S(1)}, f32[256]{0:T(256)}, u32[]{:S(2)}) copy-start(f32[256]{0:T(256)} %rsqrt.55) | copy-start | bytes 3076
  166.3 3.9 copy-start.14
  170.2 8.6 %copy-start = (f32[32,8,3072]{2,1,0:T(8,128)}, f32[32,8,3072]{2,1,0:T(8,128)S(1)}, u32[]{:S(2)}) copy-start(f32[32,8,3072]{2,1,0:T(8,128)S(1)} %fusion.value_ref.gate_ref) | copy-start | bytes 9437188
  170.4 8.5 %collective-permute-start.1 = (f32[3,1536]{1,0:T(4,128)S(1)}, f32[3,1536]{1,0:T(4,128)S(1)}, u32[]{:S(2)}, u32[]{:S(2)}) collective-permute-start(f32[3,1536]{1,0:T(4,128)S(1)} %fusion.27), channel_id=1, source_target_pairs={{0,4},{4,8},{8,12},{12,16},{16,20},{20,24},{24,28},{1,5},{5,9},{9,... | collective-permute-start | bytes 55304 | tf_op jit(solution)/shard_map/ppermute | solution.py:58
  205.9 5.2 copy-start.27
  205.9 5.3 copy-start.32
  206.0 30.0 %all-to-all-start.2 = ((bf16[4,384,768]{2,1,0:T(8,128)(2,1)}), bf16[4,384,768]{2,1,0:T(8,128)(2,1)}, u32[]{:S(2)}, u32[]{:S(2)}) async-start(bf16[4,384,768]{2,1,0:T(8,128)(2,1)} %get-tuple-element.175), calls=%async_computation.2 | async-start | bytes 4718592 | tf_op jit(solution)/shard_map/all_to_all | solution.py:1291
  211.2 17.8 %copy-start.18 = (f32[256,16]{1,0:T(8,128)S(1)}, f32[256,16]{1,0:T(8,128)}, u32[]{:S(2)}) copy-start(f32[256,16]{1,0:T(8,128)} %get-tuple-element.172) | copy-start | bytes 49156
  236.0 53.0 %copy-start.9 = (bf16[320,256]{1,0:T(8,128)(2,1)S(1)}, bf16[320,256]{1,0:T(8,128)(2,1)}, u32[]{:S(2)}) copy-start(bf16[320,256]{1,0:T(8,128)(2,1)} %get-tuple-element.168.fill_ref) | copy-start | bytes 491524
  236.0 55.0 %copy-start.29 = (f32[256,1]{1,0:T(8,128)S(1)}, f32[256,1]{1,0:T(8,128)}, u32[]{:S(2)}) copy-start(f32[256,1]{1,0:T(8,128)} %get-tuple-element.170) | copy-start | bytes 3076
  288.9 3.6 copy-start.6
  288.9 3.6 copy-start.28
  293.9 55.4 %copy-start.2 = (f32[256,768]{1,0:T(8,128)S(1)}, f32[256,768]{1,0:T(8,128)}, u32[]{:S(2)}) copy-start(f32[256,768]{1,0:T(8,128)} %get-tuple-element.169) | copy-start | bytes 2359300
  293.9 55.4 %copy-start.10 = (bf16[320,256]{1,0:T(8,128)(2,1)S(1)}, bf16[320,256]{1,0:T(8,128)(2,1)}, u32[]{:S(2)}) copy-start(bf16[320,256]{1,0:T(8,128)(2,1)} %get-tuple-element.168.fill_ref) | copy-start | bytes 491524
  380.6 5.1 copy-start.34
  380.6 5.7 copy-start.43
  380.6 165.3 %all-to-all-start.3 = ((bf16[4,1536,384]{2,1,0:T(8,128)(2,1)}), bf16[4,1536,384]{2,1,0:T(8,128)(2,1)}, u32[]{:S(2)}, u32[]{:S(2)}) async-start(bf16[4,1536,384]{2,1,0:T(8,128)(2,1)} %get-tuple-element.231), calls=%async_computation.3 | async-start | bytes 9437184 | tf_op jit(solution)/shard_map/all_to_all | solution.py:1291
  385.6 297.5 %reduce-scatter.2.cloned.1.call-start = ((), (), s32[]{:S(2)}) async-start(), calls=%async_computation.6 | async-start | bytes 8110080 | tf_op jit(solution)/shard_map/reduce_scatter | solution.py:1875
  413.2 10.4 %copy-start.19 = (f32[256,16]{1,0:T(8,128)S(1)}, f32[256,16]{1,0:T(8,128)}, u32[]{:S(2)}) copy-start(f32[256,16]{1,0:T(8,128)} %get-tuple-element.172) | copy-start | bytes 49156
  413.2 10.4 %copy-start.26 = (bf16[256,768]{1,0:T(8,128)(2,1)S(1)}, bf16[256,768]{1,0:T(8,128)(2,1)}, u32[]{:S(2)}) copy-start(bf16[256,768]{1,0:T(8,128)(2,1)} %get-tuple-element.204) | copy-start | bytes 1179652
  413.2 26.3 %copy-start.42 = (f32[3]{0:T(128)S(1)}, f32[3]{0:T(128)}, u32[]{:S(2)}) copy-start(f32[3]{0:T(128)} %copy-done.41) | copy-start | bytes 40
  422.3 17.3 %collective-permute-start.2 = (f32[3,1536]{1,0:T(4,128)}, f32[3,1536]{1,0:T(4,128)S(1)}, u32[]{:S(2)}, u32[]{:S(2)}) collective-permute-start(f32[3,1536]{1,0:T(4,128)} %get-tuple-element.201), channel_id=1, source_target_pairs={{4,0},{8,4},{12,8},{16,12},{20,16},{24,20},{28,24},{5,1},{9,5},{13... | collective-permute-start | bytes 55304 | tf_op jit(solution)/shard_map/ppermute | solution.py:58
  453.3 2.1 copy-start.40
  545.9 5.4 copy-start.13
  546.0 130.7 %all-to-all-start.4 = ((bf16[4,1536,384]{2,1,0:T(8,128)(2,1)}), bf16[4,1536,384]{2,1,0:T(8,128)(2,1)}, u32[]{:S(2)}, u32[]{:S(2)}) async-start(bf16[4,1536,384]{2,1,0:T(8,128)(2,1)} %get-tuple-element.253), calls=%async_computation.5 | async-start | bytes 9437184 | tf_op jit(solution)/shard_map/all_to_all | solution.py:1291
  579.1 10.5 %copy-start.17 = (f32[256,16]{1,0:T(8,128)S(1)}, f32[256,16]{1,0:T(8,128)}, u32[]{:S(2)}) copy-start(f32[256,16]{1,0:T(8,128)} %get-tuple-element.154) | copy-start | bytes 49156
  579.1 10.5 %copy-start.25 = (bf16[256,768]{1,0:T(8,128)(2,1)S(1)}, bf16[256,768]{1,0:T(8,128)(2,1)}, u32[]{:S(2)}) copy-start(bf16[256,768]{1,0:T(8,128)(2,1)} %get-tuple-element.237) | copy-start | bytes 1179652
  588.2 18.7 %collective-permute-start.3 = (f32[3,1536]{1,0:T(4,128)}, f32[3,1536]{1,0:T(4,128)S(1)}, u32[]{:S(2)}, u32[]{:S(2)}) collective-permute-start(f32[3,1536]{1,0:T(4,128)} %get-tuple-element.230), channel_id=1, source_target_pairs={{4,0},{8,4},{12,8},{16,12},{20,16},{24,20},{28,24},{5,1},{9,5},{13... | collective-permute-start | bytes 55304 | tf_op jit(solution)/shard_map/ppermute | solution.py:58
  (8 other events, 11.2 us)
Sparse Core Ops, SparseCore 0:
  453.4 143.6 reduce-scatter.1

commit v5 on v4

--- a/solution.py
+++ b/solution.py
@@ -250,6 +250,56 @@
         turned = pltpu.roll(value_ref[steps - taps + 1 + j], 1, axis=0)
         extended[j] = jnp.where(place == 0, rim_ref[j : j + 1, :], turned)
     extended[taps - 1 :] = value_ref[...]
+
+
+def enter_kernel(first, gain_ref, weight_ref, *refs):
+    low = jnp.bfloat16
+    if first:
+        current_ref, tail_ref, normed_ref, projected_ref, rim_ref, before = refs
+    else:
+        middle_ref, share_ref, fill_ref, returned_ref, current_ref, taken_ref, normed_ref, projected_ref = refs
+
+    @pl.when(pl.program_id(0) == 0)
+    def _():
+        if first:
+            before[...] = rms_scale(tail_ref[...], gain_ref[...]).astype(low)
+        else:
+            taken = dot_tn(fill_ref[...], returned_ref[...])
+            taken_ref[...] = taken
+            current_ref[...] = middle_ref[...] + share_ref[...] * taken
+        normed_ref[...] = rms_scale(current_ref[...], gain_ref[...]).astype(low)
+
+    projected_ref[...] = dot_nn(normed_ref[...], weight_ref[...])
+    if first:
+        rim_ref[...] = dot_nn(before[...], weight_ref[...])
+
+
+def mixer_enter(layer, gain, in_weight, *arrays):
+    first = len(arrays) == 2
+    _, width, columns = in_weight.shape
+    tokens = arrays[0].shape[0]
+    span = 4 * LANES
+    low = jnp.bfloat16
+    normed = (whole((tokens, width)), shaped((tokens, width), low))
+    projected = (pl.BlockSpec((tokens, span), lambda c: (0, c)), shaped((tokens, columns)))
+    if first:
+        rows = arrays[1].shape[0]
+        outs = [normed, projected, (pl.BlockSpec((rows, span), lambda c: (0, c)), shaped((rows, columns)))]
+        scratch = [VMEM((rows, width), low)]
+    else:
+        full = (whole((tokens, width)), shaped((tokens, width)))
+        outs, scratch = [full, full, normed, projected], []
+    return plain_call(
+        functools.partial(enter_kernel, first),
+        (columns // span,),
+        [layer_whole(layer, (1, width)), pl.BlockSpec((None, width, span), lambda c: (layer, 0, c))]
+        + [whole(array.shape) for array in arrays],
+        [spec for spec, _ in outs],
+        [shape for _, shape in outs],
+        scratch,
+        (gain, in_weight) + arrays,
+        5,
+    )
 
 
 def front_kernel(dims, value_ref, rim_ref, mask_ref, reset_ref, conv_ref, conv_bias_ref, state_ref,
@@ -328,7 +378,7 @@
     return plain_call(
         functools.partial(front_kernel, (taps, rank, states, steps, channels)),
         (1,),
-        [value, whole(rim.shape), whole(masks.shape), whole(reset.shape),
+        [value, whole((rim.shape[0], channels)), whole(masks.shape), whole(reset.shape),
          layer_whole(layer, conv_weight.shape[1:]), layer_whole(layer, conv_bias.shape[1:]),
          layer_whole(layer, state_weight.shape[1:]), layer_whole(layer, step_weight.shape[1:]),
          layer_whole(layer, step_bias.shape[1:]), layer_whole(layer, decay_log.shape[1:])],
@@ -345,7 +395,8 @@
 
 def run_kernel(dims, size_ref, act_ref, selection_ref, reset_ref, decay_ref, link_ref, link_size_ref,
                entering_ref, gate_ref, skip_ref, out_weight_ref, current_ref, norm_ref, router_ref, fill_ref,
-               mixed_ref, gated_ref, begin_ref, middle_ref, routed_ref, logits_ref, outbound_ref,
+               onehot_ref, keep_ref,
+               mixed_ref, gated_ref, begin_ref, middle_ref, routed_ref, shares_ref, weight_ref, outbound_ref,
                in_maps, out_maps, pushed):
     rank, states, steps, tiles = dims
 
@@ -393,12 +444,16 @@
     def _():
         routed = rms_scale(middle_ref[...], norm_ref[...]).astype(jnp.bfloat16)
         routed_ref[...] = routed
-        logits_ref[...] = dot_nn(routed, router_ref[...])
+        logits = dot_nn(routed, router_ref[...])
+        raised = jnp.exp(logits - jnp.max(logits, axis=1, keepdims=True))
+        shares = raised / jnp.sum(raised, axis=1, keepdims=True)
+        shares_ref[...] = shares
+        weight_ref[...] = keep_ref[...] * jnp.sum(shares * onehot_ref[...], axis=1, keepdims=True)
         outbound_ref[...] = dot_nn(fill_ref[...], routed).astype(jnp.bfloat16)
 
 
 def mixer_run(layer, size, act, selection, reset, decay_log, link, link_size, entering, projected, skip_weight,
-              out_weight, current, norm_expert, router, fill):
+              out_weight, current, norm_expert, router, fill, onehot, keep):
     steps, _, channels = size.shape
     tokens = steps * CHUNKS
     states, width, experts = decay_log.shape[1], current.shape[1], router.shape[2]
@@ -412,9 +467,10 @@
         [slab(steps), rows_of(tokens), whole(selection.shape), whole(reset.shape),
          layer_rows(layer, states), slab(states), rows_of(CHUNKS), rows_of(states), slab(steps, tiles),
          layer_rows(layer, 1), layer_columns(layer, width), whole(current.shape),
-         layer_whole(layer, (1, width)), layer_whole(layer, (width, experts)), whole(fill.shape)],
+         layer_whole(layer, (1, width)), layer_whole(layer, (width, experts)), whole(fill.shape),
+         whole(onehot.shape), whole(keep.shape)],
         [slab(steps), rows_of(tokens), slab(states), whole((tokens, width)), whole((tokens, width)),
-         whole((tokens, experts)), whole((fill.shape[0], width))],
+         whole((tokens, experts)), whole((tokens, 1)), whole((fill.shape[0], width))],
         [
             shaped((steps, CHUNKS, channels)),
             shaped((tokens, channels), low),
@@ -422,11 +478,12 @@
             shaped((tokens, width)),
             shaped((tokens, width), low),
             shaped((tokens, experts)),
+            shaped((tokens, 1)),
             shaped((fill.shape[0], width), low),
         ],
         [maps, maps, VMEM((steps, CHUNKS, TILE), jnp.float32)],
         (size, act, selection, reset, decay_log, link, link_size, entering, projected, skip_weight, out_weight,
-         current, norm_expert, router, fill),
+         current, norm_expert, router, fill, onehot, keep),
         22,
     )
 
@@ -965,21 +1022,22 @@
     return 0.5 * (1.0 + lax.erf(values * 0.7071067811865476))
 
 
-def expert_kernel(dims, backward, beside, which, *refs):
+def expert_kernel(dims, kinds, beside, which, *refs):
     count, groups, members, block, share, width, hidden = dims
-    out_ref, perm_ref, up_hbm, down_hbm, *refs = refs
-    if backward:
+    flows = len(kinds)
+    out_refs, (perm_ref, up_hbm, down_hbm, *refs) = refs[:flows], refs[flows:]
+    if kinds == (True,):
         pre_hbm, *refs = refs
     if beside:
         next_hbm, *refs = refs
-    ret_ref, rows_hbm, *refs = refs
-    if not backward:
+    results, refs = [refs[3 * f : 3 * f + 3] for f in range(flows)], refs[3 * flows :]
+    if kinds == (False,):
         pre_hbm, *refs = refs
-    low_hbm, *scratch = refs
     if beside:
-        met_hbm, *scratch, leaving, met, next_send, next_recv, next_local = scratch
-    (arrived, own, rows, pre, low, part, got, final, landed, up, down, total,
-     there_send, there_recv, row_send, row_recv, sum_send, sum_recv, back_send, back_recv, local) = scratch
+        met_hbm, *refs = refs
+        *refs, leaving, met, next_send, next_recv, next_local = refs
+    pre, up, down, total, local, *refs = refs
+    scratch = [refs[16 * f : 16 * f + 16] for f in range(flows)]
     f32, bf16 = jnp.float32, jnp.bfloat16
     here = lax.axis_index("wide")
     group = lax.axis_index("narrow")
@@ -991,12 +1049,13 @@
     others = [(2 * away + c, 2 * lax.rem(line + away, lines) + c) for away in range(1, lines) for c in (0, 1)]
     early = 2 * (share // groups) // 16 * 16
     head, tail = pl.ds(0, early), pl.ds(early, share - early)
+    ways = [(away, turn) for turn in range(members) for away in list(range(1, quads)) + [0] if away or turn]
 
     loads = [
         pltpu.make_async_copy(up_hbm, up, local.at[0]),
         pltpu.make_async_copy(down_hbm, down, local.at[1]),
     ]
-    if backward:
+    if kinds == (True,):
         loads.append(pltpu.make_async_copy(pre_hbm, pre, local.at[2]))
     for load in loads:
         load.start()
@@ -1007,6 +1066,10 @@
 
     def window_at(away, turn):
         return lax.rem(quad + away, quads) * members + lax.rem(member + turn, members)
+
+    def span(window, part=None):
+        start, size = (0, share) if part is None else ((0, early), (early, share - early))[part]
+        return pl.ds(pl.multiple_of(window * share + start, 16), size)
 
     barrier = pltpu.get_barrier_semaphore()
     for peer in [near_group] + [other for _, other in others]:
@@ -1017,8 +1080,8 @@
                 pl.semaphore_signal(
                     barrier, inc=1, device_id=(window_at(away, turn), group), device_id_type=MESH)
     pl.semaphore_wait(barrier, groups - 1 + count - 1)
-
-    there = []
+    order = perm_ref[...].reshape(members, share, groups * block)
+    sent, saves = [], []
 
     def hand_over(k, source, target, send, recv):
         if k:
@@ -1031,53 +1094,174 @@
             src_ref=source, dst_ref=target.at[landing], send_sem=send.at[k], recv_sem=recv.at[signal],
             device_id=(here, peer), device_id_type=MESH)
         copy.start()
-        return copy
-
-    def taken(k, target, send, recv):
+        sent.append(copy)
+
+    def taken(k, like, target, send, recv):
         pltpu.make_async_remote_copy(
-            src_ref=out_ref.at[group], dst_ref=target.at[0], send_sem=send.at[k], recv_sem=recv.at[k],
+            src_ref=like, dst_ref=target.at[0], send_sem=send.at[k], recv_sem=recv.at[k],
             device_id=(here, near_group), device_id_type=MESH).wait_recv()
 
-    there = [hand_over(0, out_ref.at[near_group], arrived, there_send, there_recv)]
-    for k, (_, other) in enumerate(others):
-        there.append(hand_over(1 + k, out_ref.at[other], arrived, there_send, there_recv))
-    arrived[core] = out_ref[group]
-
-    def span(window, part=None):
-        start, size = (0, share) if part is None else ((0, early), (early, share - early))[part]
-        return pl.ds(pl.multiple_of(window * share + start, 16), size)
-
-    sent = []
-    ways = [(away, turn) for turn in range(members) for away in list(range(1, quads)) + [0] if away or turn]
-
-    def carry(away, turn, part):
-        window = window_at(away, turn)
-        copy = pltpu.make_async_remote_copy(
-            src_ref=own.at[lax.rem(member + turn, members), (head, tail)[part]],
-            dst_ref=rows.at[span(here, part), :],
-            send_sem=row_send.at[away, turn, part], recv_sem=row_recv.at[away, turn, part],
-            device_id=(window, group), device_id_type=MESH)
-        copy.start()
-        sent.append(copy)
-
-    taken(0, arrived, there_send, there_recv)
-    order = perm_ref[...].reshape(members, share, groups * block)
-    first = arrived[pl.ds(0, 2)].reshape(2 * block, width)
-    own[:, head] = dot_nn(
-        order[:, :early, : 2 * block].reshape(members * early, 2 * block), first
-    ).astype(bf16).reshape(members, early, width)
-    for away, turn in ways:
-        carry(away, turn, 0)
-    for k in range(1, groups - 1):
-        taken(k, arrived, there_send, there_recv)
-    own[:, tail] = dot_nn(
-        order[:, early:].reshape(members * (share - early), groups * block),
-        arrived[...].reshape(groups * block, width),
-    ).astype(bf16).reshape(members, share - early, width)
-    for away, turn in ways:
-        carry(away, turn, 1)
-    rows[span(here), :] = own[member]
-    beside_copies = []
+    class Flow:
+        def __init__(self, backward, out_ref, result, scratch):
+            self.backward, self.out_ref = backward, out_ref
+            self.ret_ref, self.rows_hbm, self.low_hbm = result
+            (self.arrived, self.own, self.rows, self.low, self.part, self.got, self.final, self.landed,
+             self.there_send, self.there_recv, self.row_send, self.row_recv, self.sum_send, self.sum_recv,
+             self.back_send, self.back_recv) = scratch
+
+        def to_groups(self):
+            there = self.there_send, self.there_recv
+            hand_over(0, self.out_ref.at[near_group], self.arrived, *there)
+            for k, (_, other) in enumerate(others):
+                hand_over(1 + k, self.out_ref.at[other], self.arrived, *there)
+            self.arrived[core] = self.out_ref[group]
+
+        def carry(self, part):
+            for away, turn in ways:
+                copy = pltpu.make_async_remote_copy(
+                    src_ref=self.own.at[lax.rem(member + turn, members), (head, tail)[part]],
+                    dst_ref=self.rows.at[span(here, part), :],
+                    send_sem=self.row_send.at[away, turn, part], recv_sem=self.row_recv.at[away, turn, part],
+                    device_id=(window_at(away, turn), group), device_id_type=MESH)
+                copy.start()
+                sent.append(copy)
+
+        def to_experts(self):
+            there = self.there_send, self.there_recv
+            taken(0, self.out_ref.at[group], self.arrived, *there)
+            first = self.arrived[pl.ds(0, 2)].reshape(2 * block, width)
+            self.own[:, head] = dot_nn(
+                order[:, :early, : 2 * block].reshape(members * early, 2 * block), first
+            ).astype(bf16).reshape(members, early, width)
+            self.carry(0)
+            for k in range(1, groups - 1):
+                taken(k, self.out_ref.at[group], self.arrived, *there)
+            self.own[:, tail] = dot_nn(
+                order[:, early:].reshape(members * (share - early), groups * block),
+                self.arrived[...].reshape(groups * block, width),
+            ).astype(bf16).reshape(members, share - early, width)
+            self.carry(1)
+            self.rows[span(here), :] = self.own[member]
+
+        def arrive(self, away, turn):
+            window = lax.rem(quad + quads - away, quads) * members + lax.rem(member + members - turn, members)
+            for part in (0, 1):
+                pltpu.make_async_remote_copy(
+                    src_ref=self.own.at[member, (head, tail)[part]], dst_ref=self.rows.at[span(window, part), :],
+                    send_sem=self.row_send.at[away, turn, part], recv_sem=self.row_recv.at[away, turn, part],
+                    device_id=(window, group), device_id_type=MESH).wait_recv()
+            return window
+
+        def compute(self, windows):
+            size = len(windows) * share
+
+            def one(s, carry):
+                x = jnp.concatenate([self.rows[span(w), :] for w in windows], axis=0)
+                if self.backward:
+                    grad_hidden = dot_nt(x, down[s])
+                    before = jnp.concatenate([pre[s, span(w), :] for w in windows], axis=0)
+                    slope = bell(before) + before * (
+                        0.3989422804014327 * jnp.exp(-0.5 * before * before))
+                    middle = (grad_hidden * slope).astype(bf16)
+                    y = dot_nt(middle, up[s])
+                else:
+                    before = dot_nn(x, up[s])
+                    middle = (before * bell(before)).astype(bf16)
+                    y = dot_nn(middle, down[s])
+                for index, w in enumerate(windows):
+                    piece = slice(index * share, (index + 1) * share)
+                    if not self.backward:
+                        pre[s, span(w), :] = before[piece]
+                    self.low[s, span(w), :] = middle[piece]
+
+                @pl.when(s == 0)
+                def _():
+                    total[:size] = y
+
+                @pl.when(s > 0)
+                def _():
+                    total[:size] += y
+
+                return carry
+
+            lax.fori_loop(0, members, one, 0)
+            for index, w in enumerate(windows):
+                self.part[w] = total[index * share : (index + 1) * share].astype(bf16)
+
+        def give_back(self, away, turn, window, part):
+            copy = pltpu.make_async_remote_copy(
+                src_ref=self.part.at[window, (head, tail)[part]], dst_ref=self.got.at[here, (head, tail)[part]],
+                send_sem=self.sum_send.at[away, turn, part], recv_sem=self.sum_recv.at[away, turn, part],
+                device_id=(window, group), device_id_type=MESH)
+            copy.start()
+            sent.append(copy)
+
+        def work(self, first_save):
+            windows = [here] + [self.arrive(0, turn) for turn in range(1, members)]
+            self.compute(windows)
+            for part in (1, 0):
+                for turn in range(1, members):
+                    self.give_back(0, turn, windows[turn], part)
+            self.got[here] = self.part[here]
+            late = []
+            for away in range(1, quads):
+                for first in range(0, members, 2):
+                    windows = [self.arrive(away, turn) for turn in (first, first + 1)]
+                    self.compute(windows)
+                    for turn in (first, first + 1):
+                        self.give_back(away, turn, windows[turn - first], 1)
+                        late.append((away, turn, windows[turn - first]))
+            for away, turn, window in late:
+                self.give_back(away, turn, window, 0)
+            for k, (source, target) in enumerate(((self.rows, self.rows_hbm), (self.low, self.low_hbm))):
+                saves.append(pltpu.make_async_copy(source, target, local.at[first_save + k]))
+                saves[-1].start()
+
+        def returned(self, part):
+            place = (head, tail)[part]
+            for away, turn in ways:
+                window = window_at(away, turn)
+                pltpu.make_async_remote_copy(
+                    src_ref=self.part.at[here, place], dst_ref=self.got.at[window, place],
+                    send_sem=self.sum_send.at[away, turn, part], recv_sem=self.sum_recv.at[away, turn, part],
+                    device_id=(window, group), device_id_type=MESH).wait_recv()
+            summed = self.got[pl.ds(0, members), place].astype(f32)
+            for q in range(1, quads):
+                summed = summed + self.got[pl.ds(q * members, members), place].astype(f32)
+            return summed.astype(bf16)
+
+        def leave(self):
+            back = self.back_send, self.back_recv
+            later = self.returned(1)
+            rest = groups - 2
+            self.final[pl.ds(2, rest)] = dot_tn(
+                order[:, early:, 2 * block :].reshape(members * (share - early), rest * block),
+                later.reshape(members * (share - early), width),
+            ).astype(bf16).reshape(rest, block, width)
+            for k, (place, _) in enumerate(others):
+                hand_over(1 + k, self.final.at[place], self.landed, *back)
+            sooner = self.returned(0)
+            self.final[pl.ds(0, 2)] = (
+                dot_tn(order[:, :early, : 2 * block].reshape(members * early, 2 * block),
+                       sooner.reshape(members * early, width))
+                + dot_tn(order[:, early:, : 2 * block].reshape(members * (share - early), 2 * block),
+                         later.reshape(members * (share - early), width))
+            ).astype(bf16).reshape(2, block, width)
+            hand_over(0, self.final.at[1 - core], self.landed, *back)
+            self.ret_ref[group] = self.final[core]
+
+        def land(self):
+            for k in range(groups - 1):
+                taken(k, self.out_ref.at[group], self.landed, self.back_send, self.back_recv)
+            self.ret_ref[near_group] = self.landed[1 - core]
+            for place, other in others:
+                self.ret_ref[other] = self.landed[place]
+
+    travels = [Flow(*parts) for parts in zip(kinds, out_refs, results, scratch)]
+    for flow in travels:
+        flow.to_groups()
+    for flow in travels:
+        flow.to_experts()
 
     def send_beside(turns):
         for turn in turns if beside else ():
@@ -1088,146 +1272,37 @@
             copy.start()
             beside_copies.append(copy)
 
+    beside_copies = []
     if beside:
         next_load.wait()
         met[member] = leaving[member]
     send_beside([1])
-
-    def arrive(away, turn):
-        window = lax.rem(quad + quads - away, quads) * members + lax.rem(member + members - turn, members)
-        for part in (0, 1):
-            pltpu.make_async_remote_copy(
-                src_ref=own.at[member, (head, tail)[part]], dst_ref=rows.at[span(window, part), :],
-                send_sem=row_send.at[away, turn, part], recv_sem=row_recv.at[away, turn, part],
-                device_id=(window, group), device_id_type=MESH).wait_recv()
-        return window
-
-    def compute(windows):
-        size = len(windows) * share
-
-        def one(s, carry):
-            x = jnp.concatenate([rows[span(w), :] for w in windows], axis=0)
-            if backward:
-                grad_hidden = dot_nt(x, down[s])
-                before = jnp.concatenate([pre[s, span(w), :] for w in windows], axis=0)
-                slope = bell(before) + before * (0.3989422804014327 * jnp.exp(-0.5 * before * before))
-                middle = (grad_hidden * slope).astype(bf16)
-                y = dot_nt(middle, up[s])
-            else:
-                before = dot_nn(x, up[s])
-                middle = (before * bell(before)).astype(bf16)
-                y = dot_nn(middle, down[s])
-            for index, w in enumerate(windows):
-                piece = slice(index * share, (index + 1) * share)
-                if not backward:
-                    pre[s, span(w), :] = before[piece]
-                low[s, span(w), :] = middle[piece]
-
-            @pl.when(s == 0)
-            def _():
-                total[:size] = y
-
-            @pl.when(s > 0)
-            def _():
-                total[:size] += y
-
-            return carry
-
-        lax.fori_loop(0, members, one, 0)
-        for index, w in enumerate(windows):
-            part[w] = total[index * share : (index + 1) * share].astype(bf16)
-
-    def give_back(away, turn, window, part):
-        copy = pltpu.make_async_remote_copy(
-            src_ref=part_rows(window, part), dst_ref=got.at[here, (head, tail)[part]],
-            send_sem=sum_send.at[away, turn, part], recv_sem=sum_recv.at[away, turn, part],
-            device_id=(window, group), device_id_type=MESH)
-        copy.start()
-        sent.append(copy)
-
-    def part_rows(window, which):
-        return part.at[window, (head, tail)[which]]
-
     for load in loads:
         load.wait()
-    windows = [here] + [arrive(0, turn) for turn in range(1, members)]
-    compute(windows)
-    for which in (1, 0):
-        for turn in range(1, members):
-            give_back(0, turn, windows[turn], which)
-    got[here] = part[here]
-    late = []
-    for away in range(1, quads):
-        for first in range(0, members, 2):
-            windows = [arrive(away, turn) for turn in (first, first + 1)]
-            compute(windows)
-            for turn in (first, first + 1):
-                give_back(away, turn, windows[turn - first], 1)
-                late.append((away, turn, windows[turn - first]))
-    for away, turn, window in late:
-        give_back(away, turn, window, 0)
+    for f, flow in enumerate(travels):
+        flow.work(3 + 2 * f)
     send_beside(range(2, members))
-
-    saves = [
-        pltpu.make_async_copy(rows, rows_hbm, local.at[3]),
-        pltpu.make_async_copy(low, low_hbm, local.at[4]),
-    ]
-    if not backward:
+    if kinds == (False,):
         saves.append(pltpu.make_async_copy(pre, pre_hbm, local.at[2]))
-    for save in saves:
-        save.start()
-
-    def returned(which):
-        for away, turn in ways:
-            window = window_at(away, turn)
-            pltpu.make_async_remote_copy(
-                src_ref=part_rows(here, which), dst_ref=got.at[window, (head, tail)[which]],
-                send_sem=sum_send.at[away, turn, which], recv_sem=sum_recv.at[away, turn, which],
-                device_id=(window, group), device_id_type=MESH).wait_recv()
-        place = (head, tail)[which]
-        summed = got[pl.ds(0, members), place].astype(f32)
-        for q in range(1, quads):
-            summed = summed + got[pl.ds(q * members, members), place].astype(f32)
-        return summed.astype(bf16)
-
-    later = returned(1)
-    rest = groups - 2
-    final[pl.ds(2, rest)] = dot_tn(
-        order[:, early:, 2 * block :].reshape(members * (share - early), rest * block),
-        later.reshape(members * (share - early), width),
-    ).astype(bf16).reshape(rest, block, width)
-    home = []
-    for k, (place, _) in enumerate(others):
-        home.append(hand_over(1 + k, final.at[place], landed, back_send, back_recv))
-    sooner = returned(0)
-    final[pl.ds(0, 2)] = (
-        dot_tn(order[:, :early, : 2 * block].reshape(members * early, 2 * block),
-               sooner.reshape(members * early, width))
-        + dot_tn(order[:, early:, : 2 * block].reshape(members * (share - early), 2 * block),
-                 later.reshape(members * (share - early), width))
-    ).astype(bf16).reshape(2, block, width)
-    home.append(hand_over(0, final.at[1 - core], landed, back_send, back_recv))
-    ret_ref[group] = final[core]
-    for k in range(groups - 1):
-        taken(k, landed, back_send, back_recv)
-    ret_ref[near_group] = landed[1 - core]
-    for place, other in others:
-        ret_ref[other] = landed[place]
+        saves[-1].start()
+    for flow in travels:
+        flow.leave()
+    for flow in travels:
+        flow.land()
     if beside:
         for copy in beside_copies:
             copy.wait_recv()
         saves.append(pltpu.make_async_copy(met, met_hbm, next_local.at[1]))
         saves[-1].start()
-    for copy in there + sent + home + beside_copies:
+    for copy in sent + beside_copies:
         copy.wait_send()
     for save in saves:
         save.wait()
 
 
-def expert_pass(outbound, perm, weights, pre, identity, beside=None, which=None):
+def expert_pass(outbounds, kinds, perm, weights, pre, identity, beside=None, which=None):
     count, groups = lax.axis_size("wide"), lax.axis_size("narrow")
-    backward = pre is not None
-    _, block, width = outbound.shape
+    _, block, width = outbounds[0].shape
     members, _, hidden = weights[0].shape
     share = perm.shape[0] // members
     quads = count // members
@@ -1235,40 +1310,49 @@
     low, f32 = jnp.bfloat16, jnp.float32
     dims = (count, groups, members, block, share, width, hidden)
     inside = pl.BlockSpec(memory_space=VMEM)
-    args = (outbound, perm) + tuple(weights) + ((pre,) if backward else ())
+    args = tuple(outbounds) + (perm,) + tuple(weights) + (() if pre is None else (pre,))
     args += () if beside is None else (beside,)
-    outs = [shaped((groups, block, width), low), shaped((total, width), low)]
-    outs += ([] if backward else [shaped((members, total, hidden))]) + [shaped((members, total, hidden), low)]
+    out_specs, outs = [], []
+    for _ in kinds:
+        out_specs += [inside, ANYWHERE, ANYWHERE]
+        outs += [shaped((groups, block, width), low), shaped((total, width), low),
+                 shaped((members, total, hidden), low)]
+    if kinds == (False,):
+        outs.append(shaped((members, total, hidden)))
     dma = pltpu.SemaphoreType.DMA
-    more = []
-    if beside is not None:
-        shape = beside.shape[-3:]
-        outs.append(shaped(shape, low))
-        more = [VMEM(shape, low), VMEM(shape, low), dma((members,)), dma((members,)), dma((2,))]
-    return pl.pallas_call(
-        functools.partial(expert_kernel, dims, backward, beside is not None, which),
-        out_shape=outs,
-        in_specs=[inside, inside] + [ANYWHERE] * (len(args) - 2),
-        out_specs=[inside] + [ANYWHERE] * (len(outs) - 1),
-        scratch_shapes=[
+    scratch = [
+        VMEM((members, total, hidden), f32),
+        VMEM((members, width, hidden), low),
+        VMEM((members, hidden, width), low),
+        VMEM((members * share, width), f32),
+        dma((3 + 2 * len(kinds),)),
+    ]
+    for _ in kinds:
+        scratch += [
             VMEM((groups, block, width), low),
             VMEM((members, share, width), low),
             VMEM((total, width), low),
-            VMEM((members, total, hidden), f32),
             VMEM((members, total, hidden), low),
             VMEM((count, share, width), low),
             VMEM((count, share, width), low),
             VMEM((groups, block, width), low),
             VMEM((groups, block, width), low),
-            VMEM((members, width, hidden), low),
-            VMEM((members, hidden, width), low),
-            VMEM((members * share, width), f32),
             dma((groups - 1,)), dma((groups - 1,)),
             dma((quads, members, 2)), dma((quads, members, 2)),
             dma((quads, members, 2)), dma((quads, members, 2)),
             dma((groups - 1,)), dma((groups - 1,)),
-            dma((5,)),
-        ] + more,
+        ]
+    if beside is not None:
+        shape = beside.shape[-3:]
+        outs.append(shaped(shape, low))
+        scratch += [VMEM(shape, low), VMEM(shape, low), dma((members,)), dma((members,)), dma((2,))]
+    out_specs += [ANYWHERE] * (len(outs) - len(out_specs))
+    return pl.pallas_call(
+        functools.partial(expert_kernel, dims, tuple(kinds), beside is not None, which),
+        out_shape=outs,
+        in_specs=[inside] * (len(kinds) + 1) + [ANYWHERE] * (len(args) - len(kinds) - 1),
+        out_specs=out_specs,
+        scratch_shapes=scratch,
         compiler_params=pltpu.CompilerParams(
             collective_id=identity, has_side_effects=True, vmem_limit_bytes=60 * MIB
         ),
@@ -1580,9 +1664,10 @@
     )(*[array.reshape(count, lines, 2, array.shape[1], width) for array in arrays])
 
 
-def inward_kernel(dims, grad_ref, weight_ref, edge_ref, handed_ref, normed_ref, begin_ref, gain_ref, passed_ref,
-                  out_ref, channel_ref, router_ref, expert_ref, packed_ref, new_ref, rows, features, held_block):
+def inward_kernel(dims, grad_ref, weight_ref, edge_ref, handed_ref, keep_ref, normed_ref, begin_ref, gain_ref,
+                  passed_ref, out_ref, channel_ref, router_ref, expert_ref, packed_ref, new_ref, *refs):
     blocks, wide, tall, held, fold, marks, spare, steps = dims
+    *turned_ref, rows, features, held_block = refs
     owners, count, _ = packed_ref.shape
     f32, low = jnp.float32, jnp.bfloat16
     step = pl.program_id(0)
@@ -1593,7 +1678,7 @@
 
     @pl.when(lax.rem(step, blocks) < blocks // 2)
     def _():
-        edge = edge_ref[...] + handed_ref[...]
+        edge = edge_ref[...] + handed_ref[...] * keep_ref[...]
         ends = grad_ref[tokens - edited :, :].astype(f32)
         place = lax.broadcasted_iota(jnp.int32, ends.shape, 0)
         for j in range(last):
@@ -1616,6 +1701,10 @@
     def _():
         grad, norm_grad = rms_back(begin_ref[...], gain_ref[...], new_ref[...])
         new_ref[...] = passed_ref[...] + grad
+        if turned_ref:
+            by_step = new_ref[...].reshape(steps, CHUNKS, grad.shape[1])
+            for chunk in range(CHUNKS):
+                turned_ref[0][chunk * steps : (chunk + 1) * steps, :] = by_step[:, chunk, :]
         experts = router_ref.shape[1]
         lane = lax.broadcasted_iota(jnp.int32, (experts, 2 * LANES), 1)
         row = lax.broadcasted_iota(jnp.int32, (experts, 2 * LANES), 0)
@@ -1652,7 +1741,7 @@
             packed_ref[...] = rows[...].astype(low)
 
 
-def mixer_inward(layer, grad_projected, in_weight, edge, handed, normed, begin, gain, passed, grad_out, channel,
+def mixer_inward(layer, grad_projected, in_weight, edge, handed, keep, normed, begin, gain, passed, grad_out, channel,
                  grad_router, grad_expert, devices, spare):
     tokens, columns = grad_projected.shape
     width = normed.shape[1]
@@ -1666,6 +1755,7 @@
     span = owners * wide
     taps = edge.shape[0]
     inner = edge.shape[1] // span
+    turned = layer == 0
 
     def at(i):
         return jnp.maximum(i - blocks, 0)
@@ -1677,15 +1767,17 @@
          pl.BlockSpec((None, width, span), lambda i: (layer, 0, jnp.minimum(i, blocks - 1))),
          pl.BlockSpec((taps, span), lambda i: (0, jnp.minimum(i % blocks, inner - 1))),
          pl.BlockSpec((taps, span), lambda i: (0, jnp.minimum(i % blocks, inner - 1))),
-         whole(normed.shape), whole(begin.shape), layer_whole(layer, (1, width)), whole(passed.shape),
+         whole(keep.shape), whole(normed.shape), whole(begin.shape), layer_whole(layer, (1, width)), whole(passed.shape),
          pl.BlockSpec((owners * tall, width), lambda i: (at(i), 0)),
          pl.BlockSpec((owners * held, 2 * LANES), lambda i: (at(i), 0)),
          whole(grad_router.shape), whole(grad_expert.shape)],
-        [pl.BlockSpec((owners, count, width), lambda i: (at(i), 0, 0)), whole((tokens, width))],
-        [shaped((devices, count, width), jnp.bfloat16), shaped((tokens, width))],
+        [pl.BlockSpec((owners, count, width), lambda i: (at(i), 0, 0)), whole((tokens, width))]
+        + turned * [whole((tokens, width))],
+        [shaped((devices, count, width), jnp.bfloat16), shaped((tokens, width))]
+        + turned * [shaped((tokens, width))],
         [VMEM((owners, count, width), jnp.float32), VMEM((width, 2 * LANES), jnp.float32),
          VMEM((tokens, span), jnp.bfloat16)],
-        (grad_projected, in_weight, edge, handed, normed, begin, gain, passed, grad_out, channel, grad_router,
+        (grad_projected, in_weight, edge, handed, keep, normed, begin, gain, passed, grad_out, channel, grad_router,
          grad_expert),
         9,
     )
@@ -1795,14 +1887,17 @@
         doc_start, expert_choice, slot_index, taps, experts, groups, block, capacity)
 
     for layer in range(layers):
+        if layer == 0:
+            normed, projected, rim = mixer_enter(layer, norm_mix, in_weight, current, tail.astype(f32))
+            projected = cube(projected)
+        else:
+            current, back_rows, normed, projected = mixer_enter(
+                layer, norm_mix, in_weight, middle, weight, fills[layer - 1],
+                returned.reshape(groups * block, width))
+            saved[-1]["back_rows"] = back_rows
+            projected = cube(projected)
+            rim = passed_along(projected[steps - taps + 1 :, CHUNKS - 1, :inner] * keep_mask, 1)
         begin = current
-        normed = rms_scale(current, norm_mix[layer]).astype(low)
-        projected = cube(dot_nn(normed, in_weight[layer]))
-        if layer == 0:
-            before = rms_scale(tail.astype(f32), norm_mix[layer]).astype(low)
-            rim = dot_nn(before, in_weight[layer, :, :inner])
-        else:
-            rim = passed_along(projected[steps - taps + 1 :, CHUNKS - 1, :inner] * keep_mask, 1)
         act, selection, size, link, link_size, total, total_size = mixer_front(
             layer, projected, rim, masks, reset, conv_weight, conv_bias, state_weight, step_weight, step_bias,
             decay_log)
@@ -1810,24 +1905,29 @@
             total, order = lax.optimization_barrier((total, order))
         entering, ready = handed_ahead(layer, total, total_size, decay_log, [(expert_down, layer)], layer)
         weights[layer] += between_members([ready])
-        mixed, gated, begins, middle, routed, logits, outbound = mixer_run(
+        mixed, gated, begins, middle, routed, shares, weight, outbound = mixer_run(
             layer, size, act, selection, reset, decay_log, link, link_size, entering, projected, skip_weight,
-            out_weight, current, norm_expert, router, fills[layer])
-        returned, kept_rows, pre_act, hidden_low, *following = expert_pass(
-            outbound.reshape(groups, block, width), order, weights[layer], None, 4 + layer,
-            expert_up if layer + 1 < layers else None, layer + 1)
-        if following:
-            weights[layer + 1] = following
-        shares = jax.nn.softmax(logits, axis=-1)
-        gate = jnp.sum(shares * onehots[layer], axis=1, keepdims=True)
-        back_rows = dot_tn(fills[layer], returned.reshape(groups * block, width))
-        current = middle + (keeps[layer] * gate) * back_rows
+            out_weight, current, norm_expert, router, fills[layer], onehots[layer], keeps[layer])
+        pre_act = None
+        outbound = outbound.reshape(groups, block, width)
+        if layer + 1 < layers:
+            returned, kept_rows, hidden_low, pre_act, following = expert_pass(
+                [outbound], (False,), order, weights[layer], None, 4 + layer, expert_up, layer + 1)
+            weights[layer + 1] = [following]
+        else:
+            grad = to_steps(cotangent[0]).reshape(tokens, width).astype(f32)
+            grad_rows_low = (weight * grad).astype(low)
+            returning = dot_nn(fills[layer], grad_rows_low).astype(low).reshape(groups, block, width)
+            returned, kept_rows, hidden_low, inbound, grad_rows, grad_pre = expert_pass(
+                [outbound, returning], (False, True), order, weights[layer], None, 4 + layer)
         saved.append(dict(
             begin=begin, normed=normed, projected=projected, rim=rim, act=act, selection=selection, size=size,
-            begins=begins, mixed=mixed, gated=gated, middle=middle, routed=routed, shares=shares, gate=gate,
-            kept_rows=kept_rows, pre_act=pre_act, hidden_low=hidden_low, back_rows=back_rows))
+            begins=begins, mixed=mixed, gated=gated, middle=middle, routed=routed, shares=shares, weight=weight,
+            kept_rows=kept_rows, pre_act=pre_act, hidden_low=hidden_low))
+    back_rows = dot_tn(fills[-1], returned.reshape(groups * block, width))
+    saved[-1]["back_rows"] = back_rows
+    current = middle + weight * back_rows
     output = to_tokens(cube(current.astype(low)))[None]
-    grad = to_steps(cotangent[0]).reshape(tokens, width).astype(f32)
     sums = [None] * layers
     wide_grads = ()
     expert_grads = [None] * layers
@@ -1836,14 +1936,15 @@
     spare = 160
     for layer in range(layers - 1, -1, -1):
         entry = saved[layer]
-        fill, keep, gate = fills[layer], keeps[layer], entry["gate"]
-        grad_rows_low = ((keep * gate) * grad).astype(low)
-        grad_gate = keep * jnp.sum(grad * entry["back_rows"], axis=1, keepdims=True)
-        outbound = dot_nn(fill, grad_rows_low).astype(low).reshape(groups, block, width)
-        inbound, grad_rows, grad_pre = expert_pass(
-            outbound, order, weights[layer], entry["pre_act"], 6 + layer)
+        fill, weight = fills[layer], entry["weight"]
+        weighted = weight * jnp.sum(grad * entry["back_rows"], axis=1, keepdims=True)
+        if layer + 1 < layers:
+            grad_rows_low = (weight * grad).astype(low)
+            outbound = dot_nn(fill, grad_rows_low).astype(low).reshape(groups, block, width)
+            inbound, grad_rows, grad_pre = expert_pass(
+                [outbound], (True,), order, weights[layer], entry["pre_act"], 6 + layer)
         grad_sent = dot_tn(fill, inbound.reshape(groups * block, width))
-        grad_logits_low = ((grad_gate * gate) * (onehots[layer] - entry["shares"])).astype(low)
+        grad_logits_low = (weighted * (onehots[layer] - entry["shares"])).astype(low)
         grad_router = dot_tn(entry["routed"], grad_logits_low)
         grad_routed = grad_sent + dot_nt(grad_logits_low, router[layer])
         grad_middle, grad_norm_expert = rms_back(entry["middle"], norm_expert[layer], grad_routed)
@@ -1862,12 +1963,12 @@
         grad_projected, edge, rim_grad, channel = mixer_conv_back(
             layer, grad_act, grad_selection, state_weight, entry["projected"], entry["rim"], masks, conv_weight,
             conv_bias, entry["act"], grad_step, grad_decay, grad_bias, grad_skip, grad_igate)
-        handed = passed_along(rim_grad, -1) * keep_mask
+        handed = passed_along(rim_grad, -1)
         if layer + 1 < layers:
             wide_grads = widened(layer + 1, layers, expert_grads[layer + 1], width, expert_up.shape[3], wide_grads)
-            handed, *wide_grads = lax.optimization_barrier((handed, *wide_grads))
-        blocks, grad = mixer_inward(
-            layer, grad_projected, in_weight, edge, handed, entry["normed"], entry["begin"], norm_mix, grad,
+            edge, *wide_grads = lax.optimization_barrier((edge, *wide_grads))
+        blocks, grad, *turned = mixer_inward(
+            layer, grad_projected, in_weight, edge, handed, keep_mask, entry["normed"], entry["begin"], norm_mix, grad,
             grad_out, channel, grad_router, grad_norm_expert.reshape(1, width), devices, spare)
         if layer:
             blocks, grad = lax.optimization_barrier((blocks, grad))
@@ -1884,7 +1985,7 @@
         grad_norm_mix, jnp.swapaxes(grad_in, 1, 2), grad_conv, grad_conv_bias, grad_state, grad_step,
         grad_step_bias, grad_decay, grad_skip, grad_out, grad_norm_expert, jnp.swapaxes(grad_router, 1, 2))
     up_grads, down_grads = widened(0, layers, expert_grads[0], width, expert_up.shape[3], wide_grads)
-    output_grad = to_tokens(cube(grad))[None]
+    output_grad = turned[0][None]
     return (output, output_grad, *shared, up_grads, down_grads)
 
 

time: 699 us -> 676 us (0.967)
  matrix products: 27.1 us -> 9.19 us
  other arithmetic: 18.8 us -> 10.2 us
    pallas_call x14 -> x16, Pallas kernels: 196 us -> 213 us  [plain_call(): pl.pallas_call(kernel, grid=grid, in_specs=in_specs, out_specs=out_specs,...]
    pallas_call x4 -> x3, Pallas kernels: 233 us -> 216 us  [expert_pass(): pl.pallas_call(functools.partial(expert_kernel, dims, tuple(kinds), besid...]
    dot_general x5 -> x2, matrix products: 15 us -> 2.58 us  [dot_nn(): lax.dot_general(left, right, (((1,), (0,)), ((), ())), preferred_element_...]
    all_to_all x5, waiting for transfers between devices: 4.35 us -> 12.2 us  [between_members(): lax.all_to_all(values, 'wide', split_axis=0, concat_axis=0, tiled=True, a...]
  transfers between devices with their start and end apart: 10 -> 10, of which waited for: 4 -> 5; matrix products, arithmetic and copies ran while one was open for 6% -> 3% of each run, Pallas kernels for 45% -> 47%
where the time goes in v5:
time: 676 us; the launch traced here: 666 us
  Pallas kernels  541 us (80%)
  starting transfers between devices  38.9 us (6%)
  waiting for transfers between devices  37.2 us (6%)
  between operations  15.1 us (2%)
  local copies, waits for them, and re-layouts  14.9 us (2%)
  other arithmetic  10.2 us (2%)
  matrix products  9.19 us (1%)
    pallas_call x3, Pallas kernels, expert_pass(): pl.pallas_call(functools.partial(expert_kernel, dims, tuple(kinds), besid...  216 us
    pallas_call x16, Pallas kernels, plain_call(): pl.pallas_call(kernel, grid=grid, in_specs=in_specs, out_specs=out_specs,...  213 us
    pallas_call x4, Pallas kernels, link_call(): pl.pallas_call(kernel, out_shape=[shaped((states, channels))] + out_shape...  57.6 us
    pallas_call x1, Pallas kernels, summed_shares(): pl.pallas_call(functools.partial(sum_kernel, (count, lines, sizes, first,...  47.5 us
    ppermute x4, waiting for transfers between devices, passed_along(): lax.ppermute(x, 'wide', [(i, i + by) for i in range(size) if 0 <= i + by...  25 us
    all_to_all x5, starting transfers between devices, between_members(): lax.all_to_all(values, 'wide', split_axis=0, concat_axis=0, tiled=True, a...  23.9 us
    ppermute x4, starting transfers between devices, passed_along(): lax.ppermute(x, 'wide', [(i, i + by) for i in range(size) if 0 <= i + by...  14.9 us
  transfers between devices with their start and end apart: 10, of which 5 were waited for; matrix products, arithmetic and copies ran while one was open for 3% of the time, Pallas kernels for 47%

profile of v5, /device:TPU:0, one launch (start us, length us, event | category | flops | bytes accessed | tf_op | source)
XLA Modules:
  0.0 666.4 jit_solution(2598715397450016872)
XLA Ops:
  9.2 4.9 collective-permute-start
  14.0 2.5 shard_map.306
  16.6 3.9 all-to-all-start
  26.1 2.2 shard_map.308
  28.3 6.9 %shard_map.307 = (bf16[256,768]{1,0:T(8,128)(2,1)}, f32[256,3072]{1,0:T(8,128)}, f32[3,3072]{1,0:T(4,128)}) custom-call(f32[2,1,768]{2,1,0:T(1,128)} %broadcast_in_dim.33.gain_ref, bf16[2,768,3072]{2,1,0:T(8,128)(2,1)} %weight_ref.7, f32[256,768]{1,0:T(8,128)} %bitcast.85, f32[3,768]{1,0:T(4,128)} %convert_element_type.75.refs_1_), custom_call_target="tpu_custom_call" | custom-call | flops 750000000 | bytes 10000 | tf_op jit(solution)/shard_map/pallas_call | solution.py:141
  35.2 14.0 %shard_map.309 = (bf16[256,1536]{1,0:T(8,128)(2,1)}, f32[32,8,80]{2,1,0:T(8,128)}, f32[32,8,1536]{2,1,0:T(8,128)}, f32[16,8,1536]{2,1,0:T(8,128)}, f32[8,1536]{1...) custom-call(f32[32,8,3072]{2,1,0:T(8,128)} %bitcast.81, f32[3,3072]{1,0:T(4,128)} %get-tuple-element.147.rim_ref, ...), custom_call_target="tpu_custom_call" | custom-call | flops 2700000000 | bytes 10000 | tf_op jit(solution)/shard_map/pallas_call | solution.py:141
  49.2 13.5 %shard_map.310 = (f32[16,1536]{1,0:T(8,128)}, bf16[4,384,768]{2,1,0:T(8,128)(2,1)}) custom-call(f32[16,1536]{1,0:T(8,128)} %get-tuple-element.157.total_ref, f32[1,1536]{1,0:T(1,128)} %get-tuple-element.158.size_ref, f32[2,16,1536]{2,1,0:T(8,128)} %decay_ref.23, bf16[2,4,384,768]{3,2,1,0:T(8,128)(2,1)} %refs_0_.3), custom_call_target="tpu_custom_call" | custom-call | flops 1800000000 | bytes 10000 | tf_op jit(solution)/shard_map/pallas_call | solution.py:911
  62.7 1.4 copy-done.5
  64.2 4.5 all-to-all-start.1
  70.8 16.0 %shard_map.311 = (f32[32,8,1536]{2,1,0:T(8,128)}, bf16[256,1536]{1,0:T(8,128)(2,1)}, f32[16,8,1536]{2,1,0:T(8,128)}, f32[256,768]{1,0:T(8,128)}, bf16[256,768]{1...) custom-call(f32[32,8,1536]{2,1,0:T(8,128)} %get-tuple-element.151.size_ref, ...), custom_call_target="tpu_custom_call" | custom-call | flops 3300000000 | bytes 10000 | tf_op jit(solution)/shard_map/pallas_call | solution.py:141
  86.8 7.1 %all-to-all-done.1.refs_3_ = bf16[4,384,768]{2,1,0:T(8,128)(2,1)} async-done(((bf16[4,384,768]{2,1,0:T(8,128)(2,1)}), bf16[4,384,768]{2,1,0:T(8,128)(2,1)}, u32[]{:S(2)}, u32[]{:S(2)}) %all-to-all-start.1) | async-done | bytes 2359328 | tf_op jit(solution)/shard_map/all_to_all | solution.py:1375
  93.9 65.6 %shard_map.312 = (bf16[4,80,768]{2,1,0:T(8,128)(2,1)}, bf16[640,768]{1,0:T(8,128)(2,1)}, bf16[4,640,384]{2,1,0:T(8,128)(2,1)}, f32[4,640,384]{2,1,0:T(8,128)}, bf16[4,768,384]{2,1,0:T(8,128)(2,1)}) custom-call(bf16[4,80,768]{2,1,0:T(8,128)(2,1)} %bitcast.104, bf16[320,320]{1,0:T(8,128)(2,1)} %fusion.2.refs_1_.refs_2_, bf16[4,768,384]{2,1,0:T(8,128)(2,1)} %copy-done.5, ...), custom_call_target="tpu_custom_call" | custom-call | flops 9749999616 | bytes 10000 | tf_op jit(solution)/shard_map/pallas_call | solution.py:1350
  159.5 7.7 %shard_map.313 = (f32[256,768]{1,0:T(8,128)}, f32[256,768]{1,0:T(8,128)}, bf16[256,768]{1,0:T(8,128)(2,1)}, f32[256,3072]{1,0:T(8,128)}) custom-call(f32[2,1,768]{2,1,0:T(1,128)} %broadcast_in_dim.33.gain_ref, bf16[2,768,3072]{2,1,0:T(8,128)(2,1)} %weight_ref.7, f32[256,768]{1,0:T(8,128)} %get-tuple-element.163.refs_0_, ...), custom_call_target="tpu_custom_call" | custom-call | flops 750000000 | bytes 10000 | tf_op jit(solution)/shard_map/pallas_call | solution.py:141
  168.2 7.4 %collective-permute-start.1 = (f32[3,1536]{1,0:T(4,128)S(1)}, f32[3,1536]{1,0:T(4,128)S(1)}, u32[]{:S(2)}, u32[]{:S(2)}) collective-permute-start(f32[3,1536]{1,0:T(4,128)S(1)} %fusion.7), channel_id=1, source_target_pairs={{0,4},{4,8},{8,12},{12,16},{16,20},{20,24},{24,28},{1,5},{5,9},{9,... | collective-permute-start | bytes 55304 | tf_op jit(solution)/shard_map/ppermute | solution.py:58
  175.7 1.5 collective-permute-done.1.rim_ref
  177.8 14.0 %shard_map.314 = (bf16[256,1536]{1,0:T(8,128)(2,1)}, f32[32,8,80]{2,1,0:T(8,128)}, f32[32,8,1536]{2,1,0:T(8,128)}, f32[16,8,1536]{2,1,0:T(8,128)}, f32[8,1536]{1...) custom-call(f32[32,8,3072]{2,1,0:T(8,128)} %bitcast.77, f32[3,1536]{1,0:T(4,128)} %copy-done.22, ...), custom_call_target="tpu_custom_call" | custom-call | flops 2700000000 | bytes 10000 | tf_op jit(solution)/shard_map/pallas_call | solution.py:141
  191.8 12.4 %shard_map.315 = (f32[16,1536]{1,0:T(8,128)}, bf16[4,384,768]{2,1,0:T(8,128)(2,1)}) custom-call(f32[16,1536]{1,0:T(8,128)} %get-tuple-element.176.total_ref, f32[1,1536]{1,0:T(1,128)} %get-tuple-element.177.size_ref, f32[2,16,1536]{2,1,0:T(8,128)} %decay_ref.23, bf16[2,4,384,768]{3,2,1,0:T(8,128)(2,1)} %refs_0_.3), custom_call_target="tpu_custom_call" | custom-call | flops 1800000000 | bytes 10000 | tf_op jit(solution)/shard_map/pallas_call | solution.py:911
  204.3 5.1 all-to-all-start.2
  209.5 16.0 %shard_map.316 = (f32[32,8,1536]{2,1,0:T(8,128)}, bf16[256,1536]{1,0:T(8,128)(2,1)}, f32[16,8,1536]{2,1,0:T(8,128)}, f32[256,768]{1,0:T(8,128)}, bf16[256,768]{1...) custom-call(f32[32,8,1536]{2,1,0:T(8,128)} %get-tuple-element.171.size_ref, ...), custom_call_target="tpu_custom_call" | custom-call | flops 3300000000 | bytes 10000 | tf_op jit(solution)/shard_map/pallas_call | solution.py:141
  226.5 1.3 multiply_reduce_fusion.6
  227.8 1.4 convolution_convert_fusion.1
  229.3 5.1 all-to-all-done.2.refs_4_
  234.4 93.8 %shard_map.317 = (bf16[4,80,768]{2,1,0:T(8,128)(2,1)}, bf16[640,768]{1,0:T(8,128)(2,1)}, bf16[4,640,384]{2,1,0:T(8,128)(2,1)}, bf16[4,80,768]{2,1,0:T(8,128)(2,1...) custom-call(bf16[4,80,768]{2,1,0:T(8,128)(2,1)} %bitcast.103, bf16[4,80,768]{2,1,0:T(8,128)(2,1)} %bitcast.91, ...), custom_call_target="tpu_custom_call" | custom-call | flops 9749999616 | bytes 10000 | tf_op jit(solution)/shard_map/pallas_call | solution.py:1350
  328.2 1.9 fusion.1
  332.3 1.6 fusion.27
  333.9 13.1 %shard_map.318 = (f32[32,8,1536]{2,1,0:T(8,128)}, bf16[256,3072]{1,0:T(8,128)(2,1)}, f32[1,1536]{1,0:T(1,128)}, bf16[1536,768]{1,0:T(8,128)(2,1)}, f32[16,8,1536...) custom-call(bf16[256,768]{1,0:T(8,128)(2,1)} %get-tuple-element.284.grad_ref, ...), custom_call_target="tpu_custom_call" | custom-call | flops 2100000000 | bytes 10000 | tf_op jit(solution)/shard_map/pallas_call | solution.py:141
  347.0 15.6 %shard_map.319 = (f32[16,1536]{1,0:T(8,128)}, bf16[4,1536,384]{2,1,0:T(8,128)(2,1)}) custom-call(f32[16,1536]{1,0:T(8,128)} %get-tuple-element.197.total_ref, f32[1,1536]{1,0:T(1,128)} %get-tuple-element.198.size_ref, f32[2,16,1536]{2,1,0:T(8,128)} %decay_ref.23, bf16[640,768]{1,0:T(8,128)(2,1)} %get-tuple-element.199.rows_hbm, ...), custom_call_target="tpu_custom_call" | custom-call | flops 1800000000 | bytes 10000 | tf_op jit(solution)/shard_map/pallas_call | solution.py:911
  362.6 5.2 all-to-all-start.3
  368.6 26.9 %shard_map.320 = (f32[32,8,1536]{2,1,0:T(8,128)}, f32[16,1536]{1,0:T(8,128)}, f32[1,1536]{1,0:T(1,128)}, f32[48,1536]{1,0:T(8,128)}, bf16[256,80]{1,0:T(8,128)(2,1)}) custom-call(f32[32,8,1536]{2,1,0:T(8,128)} %get-tuple-element.171.size_ref, bf16[256,1536]{1,0:T(8,128)(2,1)} %get-tuple-element.172.act_ref, f32[32,8,1536]{2,1,0:T(8,128)} %get-tuple-element.193.grad_ref, ...), custom_call_target="tpu_custom_call" | custom-call | flops 5249999872 | bytes 10000 | tf_op jit(solution)/shard_map/pallas_call | solution.py:141
  395.6 9.1 %shard_map.321 = (bf16[256,3072]{1,0:T(8,128)(2,1)}, f32[3,1536]{1,0:T(4,128)}, f32[3,1536]{1,0:T(4,128)}, bf16[1536,256]{1,0:T(8,128)(2,1)}) custom-call(f32[32,8,1536]{2,1,0:T(8,128)} %get-tuple-element.204.grad_act_ref, bf16[256,80]{1,0:T(8,128)(2,1)} %get-tuple-element.205.grad_selection_ref, ...), custom_call_target="tpu_custom_call", output_to_operand_aliasing={{0}: (13, {})} | custom-call | flops 1500000000 | bytes 10000 | tf_op jit(solution)/shard_map/pallas_call | solution.py:141
  404.7 1.3 collective-permute-start.2
  407.6 14.1 %collective-permute-done.2.handed_ref = f32[3,1536]{1,0:T(4,128)S(1)} collective-permute-done((f32[3,1536]{1,0:T(4,128)}, f32[3,1536]{1,0:T(4,128)S(1)}, u32[]{:S(2)}, u32[]{:S(2)}) %collective-permute-start.2) | collective-permute-done | bytes 18464 | tf_op jit(solution)/shard_map/ppermute | solution.py:58
  422.3 13.2 %shard_map.322 = (bf16[32,160,768]{2,1,0:T(8,128)(2,1)}, f32[256,768]{1,0:T(8,128)}) custom-call(bf16[256,3072]{1,0:T(8,128)(2,1)} %get-tuple-element.211.grad_ref, bf16[2,768,3072]{2,1,0:T(8,128)(2,1)} %weight_ref.7, f32[3,1536]{1,0:T(4,128)} %get-tuple-element.212.edge_ref, f32[3,1536]{1,0:T(4,128)} %copy-done.20, f32[3,1]{1,0:T(4,128)} %copy.66.keep_ref, ...), custom_call_target="tpu_custom_call" | custom-call | flops 1350000000 | bytes 10000 | tf_op jit(solution)/shard_map/pallas_call | solution.py:141
  438.9 57.0 %shard_map.323 = (bf16[4,80,768]{2,1,0:T(8,128)(2,1)}, bf16[640,768]{1,0:T(8,128)(2,1)}, bf16[4,640,384]{2,1,0:T(8,128)(2,1)}) custom-call(bf16[4,80,768]{2,1,0:T(8,128)(2,1)} %bitcast.94, bf16[320,320]{1,0:T(8,128)(2,1)} %fusion.2.refs_1_.refs_2_, bf16[4,768,384]{2,1,0:T(8,128)(2,1)} %copy-done.5, bf16[4,384,768]{2,1,0:T(8,128)(2,1)} %all-to-all-done.1.refs_3_, ...), custom_call_target="tpu_custom_call" | custom-call | flops 9749999616 | bytes 10000 | tf_op jit(solution)/shard_map/pallas_call | solution.py:1350
  495.9 1.6 multiply_reduce_fusion
  497.5 1.3 fusion.26
  498.8 13.0 %shard_map.324 = (f32[32,8,1536]{2,1,0:T(8,128)}, bf16[256,3072]{1,0:T(8,128)(2,1)}, f32[1,1536]{1,0:T(1,128)}, bf16[1536,768]{1,0:T(8,128)(2,1)}, f32[16,8,1536...) custom-call(bf16[256,768]{1,0:T(8,128)(2,1)} %get-tuple-element.282.grad_ref, ...), custom_call_target="tpu_custom_call" | custom-call | flops 2100000000 | bytes 10000 | tf_op jit(solution)/shard_map/pallas_call | solution.py:141
  511.8 16.1 %shard_map.325 = (f32[16,1536]{1,0:T(8,128)}, bf16[4,1536,384]{2,1,0:T(8,128)(2,1)}) custom-call(f32[16,1536]{1,0:T(8,128)} %get-tuple-element.229.total_ref, f32[1,1536]{1,0:T(1,128)} %get-tuple-element.230.size_ref, f32[2,16,1536]{2,1,0:T(8,128)} %decay_ref.23, bf16[640,768]{1,0:T(8,128)(2,1)} %get-tuple-element.231.rows_hbm, ...), custom_call_target="tpu_custom_call" | custom-call | flops 1800000000 | bytes 10000 | tf_op jit(solution)/shard_map/pallas_call | solution.py:911
  527.9 5.2 all-to-all-start.4
  534.5 27.0 %shard_map.326 = (f32[32,8,1536]{2,1,0:T(8,128)}, f32[16,1536]{1,0:T(8,128)}, f32[1,1536]{1,0:T(1,128)}, f32[48,1536]{1,0:T(8,128)}, bf16[256,80]{1,0:T(8,128)(2,1)}) custom-call(f32[32,8,1536]{2,1,0:T(8,128)} %get-tuple-element.151.size_ref, bf16[256,1536]{1,0:T(8,128)(2,1)} %get-tuple-element.152.act_ref, f32[32,8,1536]{2,1,0:T(8,128)} %get-tuple-element.225.grad_ref, ...), custom_call_target="tpu_custom_call" | custom-call | flops 5249999872 | bytes 10000 | tf_op jit(solution)/shard_map/pallas_call | solution.py:141
  561.5 9.1 %shard_map.327 = (bf16[256,3072]{1,0:T(8,128)(2,1)}, f32[3,1536]{1,0:T(4,128)}, f32[3,1536]{1,0:T(4,128)}, bf16[1536,256]{1,0:T(8,128)(2,1)}) custom-call(f32[32,8,1536]{2,1,0:T(8,128)} %get-tuple-element.236.grad_act_ref, bf16[256,80]{1,0:T(8,128)(2,1)} %get-tuple-element.237.grad_selection_ref, ...), custom_call_target="tpu_custom_call", output_to_operand_aliasing={{0}: (13, {})} | custom-call | flops 1500000000 | bytes 10000 | tf_op jit(solution)/shard_map/pallas_call | solution.py:141
  570.6 1.3 collective-permute-start.3
  573.0 6.4 shard_map.328
  579.4 9.4 %collective-permute-done.3.handed_ref = f32[3,1536]{1,0:T(4,128)S(1)} collective-permute-done((f32[3,1536]{1,0:T(4,128)}, f32[3,1536]{1,0:T(4,128)S(1)}, u32[]{:S(2)}, u32[]{:S(2)}) %collective-permute-start.3) | collective-permute-done | bytes 18464 | tf_op jit(solution)/shard_map/ppermute | solution.py:58
  589.4 13.7 %shard_map.329 = (bf16[32,160,768]{2,1,0:T(8,128)(2,1)}, f32[256,768]{1,0:T(8,128)}, f32[256,768]{1,0:T(8,128)}) custom-call(bf16[256,3072]{1,0:T(8,128)(2,1)} %get-tuple-element.243.grad_ref, bf16[2,768,3072]{2,1,0:T(8,128)(2,1)} %weight_ref.7, f32[3,1536]{1,0:T(4,128)} %get-tuple-element.248.edge_ref, f32[3,1536]{1,0:T(4,128)} %copy-done.19, ...), custom_call_target="tpu_custom_call" | custom-call | flops 1350000000 | bytes 10000 | tf_op jit(solution)/shard_map/pallas_call | solution.py:141
  603.1 47.5 %shard_map.330.refs_0_ = f32[160,768]{1,0:T(8,128)} custom-call(bf16[8,2,2,160,768]{4,3,2,1,0:T(8,128)(2,1)} %bitcast.101), custom_call_target="tpu_custom_call" | custom-call | flops 8999999488 | bytes 10000 | tf_op jit(solution)/shard_map/pallas_call | solution.py:1642
  650.6 6.4 shard_map.332
  657.0 2.1 shard_map.331
  (110 shorter events, 23.8 us)
Async XLA Ops:
  8.4 159.8 %copy-start.27 = (f32[3]{0:T(128)}, f32[3]{0:T(128)S(1)}, u32[]{:S(2)}) copy-start(f32[3]{0:T(128)S(1)} %get-tuple-element.287) | copy-start | bytes 40
  9.2 7.5 %collective-permute-start = (bf16[3,768]{1,0:T(4,128)(2,1)S(1)}, bf16[3,768]{1,0:T(4,128)(2,1)S(1)}, u32[]{:S(2)}, u32[]{:S(2)}) collective-permute-start(bf16[3,768]{1,0:T(4,128)(2,1)S(1)} %bitcast_multiply_fusion.2), channel_id=1, source_target_pairs={{0,4},{4,8},{8,12},{12,16},{16,20},{20,24},{24,28},{1,5},{5,9},{9,... | collective-permute-start | bytes 13832 | tf_op jit(solution)/shard_map/ppermute | solution.py:58
  16.6 4.0 copy-start.26
  16.6 4.6 copy-start.23
  16.6 5.2 copy-start.24
  16.6 5.8 copy-start.12
  16.6 6.9 %copy-start.13 = (bf16[1,256,768]{2,1,0:T(8,128)(2,1)S(1)}, bf16[1,256,768]{2,1,0:T(8,128)(2,1)}, u32[]{:S(2)}) copy-start(bf16[1,256,768]{2,1,0:T(8,128)(2,1)} %param.19) | copy-start | bytes 1179652
  16.6 46.1 %all-to-all-start = ((bf16[4,768,384]{2,1,0:T(8,128)(2,1)}), bf16[4,768,384]{2,1,0:T(8,128)(2,1)S(1)}, u32[]{:S(2)}, u32[]{:S(2)}) async-start(bf16[4,768,384]{2,1,0:T(8,128)(2,1)} %shard_map.306), calls=%async_computation | async-start | bytes 4718592 | tf_op jit(solution)/shard_map/all_to_all | solution.py:1375
  62.7 1.5 copy-start.5
  62.7 6.0 copy-start.21
  62.7 6.6 copy-start.25
  62.7 7.2 %copy-start.17 = (bf16[2,768,16]{1,2,0:T(8,128)(2,1)S(1)}, bf16[2,768,16]{1,2,0:T(8,128)(2,1)}, u32[]{:S(2)}) copy-start(bf16[2,768,16]{1,2,0:T(8,128)(2,1)} %param.34) | copy-start | bytes 147460
  64.2 29.7 %all-to-all-start.1 = ((bf16[4,384,768]{2,1,0:T(8,128)(2,1)}), bf16[4,384,768]{2,1,0:T(8,128)(2,1)}, u32[]{:S(2)}, u32[]{:S(2)}) async-start(bf16[4,384,768]{2,1,0:T(8,128)(2,1)} %get-tuple-element.168), calls=%async_computation.1 | async-start | bytes 4718592 | tf_op jit(solution)/shard_map/all_to_all | solution.py:1375
  168.2 8.9 %collective-permute-start.1 = (f32[3,1536]{1,0:T(4,128)S(1)}, f32[3,1536]{1,0:T(4,128)S(1)}, u32[]{:S(2)}, u32[]{:S(2)}) collective-permute-start(f32[3,1536]{1,0:T(4,128)S(1)} %fusion.7), channel_id=1, source_target_pairs={{0,4},{4,8},{8,12},{12,16},{16,20},{20,24},{24,28},{1,5},{5,9},{9,... | collective-permute-start | bytes 55304 | tf_op jit(solution)/shard_map/ppermute | solution.py:58
  177.2 0.6 copy-start.22
  204.2 5.1 copy-start.14
  204.3 30.1 %all-to-all-start.2 = ((bf16[4,384,768]{2,1,0:T(8,128)(2,1)}), bf16[4,384,768]{2,1,0:T(8,128)(2,1)}, u32[]{:S(2)}, u32[]{:S(2)}) async-start(bf16[4,384,768]{2,1,0:T(8,128)(2,1)} %get-tuple-element.187), calls=%async_computation.2 | async-start | bytes 4718592 | tf_op jit(solution)/shard_map/all_to_all | solution.py:1375
  209.5 18.4 %copy-start.3 = (bf16[320,256]{1,0:T(8,128)(2,1)S(1)}, bf16[320,256]{1,0:T(8,128)(2,1)}, u32[]{:S(2)}) copy-start(bf16[320,256]{1,0:T(8,128)(2,1)} %get-tuple-element.180.fill_ref) | copy-start | bytes 491524
  328.2 2.1 copy-start.10
  328.2 2.2 copy-start.9
  328.2 3.5 copy-start.1
  328.2 3.5 copy-start.11
  362.6 5.2 copy-start.28
  362.6 5.9 copy-start
  362.6 165.3 %all-to-all-start.3 = ((bf16[4,1536,384]{2,1,0:T(8,128)(2,1)}), bf16[4,1536,384]{2,1,0:T(8,128)(2,1)}, u32[]{:S(2)}, u32[]{:S(2)}) async-start(bf16[4,1536,384]{2,1,0:T(8,128)(2,1)} %get-tuple-element.245), calls=%async_computation.3 | async-start | bytes 9437184 | tf_op jit(solution)/shard_map/all_to_all | solution.py:1375
  367.8 289.3 %reduce-scatter.2.cloned.1.call-start = ((), (), s32[]{:S(2)}) async-start(), calls=%async_computation.6 | async-start | bytes 8110080 | tf_op jit(solution)/shard_map/reduce_scatter | solution.py:1976
  395.6 10.4 %copy-start.16 = (bf16[256,768]{1,0:T(8,128)(2,1)S(1)}, bf16[256,768]{1,0:T(8,128)(2,1)}, u32[]{:S(2)}) copy-start(bf16[256,768]{1,0:T(8,128)(2,1)} %get-tuple-element.217) | copy-start | bytes 1179652
  404.7 17.1 %collective-permute-start.2 = (f32[3,1536]{1,0:T(4,128)}, f32[3,1536]{1,0:T(4,128)S(1)}, u32[]{:S(2)}, u32[]{:S(2)}) collective-permute-start(f32[3,1536]{1,0:T(4,128)} %get-tuple-element.213), channel_id=1, source_target_pairs={{4,0},{8,4},{12,8},{16,12},{20,16},{24,20},{28,24},{5,1},{9,5},{13... | collective-permute-start | bytes 55304 | tf_op jit(solution)/shard_map/ppermute | solution.py:58
  421.7 0.6 copy-start.20
  435.6 1.1 copy-start.2
  435.6 1.4 copy-start.6
  435.6 1.7 copy-start.8
  435.6 1.8 copy-start.7
  435.6 1.8 copy-start.18
  435.6 2.1 copy-start.4
  527.9 122.7 %all-to-all-start.4 = ((bf16[4,1536,384]{2,1,0:T(8,128)(2,1)}), bf16[4,1536,384]{2,1,0:T(8,128)(2,1)}, u32[]{:S(2)}, u32[]{:S(2)}) async-start(bf16[4,1536,384]{2,1,0:T(8,128)(2,1)} %get-tuple-element.269), calls=%async_computation.5 | async-start | bytes 9437184 | tf_op jit(solution)/shard_map/all_to_all | solution.py:1375
  561.5 10.4 %copy-start.15 = (bf16[256,768]{1,0:T(8,128)(2,1)S(1)}, bf16[256,768]{1,0:T(8,128)(2,1)}, u32[]{:S(2)}) copy-start(bf16[256,768]{1,0:T(8,128)(2,1)} %get-tuple-element.253) | copy-start | bytes 1179652
  570.6 18.2 %collective-permute-start.3 = (f32[3,1536]{1,0:T(4,128)}, f32[3,1536]{1,0:T(4,128)S(1)}, u32[]{:S(2)}, u32[]{:S(2)}) collective-permute-start(f32[3,1536]{1,0:T(4,128)} %get-tuple-element.249), channel_id=1, source_target_pairs={{4,0},{8,4},{12,8},{16,12},{20,16},{24,20},{28,24},{5,1},{9,5},{13... | collective-permute-start | bytes 55304 | tf_op jit(solution)/shard_map/ppermute | solution.py:58
  588.8 0.6 copy-start.19
Sparse Core Ops, SparseCore 0:
  435.8 142.9 reduce-scatter.1

commit v6 on v5

--- a/solution.py
+++ b/solution.py
@@ -110,7 +110,7 @@
         out_shape=shapes,
         in_specs=[inside] * 3,
         out_specs=[inside] * len(shapes),
-        compiler_params=pltpu.CompilerParams(vmem_limit_bytes=60 * MIB),
+        compiler_params=pltpu.CompilerParams(vmem_limit_bytes=63 * MIB),
         cost_estimate=microseconds(3),
     )(doc_start, expert_choice, slot_index)
     return reset, masks, rest[:layers], rest[layers : 2 * layers], rest[2 * layers :]
@@ -134,7 +134,7 @@
 
 
 def microseconds(count):
-    return pl.CostEstimate(flops=int(count * 1.5e8), transcendentals=0, bytes_accessed=10000)
+    return pl.CostEstimate(flops=int(count * 2.0e7), transcendentals=0, bytes_accessed=10000)
 
 
 def plain_call(kernel, grid, in_specs, out_specs, out_shapes, scratch, args, cost, aliases=None):
@@ -147,7 +147,7 @@
         scratch_shapes=scratch,
         input_output_aliases=aliases or {},
         compiler_params=pltpu.CompilerParams(
-            dimension_semantics=("arbitrary",), vmem_limit_bytes=60 * MIB
+            dimension_semantics=("arbitrary",), vmem_limit_bytes=63 * MIB
         ),
         cost_estimate=microseconds(cost),
     )(*args)
@@ -915,7 +915,7 @@
         out_specs=[inside] + [ANYWHERE] * len(out_shapes),
         scratch_shapes=link_scratch(lax.axis_size("wide"), states, channels) + scratch,
         compiler_params=pltpu.CompilerParams(
-            collective_id=identity, has_side_effects=True, vmem_limit_bytes=60 * MIB
+            collective_id=identity, has_side_effects=True, vmem_limit_bytes=63 * MIB
         ),
         cost_estimate=microseconds(12),
     )(total, size, decay_log, *beside)
@@ -952,70 +952,17 @@
         identity)
 
 
-def behind_kernel(layer, count, total_ref, size_ref, decay_ref, rows_hbm, pre_hbm, hidden_hbm, grad_hbm,
-                  out_ref, *refs):
-    outs = len(refs) - LINK_REFS - 6
-    outs //= 2
-    targets, scratch = refs[:outs], refs[outs : outs + LINK_REFS]
-    rows, pre, hidden_rows, grad, *found = refs[outs + LINK_REFS : -2]
-    got, put = refs[-2:]
-    members, _, hidden = pre.shape
-    width = rows.shape[1]
-    low = jnp.bfloat16
-    loads = [
-        pltpu.make_async_copy(source, target, got.at[i])
-        for i, (source, target) in enumerate(
-            ((rows_hbm, rows), (pre_hbm, pre), (hidden_hbm, hidden_rows), (grad_hbm, grad)))
-    ]
-    for load in loads:
-        load.start()
-    stores = [
-        [pltpu.make_async_copy(found[i].at[s], targets[i].at[s], put.at[i, s]) for i in range(outs)]
-        for s in range(members)
-    ]
-
-    def weights(s):
-        up = dot_tn(rows[...], pre[s]).astype(low)
-        down = dot_tn(hidden_rows[s], grad[...]).astype(low)
-        if outs == 2:
-            found[0][s], found[1][s] = up, down
-        else:
-            found[0][s, :width] = up
-            for f in range(width // hidden):
-                found[0][s, width + f * hidden : width + (f + 1) * hidden] = down[
-                    :, f * hidden : (f + 1) * hidden]
-        for store in stores[s]:
-            store.start()
-
-    def between():
-        for load in loads:
-            load.wait()
-        weights(0)
-
-    def after():
-        for s in range(1, members):
-            weights(s)
-
-    hand_on(layer, count, True, total_ref, size_ref, decay_ref, out_ref, scratch, between, after)
-    for pair in stores:
-        for store in pair:
-            store.wait()
-
-
-def handed_back(layer, total, size, decay_log, rows, pre, hidden_rows, grad_rows, identity):
-    members, _, hidden = pre.shape
-    width = rows.shape[1]
-    low = jnp.bfloat16
-    sizes = [(2 * width, hidden)] if folds(width, hidden) else [(width, hidden), (hidden, width)]
-    shapes = [(members,) + size for size in sizes]
+def behind_kernel(layer, count, total_ref, size_ref, decay_ref, out_ref, *scratch):
+    def nothing():
+        pass
+
+    hand_on(layer, count, True, total_ref, size_ref, decay_ref, out_ref, scratch, nothing, nothing)
+
+
+def handed_back(layer, total, size, decay_log, identity):
     return link_call(
         functools.partial(behind_kernel, layer, lax.axis_size("wide")),
-        total, size, decay_log, [rows, pre, hidden_rows, grad_rows],
-        [shaped(shape, low) for shape in shapes],
-        [VMEM(array.shape, low) for array in (rows, pre, hidden_rows, grad_rows)]
-        + [VMEM(shape, low) for shape in shapes]
-        + [pltpu.SemaphoreType.DMA((4,)), pltpu.SemaphoreType.DMA((len(shapes), members))],
-        identity)
+        total, size, decay_log, [], [], [], identity)[0]
 
 
 def bell(values):
@@ -1026,18 +973,24 @@
     count, groups, members, block, share, width, hidden = dims
     flows = len(kinds)
     out_refs, (perm_ref, up_hbm, down_hbm, *refs) = refs[:flows], refs[flows:]
+    learns, outs = True in kinds, 1 if kinds == (True,) and folds(width, hidden) else 2
     if kinds == (True,):
-        pre_hbm, *refs = refs
+        pre_hbm, kept_hbm, hidden_hbm, *refs = refs
     if beside:
         next_hbm, *refs = refs
-    results, refs = [refs[3 * f : 3 * f + 3] for f in range(flows)], refs[3 * flows :]
-    if kinds == (False,):
-        pre_hbm, *refs = refs
+    ret_refs, refs = refs[:flows], refs[flows:]
+    if learns:
+        targets, refs = refs[:outs], refs[outs:]
+    else:
+        rows_hbm, low_hbm, pre_hbm, *refs = refs
     if beside:
         met_hbm, *refs = refs
         *refs, leaving, met, next_send, next_recv, next_local = refs
     pre, up, down, total, local, *refs = refs
-    scratch = [refs[16 * f : 16 * f + 16] for f in range(flows)]
+    scratch, refs = [refs[16 * f : 16 * f + 16] for f in range(flows)], refs[16 * flows :]
+    if learns:
+        *found, put = refs[: outs + 1]
+        kept_rows, kept_hidden = refs[outs + 1 :] if kinds == (True,) else (scratch[0][2], scratch[0][3])
     f32, bf16 = jnp.float32, jnp.bfloat16
     here = lax.axis_index("wide")
     group = lax.axis_index("narrow")
@@ -1057,6 +1010,8 @@
     ]
     if kinds == (True,):
         loads.append(pltpu.make_async_copy(pre_hbm, pre, local.at[2]))
+        loads.append(pltpu.make_async_copy(kept_hbm, kept_rows, local.at[3]))
+        loads.append(pltpu.make_async_copy(hidden_hbm, kept_hidden, local.at[4]))
     for load in loads:
         load.start()
     if beside:
@@ -1102,9 +1057,8 @@
             device_id=(here, near_group), device_id_type=MESH).wait_recv()
 
     class Flow:
-        def __init__(self, backward, out_ref, result, scratch):
-            self.backward, self.out_ref = backward, out_ref
-            self.ret_ref, self.rows_hbm, self.low_hbm = result
+        def __init__(self, backward, out_ref, ret_ref, scratch):
+            self.backward, self.out_ref, self.ret_ref = backward, out_ref, ret_ref
             (self.arrived, self.own, self.rows, self.low, self.part, self.got, self.final, self.landed,
              self.there_send, self.there_recv, self.row_send, self.row_recv, self.sum_send, self.sum_recv,
              self.back_send, self.back_recv) = scratch
@@ -1196,7 +1150,7 @@
             copy.start()
             sent.append(copy)
 
-        def work(self, first_save):
+        def work(self):
             windows = [here] + [self.arrive(0, turn) for turn in range(1, members)]
             self.compute(windows)
             for part in (1, 0):
@@ -1213,9 +1167,6 @@
                         late.append((away, turn, windows[turn - first]))
             for away, turn, window in late:
                 self.give_back(away, turn, window, 0)
-            for k, (source, target) in enumerate(((self.rows, self.rows_hbm), (self.low, self.low_hbm))):
-                saves.append(pltpu.make_async_copy(source, target, local.at[first_save + k]))
-                saves[-1].start()
 
         def returned(self, part):
             place = (head, tail)[part]
@@ -1257,7 +1208,7 @@
             for place, other in others:
                 self.ret_ref[other] = self.landed[place]
 
-    travels = [Flow(*parts) for parts in zip(kinds, out_refs, results, scratch)]
+    travels = [Flow(*parts) for parts in zip(kinds, out_refs, ret_refs, scratch)]
     for flow in travels:
         flow.to_groups()
     for flow in travels:
@@ -1279,12 +1230,29 @@
     send_beside([1])
     for load in loads:
         load.wait()
-    for f, flow in enumerate(travels):
-        flow.work(3 + 2 * f)
+    for flow in travels:
+        flow.work()
     send_beside(range(2, members))
-    if kinds == (False,):
-        saves.append(pltpu.make_async_copy(pre, pre_hbm, local.at[2]))
-        saves[-1].start()
+    if learns:
+        back = travels[-1]
+        for s in range(members):
+            grads = [dot_tn(kept_rows[...], back.low[s]).astype(bf16),
+                     dot_tn(kept_hidden[s], back.rows[...]).astype(bf16)]
+            if outs == 2:
+                found[0][s], found[1][s] = grads
+            else:
+                found[0][s, :width] = grads[0]
+                for f in range(width // hidden):
+                    found[0][s, width + f * hidden : width + (f + 1) * hidden] = grads[1][
+                        :, f * hidden : (f + 1) * hidden]
+            for i in range(outs):
+                saves.append(pltpu.make_async_copy(found[i].at[s], targets[i].at[s], put.at[i, s]))
+                saves[-1].start()
+    else:
+        held = ((travels[0].rows, rows_hbm), (travels[0].low, low_hbm), (pre, pre_hbm))
+        for k, (source, target) in enumerate(held):
+            saves.append(pltpu.make_async_copy(source, target, local.at[2 + k]))
+            saves[-1].start()
     for flow in travels:
         flow.leave()
     for flow in travels:
@@ -1300,7 +1268,7 @@
         save.wait()
 
 
-def expert_pass(outbounds, kinds, perm, weights, pre, identity, beside=None, which=None):
+def expert_pass(outbounds, kinds, perm, weights, identity, known=(), beside=None, which=None):
     count, groups = lax.axis_size("wide"), lax.axis_size("narrow")
     _, block, width = outbounds[0].shape
     members, _, hidden = weights[0].shape
@@ -1310,22 +1278,16 @@
     low, f32 = jnp.bfloat16, jnp.float32
     dims = (count, groups, members, block, share, width, hidden)
     inside = pl.BlockSpec(memory_space=VMEM)
-    args = tuple(outbounds) + (perm,) + tuple(weights) + (() if pre is None else (pre,))
+    args = tuple(outbounds) + (perm,) + tuple(weights) + tuple(known)
     args += () if beside is None else (beside,)
-    out_specs, outs = [], []
-    for _ in kinds:
-        out_specs += [inside, ANYWHERE, ANYWHERE]
-        outs += [shaped((groups, block, width), low), shaped((total, width), low),
-                 shaped((members, total, hidden), low)]
-    if kinds == (False,):
-        outs.append(shaped((members, total, hidden)))
+    outs = [shaped((groups, block, width), low) for _ in kinds]
     dma = pltpu.SemaphoreType.DMA
     scratch = [
         VMEM((members, total, hidden), f32),
         VMEM((members, width, hidden), low),
         VMEM((members, hidden, width), low),
         VMEM((members * share, width), f32),
-        dma((3 + 2 * len(kinds),)),
+        dma((5,)),
     ]
     for _ in kinds:
         scratch += [
@@ -1342,19 +1304,29 @@
             dma((quads, members, 2)), dma((quads, members, 2)),
             dma((groups - 1,)), dma((groups - 1,)),
         ]
+    if True in kinds:
+        sizes = [(width, hidden), (hidden, width)]
+        if len(kinds) == 1 and folds(width, hidden):
+            sizes = [(2 * width, hidden)]
+        outs += [shaped((members,) + size, low) for size in sizes]
+        scratch += [VMEM((members,) + size, low) for size in sizes] + [dma((len(sizes), members))]
+        if len(kinds) == 1:
+            scratch += [VMEM((total, width), low), VMEM((members, total, hidden), low)]
+    else:
+        outs += [shaped((total, width), low), shaped((members, total, hidden), low),
+                 shaped((members, total, hidden))]
     if beside is not None:
         shape = beside.shape[-3:]
         outs.append(shaped(shape, low))
         scratch += [VMEM(shape, low), VMEM(shape, low), dma((members,)), dma((members,)), dma((2,))]
-    out_specs += [ANYWHERE] * (len(outs) - len(out_specs))
     return pl.pallas_call(
         functools.partial(expert_kernel, dims, tuple(kinds), beside is not None, which),
         out_shape=outs,
         in_specs=[inside] * (len(kinds) + 1) + [ANYWHERE] * (len(args) - len(kinds) - 1),
-        out_specs=out_specs,
+        out_specs=[inside] * len(kinds) + [ANYWHERE] * (len(outs) - len(kinds)),
         scratch_shapes=scratch,
         compiler_params=pltpu.CompilerParams(
-            collective_id=identity, has_side_effects=True, vmem_limit_bytes=60 * MIB
+            collective_id=identity, has_side_effects=True, vmem_limit_bytes=63 * MIB
         ),
         cost_estimate=microseconds(65),
     )(*args)
@@ -1399,7 +1371,7 @@
         out_specs=ANYWHERE,
         scratch_shapes=[
             VMEM(shape, values.dtype), pltpu.SemaphoreType.DMA(shape[:1]), pltpu.SemaphoreType.DMA(shape[:1])],
-        compiler_params=pltpu.CompilerParams(vmem_limit_bytes=60 * MIB),
+        compiler_params=pltpu.CompilerParams(vmem_limit_bytes=63 * MIB),
         cost_estimate=microseconds(2),
     )(values)
 
@@ -1434,7 +1406,7 @@
         [shaped((layers, experts, width, hidden)), shaped((layers, experts, hidden, width))],
         [],
         tuple(arrays) + tuple(held),
-        60,
+        450,
         {count + k: k for k in range(len(held))},
     )
 
@@ -1635,7 +1607,7 @@
         arrays = [jnp.pad(packed, ((0, 0), (0, -packed.shape[1] % 16), (0, 0)))]
     sizes = tuple(array.shape[1] for array in arrays)
     rows = sum(sizes)
-    first = max(32, rows * 11 // 20 // 16 * 16)
+    first = max(32, rows * 12 // 20 // 16 * 16)
     later = rows - first
     low = jnp.bfloat16
     dma = pltpu.SemaphoreType.DMA
@@ -1658,7 +1630,7 @@
             dma((lines - 1,)), dma((lines - 1,)),
         ],
         compiler_params=pltpu.CompilerParams(
-            collective_id=identity, has_side_effects=True, vmem_limit_bytes=60 * MIB
+            collective_id=identity, has_side_effects=True, vmem_limit_bytes=63 * MIB
         ),
         cost_estimate=microseconds(60),
     )(*[array.reshape(count, lines, 2, array.shape[1], width) for array in arrays])
@@ -1827,7 +1799,7 @@
         out_shape=[shaped((layers,) + shape) for shape in shapes],
         in_specs=[inside] * layers,
         out_specs=[inside] * len(shapes),
-        compiler_params=pltpu.CompilerParams(vmem_limit_bytes=60 * MIB),
+        compiler_params=pltpu.CompilerParams(vmem_limit_bytes=63 * MIB),
         cost_estimate=microseconds(3),
     )(*sums)
 
@@ -1908,22 +1880,23 @@
         mixed, gated, begins, middle, routed, shares, weight, outbound = mixer_run(
             layer, size, act, selection, reset, decay_log, link, link_size, entering, projected, skip_weight,
             out_weight, current, norm_expert, router, fills[layer], onehots[layer], keeps[layer])
-        pre_act = None
         outbound = outbound.reshape(groups, block, width)
         if layer + 1 < layers:
             returned, kept_rows, hidden_low, pre_act, following = expert_pass(
-                [outbound], (False,), order, weights[layer], None, 4 + layer, expert_up, layer + 1)
+                [outbound], (False,), order, weights[layer], 4 + layer, (), expert_up, layer + 1)
+            known = (pre_act, kept_rows, hidden_low)
             weights[layer + 1] = [following]
         else:
             grad = to_steps(cotangent[0]).reshape(tokens, width).astype(f32)
             grad_rows_low = (weight * grad).astype(low)
             returning = dot_nn(fills[layer], grad_rows_low).astype(low).reshape(groups, block, width)
-            returned, kept_rows, hidden_low, inbound, grad_rows, grad_pre = expert_pass(
-                [outbound, returning], (False, True), order, weights[layer], None, 4 + layer)
+            returned, inbound, *ready = expert_pass(
+                [outbound, returning], (False, True), order, weights[layer], 4 + layer)
+            known = None
         saved.append(dict(
             begin=begin, normed=normed, projected=projected, rim=rim, act=act, selection=selection, size=size,
             begins=begins, mixed=mixed, gated=gated, middle=middle, routed=routed, shares=shares, weight=weight,
-            kept_rows=kept_rows, pre_act=pre_act, hidden_low=hidden_low))
+            known=known))
     back_rows = dot_tn(fills[-1], returned.reshape(groups * block, width))
     saved[-1]["back_rows"] = back_rows
     current = middle + weight * back_rows
@@ -1941,8 +1914,8 @@
         if layer + 1 < layers:
             grad_rows_low = (weight * grad).astype(low)
             outbound = dot_nn(fill, grad_rows_low).astype(low).reshape(groups, block, width)
-            inbound, grad_rows, grad_pre = expert_pass(
-                [outbound], (True,), order, weights[layer], entry["pre_act"], 6 + layer)
+            inbound, *ready = expert_pass(
+                [outbound], (True,), order, weights[layer], 6 + layer, entry["known"])
         grad_sent = dot_tn(fill, inbound.reshape(groups * block, width))
         grad_logits_low = (weighted * (onehots[layer] - entry["shares"])).astype(low)
         grad_router = dot_tn(entry["routed"], grad_logits_low)
@@ -1953,10 +1926,10 @@
         grad_y, grad_igate, grad_skip, grad_out, link, link_size, total, total_size = mixer_turn(
             layer, grad_low, out_weight, entry["projected"], entry["mixed"], entry["act"], entry["gated"],
             entry["size"], entry["selection"], reset, decay_log)
-        entering, *ready = handed_back(
-            layer, total, total_size, decay_log, entry["kept_rows"], grad_pre, entry["hidden_low"], grad_rows,
-            2 + layer)
-        expert_grads[layer] = between_members(ready)
+        entering = handed_back(layer, total, total_size, decay_log, 2 + layer)
+        at_once = ready[: len(ready) // 2] if layer + 1 == layers else []
+        *later, entering = lax.optimization_barrier((*ready[len(at_once) :], entering))
+        expert_grads[layer] = between_members(at_once + later)
         grad_act, grad_decay, grad_bias, grad_step, grad_selection = mixer_back(
             layer, entry["size"], entry["act"], grad_y, decay_log, entry["selection"], reset,
             entry["begins"], link, link_size, entering, step_weight, step_bias, skip_weight)

time: 676 us -> 675 us (level)
  waiting for transfers between devices: 37.2 us -> 28 us
    ppermute x4, waiting for transfers between devices: 25 us -> 14.5 us  [passed_along(): lax.ppermute(x, 'wide', [(i, i + by) for i in range(size) if 0 <= i + by...]
    all_to_all x5 -> x6, starting transfers between devices: 23.9 us -> 29.5 us  [between_members(): lax.all_to_all(values, 'wide', split_axis=0, concat_axis=0, tiled=True, a...]
  transfers between devices with their start and end apart: 10 -> 11, of which waited for: 5 -> 5; matrix products, arithmetic and copies ran while one was open for 3% -> 4% of each run, Pallas kernels for 47% -> 52%
where the time goes in v6:
time: 675 us; the launch traced here: 665 us
  Pallas kernels  543 us (80%)
  starting transfers between devices  44.6 us (7%)
  waiting for transfers between devices  28 us (4%)
  between operations  15.2 us (2%)
  local copies, waits for them, and re-layouts  14.3 us (2%)
  matrix products  9.85 us (1%)
  other arithmetic  9.27 us (1%)
    pallas_call x3, Pallas kernels, expert_pass(): pl.pallas_call(functools.partial(expert_kernel, dims, tuple(kinds), besid...  218 us
    pallas_call x16, Pallas kernels, plain_call(): pl.pallas_call(kernel, grid=grid, in_specs=in_specs, out_specs=out_specs,...  212 us
    pallas_call x4, Pallas kernels, link_call(): pl.pallas_call(kernel, out_shape=[shaped((states, channels))] + out_shape...  63.7 us
    pallas_call x1, Pallas kernels, summed_shares(): pl.pallas_call(functools.partial(sum_kernel, (count, lines, sizes, first,...  43.3 us
    all_to_all x6, starting transfers between devices, between_members(): lax.all_to_all(values, 'wide', split_axis=0, concat_axis=0, tiled=True, a...  29.5 us
    ppermute x4, starting transfers between devices, passed_along(): lax.ppermute(x, 'wide', [(i, i + by) for i in range(size) if 0 <= i + by...  15.1 us
    ppermute x4, waiting for transfers between devices, passed_along(): lax.ppermute(x, 'wide', [(i, i + by) for i in range(size) if 0 <= i + by...  14.5 us
  transfers between devices with their start and end apart: 11, of which 5 were waited for; matrix products, arithmetic and copies ran while one was open for 4% of the time, Pallas kernels for 52%

profile of v6, /device:TPU:0, one launch (start us, length us, event | category | flops | bytes accessed | tf_op | source)
XLA Modules:
  0.0 664.7 jit_solution(11077732068547677909)
XLA Ops:
  9.2 4.9 collective-permute-start
  14.0 2.5 shard_map.306
  16.6 4.7 all-to-all-start
  23.7 1.2 copy.57.state_ref
  26.9 2.2 shard_map.308
  29.1 6.9 %shard_map.307 = (bf16[256,768]{1,0:T(8,128)(2,1)}, f32[256,3072]{1,0:T(8,128)}, f32[3,3072]{1,0:T(4,128)}) custom-call(f32[2,1,768]{2,1,0:T(1,128)} %broadcast_in_dim.33.gain_ref, bf16[2,768,3072]{2,1,0:T(8,128)(2,1)} %weight_ref.7, f32[256,768]{1,0:T(8,128)} %bitcast.85, f32[3,768]{1,0:T(4,128)} %convert_element_type.75.refs_1_), custom_call_target="tpu_custom_call" | custom-call | flops 100000000 | bytes 10000 | tf_op jit(solution)/shard_map/pallas_call | solution.py:141
  36.0 14.0 %shard_map.309 = (bf16[256,1536]{1,0:T(8,128)(2,1)}, f32[32,8,80]{2,1,0:T(8,128)}, f32[32,8,1536]{2,1,0:T(8,128)}, f32[16,8,1536]{2,1,0:T(8,128)}, f32[8,1536]{1...) custom-call(f32[32,8,3072]{2,1,0:T(8,128)} %bitcast.81, f32[3,3072]{1,0:T(4,128)} %get-tuple-element.144.rim_ref, ...), custom_call_target="tpu_custom_call" | custom-call | flops 360000000 | bytes 10000 | tf_op jit(solution)/shard_map/pallas_call | solution.py:141
  50.0 13.6 %shard_map.310 = (f32[16,1536]{1,0:T(8,128)}, bf16[4,384,768]{2,1,0:T(8,128)(2,1)}) custom-call(f32[16,1536]{1,0:T(8,128)} %get-tuple-element.154.total_ref, f32[1,1536]{1,0:T(1,128)} %get-tuple-element.155.size_ref, f32[2,16,1536]{2,1,0:T(8,128)} %decay_ref.23, bf16[2,4,384,768]{3,2,1,0:T(8,128)(2,1)} %refs_0_.3), custom_call_target="tpu_custom_call" | custom-call | flops 240000000 | bytes 10000 | tf_op jit(solution)/shard_map/pallas_call | solution.py:911
  63.7 4.6 all-to-all-start.1
  70.5 16.0 %shard_map.311 = (f32[32,8,1536]{2,1,0:T(8,128)}, bf16[256,1536]{1,0:T(8,128)(2,1)}, f32[16,8,1536]{2,1,0:T(8,128)}, f32[256,768]{1,0:T(8,128)}, bf16[256,768]{1...) custom-call(f32[32,8,1536]{2,1,0:T(8,128)} %get-tuple-element.148.size_ref, ...), custom_call_target="tpu_custom_call" | custom-call | flops 440000000 | bytes 10000 | tf_op jit(solution)/shard_map/pallas_call | solution.py:141
  86.5 7.1 %all-to-all-done.1.refs_3_ = bf16[4,384,768]{2,1,0:T(8,128)(2,1)} async-done(((bf16[4,384,768]{2,1,0:T(8,128)(2,1)}), bf16[4,384,768]{2,1,0:T(8,128)(2,1)}, u32[]{:S(2)}, u32[]{:S(2)}) %all-to-all-start.1) | async-done | bytes 2359328 | tf_op jit(solution)/shard_map/all_to_all | solution.py:1347
  93.5 65.6 %shard_map.312 = (bf16[4,80,768]{2,1,0:T(8,128)(2,1)}, bf16[640,768]{1,0:T(8,128)(2,1)}, bf16[4,640,384]{2,1,0:T(8,128)(2,1)}, f32[4,640,384]{2,1,0:T(8,128)}, bf16[4,768,384]{2,1,0:T(8,128)(2,1)}) custom-call(bf16[4,80,768]{2,1,0:T(8,128)(2,1)} %bitcast.96, bf16[320,320]{1,0:T(8,128)(2,1)} %fusion.2.refs_1_.refs_2_, ...), custom_call_target="tpu_custom_call" | custom-call | flops 1300000000 | bytes 10000 | tf_op jit(solution)/shard_map/pallas_call | solution.py:1322
  159.2 7.7 %shard_map.313 = (f32[256,768]{1,0:T(8,128)}, f32[256,768]{1,0:T(8,128)}, bf16[256,768]{1,0:T(8,128)(2,1)}, f32[256,3072]{1,0:T(8,128)}) custom-call(f32[2,1,768]{2,1,0:T(1,128)} %broadcast_in_dim.33.gain_ref, bf16[2,768,3072]{2,1,0:T(8,128)(2,1)} %weight_ref.7, f32[256,768]{1,0:T(8,128)} %get-tuple-element.160.refs_0_, ...), custom_call_target="tpu_custom_call" | custom-call | flops 100000000 | bytes 10000 | tf_op jit(solution)/shard_map/pallas_call | solution.py:141
  167.9 7.4 %collective-permute-start.1 = (f32[3,1536]{1,0:T(4,128)S(1)}, f32[3,1536]{1,0:T(4,128)S(1)}, u32[]{:S(2)}, u32[]{:S(2)}) collective-permute-start(f32[3,1536]{1,0:T(4,128)S(1)} %fusion.7), channel_id=1, source_target_pairs={{0,4},{4,8},{8,12},{12,16},{16,20},{20,24},{24,28},{1,5},{5,9},{9,... | collective-permute-start | bytes 55304 | tf_op jit(solution)/shard_map/ppermute | solution.py:58
  175.3 1.5 collective-permute-done.1.rim_ref
  177.4 14.0 %shard_map.314 = (bf16[256,1536]{1,0:T(8,128)(2,1)}, f32[32,8,80]{2,1,0:T(8,128)}, f32[32,8,1536]{2,1,0:T(8,128)}, f32[16,8,1536]{2,1,0:T(8,128)}, f32[8,1536]{1...) custom-call(f32[32,8,3072]{2,1,0:T(8,128)} %bitcast.77, f32[3,1536]{1,0:T(4,128)} %copy-done.24, ...), custom_call_target="tpu_custom_call" | custom-call | flops 360000000 | bytes 10000 | tf_op jit(solution)/shard_map/pallas_call | solution.py:141
  191.4 12.4 %shard_map.315 = (f32[16,1536]{1,0:T(8,128)}, bf16[4,384,768]{2,1,0:T(8,128)(2,1)}) custom-call(f32[16,1536]{1,0:T(8,128)} %get-tuple-element.173.total_ref, f32[1,1536]{1,0:T(1,128)} %get-tuple-element.174.size_ref, f32[2,16,1536]{2,1,0:T(8,128)} %decay_ref.23, bf16[2,4,384,768]{3,2,1,0:T(8,128)(2,1)} %refs_0_.3), custom_call_target="tpu_custom_call" | custom-call | flops 240000000 | bytes 10000 | tf_op jit(solution)/shard_map/pallas_call | solution.py:911
  203.9 5.1 all-to-all-start.2
  209.1 16.0 %shard_map.316 = (f32[32,8,1536]{2,1,0:T(8,128)}, bf16[256,1536]{1,0:T(8,128)(2,1)}, f32[16,8,1536]{2,1,0:T(8,128)}, f32[256,768]{1,0:T(8,128)}, bf16[256,768]{1...) custom-call(f32[32,8,1536]{2,1,0:T(8,128)} %get-tuple-element.168.size_ref, ...), custom_call_target="tpu_custom_call" | custom-call | flops 440000000 | bytes 10000 | tf_op jit(solution)/shard_map/pallas_call | solution.py:141
  226.2 1.5 convolution_convert_fusion.1
  227.6 6.4 all-to-all-done.2.refs_4_
  234.0 93.9 %shard_map.317 = (bf16[4,80,768]{2,1,0:T(8,128)(2,1)}, bf16[4,80,768]{2,1,0:T(8,128)(2,1)}, bf16[4,768,384]{2,1,0:T(8,128)(2,1)}, bf16[4,384,768]{2,1,0:T(8,128)(2,1)}) custom-call(bf16[4,80,768]{2,1,0:T(8,128)(2,1)} %bitcast.94, bf16[4,80,768]{2,1,0:T(8,128)(2,1)} %bitcast.90, bf16[320,320]{1,0:T(8,128)(2,1)} %fusion.2.refs_1_.refs_2_, ...), custom_call_target="tpu_custom_call" | custom-call | flops 1300000000 | bytes 10000 | tf_op jit(solution)/shard_map/pallas_call | solution.py:1322
  327.9 4.9 all-to-all-start.3
  335.0 1.6 multiply_reduce_fusion.4
  336.5 1.7 fusion.27
  338.2 12.9 %shard_map.318 = (f32[32,8,1536]{2,1,0:T(8,128)}, bf16[256,3072]{1,0:T(8,128)(2,1)}, f32[1,1536]{1,0:T(1,128)}, bf16[1536,768]{1,0:T(8,128)(2,1)}, f32[16,8,1536...) custom-call(bf16[256,768]{1,0:T(8,128)(2,1)} %get-tuple-element.278.grad_ref, ...), custom_call_target="tpu_custom_call" | custom-call | flops 280000000 | bytes 10000 | tf_op jit(solution)/shard_map/pallas_call | solution.py:141
  351.2 20.8 %shard_map.319.entering_ref = f32[16,1536]{1,0:T(8,128)} custom-call(f32[16,1536]{1,0:T(8,128)} %get-tuple-element.195.total_ref, f32[1,1536]{1,0:T(1,128)} %get-tuple-element.196.size_ref, f32[2,16,1536]{2,1,0:T(8,128)} %decay_ref.23), custom_call_target="tpu_custom_call" | custom-call | flops 240000000 | bytes 10000 | tf_op jit(solution)/shard_map/pallas_call | solution.py:911
  372.0 4.5 all-to-all-start.4
  377.3 26.9 %shard_map.320 = (f32[32,8,1536]{2,1,0:T(8,128)}, f32[16,1536]{1,0:T(8,128)}, f32[1,1536]{1,0:T(1,128)}, f32[48,1536]{1,0:T(8,128)}, bf16[256,80]{1,0:T(8,128)(2,1)}) custom-call(f32[32,8,1536]{2,1,0:T(8,128)} %get-tuple-element.168.size_ref, bf16[256,1536]{1,0:T(8,128)(2,1)} %get-tuple-element.169.act_ref, f32[32,8,1536]{2,1,0:T(8,128)} %get-tuple-element.190.grad_ref, ...), custom_call_target="tpu_custom_call" | custom-call | flops 700000000 | bytes 10000 | tf_op jit(solution)/shard_map/pallas_call | solution.py:141
  404.2 9.1 %shard_map.321 = (bf16[256,3072]{1,0:T(8,128)(2,1)}, f32[3,1536]{1,0:T(4,128)}, f32[3,1536]{1,0:T(4,128)}, bf16[1536,256]{1,0:T(8,128)(2,1)}) custom-call(f32[32,8,1536]{2,1,0:T(8,128)} %get-tuple-element.198.grad_act_ref, bf16[256,80]{1,0:T(8,128)(2,1)} %get-tuple-element.199.grad_selection_ref, ...), custom_call_target="tpu_custom_call", output_to_operand_aliasing={{0}: (13, {})} | custom-call | flops 200000000 | bytes 10000 | tf_op jit(solution)/shard_map/pallas_call | solution.py:141
  413.3 1.5 collective-permute-start.2
  416.4 2.8 collective-permute-done.2.handed_ref
  419.8 13.0 %shard_map.322 = (bf16[32,160,768]{2,1,0:T(8,128)(2,1)}, f32[256,768]{1,0:T(8,128)}) custom-call(bf16[256,3072]{1,0:T(8,128)(2,1)} %get-tuple-element.205.grad_ref, bf16[2,768,3072]{2,1,0:T(8,128)(2,1)} %weight_ref.7, f32[3,1536]{1,0:T(4,128)} %get-tuple-element.206.edge_ref, f32[3,1536]{1,0:T(4,128)} %copy-done.26, f32[3,1]{1,0:T(4,128)} %copy.66.keep_ref, ...), custom_call_target="tpu_custom_call" | custom-call | flops 180000000 | bytes 10000 | tf_op jit(solution)/shard_map/pallas_call | solution.py:141
  436.3 58.0 %shard_map.323 = (bf16[4,80,768]{2,1,0:T(8,128)(2,1)}, bf16[4,1536,384]{2,1,0:T(8,128)(2,1)}) custom-call(bf16[4,80,768]{2,1,0:T(8,128)(2,1)} %bitcast.91, bf16[320,320]{1,0:T(8,128)(2,1)} %fusion.2.refs_1_.refs_2_, bf16[4,768,384]{2,1,0:T(8,128)(2,1)} %all-to-all-done.refs_2_, bf16[4,384,768]{2,1,0:T(8,128)(2,1)} %all-to-all-done.1.refs_3_, ...), custom_call_target="tpu_custom_call" | custom-call | flops 1300000000 | bytes 10000 | tf_op jit(solution)/shard_map/pallas_call | solution.py:1322
  496.5 1.6 multiply_reduce_fusion
  498.1 1.3 fusion.26
  499.4 13.0 %shard_map.324 = (f32[32,8,1536]{2,1,0:T(8,128)}, bf16[256,3072]{1,0:T(8,128)(2,1)}, f32[1,1536]{1,0:T(1,128)}, bf16[1536,768]{1,0:T(8,128)(2,1)}, f32[16,8,1536...) custom-call(bf16[256,768]{1,0:T(8,128)(2,1)} %get-tuple-element.276.grad_ref, ...), custom_call_target="tpu_custom_call" | custom-call | flops 280000000 | bytes 10000 | tf_op jit(solution)/shard_map/pallas_call | solution.py:141
  512.4 16.8 %shard_map.325.entering_ref = f32[16,1536]{1,0:T(8,128)} custom-call(f32[16,1536]{1,0:T(8,128)} %get-tuple-element.226.total_ref, f32[1,1536]{1,0:T(1,128)} %get-tuple-element.227.size_ref, f32[2,16,1536]{2,1,0:T(8,128)} %decay_ref.23), custom_call_target="tpu_custom_call" | custom-call | flops 240000000 | bytes 10000 | tf_op jit(solution)/shard_map/pallas_call | solution.py:911
  529.2 5.7 all-to-all-start.5
  535.8 26.9 %shard_map.326 = (f32[32,8,1536]{2,1,0:T(8,128)}, f32[16,1536]{1,0:T(8,128)}, f32[1,1536]{1,0:T(1,128)}, f32[48,1536]{1,0:T(8,128)}, bf16[256,80]{1,0:T(8,128)(2,1)}) custom-call(f32[32,8,1536]{2,1,0:T(8,128)} %get-tuple-element.148.size_ref, bf16[256,1536]{1,0:T(8,128)(2,1)} %get-tuple-element.149.act_ref, f32[32,8,1536]{2,1,0:T(8,128)} %get-tuple-element.221.grad_ref, ...), custom_call_target="tpu_custom_call" | custom-call | flops 700000000 | bytes 10000 | tf_op jit(solution)/shard_map/pallas_call | solution.py:141
  562.7 9.1 %shard_map.327 = (bf16[256,3072]{1,0:T(8,128)(2,1)}, f32[3,1536]{1,0:T(4,128)}, f32[3,1536]{1,0:T(4,128)}, bf16[1536,256]{1,0:T(8,128)(2,1)}) custom-call(f32[32,8,1536]{2,1,0:T(8,128)} %get-tuple-element.229.grad_act_ref, bf16[256,80]{1,0:T(8,128)(2,1)} %get-tuple-element.230.grad_selection_ref, ...), custom_call_target="tpu_custom_call", output_to_operand_aliasing={{0}: (13, {})} | custom-call | flops 200000000 | bytes 10000 | tf_op jit(solution)/shard_map/pallas_call | solution.py:141
  571.8 1.3 collective-permute-start.3
  574.7 6.4 shard_map.328
  581.1 10.2 %collective-permute-done.3.handed_ref = f32[3,1536]{1,0:T(4,128)S(1)} collective-permute-done((f32[3,1536]{1,0:T(4,128)}, f32[3,1536]{1,0:T(4,128)S(1)}, u32[]{:S(2)}, u32[]{:S(2)}) %collective-permute-start.3) | collective-permute-done | bytes 18464 | tf_op jit(solution)/shard_map/ppermute | solution.py:58
  592.0 13.6 %shard_map.329 = (bf16[32,160,768]{2,1,0:T(8,128)(2,1)}, f32[256,768]{1,0:T(8,128)}, f32[256,768]{1,0:T(8,128)}) custom-call(bf16[256,3072]{1,0:T(8,128)(2,1)} %get-tuple-element.236.grad_ref, bf16[2,768,3072]{2,1,0:T(8,128)(2,1)} %weight_ref.7, f32[3,1536]{1,0:T(4,128)} %get-tuple-element.242.edge_ref, f32[3,1536]{1,0:T(4,128)} %copy-done.25, ...), custom_call_target="tpu_custom_call" | custom-call | flops 180000000 | bytes 10000 | tf_op jit(solution)/shard_map/pallas_call | solution.py:141
  605.6 43.3 %shard_map.330.refs_0_ = f32[160,768]{1,0:T(8,128)} custom-call(bf16[8,2,2,160,768]{4,3,2,1,0:T(8,128)(2,1)} %bitcast.89), custom_call_target="tpu_custom_call" | custom-call | flops 1200000000 | bytes 10000 | tf_op jit(solution)/shard_map/pallas_call | solution.py:1614
  648.9 6.4 shard_map.332
  655.3 2.1 shard_map.331
  (122 shorter events, 24.8 us)
Async XLA Ops:
  8.4 159.5 %copy-start.32 = (f32[3]{0:T(128)}, f32[3]{0:T(128)S(1)}, u32[]{:S(2)}) copy-start(f32[3]{0:T(128)S(1)} %get-tuple-element.281) | copy-start | bytes 40
  9.2 7.5 %collective-permute-start = (bf16[3,768]{1,0:T(4,128)(2,1)S(1)}, bf16[3,768]{1,0:T(4,128)(2,1)S(1)}, u32[]{:S(2)}, u32[]{:S(2)}) collective-permute-start(bf16[3,768]{1,0:T(4,128)(2,1)S(1)} %bitcast_multiply_fusion.2), channel_id=1, source_target_pairs={{0,4},{4,8},{8,12},{12,16},{16,20},{20,24},{24,28},{1,5},{5,9},{9,... | collective-permute-start | bytes 13832 | tf_op jit(solution)/shard_map/ppermute | solution.py:58
  16.6 4.7 copy-start.31
  16.6 5.3 copy-start.17
  16.6 6.5 copy-start.28
  16.6 7.1 %copy-start.15 = (bf16[2,1536,80]{1,2,0:T(8,128)(2,1)S(1)}, bf16[2,1536,80]{1,2,0:T(8,128)(2,1)}, u32[]{:S(2)}) copy-start(bf16[2,1536,80]{1,2,0:T(8,128)(2,1)} %param.27) | copy-start | bytes 1474564
  16.6 47.0 %all-to-all-start = ((bf16[4,768,384]{2,1,0:T(8,128)(2,1)}), bf16[4,768,384]{2,1,0:T(8,128)(2,1)}, u32[]{:S(2)}, u32[]{:S(2)}) async-start(bf16[4,768,384]{2,1,0:T(8,128)(2,1)} %shard_map.306), calls=%async_computation | async-start | bytes 4718592 | tf_op jit(solution)/shard_map/all_to_all | solution.py:1347
  21.3 3.5 copy-start.29
  63.6 4.7 copy-start.30
  63.6 5.3 copy-start.27
  63.6 5.9 copy-start.21
  63.7 29.9 %all-to-all-start.1 = ((bf16[4,384,768]{2,1,0:T(8,128)(2,1)}), bf16[4,384,768]{2,1,0:T(8,128)(2,1)}, u32[]{:S(2)}, u32[]{:S(2)}) async-start(bf16[4,384,768]{2,1,0:T(8,128)(2,1)} %get-tuple-element.165), calls=%async_computation.1 | async-start | bytes 4718592 | tf_op jit(solution)/shard_map/all_to_all | solution.py:1347
  167.9 8.9 %collective-permute-start.1 = (f32[3,1536]{1,0:T(4,128)S(1)}, f32[3,1536]{1,0:T(4,128)S(1)}, u32[]{:S(2)}, u32[]{:S(2)}) collective-permute-start(f32[3,1536]{1,0:T(4,128)S(1)} %fusion.7), channel_id=1, source_target_pairs={{0,4},{4,8},{8,12},{12,16},{16,20},{20,24},{24,28},{1,5},{5,9},{9,... | collective-permute-start | bytes 55304 | tf_op jit(solution)/shard_map/ppermute | solution.py:58
  176.8 0.6 copy-start.24
  203.9 5.1 copy-start.18
  203.9 30.1 %all-to-all-start.2 = ((bf16[4,384,768]{2,1,0:T(8,128)(2,1)}), bf16[4,384,768]{2,1,0:T(8,128)(2,1)}, u32[]{:S(2)}, u32[]{:S(2)}) async-start(bf16[4,384,768]{2,1,0:T(8,128)(2,1)} %get-tuple-element.184), calls=%async_computation.2 | async-start | bytes 4718592 | tf_op jit(solution)/shard_map/all_to_all | solution.py:1347
  209.1 17.1 %copy-start.4 = (bf16[320,256]{1,0:T(8,128)(2,1)S(1)}, bf16[320,256]{1,0:T(8,128)(2,1)}, u32[]{:S(2)}) copy-start(bf16[320,256]{1,0:T(8,128)(2,1)} %get-tuple-element.177.fill_ref) | copy-start | bytes 491524
  327.9 5.1 copy-start.1
  327.9 5.2 copy-start.16
  327.9 44.1 %all-to-all-start.3 = ((bf16[4,768,384]{2,1,0:T(8,128)(2,1)}), bf16[4,768,384]{2,1,0:T(8,128)(2,1)}, u32[]{:S(2)}, u32[]{:S(2)}) async-start(bf16[4,768,384]{2,1,0:T(8,128)(2,1)} %get-tuple-element.238), calls=%async_computation.3 | async-start | bytes 4718592 | tf_op jit(solution)/shard_map/all_to_all | solution.py:1347
  332.9 1.2 copy-start.14
  332.9 1.3 copy-start.13
  332.9 1.3 copy-start.23
  332.9 1.4 copy-start.22
  334.3 0.6 copy-start.10
  372.0 4.6 copy-start.33
  372.0 157.2 %all-to-all-start.4 = ((bf16[4,384,768]{2,1,0:T(8,128)(2,1)}), bf16[4,384,768]{2,1,0:T(8,128)(2,1)}, u32[]{:S(2)}, u32[]{:S(2)}) async-start(bf16[4,384,768]{2,1,0:T(8,128)(2,1)} %get-tuple-element.239), calls=%async_computation.4 | async-start | bytes 4718592 | tf_op jit(solution)/shard_map/all_to_all | solution.py:1347
  376.5 278.8 %reduce-scatter.2.cloned.1.call-start = ((), (), s32[]{:S(2)}) async-start(), calls=%async_computation.7 | async-start | bytes 8110080 | tf_op jit(solution)/shard_map/reduce_scatter | solution.py:1949
  404.2 10.6 %copy-start.11 = (bf16[256,16]{1,0:T(8,128)(2,1)S(1)}, bf16[256,16]{1,0:T(8,128)(2,1)}, u32[]{:S(2)}) copy-start(bf16[256,16]{1,0:T(8,128)(2,1)} %copy-done.10) | copy-start | bytes 24580
  404.2 10.6 %copy-start.20 = (bf16[256,768]{1,0:T(8,128)(2,1)S(1)}, bf16[256,768]{1,0:T(8,128)(2,1)}, u32[]{:S(2)}) copy-start(bf16[256,768]{1,0:T(8,128)(2,1)} %get-tuple-element.211) | copy-start | bytes 1179652
  413.3 5.9 collective-permute-start.2
  419.2 0.6 copy-start.26
  432.8 1.1 copy-start
  432.8 1.4 copy-start.2
  432.8 1.6 copy-start.7
  433.9 1.0 copy-start.12
  434.0 1.2 copy-start.5
  494.3 3.8 copy-start.3
  495.5 2.6 copy-start.8
  529.2 5.7 copy-start.6
  529.2 119.7 %all-to-all-start.5 = ((bf16[4,1536,384]{2,1,0:T(8,128)(2,1)}), bf16[4,1536,384]{2,1,0:T(8,128)(2,1)}, u32[]{:S(2)}, u32[]{:S(2)}) async-start(bf16[4,1536,384]{2,1,0:T(8,128)(2,1)} %get-tuple-element.263), calls=%async_computation.6 | async-start | bytes 9437184 | tf_op jit(solution)/shard_map/all_to_all | solution.py:1347
  562.7 11.0 %copy-start.9 = (bf16[256,16]{1,0:T(8,128)(2,1)S(1)}, bf16[256,16]{1,0:T(8,128)(2,1)}, u32[]{:S(2)}) copy-start(bf16[256,16]{1,0:T(8,128)(2,1)} %copy-done.8) | copy-start | bytes 24580
  562.7 11.0 %copy-start.19 = (bf16[256,768]{1,0:T(8,128)(2,1)S(1)}, bf16[256,768]{1,0:T(8,128)(2,1)}, u32[]{:S(2)}) copy-start(bf16[256,768]{1,0:T(8,128)(2,1)} %get-tuple-element.247) | copy-start | bytes 1179652
  571.8 19.6 %collective-permute-start.3 = (f32[3,1536]{1,0:T(4,128)}, f32[3,1536]{1,0:T(4,128)S(1)}, u32[]{:S(2)}, u32[]{:S(2)}) collective-permute-start(f32[3,1536]{1,0:T(4,128)} %get-tuple-element.243), channel_id=1, source_target_pairs={{4,0},{8,4},{12,8},{16,12},{20,16},{24,20},{28,24},{5,1},{9,5},{13... | collective-permute-start | bytes 55304 | tf_op jit(solution)/shard_map/ppermute | solution.py:58
  591.4 0.6 copy-start.25
Sparse Core Ops, SparseCore 0:
  433.0 145.4 reduce-scatter.1
